TPU v7x, 32 devices: a whole 2x2x4 slice. The times are simulated.
32 devices in a mesh: group: 4 (over y, x), shard: 8 (over z, core).
Axes of the slice: x: 2, y: 2, z: 4, core: 2. Of those that a mesh axis runs over, the one named last changes fastest.
Arguments:
- step_count: int32 [1], replicated, may hold values from 2 to 8
- block_order: int32 [224], replicated, may hold values from 0 to 223, as said below
- saved_tiles: bfloat16 [32, 4, 18, 18, 256], P(('group', 'shard')), may hold values from -6 to 6
- pre_act: bfloat16 [16384, 256], P(('group', 'shard')), may hold values from -6 to 6
- grad_output: bfloat16 [16384, 256], P(('group', 'shard')), may hold values from -0.09375 to 0.09375
- pointwise_live: bfloat16 [256, 256], replicated, may hold values from -0.375 to 0.375
- master_rows: float32 [7168, 256], P('shard'), may hold values from -0.25 to 0.25, as said below
- row_moment: float32 [7168], P('shard'), may hold values from 0.5 to 30, as said below
- col_moment: float32 [2, 256], replicated, may hold values from 0.03 to 0.3
- next_tiles: bfloat16 [32, 4, 18, 18, 256], P(('group', 'shard')), may hold values from -6 to 6
Outputs:
- update_rows: float32 [7168, 256], P('shard')
- new_master: float32 [7168, 256], P('shard')
- new_row_moment: float32 [7168], P('shard')
- new_col_moment: float32 [2, 256], replicated
- next_output: bfloat16 [16384, 256], P(('group', 'shard'))
Inputs may be any that keep to these rules, and one draw needn't show every extreme that they name: `block_order`: a permutation of 0 to 223. `master_rows`: rows of the 3x3x3 kernel are of order (6912) ** -0.5 and rows of the 1x1x1 kernel of order 256 ** -0.5. `row_moment`: positive row factors.
All inputs are finite; a program needn't handle non-finite values.
Results may differ from a plain program's by a relative error of at most 0.023.
Values may be sent and summed in bfloat16 or wider, within the bound.
No kernel may reach another device: no remote copies, remote signals or barrier semaphores. Data moves between devices by JAX's collectives and lax.ppermute only.
A program may use at most 64 MiB of HBM per device.

v0:
```python
import jax
import jax.numpy as jnp
from jax import lax
from jax.sharding import PartitionSpec as P

CI = 256
CO = 256
BLK = 32
FR = 2
HW = 16
NB3 = 216
NB = 224


learn_rate = 0.002
decay_power = 0.8


def silu_slope(values):
    sigma = jax.nn.sigmoid(values)
    return sigma * (1.0 + values * (1.0 - sigma))


def tap_views(frames):
    views = []
    for frame_off in range(3):
        for row_off in range(3):
            for col_off in range(3):
                window = frames[
                    frame_off : frame_off + FR, row_off : row_off + HW, col_off : col_off + HW, :
                ]
                views.append(window.reshape(FR * HW * HW, CI))
    return views


def contract_rows(left, right):
    return lax.dot_general(
        left, right, (((0,), (0,)), ((), ())), preferred_element_type=jnp.float32
    )


def kernel_sums(values, is_small):
    large_part = jnp.sum(jnp.where(is_small[:, None], 0.0, values), axis=0)
    small_part = jnp.sum(jnp.where(is_small[:, None], values, 0.0), axis=0)
    return jnp.stack([large_part, small_part])


def shards(
    step_count,
    block_order,
    saved_tiles,
    pre_act,
    grad_output,
    pointwise_live,
    master_rows,
    row_moment,
    col_moment,
    next_tiles,
):
    pre_float = pre_act.astype(jnp.float32)
    activation = jax.nn.silu(pre_float).astype(jnp.bfloat16)
    grad_act = lax.dot_general(
        grad_output, pointwise_live, (((1,), (1,)), ((), ())), preferred_element_type=jnp.float32
    )
    grad_pre = (grad_act * silu_slope(pre_float)).astype(jnp.bfloat16)
    pieces = [contract_rows(view, grad_pre) for view in tap_views(saved_tiles[0])]
    pieces.append(contract_rows(activation, grad_output))
    own_term = jnp.concatenate(pieces, axis=0).astype(jnp.bfloat16)
    total_rows = NB * BLK
    stored = jnp.take(own_term.reshape(NB, BLK, CO), block_order, axis=0).reshape(total_rows, CO)
    own_rows = master_rows.shape[0]
    partial_value = lax.psum_scatter(stored, "shard", scatter_dimension=0, tiled=True).astype(
        jnp.float32
    )
    gradient = lax.psum(partial_value, "group")
    owner = lax.axis_index("shard")
    own_count = own_rows // BLK
    own_blocks = lax.dynamic_slice_in_dim(block_order, owner * own_count, own_count)
    is_small = jnp.repeat(own_blocks >= NB3, BLK, total_repeat_length=own_rows)
    decay_rate = 1.0 - step_count.astype(jnp.float32)[0] ** (-decay_power)
    counts = jnp.array([27 * CI, CO], jnp.float32)
    squares = gradient * gradient
    new_row = decay_rate * row_moment + (1.0 - decay_rate) * jnp.mean(squares, axis=1)
    col_part = kernel_sums(squares, is_small)
    row_part = kernel_sums(new_row[:, None], is_small)[:, 0]
    weighted = kernel_sums(squares / new_row[:, None], is_small)
    col_total, weight_total, row_total = lax.psum((col_part, weighted, row_part), "shard")
    new_col = decay_rate * col_moment + (1.0 - decay_rate) * col_total / counts[:, None]
    row_mean = row_total / counts
    col_rows = jnp.where(is_small[:, None], new_col[1], new_col[0])
    mean_rows = jnp.where(is_small, row_mean[1], row_mean[0])
    scaled = gradient / jnp.sqrt(new_row[:, None] * col_rows / mean_rows[:, None])
    square_total = row_mean * jnp.sum(weight_total / new_col, axis=1)
    clip_factor = jnp.maximum(1.0, jnp.sqrt(square_total / (counts * CO)))
    update_rows = scaled / jnp.where(is_small, clip_factor[1], clip_factor[0])[:, None]
    new_master = master_rows - learn_rate * update_rows
    weights_low = new_master.astype(jnp.bfloat16)
    gathered = lax.all_gather(weights_low, "shard", axis=0, tiled=True)
    inverse = jnp.zeros((NB,), jnp.int32).at[block_order].set(jnp.arange(NB, dtype=jnp.int32))
    natural = jnp.take(gathered.reshape(NB, BLK, CO), inverse, axis=0).reshape(total_rows, CO)
    spatial = natural[: 27 * CI].reshape(27, CI, CO)
    pointwise = natural[27 * CI :]
    hidden_sum = jnp.zeros((FR * HW * HW, CO), jnp.float32)
    for index_tap, view in enumerate(tap_views(next_tiles[0])):
        hidden_sum = hidden_sum + jnp.dot(
            view, spatial[index_tap], preferred_element_type=jnp.float32
        )
    hidden_act = jax.nn.silu(hidden_sum).astype(jnp.bfloat16)
    next_output = jnp.dot(hidden_act, pointwise, preferred_element_type=jnp.float32).astype(
        jnp.bfloat16
    )
    return (update_rows, new_master, new_row, new_col, next_output)


def solution(mesh):
    in_specs = (
        P(),
        P(),
        P(("group", "shard"), None, None, None, None),
        P(("group", "shard"), None),
        P(("group", "shard"), None),
        P(),
        P("shard", None),
        P("shard"),
        P(),
        P(("group", "shard"), None, None, None, None),
    )
    out_specs = (P("shard", None), P("shard", None), P("shard"), P(), P(("group", "shard"), None))
    return jax.shard_map(shards, mesh=mesh, in_specs=in_specs, out_specs=out_specs, check_vma=False)
```

profile of v0, /device:TPU:0, one launch (start us, length us, event | category | flops | bytes accessed | tf_op | source)
XLA Modules:
  0.0 234.2 jit_solution(2477971597655722326)
XLA Ops:
  7.2 1.3 copy.106
  11.0 0.9 fusion.16
  11.9 0.9 fusion.18
  16.6 0.9 fusion.28
  18.4 0.9 fusion.32
  24.0 0.9 fusion.44
  25.0 0.9 fusion.46
  29.6 0.9 fusion.56
  34.3 0.9 fusion.66
  35.2 1.0 fusion.12
  36.3 4.9 %gather_fusion = bf16[224,32,256]{2,1,0:T(8,128)(2,1)} fusion(bf16[224,32,256]{2,1,0:T(8,128)(2,1)} %bitcast.55, s32[1024]{0:T(1024)S(1)} %pad_clamp_fusion.1), kind=kCustom, calls=%fused_computation.clone | custom fusion | bytes 7340928 | tf_op jit(solution)/shard_map/jit(_take)/gather | solution.py:70
  41.1 3.8 %broadcast_select_fusion.1 = bf16[224,32,256]{2,1,0:T(8,128)(2,1)} fusion(bf16[224,32,256]{2,1,0:T(8,128)(2,1)} %gather_fusion, pred[224]{0:T(512)(128)(4,1)S(1)} %compare_and_fusion.1), kind=kLoop, calls=%fused_computation.4 | loop fusion | flops 1835008 | bytes 7340256 | tf_op jit(solution)/shard_map/jit(_take)/select_n | solution.py:70
  47.4 4.5 %select_reduce_fusion.4 = (pred[896]{0:T(1024)(128)(4,1)S(1)}, pred[896]{0:T(1024)(128)(4,1)S(1)}, pred[896]{0:T(1024)(128)(4,1)S(1)}, pred[896]{0:T(1024)(128)(...) fusion(pred[]{:T(512)} %bitcast.81, ...), kind=kLoop, calls=%fused_computation.151 | loop fusion | flops 31360 | bytes 26887 | tf_op jit(solution)/shard_map/jit(_take)/gather | solution.py:79
  51.9 41.0 %reduce-scatter.2.cloned.1.call-done = bf16[896,256]{1,0:T(8,128)(2,1)} async-done(((bf16[7168,256]{1,0:T(8,128)(2,1)}), bf16[896,256]{1,0:T(8,128)(2,1)}) %reduce-scatter.2.cloned.1.call-update) | async-done | bytes 458768 | tf_op jit(solution)/shard_map/reduce_scatter | solution.py:72
  92.9 35.3 %all-reduce.2 = f32[896,256]{1,0:T(8,128)S(1)} all-reduce(bf16[896,256]{1,0:T(8,128)(2,1)} %reduce-scatter.2.cloned.1.call-done), channel_id=1, replica_groups=mesh['group'=4,'shard'=8] {'group'}, use_global_device_ids=true, to_apply=%region_1.3 | all-reduce | flops 229376 | bytes 1376256 | tf_op jit(solution)/shard_map/psum | solution.py:75
  128.4 13.9 %select_reduce_fusion.6 = (f32[]{:T(128)}, f32[]{:T(128)}, f32[896]{0:T(1024)S(1)}, pred[896]{0:T(1024)(128)(4,1)S(1)}) fusion(f32[896]{0:T(1024)S(1)} %multiply_reduce_fusion, f32[]{:T(128)S(6)} %mul.75, f32[896]{0:T(1024)S(1)} %copy-done.26, f32[]{:T(128)} %bitcast.57, pred[896]{0:T(1024)(128)(4,1)S(1)} %get-tuple-element.47, ...), kind=kLoop, calls=%fused_computation.185 | loop fusion | flops 33150 | bytes 35009 | tf_op jit(solution)/shard_map/reduce_sum | solution.py:43
  142.7 1.4 maximum_bitcast_fusion
  144.1 16.7 %all-reduce = (f32[2]{0:T(128)S(1)}, f32[2,256]{1,0:T(2,128)S(1)}, f32[2,256]{1,0:T(2,128)S(1)}) all-reduce(f32[2]{0:T(128)S(1)} %maximum_bitcast_fusion, f32[2,256]{1,0:T(2,128)S(1)} %get-tuple-element.181, f32[2,256]{1,0:T(2,128)S(1)} %get-tuple-element.180), channel_id=1, replica_groups=mesh['group'=4,'shard'=8] {'shard'}, use_global_device_ids=true, to_apply=%region_8.10 | all-reduce | flops 1026 | bytes 8208 | tf_op jit(solution)/shard_map/psum | solution.py:87
  162.2 2.6 %broadcast_select_fusion.3 = (f32[896]{0:T(1024)S(1)}, f32[896]{0:T(1024)S(1)}) fusion(pred[896]{0:T(1024)(128)(4,1)S(1)} %get-tuple-element.59, f32[]{:T(128)} %bitcast.96, f32[]{:T(128)} %bitcast.95, f32[]{:T(128)} %bitcast.100, f32[]{:T(128)} %bitcast.99), kind=kLoop, calls=%fused_computation.195 | loop fusion | flops 1792 | bytes 8080 | tf_op jit(solution)/shard_map/jit(_where)/select_n | solution.py:91
  164.8 2.0 fusion.89
  166.9 1.5 scatter_custom_fusion
  168.5 1.4 fusion.94
  170.0 2.1 fusion.93
  172.0 34.5 %all-gather.2.cloned.1.call-done = bf16[7168,256]{1,0:T(8,128)(2,1)} async-done(((bf16[896,256]{1,0:T(8,128)(2,1)}), bf16[7168,256]{1,0:T(8,128)(2,1)}) %all-gather.2.cloned.1.call-update) | async-done | bytes 3670032 | tf_op jit(solution)/shard_map/all_gather | solution.py:98
  206.5 4.9 %gather_fusion.1 = bf16[224,32,256]{2,1,0:T(8,128)(2,1)} fusion(bf16[224,32,256]{2,1,0:T(8,128)(2,1)} %bitcast.447, s32[1024]{0:T(1024)S(1)} %pad_clamp_fusion), kind=kCustom, calls=%fused_computation.1.clone | custom fusion | bytes 7340928 | tf_op jit(solution)/shard_map/jit(_take)/gather | solution.py:100
  211.4 2.5 %broadcast_select_fusion = bf16[224,32,256]{2,1,0:T(8,128)(2,1)S(1)} fusion(bf16[224,32,256]{2,1,0:T(8,128)(2,1)} %gather_fusion.1, pred[224]{0:T(512)(128)(4,1)S(1)} %compare_and_fusion), kind=kLoop, calls=%fused_computation.3 | loop fusion | flops 1835008 | bytes 7340256 | tf_op jit(solution)/shard_map/jit(_take)/select_n | solution.py:100
  214.0 1.0 fusion.91
  216.6 1.0 convolution_bitcast_fusion.6
  217.6 1.0 convolution_bitcast_fusion.7
  218.7 1.0 convolution_bitcast_fusion.8
  223.5 1.1 fusion.10
  224.5 2.9 %convolution_convert_fusion = bf16[512,256]{1,0:T(8,128)(2,1)} fusion(bf16[256,256]{1,0:T(8,128)(2,1)} %bitcast.502, f32[512,256]{1,0:T(8,128)S(1)} %convolution_bitcast_fusion, f32[512,256]{1,0:T(8,128)S(1)} %convolution_bitcast_fusion.1, f32[512,256]{1,0:T(8,128)S(1)} %convolution_bitcast_fusion.2, f32[512,256]{1,0:T(8,128)S(1)} %convolution_bitcast_fusion.3, ...), kind=kOutput, calls=%fused_computation.43 | convolution fusion | flops 136314880 | bytes 6029312 | tf_op jit(solution)/shard_map/dot_general | solution.py:109
  (136 shorter events, 28.1 us)
Async XLA Ops:
  7.2 2.3 copy-start
  7.2 85.7 %reduce-scatter.2.cloned.1.call-start = ((), (), s32[]{:S(2)}) async-start(), calls=%async_computation.1 | async-start | bytes 4128768 | tf_op jit(solution)/shard_map/reduce_scatter | solution.py:72
  44.9 2.4 %copy-start.24 = (s32[7,128]{1,0:T(8,128)S(1)}, s32[7,128]{1,0:T(8,128)}, u32[]{:S(2)}) copy-start(s32[7,128]{1,0:T(8,128)} %constant.130.clone.1) | copy-start | bytes 10756
  44.9 83.5 %copy-start.26 = (f32[896]{0:T(1024)S(1)}, f32[896]{0:T(1024)}, u32[]{:S(2)}) copy-start(f32[896]{0:T(1024)} %param.22) | copy-start | bytes 10756
  44.9 115.9 %copy-start.27 = (f32[2,256]{1,0:T(2,128)S(1)}, f32[2,256]{1,0:T(2,128)}, u32[]{:S(2)}) copy-start(f32[2,256]{1,0:T(2,128)} %param.23) | copy-start | bytes 6148
  44.9 115.9 %copy-start.28 = (f32[2]{0:T(128)S(1)}, f32[2]{0:T(128)}, u32[]{:S(2)}) copy-start(f32[2]{0:T(128)} %constant.144) | copy-start | bytes 28
  44.9 116.1 %copy-start.30 = (f32[2]{0:T(128)S(1)}, f32[2]{0:T(128)}, u32[]{:S(2)}) copy-start(f32[2]{0:T(128)} %constant.147) | copy-start | bytes 28
  44.9 119.9 %copy-start.21 = (f32[896,256]{1,0:T(8,128)S(1)}, f32[896,256]{1,0:T(8,128)}, u32[]{:S(2)}) copy-start(f32[896,256]{1,0:T(8,128)} %param.21) | copy-start | bytes 2752516
  44.9 161.6 %all-gather.2.cloned.1.call-start = ((), (), s32[]{:S(2)}) async-start(), calls=%async_computation.2 | async-start | bytes 4128768 | tf_op jit(solution)/shard_map/all_gather | solution.py:98
  128.2 40.2 %copy-start.22 = (bf16[1,4,18,18,256]{4,1,3,2,0:T(4,128)(2,1)S(1)}, bf16[1,4,18,18,256]{4,1,3,2,0:T(4,128)(2,1)}, u32[]{:S(2)}) copy-start(bf16[1,4,18,18,256]{4,1,3,2,0:T(4,128)(2,1)} %param.24) | copy-start | bytes 1990660
  142.3 27.7 %copy-start.23 = (f32[896]{0:T(1024)}, f32[896]{0:T(1024)S(1)}, u32[]{:S(2)}) copy-start(f32[896]{0:T(1024)S(1)} %get-tuple-element.58) | copy-start | bytes 10756
  161.0 9.0 %copy-start.25 = (f32[2,256]{1,0:T(2,128)}, f32[2,256]{1,0:T(2,128)S(1)}, u32[]{:S(2)}) copy-start(f32[2,256]{1,0:T(2,128)S(1)} %get-tuple-element.57) | copy-start | bytes 6148
  214.9 1.4 copy-start.4
  214.9 1.7 copy-start.3
  214.9 2.7 %copy-start.2 = (bf16[2,16,16,256]{3,2,1,0:T(8,128)(2,1)S(1)}, bf16[2,16,16,256]{3,2,1,0:T(8,128)(2,1)}, u32[]{:S(2)}) copy-start(bf16[2,16,16,256]{3,2,1,0:T(8,128)(2,1)} %get-tuple-element.96) | copy-start | bytes 786436
  215.2 3.5 %copy-start.1 = (bf16[2,16,16,256]{3,2,1,0:T(8,128)(2,1)S(1)}, bf16[2,16,16,256]{3,2,1,0:T(8,128)(2,1)}, u32[]{:S(2)}) copy-start(bf16[2,16,16,256]{3,2,1,0:T(8,128)(2,1)} %get-tuple-element.97) | copy-start | bytes 786436
  215.4 4.3 %copy-start.20 = (bf16[2,16,16,256]{3,2,1,0:T(8,128)(2,1)S(1)}, bf16[2,16,16,256]{3,2,1,0:T(8,128)(2,1)}, u32[]{:S(2)}) copy-start(bf16[2,16,16,256]{3,2,1,0:T(8,128)(2,1)} %get-tuple-element.113) | copy-start | bytes 786436
  215.9 4.1 %copy-start.19 = (bf16[2,16,16,256]{3,2,1,0:T(8,128)(2,1)S(1)}, bf16[2,16,16,256]{3,2,1,0:T(8,128)(2,1)}, u32[]{:S(2)}) copy-start(bf16[2,16,16,256]{3,2,1,0:T(8,128)(2,1)} %get-tuple-element.112) | copy-start | bytes 786436
  216.1 4.1 %copy-start.18 = (bf16[2,16,16,256]{3,2,1,0:T(8,128)(2,1)S(1)}, bf16[2,16,16,256]{3,2,1,0:T(8,128)(2,1)}, u32[]{:S(2)}) copy-start(bf16[2,16,16,256]{3,2,1,0:T(8,128)(2,1)} %get-tuple-element.111) | copy-start | bytes 786436
  216.6 3.9 %copy-start.17 = (bf16[2,16,16,256]{3,2,1,0:T(8,128)(2,1)S(1)}, bf16[2,16,16,256]{3,2,1,0:T(8,128)(2,1)}, u32[]{:S(2)}) copy-start(bf16[2,16,16,256]{3,2,1,0:T(8,128)(2,1)} %get-tuple-element.110) | copy-start | bytes 786436
  217.6 3.1 %copy-start.16 = (bf16[2,16,16,256]{3,2,1,0:T(8,128)(2,1)S(1)}, bf16[2,16,16,256]{3,2,1,0:T(8,128)(2,1)}, u32[]{:S(2)}) copy-start(bf16[2,16,16,256]{3,2,1,0:T(8,128)(2,1)} %get-tuple-element.109) | copy-start | bytes 786436
  219.7 1.3 copy-start.14
  220.0 1.3 copy-start.12
  220.2 1.3 copy-start.15
  220.5 1.3 copy-start.13
  220.7 1.3 copy-start.11
  221.0 1.3 copy-start.10
  221.2 1.3 copy-start.9
  221.5 1.3 copy-start.8
  221.7 1.2 copy-start.7
  222.0 1.2 copy-start.6
  222.2 1.2 copy-start.5
  (3 other events, 2.6 us)
Sparse Core Ops, SparseCore 0:
  45.1 47.7 reduce-scatter.1
  167.0 39.4 all-gather.1
where the time goes:
time: 235 us; the launch traced here: 234 us
  waiting for transfers between devices  75.5 us (32%)
  blocking collectives  52 us (22%)
  matrix products  38.5 us (16%)
  other arithmetic  31.7 us (13%)
  local copies, waits for them, and re-layouts  21 us (9%)
  between operations  15.6 us (7%)
    reduce_scatter x1, waiting for transfers between devices, shards(): lax.psum_scatter(stored, 'shard', scatter_dimension=0, tiled=True)  41 us
    psum x1, blocking collectives, shards(): gradient = lax.psum(partial_value, 'group')  35.3 us
    all_gather x1, waiting for transfers between devices, shards(): gathered = lax.all_gather(weights_low, 'shard', axis=0, tiled=True)  34.5 us
    dot_general x28, matrix products, contract_rows(): lax.dot_general(left, right, (((0,), (0,)), ((), ())), preferred_element_...  26.2 us
    psum x1, blocking collectives, shards(): lax.psum((col_part, weighted, row_part), 'shard')  16.7 us
    reduce_sum x2, other arithmetic, kernel_sums(): large_part = jnp.sum(jnp.where(is_small[:, None], 0.0, values), axis=0)  14.3 us
    dot_general x26, matrix products, shards(): jnp.dot(view, spatial[index_tap], preferred_element_type=jnp.float32)  9.1 us
    gather x1, local copies, waits for them, and re-layouts, shards(): jnp.take(own_term.reshape(NB, BLK, CO), block_order, axis=0)  4.88 us
  transfers between devices with their start and end apart: 2, of which 2 were waited for; matrix products, arithmetic and copies ran while one was open for 5% of the time, Pallas kernels for 0%

commit v1 on v0

--- a/solution.py
+++ b/solution.py
@@ -1,6 +1,9 @@
+import functools
 import jax
 import jax.numpy as jnp
 from jax import lax
+from jax.experimental import pallas as pl
+from jax.experimental.pallas import tpu as pltpu
 from jax.sharding import PartitionSpec as P
 
 CI = 256
@@ -45,7 +48,7 @@
     return jnp.stack([large_part, small_part])
 
 
-def shards(
+def general_shards(
     step_count,
     block_order,
     saved_tiles,
@@ -112,6 +115,361 @@
     return (update_rows, new_master, new_row, new_col, next_output)
 
 
+AXES = ("group", "shard")
+SLOTS = 14
+HALF = 7
+PIX = FR * HW * HW
+SHIFTED = (FR + 2) * (HW + 2) * HW
+LOW = jnp.bfloat16
+WIDE = jnp.float32
+VMEM = pl.BlockSpec(memory_space=pltpu.VMEM)
+SMEM = pl.BlockSpec(memory_space=pltpu.SMEM)
+HBM = pl.BlockSpec(memory_space=pl.ANY)
+MASK_CORE, MASK_X, MASK_Y = 1, 8, 16
+
+
+def swap(value, mask):
+    return lax.ppermute(value, AXES, [(at, at ^ mask) for at in range(32)])
+
+
+def call(kernel, outs, in_specs, out_specs=None, scratch=(), flops=0, moved=0):
+    return pl.pallas_call(
+        kernel,
+        out_shape=[jax.ShapeDtypeStruct(shape, dtype) for shape, dtype in outs],
+        in_specs=in_specs,
+        out_specs=[VMEM] * len(outs) if out_specs is None else out_specs,
+        scratch_shapes=list(scratch),
+        compiler_params=pltpu.CompilerParams(vmem_limit_bytes=44 << 20),
+        cost_estimate=pl.CostEstimate(flops=flops, bytes_accessed=moved, transcendentals=0),
+    )
+
+
+def store_shifted(tile, out):
+    for col_off in range(3):
+        out[col_off] = tile[:, :, col_off : col_off + HW, :].reshape(SHIFTED, CI)
+
+
+def shift_kernel(tile, out):
+    store_shifted(tile, out)
+
+
+def slope_of(pre, grad, pointwise):
+    grad_act = lax.dot_general(
+        grad, pointwise, (((1,), (1,)), ((), ())), preferred_element_type=WIDE
+    )
+    return (grad_act * silu_slope(pre.astype(WIDE))).astype(LOW)
+
+
+def term_kernel(
+    at, tile, tile_peer, pre, pre_peer, grad, grad_peer, pointwise,
+    keep_a, send_a, keep_b, send_b, views, slopes, acts, grads, staged,
+):
+    axis_x, axis_y, core = at[0], at[1], at[3]
+    store_shifted(tile, views.at[0])
+    store_shifted(tile_peer, views.at[1])
+    slopes[:PIX] = slope_of(pre[...], grad[...], pointwise[...])
+    slopes[PIX:] = slope_of(pre_peer[...], grad_peer[...], pointwise[...])
+
+    def put(slot, total):
+        value = total.astype(LOW)
+        if slot < HALF:
+            for mine in range(2):
+
+                @pl.when(axis_x == mine)
+                def _():
+                    keep_a[slot] = value[mine * 128 : mine * 128 + 128]
+                    send_a[slot] = value[128 - mine * 128 : 256 - mine * 128]
+        else:
+            for mine in range(2):
+
+                @pl.when(axis_y == mine)
+                def _():
+                    for half in range(2):
+                        base, other = half * 128 + mine * 64, half * 128 + 64 - mine * 64
+                        to = slice(half * 64, half * 64 + 64)
+                        keep_b[slot - HALF, to] = value[base : base + 64]
+                        send_b[slot - HALF, to] = value[other : other + 64]
+
+    def tap_rows(tap):
+        frame_off, row_off, col_off = tap // 9, lax.rem(tap // 3, 3), lax.rem(tap, 3)
+        parts = []
+        for peer in range(2):
+            for frame in range(FR):
+                start = pl.multiple_of(((frame + frame_off) * (HW + 2) + row_off) * HW, HW)
+                parts.append(views[peer, col_off, pl.ds(start, HW * HW), :])
+        return jnp.concatenate(parts, axis=0)
+
+    for slot in range(SLOTS - 1):
+        put(slot, contract_rows(tap_rows(core * SLOTS + slot), slopes[...]))
+
+    @pl.when(core == 0)
+    def _():
+        staged[...] = contract_rows(tap_rows(SLOTS - 1), slopes[...])
+
+    @pl.when(core == 1)
+    def _():
+        acts[:PIX] = jax.nn.silu(pre[...].astype(WIDE)).astype(LOW)
+        acts[PIX:] = jax.nn.silu(pre_peer[...].astype(WIDE)).astype(LOW)
+        grads[:PIX] = grad[...]
+        grads[PIX:] = grad_peer[...]
+        staged[...] = contract_rows(acts[...], grads[...])
+
+    put(SLOTS - 1, staged[...])
+
+
+def second_kernel(at, keep_a, got_a, keep_b, got_b, next_a, send_a, next_b, send_b):
+    axis_x, axis_y = at[0], at[1]
+    for keep, got, mine, stay, send in (
+        (keep_a, got_a, axis_y, next_a, send_a),
+        (keep_b, got_b, axis_x, next_b, send_b),
+    ):
+        for which, out in ((mine, stay), (1 - mine, send)):
+            rows = pl.ds(pl.multiple_of(which * 64, 64), 64)
+            out[...] = (keep[:, rows].astype(WIDE) + got[:, rows].astype(WIDE)).astype(LOW)
+
+
+def third_kernel(at, keep_a, got_a, keep_b, got_b, own, *sends):
+    for away, out in enumerate((own,) + sends):
+        rows = pl.ds(pl.multiple_of((at[2] ^ away) * 16, 16), 16)
+        out[:HALF] = (keep_a[:, rows].astype(WIDE) + got_a[:, rows].astype(WIDE)).astype(LOW)
+        out[HALF:] = (keep_b[:, rows].astype(WIDE) + got_b[:, rows].astype(WIDE)).astype(LOW)
+
+
+def moment_kernel(at, rate, own, one, two, three, row_moment, scaled, message):
+    total = own[...].astype(WIDE) + one[...].astype(WIDE)
+    total = total + (two[...].astype(WIDE) + three[...].astype(WIDE))
+    total = total.reshape(SLOTS * 16, CO)
+    squares = total * total
+    decay = rate[0]
+    mean = jnp.sum(squares, axis=1, keepdims=True) * (1.0 / CO)
+    new_row = decay * row_moment[...] + (1.0 - decay) * mean
+    scaled[...] = (total * lax.rsqrt(new_row)).astype(LOW).reshape(SLOTS, 16, CO)
+    weighted = squares / new_row
+    cut = (SLOTS - 1) * 16
+    last_small = at[3] == 1
+    rows = []
+    for values in (squares, weighted, jnp.broadcast_to(new_row, (SLOTS * 16, CO))):
+        large = jnp.sum(values[:cut], axis=0, keepdims=True)
+        last = jnp.sum(values[cut:], axis=0, keepdims=True)
+        rows.append(large + jnp.where(last_small, 0.0, last))
+        rows.append(jnp.where(last_small, last, 0.0))
+    spread = jnp.broadcast_to(new_row, (SLOTS * 16, 128))
+    spread = jnp.concatenate([spread, jnp.zeros((32, 128), WIDE)], axis=0)
+    rows.append(jnp.transpose(spread)[:1])
+    rows.append(jnp.zeros((1, CO), WIDE))
+    message[...] = jnp.concatenate(rows, axis=0)
+
+
+def factor_kernel(rate, mine, peer, col_moment, new_col, factor):
+    total = jnp.sum(mine[...], axis=0) + jnp.sum(peer[...], axis=0)
+    decay = rate[0]
+    for kernel in range(2):
+        count = 27.0 * CI if kernel == 0 else float(CO)
+        col = decay * col_moment[kernel : kernel + 1] + (1.0 - decay) * (
+            total[kernel : kernel + 1] / count
+        )
+        row_mean = total[4 + kernel : 5 + kernel] / count
+        square = row_mean * jnp.sum(
+            total[2 + kernel : 3 + kernel] / col, axis=1, keepdims=True
+        )
+        clip = jnp.maximum(1.0, jnp.sqrt(square / (count * CO)))
+        new_col[kernel : kernel + 1] = col
+        factor[kernel : kernel + 1] = 1.0 / (jnp.sqrt(col / row_mean) * clip)
+
+
+def order_kernel(at, block_order, *refs):
+    pieces, out = refs[:-1], refs[-1]
+    count = NB // 8
+    for index, piece in enumerate(pieces):
+        flip_core, away = divmod(index, 4)
+        owner = (at[2] ^ away) * 2 + (at[3] ^ flip_core)
+
+        def move(local, carry, piece=piece, owner=owner):
+            block = block_order[owner * count + local]
+            to = pl.ds(pl.multiple_of(block * BLK, BLK), BLK)
+            out[to, :] = piece[pl.ds(pl.multiple_of(local * BLK, BLK), BLK), :]
+            return carry
+
+        lax.fori_loop(0, count, move, 0, unroll=4)
+
+
+def join_kernel(at, own, one, two, three, out_a, out_b):
+    for away, piece in enumerate((own, one, two, three)):
+        rows = pl.ds(pl.multiple_of((at[2] ^ away) * 16, 16), 16)
+        out_a[:, rows] = piece[:HALF]
+        out_b[:, rows] = piece[HALF:]
+
+
+def pair_kernel(at, mine_a, got_a, mine_b, got_b, out_a, out_b):
+    for which, mine, got, out in ((at[1], mine_a, got_a, out_a), (at[0], mine_b, got_b, out_b)):
+        out[:, pl.ds(pl.multiple_of(which * 64, 64), 64)] = mine[...]
+        out[:, pl.ds(pl.multiple_of(64 - which * 64, 64), 64)] = got[...]
+
+
+def finish_kernel(
+    at, block_order, factor, views, natural, master,
+    mine_a, got_a, mine_b, got_b, peer_a, peer_got_a, peer_b, peer_got_b,
+    update_rows, new_master, next_output, scaled, hidden, pointwise,
+):
+    axis_x, axis_y, core = at[0], at[1], at[3]
+    for index, (a_own, a_got, b_own, b_got) in enumerate(
+        ((mine_a, got_a, mine_b, got_b), (peer_a, peer_got_a, peer_b, peer_got_b))
+    ):
+        base = (core ^ index) * SLOTS
+        for which, piece in ((axis_x, a_own), (1 - axis_x, a_got)):
+            rows = pl.ds(pl.multiple_of(which * 128, 128), 128)
+            scaled[pl.ds(base, HALF), rows] = piece[...]
+        for which, piece in ((axis_y, b_own), (1 - axis_y, b_got)):
+            for half in range(2):
+                rows = pl.ds(pl.multiple_of(half * 128 + which * 64, 64), 64)
+                scaled[pl.ds(base + HALF, HALF), rows] = piece[:, half * 64 : half * 64 + 64]
+    large = learn_rate * factor[0:1]
+    total = jnp.zeros((PIX, CO), WIDE)
+    for tap in range(27):
+        frame_off, row_off, col_off = tap // 9, tap // 3 % 3, tap % 3
+        weights = natural[tap * CI : tap * CI + CI].astype(WIDE) - scaled[tap].astype(WIDE) * large
+        starts = [((frame + frame_off) * (HW + 2) + row_off) * HW for frame in range(FR)]
+        window = jnp.concatenate(
+            [views[col_off, start : start + HW * HW, :] for start in starts], axis=0
+        )
+        total = total + jnp.dot(window, weights.astype(LOW), preferred_element_type=WIDE)
+    small = learn_rate * factor[1:2]
+    weights = natural[27 * CI :].astype(WIDE) - scaled[27].astype(WIDE) * small
+    next_act = jax.nn.silu(total).astype(LOW)
+    next_output[...] = jnp.dot(
+        next_act, weights.astype(LOW), preferred_element_type=WIDE
+    ).astype(LOW)
+
+    owner = at[2] * 2 + core
+
+    def own_block(local, carry):
+        block = block_order[owner * (NB // 8) + local]
+        chosen = jnp.where(block >= NB3, factor[1:2], factor[0:1])
+        rows = pl.ds(pl.multiple_of(local * BLK, BLK), BLK)
+        start = pl.multiple_of(lax.rem(block, 8) * BLK, BLK)
+        update = scaled[block // 8, pl.ds(start, BLK), :].astype(WIDE) * chosen
+        update_rows[rows, :] = update
+        new_master[rows, :] = master[rows, :] - learn_rate * update
+        return carry
+
+    lax.fori_loop(0, NB // 8, own_block, 0, unroll=4)
+
+
+def shards(
+    step_count,
+    block_order,
+    saved_tiles,
+    pre_act,
+    grad_output,
+    pointwise_live,
+    master_rows,
+    row_moment,
+    col_moment,
+    next_tiles,
+):
+    group, shard = lax.axis_index("group"), lax.axis_index("shard")
+    axis_y, axis_x, axis_z, core = group // 2, group % 2, shard // 2, shard % 2
+    at = jnp.stack([axis_x, axis_y, axis_z, core]).astype(jnp.int32)
+    decay_rate = 1.0 - step_count.astype(WIDE) ** (-decay_power)
+
+    tile_peer = swap(saved_tiles, MASK_CORE)
+    pre_peer = swap(pre_act, MASK_CORE)
+    grad_peer = swap(grad_output, MASK_CORE)
+    part_a, part_b = (HALF, 128, CO), (HALF, 128, CO)
+    keep_a, send_a, keep_b, send_b = call(
+        term_kernel,
+        [(part_a, LOW), (part_a, LOW), (part_b, LOW), (part_b, LOW)],
+        [SMEM] + [VMEM] * 7,
+        scratch=[
+            pltpu.VMEM((2, 3, SHIFTED, CI), LOW),
+            pltpu.VMEM((2 * PIX, CO), LOW),
+            pltpu.VMEM((2 * PIX, CO), LOW),
+            pltpu.VMEM((2 * PIX, CO), LOW),
+            pltpu.VMEM((CI, CO), WIDE),
+        ],
+        flops=2 * 14 * 1024 * 256 * 256,
+        moved=6 << 20,
+    )(
+        at, saved_tiles[0], tile_peer[0], pre_act, pre_peer, grad_output, grad_peer, pointwise_live
+    )
+
+    master_low = master_rows.astype(LOW)
+    master_line = [master_low] + [swap(master_low, away * 2) for away in (1, 2, 3)]
+    master_all = master_line + [swap(piece, MASK_CORE) for piece in master_line]
+    natural = call(
+        order_kernel, [((NB * BLK, CO), LOW)], [SMEM] * 2 + [VMEM] * 8, moved=8 << 20
+    )(at, block_order, *master_all)[0]
+    moment_line = jnp.stack([row_moment] + [swap(row_moment, away * 2) for away in (1, 2, 3)])
+    moment_all = jnp.stack([moment_line, swap(moment_line, MASK_CORE)])
+    moment_stored = moment_all[jnp.arange(2) ^ core][:, jnp.arange(4) ^ axis_z]
+    moment_stored = jnp.swapaxes(moment_stored, 0, 1).reshape(NB, BLK)
+    inverse = jnp.zeros((NB,), jnp.int32).at[block_order].set(jnp.arange(NB, dtype=jnp.int32))
+    moment_natural = jnp.take(moment_stored, inverse, axis=0).reshape(2, SLOTS, 16, 16)
+    place = axis_x * 8 + axis_y * 4 + axis_z
+    own_moment = lax.dynamic_index_in_dim(
+        lax.dynamic_index_in_dim(moment_natural, core, 0, False), place, 1, False
+    ).reshape(SLOTS * 16, 1)
+    views = call(shift_kernel, [((3, SHIFTED, CI), LOW)], [VMEM], moved=3 << 20)(next_tiles[0])[0]
+
+    got_a, got_b = swap(send_a, MASK_X), swap(send_b, MASK_Y)
+    quarter = (HALF, 64, CO)
+    keep_a, send_a, keep_b, send_b = call(
+        second_kernel, [(quarter, LOW)] * 4, [SMEM] + [VMEM] * 4, moved=3 << 20
+    )(at, keep_a, got_a, keep_b, got_b)
+    got_a, got_b = swap(send_a, MASK_Y), swap(send_b, MASK_X)
+    piece = (SLOTS, 16, CO)
+    own, *sends = call(third_kernel, [(piece, LOW)] * 4, [SMEM] + [VMEM] * 4, moved=2 << 20)(
+        at, keep_a, got_a, keep_b, got_b
+    )
+    gots = [swap(send, (away + 1) * 2) for away, send in enumerate(sends)]
+    scaled, message = call(
+        moment_kernel,
+        [(piece, LOW), ((8, CO), WIDE)],
+        [SMEM] * 2 + [VMEM] * 5,
+        moved=1 << 20,
+    )(at, decay_rate, own, *gots, own_moment)
+
+    gots = [swap(scaled, away * 2) for away in (1, 2, 3)]
+    mine_a, mine_b = call(join_kernel, [(quarter, LOW)] * 2, [SMEM] + [VMEM] * 4, moved=1 << 20)(
+        at, scaled, *gots
+    )
+    got_a, got_b = swap(mine_a, MASK_Y), swap(mine_b, MASK_X)
+    mine_a, mine_b = call(
+        pair_kernel, [(part_a, LOW), (part_b, LOW)], [SMEM] + [VMEM] * 4, moved=2 << 20
+    )(at, mine_a, got_a, mine_b, got_b)
+    got_a, got_b = swap(mine_a, MASK_X), swap(mine_b, MASK_Y)
+    halves = (mine_a, got_a, mine_b, got_b)
+    peers = [swap(half, MASK_CORE) for half in halves]
+
+    line = jnp.stack([message] + [swap(message, away * 2) for away in (1, 2, 3)])
+    plane = jnp.stack([line] + [swap(line, mask) for mask in (MASK_Y, MASK_X, MASK_X + MASK_Y)])
+    plane_peer = swap(plane, MASK_CORE)
+    new_col, factor = call(
+        factor_kernel, [((2, CO), WIDE)] * 2, [SMEM] + [VMEM] * 3, moved=1 << 18
+    )(decay_rate, plane.reshape(16, 8, CO), plane_peer.reshape(16, 8, CO), col_moment)
+    rows = jnp.stack([plane, plane_peer])[:, :, :, 6, : SLOTS * 16]
+    rows = rows[jnp.arange(2) ^ core]
+    rows = rows[:, jnp.arange(4) ^ (axis_x * 2 + axis_y)]
+    rows = rows[:, :, jnp.arange(4) ^ axis_z].reshape(2, 4, 4, SLOTS, 16)
+    rows = jnp.transpose(rows, (0, 3, 1, 2, 4)).reshape(NB, BLK)
+    own_blocks = lax.dynamic_slice_in_dim(block_order, shard * (NB // 8), NB // 8)
+    new_row = jnp.take(rows, own_blocks, axis=0).reshape(-1)
+
+    update_rows, new_master, next_output = call(
+        finish_kernel,
+        [((NB // 8 * BLK, CO), WIDE), ((NB // 8 * BLK, CO), WIDE), ((PIX, CO), LOW)],
+        [SMEM] * 2 + [VMEM] * 12,
+        scratch=[
+            pltpu.VMEM((28, CI, CO), LOW),
+            pltpu.VMEM((PIX, CO), WIDE),
+            pltpu.VMEM((CI, CO), LOW),
+        ],
+        flops=2 * 28 * 512 * 256 * 256,
+        moved=16 << 20,
+    )(at, block_order, factor, views, natural, master_rows, *halves, *peers)
+    return (update_rows, new_master, new_row, new_col, next_output)
+
+
 def solution(mesh):
     in_specs = (
         P(),
@@ -126,4 +484,5 @@
         P(("group", "shard"), None, None, None, None),
     )
     out_specs = (P("shard", None), P("shard", None), P("shard"), P(), P(("group", "shard"), None))
-    return jax.shard_map(shards, mesh=mesh, in_specs=in_specs, out_specs=out_specs, check_vma=False)
+    body = shards if (mesh.shape["group"], mesh.shape["shard"]) == (4, 8) else general_shards
+    return jax.shard_map(body, mesh=mesh, in_specs=in_specs, out_specs=out_specs, check_vma=False)

time: 235 us -> 172 us (0.73)
  blocking collectives: 52 us -> 0 us
  starting transfers between devices: 0.08 us -> 47.3 us
  matrix products: 38.5 us -> 0 us
  other arithmetic: 31.7 us -> 2.01 us
  Pallas kernels: 0 us -> 23.3 us
  between operations: 15.6 us -> 1.85 us
  waiting for transfers between devices: 75.5 us -> 69.2 us
  local copies, waits for them, and re-layouts: 21 us -> 27.1 us
    ppermute x0 -> x39, waiting for transfers between devices: none -> 69.2 us  [swap(): return lax.ppermute(value, AXES, [(at, at ^ mask) for at in range(32)])]
    psum x2 -> x0, blocking collectives: 52 us -> none  [the longest x1 35.3 us: shards(): gradient = lax.psum(partial_value, 'group')]
    ppermute x0 -> x39, starting transfers between devices: none -> 47.3 us  [swap(): return lax.ppermute(value, AXES, [(at, at ^ mask) for at in range(32)])]
    reduce_scatter x1 -> x0, waiting for transfers between devices: 41 us -> none  [shards(): lax.psum_scatter(stored, 'shard', scatter_dimension=0, tiled=True)]
    dot_general x56 -> x0, matrix products: 38.5 us -> none  [the longest x28 26.2 us: contract_rows(): lax.dot_general(left, right, (((0,), (0,)), ((), ())), preferred_element_...]
    all_gather x1 -> x0, waiting for transfers between devices: 34.5 us -> none  [shards(): gathered = lax.all_gather(weights_low, 'shard', axis=0, tiled=True)]
    pallas_call x0 -> x10, Pallas kernels: none -> 23.3 us  [the longest x1 8.82 us: shards(): call(term_kernel, [(part_a, LOW), (part_a, LOW), (part_b, LOW), (part_b,...]
    unnamed x68 -> x45, local copies, waits for them, and re-layouts: 1.79 us -> 17.4 us
  transfers between devices with their start and end apart: 2 -> 39, of which waited for: 2 -> 14; matrix products, arithmetic and copies ran while one was open for 5% -> 8% of each run, Pallas kernels for 0% -> 10%
where the time goes in v1:
time: 172 us; the launch traced here: 171 us
  waiting for transfers between devices  69.2 us (40%)
  starting transfers between devices  47.3 us (28%)
  local copies, waits for them, and re-layouts  27.1 us (16%)
  Pallas kernels  23.3 us (14%)
  other arithmetic  2.01 us (1%)
  between operations  1.85 us (1%)
    ppermute x39, waiting for transfers between devices, swap(): return lax.ppermute(value, AXES, [(at, at ^ mask) for at in range(32)])  69.2 us
    ppermute x39, starting transfers between devices, swap(): return lax.ppermute(value, AXES, [(at, at ^ mask) for at in range(32)])  47.3 us
    unnamed x45, local copies, waits for them, and re-layouts  17.4 us
    pallas_call x1, Pallas kernels, shards(): call(term_kernel, [(part_a, LOW), (part_a, LOW), (part_b, LOW), (part_b,...  8.82 us
    pallas_call x1, Pallas kernels, shards(): call(finish_kernel, [((NB // 8 * BLK, CO), WIDE), ((NB // 8 * BLK, CO), W...  6.22 us
  transfers between devices with their start and end apart: 39, of which 14 were waited for; matrix products, arithmetic and copies ran while one was open for 8% of the time, Pallas kernels for 10%

profile of v1, /device:TPU:0, one launch (start us, length us, event | category | flops | bytes accessed | tf_op | source)
XLA Modules:
  0.0 170.8 jit_solution(16606987394468275209)
XLA Ops:
  0.6 3.1 %collective-permute-start.10 = (f32[896]{0:T(1024)}, f32[896]{0:T(1024)S(1)}, u32[]{:S(2)}, u32[]{:S(2)}) collective-permute-start(f32[896]{0:T(1024)} %param.17), channel_id=1, source_target_pairs={{0,2},{1,3},{2,0},{3,1},{4,6},{5,7},{6,4},{7,5},{8,10},{9,11},{10,... | collective-permute-start | bytes 10760 | tf_op jit(solution)/shard_map/ppermute | solution.py:132
  3.7 2.5 %collective-permute-start.12 = (f32[896]{0:T(1024)}, f32[896]{0:T(1024)S(1)}, u32[]{:S(2)}, u32[]{:S(2)}) collective-permute-start(f32[896]{0:T(1024)} %param.17), channel_id=1, source_target_pairs={{0,6},{1,7},{2,4},{3,5},{4,2},{5,3},{6,0},{7,1},{8,14},{9,15},{10,... | collective-permute-start | bytes 10760 | tf_op jit(solution)/shard_map/ppermute | solution.py:132
  7.4 1.3 scatter_custom_fusion
  14.9 8.8 %shard_map.137 = (bf16[7,128,256]{2,1,0:T(8,128)(2,1)S(1)}, bf16[7,128,256]{2,1,0:T(8,128)(2,1)}, bf16[7,128,256]{2,1,0:T(8,128)(2,1)S(1)}, bf16[7,128,256]{2,1,0:T(8,128)(2,1)}) custom-call(s32[4]{0:T(128)S(1)} %pad_add_fusion.at, bf16[4,18,18,256]{3,2,1,0:T(8,128)(2,1)S(1)} %bitcast.46, bf16[4,18,18,256]{3,2,1,0:T(8,128)(2,1)S(1)} %bitcast.47, ...), custom_call_target="tpu_custom_call" | custom-call | flops 1879048192 | bytes 6291456 | tf_op jit(solution)/shard_map/pallas_call | solution.py:379
  25.2 1.5 collective-permute-start.3
  26.7 1.5 collective-permute-start.4
  28.9 9.4 %collective-permute-done.3.got_a = bf16[7,128,256]{2,1,0:T(8,128)(2,1)S(1)} collective-permute-done((bf16[7,128,256]{2,1,0:T(8,128)(2,1)}, bf16[7,128,256]{2,1,0:T(8,128)(2,1)S(1)}, u32[]{:S(2)}, u32[]{:S(2)}) %collective-permute-start.3) | collective-permute-done | bytes 458784 | tf_op jit(solution)/shard_map/ppermute | solution.py:132
  41.6 1.4 shard_map.138
  43.1 1.5 collective-permute-start.5
  50.2 1.3 collective-permute-done.6.got_b
  52.1 1.5 collective-permute-start.7
  53.6 1.7 collective-permute-start.8
  55.3 1.3 collective-permute-start.9
  57.6 5.9 %collective-permute-done.8.two = bf16[14,16,256]{2,1,0:T(8,128)(2,1)S(1)} collective-permute-done((bf16[14,16,256]{2,1,0:T(8,128)(2,1)S(1)}, bf16[14,16,256]{2,1,0:T(8,128)(2,1)S(1)}, u32[]{:S(2)}, u32[]{:S(2)}) %collective-permute-start.8) | collective-permute-done | bytes 114720 | tf_op jit(solution)/shard_map/ppermute | solution.py:132
  64.4 2.3 %collective-permute-start.30 = (bf16[14,16,256]{2,1,0:T(8,128)(2,1)S(1)}, bf16[14,16,256]{2,1,0:T(8,128)(2,1)S(1)}, u32[]{:S(2)}, u32[]{:S(2)}) collective-permute-start(bf16[14,16,256]{2,1,0:T(8,128)(2,1)S(1)} %get-tuple-element.42.own), channel_id=1, source_target_pairs={{0,6},{1,7},{2,4},{3,5},{4,2},{5,3},{6,0},{7,1},{8,14},{9,15},{10,... | collective-permute-start | bytes 344072 | tf_op jit(solution)/shard_map/ppermute | solution.py:132
  66.7 1.6 collective-permute-start.23
  69.3 1.7 %collective-permute-start.21 = (bf16[896,256]{1,0:T(8,128)(2,1)S(1)}, bf16[896,256]{1,0:T(8,128)(2,1)}, u32[]{:S(2)}, u32[]{:S(2)}) collective-permute-start(bf16[896,256]{1,0:T(8,128)(2,1)S(1)} %convert_element_type.7.refs_0_), channel_id=1, source_target_pairs={{0,2},{1,3},{2,0},{3,1},{4,6},{5,7},{6,4},{7,5},{8,10},{9,11},{10,... | collective-permute-start | bytes 1376264 | tf_op jit(solution)/shard_map/ppermute | solution.py:132
  71.1 1.6 collective-permute-start.16
  72.7 27.4 %collective-permute-done.16 = f32[8,256]{1,0:T(8,128)S(1)} collective-permute-done((f32[8,256]{1,0:T(8,128)S(1)}, f32[8,256]{1,0:T(8,128)S(1)}, u32[]{:S(2)}, u32[]{:S(2)}) %collective-permute-start.16) | collective-permute-done | bytes 8224 | tf_op jit(solution)/shard_map/ppermute | solution.py:132
  100.1 12.9 %collective-permute-start.29 = (bf16[14,16,256]{2,1,0:T(8,128)(2,1)S(1)}, bf16[14,16,256]{2,1,0:T(8,128)(2,1)S(1)}, u32[]{:S(2)}, u32[]{:S(2)}) collective-permute-start(bf16[14,16,256]{2,1,0:T(8,128)(2,1)S(1)} %get-tuple-element.42.own), channel_id=1, source_target_pairs={{0,4},{1,5},{2,6},{3,7},{4,0},{5,1},{6,2},{7,3},{8,12},{9,13},{10,... | collective-permute-start | bytes 344072 | tf_op jit(solution)/shard_map/ppermute | solution.py:132
  113.0 5.5 %collective-permute-done.29.two = bf16[14,16,256]{2,1,0:T(8,128)(2,1)S(1)} collective-permute-done((bf16[14,16,256]{2,1,0:T(8,128)(2,1)S(1)}, bf16[14,16,256]{2,1,0:T(8,128)(2,1)S(1)}, u32[]{:S(2)}, u32[]{:S(2)}) %collective-permute-start.29) | collective-permute-done | bytes 114720 | tf_op jit(solution)/shard_map/ppermute | solution.py:132
  118.5 1.4 collective-permute-start.15
  120.8 2.3 %collective-permute-done.15 = f32[8,256]{1,0:T(8,128)S(1)} collective-permute-done((f32[8,256]{1,0:T(8,128)S(1)}, f32[8,256]{1,0:T(8,128)S(1)}, u32[]{:S(2)}, u32[]{:S(2)}) %collective-permute-start.15) | collective-permute-done | bytes 8224 | tf_op jit(solution)/shard_map/ppermute | solution.py:132
  123.6 1.4 collective-permute-start.32
  125.7 3.5 %collective-permute-done.31.got_a = bf16[7,64,256]{2,1,0:T(8,128)(2,1)S(1)} collective-permute-done((bf16[7,64,256]{2,1,0:T(8,128)(2,1)S(1)}, bf16[7,64,256]{2,1,0:T(8,128)(2,1)S(1)}, u32[]{:S(2)}, u32[]{:S(2)}) %collective-permute-start.31) | collective-permute-done | bytes 229408 | tf_op jit(solution)/shard_map/ppermute | solution.py:132
  129.7 2.4 %collective-permute-start.19 = (f32[4,8,256]{2,1,0:T(8,128)S(1)}, f32[4,8,256]{2,1,0:T(8,128)S(1)}, u32[]{:S(2)}, u32[]{:S(2)}) collective-permute-start(f32[4,8,256]{2,1,0:T(8,128)S(1)} %get-tuple-element.56), channel_id=1, source_target_pairs={{0,24},{1,25},{2,26},{3,27},{4,28},{5,29},{6,30},{7,31},{8,16},{9,... | collective-permute-start | bytes 98312 | tf_op jit(solution)/shard_map/ppermute | solution.py:132
  132.1 1.6 shard_map.145
  137.5 10.0 %collective-permute-done.33.got_a = bf16[7,128,256]{2,1,0:T(8,128)(2,1)} collective-permute-done((bf16[7,128,256]{2,1,0:T(8,128)(2,1)}, bf16[7,128,256]{2,1,0:T(8,128)(2,1)}, u32[]{:S(2)}, u32[]{:S(2)}) %collective-permute-start.33) | collective-permute-done | bytes 458784 | tf_op jit(solution)/shard_map/ppermute | solution.py:132
  152.7 2.3 %shard_map.143.natural = bf16[7168,256]{1,0:T(8,128)(2,1)S(1)} custom-call(s32[4]{0:T(128)S(1)} %pad_add_fusion.at, s32[224]{0:T(256)S(1)} %copy-done.13, bf16[896,256]{1,0:T(8,128)(2,1)S(1)} %convert_element_type.7.refs_0_, bf16[896,256]{1,0:T(8,128)(2,1)} %collective-permute-done.21.refs_1_, bf16[896,256]{1,0:T(8,128)(2,1)S(1)} %copy-done.8, ...), custom_call_target="tpu_custom_call" | custom-call | bytes 8388608 | tf_op jit(solution)/shard_map/pallas_call | solution.py:399
  155.0 1.8 %copy-done = bf16[7168,256]{1,0:T(8,128)(2,1)} copy-done((bf16[7168,256]{1,0:T(8,128)(2,1)}, bf16[7168,256]{1,0:T(8,128)(2,1)S(1)}, u32[]{:S(2)}) %copy-start) | copy-done | bytes 3670040
  162.6 2.0 %copy-done.1 = bf16[7168,256]{1,0:T(8,128)(2,1)S(1)} copy-done((bf16[7168,256]{1,0:T(8,128)(2,1)S(1)}, bf16[7168,256]{1,0:T(8,128)(2,1)}, u32[]{:S(2)}) %copy-start.1) | copy-done | bytes 3670040
  164.6 6.2 %shard_map.146 = (f32[896,256]{1,0:T(8,128)}, f32[896,256]{1,0:T(8,128)}, bf16[512,256]{1,0:T(8,128)(2,1)}) custom-call(s32[4]{0:T(128)S(1)} %pad_add_fusion.at, s32[224]{0:T(256)S(1)} %copy-done.13, f32[2,256]{1,0:T(2,128)S(1)} %get-tuple-element.41.factor, bf16[3,1152,256]{2,1,0:T(8,128)(2,1)S(1)} %shard_map.142.views, bf16[7168,256]{1,0:T(8,128)(2,1)S(1)} %copy-done.1, ...), custom_call_target="tpu_custom_call" | custom-call | flops 1879048192 | bytes 16777216 | tf_op jit(solution)/shard_map/pallas_call | solution.py:458
  (151 shorter events, 38.3 us)
Async XLA Ops:
  0.6 28.2 %collective-permute-start.10 = (f32[896]{0:T(1024)}, f32[896]{0:T(1024)S(1)}, u32[]{:S(2)}, u32[]{:S(2)}) collective-permute-start(f32[896]{0:T(1024)} %param.17), channel_id=1, source_target_pairs={{0,2},{1,3},{2,0},{3,1},{4,6},{5,7},{6,4},{7,5},{8,10},{9,11},{10,... | collective-permute-start | bytes 10760 | tf_op jit(solution)/shard_map/ppermute | solution.py:132
  3.7 25.2 %collective-permute-start.12 = (f32[896]{0:T(1024)}, f32[896]{0:T(1024)S(1)}, u32[]{:S(2)}, u32[]{:S(2)}) collective-permute-start(f32[896]{0:T(1024)} %param.17), channel_id=1, source_target_pairs={{0,6},{1,7},{2,4},{3,5},{4,2},{5,3},{6,0},{7,1},{8,14},{9,15},{10,... | collective-permute-start | bytes 10760 | tf_op jit(solution)/shard_map/ppermute | solution.py:132
  6.2 4.2 %collective-permute-start.2 = (bf16[512,256]{1,0:T(8,128)(2,1)}, bf16[512,256]{1,0:T(8,128)(2,1)S(1)}, u32[]{:S(2)}, u32[]{:S(2)}) collective-permute-start(bf16[512,256]{1,0:T(8,128)(2,1)} %grad.1), channel_id=1, source_target_pairs={{0,1},{1,0},{2,3},{3,2},{4,5},{5,4},{6,7},{7,6},{8,9},{9,8},{10,11... | collective-permute-start | bytes 786440 | tf_op jit(solution)/shard_map/ppermute | solution.py:132
  10.0 18.9 %collective-permute-start.11 = (f32[896]{0:T(1024)}, f32[896]{0:T(1024)S(1)}, u32[]{:S(2)}, u32[]{:S(2)}) collective-permute-start(f32[896]{0:T(1024)} %param.17), channel_id=1, source_target_pairs={{0,4},{1,5},{2,6},{3,7},{4,0},{5,1},{6,2},{7,3},{8,12},{9,13},{10,... | collective-permute-start | bytes 10760 | tf_op jit(solution)/shard_map/ppermute | solution.py:132
  25.2 13.1 %collective-permute-start.3 = (bf16[7,128,256]{2,1,0:T(8,128)(2,1)}, bf16[7,128,256]{2,1,0:T(8,128)(2,1)S(1)}, u32[]{:S(2)}, u32[]{:S(2)}) collective-permute-start(bf16[7,128,256]{2,1,0:T(8,128)(2,1)} %get-tuple-element.29), channel_id=1, source_target_pairs={{0,8},{1,9},{2,10},{3,11},{4,12},{5,13},{6,14},{7,15},{8,0},{9,1},... | collective-permute-start | bytes 1376264 | tf_op jit(solution)/shard_map/ppermute | solution.py:132
  26.7 12.9 %collective-permute-start.4 = (bf16[7,128,256]{2,1,0:T(8,128)(2,1)}, bf16[7,128,256]{2,1,0:T(8,128)(2,1)S(1)}, u32[]{:S(2)}, u32[]{:S(2)}) collective-permute-start(bf16[7,128,256]{2,1,0:T(8,128)(2,1)} %get-tuple-element.31), channel_id=1, source_target_pairs={{0,16},{1,17},{2,18},{3,19},{4,20},{5,21},{6,22},{7,23},{8,24},{9,... | collective-permute-start | bytes 1376264 | tf_op jit(solution)/shard_map/ppermute | solution.py:132
  28.8 42.2 %collective-permute-start.24 = (bf16[896,256]{1,0:T(8,128)(2,1)S(1)}, bf16[896,256]{1,0:T(8,128)(2,1)S(1)}, u32[]{:S(2)}, u32[]{:S(2)}) collective-permute-start(bf16[896,256]{1,0:T(8,128)(2,1)S(1)} %convert_element_type.7.refs_0_), channel_id=1, source_target_pairs={{0,1},{1,0},{2,3},{3,2},{4,5},{5,4},{6,7},{7,6},{8,9},{9,8},{10,11... | collective-permute-start | bytes 1376264 | tf_op jit(solution)/shard_map/ppermute | solution.py:132
  43.1 7.1 %collective-permute-start.5 = (bf16[7,64,256]{2,1,0:T(8,128)(2,1)}, bf16[7,64,256]{2,1,0:T(8,128)(2,1)S(1)}, u32[]{:S(2)}, u32[]{:S(2)}) collective-permute-start(bf16[7,64,256]{2,1,0:T(8,128)(2,1)} %get-tuple-element.33), channel_id=1, source_target_pairs={{0,16},{1,17},{2,18},{3,19},{4,20},{5,21},{6,22},{7,23},{8,24},{9,... | collective-permute-start | bytes 688136 | tf_op jit(solution)/shard_map/ppermute | solution.py:132
  44.6 6.8 %collective-permute-start.6 = (bf16[7,64,256]{2,1,0:T(8,128)(2,1)}, bf16[7,64,256]{2,1,0:T(8,128)(2,1)S(1)}, u32[]{:S(2)}, u32[]{:S(2)}) collective-permute-start(bf16[7,64,256]{2,1,0:T(8,128)(2,1)} %get-tuple-element.35), channel_id=1, source_target_pairs={{0,8},{1,9},{2,10},{3,11},{4,12},{5,13},{6,14},{7,15},{8,0},{9,1},... | collective-permute-start | bytes 688136 | tf_op jit(solution)/shard_map/ppermute | solution.py:132
  52.1 5.5 %collective-permute-start.7 = (bf16[14,16,256]{2,1,0:T(8,128)(2,1)S(1)}, bf16[14,16,256]{2,1,0:T(8,128)(2,1)S(1)}, u32[]{:S(2)}, u32[]{:S(2)}) collective-permute-start(bf16[14,16,256]{2,1,0:T(8,128)(2,1)S(1)} %get-tuple-element.37), channel_id=1, source_target_pairs={{0,2},{1,3},{2,0},{3,1},{4,6},{5,7},{6,4},{7,5},{8,10},{9,11},{10,... | collective-permute-start | bytes 344072 | tf_op jit(solution)/shard_map/ppermute | solution.py:132
  53.6 10.0 %collective-permute-start.8 = (bf16[14,16,256]{2,1,0:T(8,128)(2,1)S(1)}, bf16[14,16,256]{2,1,0:T(8,128)(2,1)S(1)}, u32[]{:S(2)}, u32[]{:S(2)}) collective-permute-start(bf16[14,16,256]{2,1,0:T(8,128)(2,1)S(1)} %get-tuple-element.38), channel_id=1, source_target_pairs={{0,4},{1,5},{2,6},{3,7},{4,0},{5,1},{6,2},{7,3},{8,12},{9,13},{10,... | collective-permute-start | bytes 344072 | tf_op jit(solution)/shard_map/ppermute | solution.py:132
  55.3 8.3 %collective-permute-start.9 = (bf16[14,16,256]{2,1,0:T(8,128)(2,1)S(1)}, bf16[14,16,256]{2,1,0:T(8,128)(2,1)S(1)}, u32[]{:S(2)}, u32[]{:S(2)}) collective-permute-start(bf16[14,16,256]{2,1,0:T(8,128)(2,1)S(1)} %get-tuple-element.39), channel_id=1, source_target_pairs={{0,6},{1,7},{2,4},{3,5},{4,2},{5,3},{6,0},{7,1},{8,14},{9,15},{10,... | collective-permute-start | bytes 344072 | tf_op jit(solution)/shard_map/ppermute | solution.py:132
  64.4 48.6 %collective-permute-start.30 = (bf16[14,16,256]{2,1,0:T(8,128)(2,1)S(1)}, bf16[14,16,256]{2,1,0:T(8,128)(2,1)S(1)}, u32[]{:S(2)}, u32[]{:S(2)}) collective-permute-start(bf16[14,16,256]{2,1,0:T(8,128)(2,1)S(1)} %get-tuple-element.42.own), channel_id=1, source_target_pairs={{0,6},{1,7},{2,4},{3,5},{4,2},{5,3},{6,0},{7,1},{8,14},{9,15},{10,... | collective-permute-start | bytes 344072 | tf_op jit(solution)/shard_map/ppermute | solution.py:132
  66.7 58.3 %collective-permute-start.23 = (bf16[896,256]{1,0:T(8,128)(2,1)S(1)}, bf16[896,256]{1,0:T(8,128)(2,1)S(1)}, u32[]{:S(2)}, u32[]{:S(2)}) collective-permute-start(bf16[896,256]{1,0:T(8,128)(2,1)S(1)} %convert_element_type.7.refs_0_), channel_id=1, source_target_pairs={{0,6},{1,7},{2,4},{3,5},{4,2},{5,3},{6,0},{7,1},{8,14},{9,15},{10,... | collective-permute-start | bytes 1376264 | tf_op jit(solution)/shard_map/ppermute | solution.py:132
  68.3 65.5 %collective-permute-start.22 = (bf16[896,256]{1,0:T(8,128)(2,1)S(1)}, bf16[896,256]{1,0:T(8,128)(2,1)S(1)}, u32[]{:S(2)}, u32[]{:S(2)}) collective-permute-start(bf16[896,256]{1,0:T(8,128)(2,1)S(1)} %convert_element_type.7.refs_0_), channel_id=1, source_target_pairs={{0,4},{1,5},{2,6},{3,7},{4,0},{5,1},{6,2},{7,3},{8,12},{9,13},{10,... | collective-permute-start | bytes 1376264 | tf_op jit(solution)/shard_map/ppermute | solution.py:132
  69.3 64.4 %collective-permute-start.21 = (bf16[896,256]{1,0:T(8,128)(2,1)S(1)}, bf16[896,256]{1,0:T(8,128)(2,1)}, u32[]{:S(2)}, u32[]{:S(2)}) collective-permute-start(bf16[896,256]{1,0:T(8,128)(2,1)S(1)} %convert_element_type.7.refs_0_), channel_id=1, source_target_pairs={{0,2},{1,3},{2,0},{3,1},{4,6},{5,7},{6,4},{7,5},{8,10},{9,11},{10,... | collective-permute-start | bytes 1376264 | tf_op jit(solution)/shard_map/ppermute | solution.py:132
  71.1 29.0 %collective-permute-start.16 = (f32[8,256]{1,0:T(8,128)S(1)}, f32[8,256]{1,0:T(8,128)S(1)}, u32[]{:S(2)}, u32[]{:S(2)}) collective-permute-start(f32[8,256]{1,0:T(8,128)S(1)} %get-tuple-element.40), channel_id=1, source_target_pairs={{0,6},{1,7},{2,4},{3,5},{4,2},{5,3},{6,0},{7,1},{8,14},{9,15},{10,... | collective-permute-start | bytes 24584 | tf_op jit(solution)/shard_map/ppermute | solution.py:132
  100.1 18.4 %collective-permute-start.29 = (bf16[14,16,256]{2,1,0:T(8,128)(2,1)S(1)}, bf16[14,16,256]{2,1,0:T(8,128)(2,1)S(1)}, u32[]{:S(2)}, u32[]{:S(2)}) collective-permute-start(bf16[14,16,256]{2,1,0:T(8,128)(2,1)S(1)} %get-tuple-element.42.own), channel_id=1, source_target_pairs={{0,4},{1,5},{2,6},{3,7},{4,0},{5,1},{6,2},{7,3},{8,12},{9,13},{10,... | collective-permute-start | bytes 344072 | tf_op jit(solution)/shard_map/ppermute | solution.py:132
  113.0 6.9 %collective-permute-start.28 = (bf16[14,16,256]{2,1,0:T(8,128)(2,1)S(1)}, bf16[14,16,256]{2,1,0:T(8,128)(2,1)S(1)}, u32[]{:S(2)}, u32[]{:S(2)}) collective-permute-start(bf16[14,16,256]{2,1,0:T(8,128)(2,1)S(1)} %get-tuple-element.42.own), channel_id=1, source_target_pairs={{0,2},{1,3},{2,0},{3,1},{4,6},{5,7},{6,4},{7,5},{8,10},{9,11},{10,... | collective-permute-start | bytes 344072 | tf_op jit(solution)/shard_map/ppermute | solution.py:132
  118.5 4.5 %collective-permute-start.15 = (f32[8,256]{1,0:T(8,128)S(1)}, f32[8,256]{1,0:T(8,128)S(1)}, u32[]{:S(2)}, u32[]{:S(2)}) collective-permute-start(f32[8,256]{1,0:T(8,128)S(1)} %get-tuple-element.40), channel_id=1, source_target_pairs={{0,4},{1,5},{2,6},{3,7},{4,0},{5,1},{6,2},{7,3},{8,12},{9,13},{10,... | collective-permute-start | bytes 24584 | tf_op jit(solution)/shard_map/ppermute | solution.py:132
  123.1 6.2 %collective-permute-start.31 = (bf16[7,64,256]{2,1,0:T(8,128)(2,1)S(1)}, bf16[7,64,256]{2,1,0:T(8,128)(2,1)S(1)}, u32[]{:S(2)}, u32[]{:S(2)}) collective-permute-start(bf16[7,64,256]{2,1,0:T(8,128)(2,1)S(1)} %get-tuple-element.43.mine_a), channel_id=1, source_target_pairs={{0,16},{1,17},{2,18},{3,19},{4,20},{5,21},{6,22},{7,23},{8,24},{9,... | collective-permute-start | bytes 688136 | tf_op jit(solution)/shard_map/ppermute | solution.py:132
  123.6 6.2 %collective-permute-start.32 = (bf16[7,64,256]{2,1,0:T(8,128)(2,1)S(1)}, bf16[7,64,256]{2,1,0:T(8,128)(2,1)S(1)}, u32[]{:S(2)}, u32[]{:S(2)}) collective-permute-start(bf16[7,64,256]{2,1,0:T(8,128)(2,1)S(1)} %get-tuple-element.44.mine_b), channel_id=1, source_target_pairs={{0,8},{1,9},{2,10},{3,11},{4,12},{5,13},{6,14},{7,15},{8,0},{9,1},... | collective-permute-start | bytes 688136 | tf_op jit(solution)/shard_map/ppermute | solution.py:132
  125.0 9.2 %collective-permute-start.18 = (f32[4,8,256]{2,1,0:T(8,128)S(1)}, f32[4,8,256]{2,1,0:T(8,128)S(1)}, u32[]{:S(2)}, u32[]{:S(2)}) collective-permute-start(f32[4,8,256]{2,1,0:T(8,128)S(1)} %get-tuple-element.56), channel_id=1, source_target_pairs={{0,8},{1,9},{2,10},{3,11},{4,12},{5,13},{6,14},{7,15},{8,0},{9,1},... | collective-permute-start | bytes 98312 | tf_op jit(solution)/shard_map/ppermute | solution.py:132
  129.2 5.1 %collective-permute-start.17 = (f32[4,8,256]{2,1,0:T(8,128)S(1)}, f32[4,8,256]{2,1,0:T(8,128)S(1)}, u32[]{:S(2)}, u32[]{:S(2)}) collective-permute-start(f32[4,8,256]{2,1,0:T(8,128)S(1)} %get-tuple-element.56), channel_id=1, source_target_pairs={{0,16},{1,17},{2,18},{3,19},{4,20},{5,21},{6,22},{7,23},{8,24},{9,... | collective-permute-start | bytes 98312 | tf_op jit(solution)/shard_map/ppermute | solution.py:132
  129.7 5.2 %collective-permute-start.19 = (f32[4,8,256]{2,1,0:T(8,128)S(1)}, f32[4,8,256]{2,1,0:T(8,128)S(1)}, u32[]{:S(2)}, u32[]{:S(2)}) collective-permute-start(f32[4,8,256]{2,1,0:T(8,128)S(1)} %get-tuple-element.56), channel_id=1, source_target_pairs={{0,24},{1,25},{2,26},{3,27},{4,28},{5,29},{6,30},{7,31},{8,16},{9,... | collective-permute-start | bytes 98312 | tf_op jit(solution)/shard_map/ppermute | solution.py:132
  134.3 13.2 %collective-permute-start.33 = (bf16[7,128,256]{2,1,0:T(8,128)(2,1)}, bf16[7,128,256]{2,1,0:T(8,128)(2,1)}, u32[]{:S(2)}, u32[]{:S(2)}) collective-permute-start(bf16[7,128,256]{2,1,0:T(8,128)(2,1)} %get-tuple-element.45.mine_a), channel_id=1, source_target_pairs={{0,8},{1,9},{2,10},{3,11},{4,12},{5,13},{6,14},{7,15},{8,0},{9,1},... | collective-permute-start | bytes 1376264 | tf_op jit(solution)/shard_map/ppermute | solution.py:132
  135.0 12.9 %collective-permute-start.34 = (bf16[7,128,256]{2,1,0:T(8,128)(2,1)}, bf16[7,128,256]{2,1,0:T(8,128)(2,1)}, u32[]{:S(2)}, u32[]{:S(2)}) collective-permute-start(bf16[7,128,256]{2,1,0:T(8,128)(2,1)} %get-tuple-element.46.mine_b), channel_id=1, source_target_pairs={{0,16},{1,17},{2,18},{3,19},{4,20},{5,21},{6,22},{7,23},{8,24},{9,... | collective-permute-start | bytes 1376264 | tf_op jit(solution)/shard_map/ppermute | solution.py:132
  136.2 20.6 %collective-permute-start.20 = (f32[4,4,8,256]{3,2,1,0:T(8,128)S(1)}, f32[4,4,8,256]{3,2,1,0:T(8,128)S(1)}, u32[]{:S(2)}, u32[]{:S(2)}) collective-permute-start(f32[4,4,8,256]{3,2,1,0:T(8,128)S(1)} %get-tuple-element.54), channel_id=1, source_target_pairs={{0,1},{1,0},{2,3},{3,2},{4,5},{5,4},{6,7},{7,6},{8,9},{9,8},{10,11... | collective-permute-start | bytes 393224 | tf_op jit(solution)/shard_map/ppermute | solution.py:132
  137.0 25.5 %collective-permute-start.35 = (bf16[7,128,256]{2,1,0:T(8,128)(2,1)}, bf16[7,128,256]{2,1,0:T(8,128)(2,1)}, u32[]{:S(2)}, u32[]{:S(2)}) collective-permute-start(bf16[7,128,256]{2,1,0:T(8,128)(2,1)} %get-tuple-element.45.mine_a), channel_id=1, source_target_pairs={{0,1},{1,0},{2,3},{3,2},{4,5},{5,4},{6,7},{7,6},{8,9},{9,8},{10,11... | collective-permute-start | bytes 1376264 | tf_op jit(solution)/shard_map/ppermute | solution.py:132
  137.2 25.3 %collective-permute-start.37 = (bf16[7,128,256]{2,1,0:T(8,128)(2,1)}, bf16[7,128,256]{2,1,0:T(8,128)(2,1)}, u32[]{:S(2)}, u32[]{:S(2)}) collective-permute-start(bf16[7,128,256]{2,1,0:T(8,128)(2,1)} %get-tuple-element.46.mine_b), channel_id=1, source_target_pairs={{0,1},{1,0},{2,3},{3,2},{4,5},{5,4},{6,7},{7,6},{8,9},{9,8},{10,11... | collective-permute-start | bytes 1376264 | tf_op jit(solution)/shard_map/ppermute | solution.py:132
  147.5 15.0 %collective-permute-start.36 = (bf16[7,128,256]{2,1,0:T(8,128)(2,1)}, bf16[7,128,256]{2,1,0:T(8,128)(2,1)}, u32[]{:S(2)}, u32[]{:S(2)}) collective-permute-start(bf16[7,128,256]{2,1,0:T(8,128)(2,1)} %collective-permute-done.33.got_a), channel_id=1, source_target_pairs={{0,1},{1,0},{2,3},{3,2},{4,5},{5,4},{6,7},{7,6},{8,9},{9,8},{10,11... | collective-permute-start | bytes 1376264 | tf_op jit(solution)/shard_map/ppermute | solution.py:132
  147.9 14.7 %collective-permute-start.38 = (bf16[7,128,256]{2,1,0:T(8,128)(2,1)}, bf16[7,128,256]{2,1,0:T(8,128)(2,1)}, u32[]{:S(2)}, u32[]{:S(2)}) collective-permute-start(bf16[7,128,256]{2,1,0:T(8,128)(2,1)} %collective-permute-done.34.got_b), channel_id=1, source_target_pairs={{0,1},{1,0},{2,3},{3,2},{4,5},{5,4},{6,7},{7,6},{8,9},{9,8},{10,11... | collective-permute-start | bytes 1376264 | tf_op jit(solution)/shard_map/ppermute | solution.py:132
  (28 other events, 319.2 us)

commit v2 on v1

--- a/solution.py
+++ b/solution.py
@@ -132,14 +132,14 @@
     return lax.ppermute(value, AXES, [(at, at ^ mask) for at in range(32)])
 
 
-def call(kernel, outs, in_specs, out_specs=None, scratch=(), flops=0, moved=0):
+def call(kernel, outs, in_specs, scratch=(), flops=0, moved=0, room=8):
     return pl.pallas_call(
         kernel,
         out_shape=[jax.ShapeDtypeStruct(shape, dtype) for shape, dtype in outs],
         in_specs=in_specs,
-        out_specs=[VMEM] * len(outs) if out_specs is None else out_specs,
+        out_specs=[VMEM] * len(outs),
         scratch_shapes=list(scratch),
-        compiler_params=pltpu.CompilerParams(vmem_limit_bytes=44 << 20),
+        compiler_params=pltpu.CompilerParams(vmem_limit_bytes=room << 20),
         cost_estimate=pl.CostEstimate(flops=flops, bytes_accessed=moved, transcendentals=0),
     )
 
@@ -235,7 +235,7 @@
         out[HALF:] = (keep_b[:, rows].astype(WIDE) + got_b[:, rows].astype(WIDE)).astype(LOW)
 
 
-def moment_kernel(at, rate, own, one, two, three, row_moment, scaled, message):
+def moment_kernel(at, rate, own, one, two, three, row_moment, scaled):
     total = own[...].astype(WIDE) + one[...].astype(WIDE)
     total = total + (two[...].astype(WIDE) + three[...].astype(WIDE))
     total = total.reshape(SLOTS * 16, CO)
@@ -243,7 +243,7 @@
     decay = rate[0]
     mean = jnp.sum(squares, axis=1, keepdims=True) * (1.0 / CO)
     new_row = decay * row_moment[...] + (1.0 - decay) * mean
-    scaled[...] = (total * lax.rsqrt(new_row)).astype(LOW).reshape(SLOTS, 16, CO)
+    scaled[:SLOTS] = (total * lax.rsqrt(new_row)).astype(LOW).reshape(SLOTS, 16, CO)
     weighted = squares / new_row
     cut = (SLOTS - 1) * 16
     last_small = at[3] == 1
@@ -257,12 +257,12 @@
     spread = jnp.concatenate([spread, jnp.zeros((32, 128), WIDE)], axis=0)
     rows.append(jnp.transpose(spread)[:1])
     rows.append(jnp.zeros((1, CO), WIDE))
-    message[...] = jnp.concatenate(rows, axis=0)
-
-
-def factor_kernel(rate, mine, peer, col_moment, new_col, factor):
-    total = jnp.sum(mine[...], axis=0) + jnp.sum(peer[...], axis=0)
-    decay = rate[0]
+    message = jnp.concatenate(rows, axis=0)
+    high = message.astype(LOW).astype(WIDE)
+    scaled[SLOTS] = jnp.concatenate([high, message - high], axis=0).astype(LOW)
+
+
+def store_factors(total, decay, col_moment, new_col, factor):
     for kernel in range(2):
         count = 27.0 * CI if kernel == 0 else float(CO)
         col = decay * col_moment[kernel : kernel + 1] + (1.0 - decay) * (
@@ -277,82 +277,115 @@
         factor[kernel : kernel + 1] = 1.0 / (jnp.sqrt(col / row_mean) * clip)
 
 
+def pack_kernel(at, master, row_moment, packed, rows, arrived):
+    quarter = (at[1] * 2 + at[0]) * (SLOTS * 16)
+    copy = pltpu.make_async_copy(
+        master.at[pl.ds(pl.multiple_of(quarter, SLOTS * 16), SLOTS * 16), :], rows, arrived
+    )
+    copy.start()
+    copy.wait()
+    packed[:SLOTS] = rows[...].astype(LOW).reshape(SLOTS, 16, CO)
+    values = jnp.concatenate([row_moment[...], jnp.zeros((9, 128), WIDE)], axis=0)
+    high = values.astype(LOW).astype(WIDE)
+    packed[SLOTS] = jnp.concatenate([high, values - high], axis=1).astype(LOW)
+
+
+def line_kernel(at, after, own, one, two, three, out):
+    for away, piece in enumerate((own, one, two, three)):
+        out[at[2] ^ away] = piece[:SLOTS].reshape(SLOTS * 16, CO)
+
+
 def order_kernel(at, block_order, *refs):
     pieces, out = refs[:-1], refs[-1]
     count = NB // 8
+    blocks = count // 4
     for index, piece in enumerate(pieces):
         flip_core, away = divmod(index, 4)
-        owner = (at[2] ^ away) * 2 + (at[3] ^ flip_core)
-
-        def move(local, carry, piece=piece, owner=owner):
-            block = block_order[owner * count + local]
-            to = pl.ds(pl.multiple_of(block * BLK, BLK), BLK)
-            out[to, :] = piece[pl.ds(pl.multiple_of(local * BLK, BLK), BLK), :]
-            return carry
-
-        lax.fori_loop(0, count, move, 0, unroll=4)
-
-
-def join_kernel(at, own, one, two, three, out_a, out_b):
+        core, quarter = at[3] ^ flip_core, (at[1] * 2 + at[0]) ^ away
+        for line in range(4):
+            for local in range(blocks):
+                block = block_order[(line * 2 + core) * count + quarter * blocks + local]
+                to = pl.ds(pl.multiple_of(block * BLK, BLK), BLK)
+                out[to, :] = piece[line, local * BLK : local * BLK + BLK]
+
+
+def join_kernel(at, after, own, one, two, three, out_a, out_b):
     for away, piece in enumerate((own, one, two, three)):
         rows = pl.ds(pl.multiple_of((at[2] ^ away) * 16, 16), 16)
         out_a[:, rows] = piece[:HALF]
         out_b[:, rows] = piece[HALF:]
 
 
-def pair_kernel(at, mine_a, got_a, mine_b, got_b, out_a, out_b):
+def pair_kernel(at, after, mine_a, got_a, mine_b, got_b, out_a, out_b):
     for which, mine, got, out in ((at[1], mine_a, got_a, out_a), (at[0], mine_b, got_b, out_b)):
         out[:, pl.ds(pl.multiple_of(which * 64, 64), 64)] = mine[...]
         out[:, pl.ds(pl.multiple_of(64 - which * 64, 64), 64)] = got[...]
 
 
 def finish_kernel(
-    at, block_order, factor, views, natural, master,
+    at, block_order, rate, col_moment, views, natural, master,
     mine_a, got_a, mine_b, got_b, peer_a, peer_got_a, peer_b, peer_got_b,
-    update_rows, new_master, next_output, scaled, hidden, pointwise,
+    update_rows, new_master, new_row, new_col, next_output, scaled, factor, row_table,
 ):
     axis_x, axis_y, core = at[0], at[1], at[3]
     for index, (a_own, a_got, b_own, b_got) in enumerate(
         ((mine_a, got_a, mine_b, got_b), (peer_a, peer_got_a, peer_b, peer_got_b))
     ):
-        base = (core ^ index) * SLOTS
+        side = core ^ index
         for which, piece in ((axis_x, a_own), (1 - axis_x, a_got)):
             rows = pl.ds(pl.multiple_of(which * 128, 128), 128)
-            scaled[pl.ds(base, HALF), rows] = piece[...]
+            scaled[side, :HALF, rows] = piece[...]
         for which, piece in ((axis_y, b_own), (1 - axis_y, b_got)):
             for half in range(2):
                 rows = pl.ds(pl.multiple_of(half * 128 + which * 64, 64), 64)
-                scaled[pl.ds(base + HALF, HALF), rows] = piece[:, half * 64 : half * 64 + 64]
+                scaled[side, HALF:, rows] = piece[:, half * 64 : half * 64 + 64]
+    message = scaled[:, SLOTS].astype(WIDE).reshape(32, 2, 8, CO)
+    message = message[:, 0] + message[:, 1]
+    store_factors(jnp.sum(message, axis=0), rate[0], col_moment, new_col, factor)
+    for index in range(32):
+        for half in range(2):
+            row_table[index * 2 + half : index * 2 + half + 1] = message[
+                index, 6:7, half * 128 : half * 128 + 128
+            ]
     large = learn_rate * factor[0:1]
     total = jnp.zeros((PIX, CO), WIDE)
     for tap in range(27):
         frame_off, row_off, col_off = tap // 9, tap // 3 % 3, tap % 3
-        weights = natural[tap * CI : tap * CI + CI].astype(WIDE) - scaled[tap].astype(WIDE) * large
+        step = scaled[tap // SLOTS, tap % SLOTS].astype(WIDE) * large
+        weights = natural[tap * CI : tap * CI + CI].astype(WIDE) - step
         starts = [((frame + frame_off) * (HW + 2) + row_off) * HW for frame in range(FR)]
         window = jnp.concatenate(
             [views[col_off, start : start + HW * HW, :] for start in starts], axis=0
         )
         total = total + jnp.dot(window, weights.astype(LOW), preferred_element_type=WIDE)
     small = learn_rate * factor[1:2]
-    weights = natural[27 * CI :].astype(WIDE) - scaled[27].astype(WIDE) * small
+    weights = natural[27 * CI :].astype(WIDE) - scaled[1, SLOTS - 1].astype(WIDE) * small
     next_act = jax.nn.silu(total).astype(LOW)
     next_output[...] = jnp.dot(
         next_act, weights.astype(LOW), preferred_element_type=WIDE
     ).astype(LOW)
 
     owner = at[2] * 2 + core
-
-    def own_block(local, carry):
-        block = block_order[owner * (NB // 8) + local]
-        chosen = jnp.where(block >= NB3, factor[1:2], factor[0:1])
-        rows = pl.ds(pl.multiple_of(local * BLK, BLK), BLK)
-        start = pl.multiple_of(lax.rem(block, 8) * BLK, BLK)
-        update = scaled[block // 8, pl.ds(start, BLK), :].astype(WIDE) * chosen
-        update_rows[rows, :] = update
-        new_master[rows, :] = master[rows, :] - learn_rate * update
-        return carry
-
-    lax.fori_loop(0, NB // 8, own_block, 0, unroll=4)
+    lane = lax.broadcasted_iota(jnp.int32, (1, 128), 1)
+    for line in range(7):
+        values = jnp.zeros((1, 128), WIDE)
+        for part in range(4):
+            local = line * 4 + part
+            block = block_order[owner * (NB // 8) + local]
+            side, slot, place = block // (8 * SLOTS), lax.rem(block // 8, SLOTS), lax.rem(block, 8)
+            chosen = jnp.where(block >= NB3, factor[1:2], factor[0:1])
+            rows = slice(local * BLK, local * BLK + BLK)
+            start = pl.multiple_of(place * BLK, BLK)
+            update = scaled[side, slot, pl.ds(start, BLK), :].astype(WIDE) * chosen
+            update_rows[rows, :] = update
+            new_master[rows, :] = master[rows, :] - learn_rate * update
+            for half in range(2):
+                at_row = (side * 16 + place * 2 + half) * 2 + slot // 8
+                to = part * 32 + half * 16
+                turn = lax.rem(128 + to - lax.rem(slot, 8) * 16, 128)
+                turned = pltpu.roll(row_table[pl.ds(at_row, 1), :], turn, 1)
+                values = jnp.where((lane >= to) & (lane < to + 16), turned, values)
+        new_row[line : line + 1] = values
 
 
 def shards(
@@ -389,18 +422,21 @@
         ],
         flops=2 * 14 * 1024 * 256 * 256,
         moved=6 << 20,
+        room=16,
     )(
         at, saved_tiles[0], tile_peer[0], pre_act, pre_peer, grad_output, grad_peer, pointwise_live
     )
 
-    master_low = master_rows.astype(LOW)
-    master_line = [master_low] + [swap(master_low, away * 2) for away in (1, 2, 3)]
-    master_all = master_line + [swap(piece, MASK_CORE) for piece in master_line]
-    natural = call(
-        order_kernel, [((NB * BLK, CO), LOW)], [SMEM] * 2 + [VMEM] * 8, moved=8 << 20
-    )(at, block_order, *master_all)[0]
-    moment_line = jnp.stack([row_moment] + [swap(row_moment, away * 2) for away in (1, 2, 3)])
-    moment_all = jnp.stack([moment_line, swap(moment_line, MASK_CORE)])
+    packed = call(
+        pack_kernel,
+        [((SLOTS + 1, 16, CO), LOW)],
+        [SMEM, HBM, VMEM],
+        scratch=[pltpu.VMEM((SLOTS * 16, CO), WIDE), pltpu.SemaphoreType.DMA],
+    )(at, master_rows, row_moment.reshape(7, 128))[0]
+    packs = [packed] + [swap(packed, away * 2) for away in (1, 2, 3)]
+    moment_line = jnp.stack([pack[SLOTS] for pack in packs])
+    moment_all = jnp.stack([moment_line, swap(moment_line, MASK_CORE)])[:, :, :7].astype(WIDE)
+    moment_all = (moment_all[..., :128] + moment_all[..., 128:]).reshape(2, 4, 896)
     moment_stored = moment_all[jnp.arange(2) ^ core][:, jnp.arange(4) ^ axis_z]
     moment_stored = jnp.swapaxes(moment_stored, 0, 1).reshape(NB, BLK)
     inverse = jnp.zeros((NB,), jnp.int32).at[block_order].set(jnp.arange(NB, dtype=jnp.int32))
@@ -422,52 +458,58 @@
         at, keep_a, got_a, keep_b, got_b
     )
     gots = [swap(send, (away + 1) * 2) for away, send in enumerate(sends)]
-    scaled, message = call(
-        moment_kernel,
-        [(piece, LOW), ((8, CO), WIDE)],
-        [SMEM] * 2 + [VMEM] * 5,
+    wide_piece = (SLOTS + 1, 16, CO)
+    scaled = call(moment_kernel, [(wide_piece, LOW)], [SMEM] * 2 + [VMEM] * 5, moved=1 << 20)(
+        at, decay_rate, own, *gots, own_moment
+    )[0]
+
+    line = call(
+        line_kernel, [((4, SLOTS * 16, CO), LOW)], [SMEM, HBM] + [VMEM] * 4, moved=1 << 20
+    )(at, own, *packs)[0]
+    plane = [line] + [swap(line, mask) for mask in (MASK_X, MASK_Y, MASK_X + MASK_Y)]
+    plane_peer = [swap(piece, MASK_CORE) for piece in plane]
+    natural = call(
+        order_kernel, [((NB * BLK, CO), LOW)], [SMEM] * 2 + [VMEM] * 8, moved=8 << 20
+    )(at, block_order, *plane, *plane_peer)[0]
+
+    gots = [swap(scaled, away * 2) for away in (1, 2, 3)]
+    mine_a, mine_b = call(
+        join_kernel,
+        [((HALF, 64, CO), LOW), ((HALF + 1, 64, CO), LOW)],
+        [SMEM, HBM] + [VMEM] * 4,
         moved=1 << 20,
-    )(at, decay_rate, own, *gots, own_moment)
-
-    gots = [swap(scaled, away * 2) for away in (1, 2, 3)]
-    mine_a, mine_b = call(join_kernel, [(quarter, LOW)] * 2, [SMEM] + [VMEM] * 4, moved=1 << 20)(
-        at, scaled, *gots
-    )
+    )(at, views, scaled, *gots)
     got_a, got_b = swap(mine_a, MASK_Y), swap(mine_b, MASK_X)
     mine_a, mine_b = call(
-        pair_kernel, [(part_a, LOW), (part_b, LOW)], [SMEM] + [VMEM] * 4, moved=2 << 20
-    )(at, mine_a, got_a, mine_b, got_b)
+        pair_kernel,
+        [((HALF, 128, CO), LOW), ((HALF + 1, 128, CO), LOW)],
+        [SMEM, HBM] + [VMEM] * 4,
+        moved=2 << 20,
+    )(at, natural, mine_a, got_a, mine_b, got_b)
     got_a, got_b = swap(mine_a, MASK_X), swap(mine_b, MASK_Y)
     halves = (mine_a, got_a, mine_b, got_b)
     peers = [swap(half, MASK_CORE) for half in halves]
 
-    line = jnp.stack([message] + [swap(message, away * 2) for away in (1, 2, 3)])
-    plane = jnp.stack([line] + [swap(line, mask) for mask in (MASK_Y, MASK_X, MASK_X + MASK_Y)])
-    plane_peer = swap(plane, MASK_CORE)
-    new_col, factor = call(
-        factor_kernel, [((2, CO), WIDE)] * 2, [SMEM] + [VMEM] * 3, moved=1 << 18
-    )(decay_rate, plane.reshape(16, 8, CO), plane_peer.reshape(16, 8, CO), col_moment)
-    rows = jnp.stack([plane, plane_peer])[:, :, :, 6, : SLOTS * 16]
-    rows = rows[jnp.arange(2) ^ core]
-    rows = rows[:, jnp.arange(4) ^ (axis_x * 2 + axis_y)]
-    rows = rows[:, :, jnp.arange(4) ^ axis_z].reshape(2, 4, 4, SLOTS, 16)
-    rows = jnp.transpose(rows, (0, 3, 1, 2, 4)).reshape(NB, BLK)
-    own_blocks = lax.dynamic_slice_in_dim(block_order, shard * (NB // 8), NB // 8)
-    new_row = jnp.take(rows, own_blocks, axis=0).reshape(-1)
-
-    update_rows, new_master, next_output = call(
+    update_rows, new_master, new_row, new_col, next_output = call(
         finish_kernel,
-        [((NB // 8 * BLK, CO), WIDE), ((NB // 8 * BLK, CO), WIDE), ((PIX, CO), LOW)],
-        [SMEM] * 2 + [VMEM] * 12,
+        [
+            ((NB // 8 * BLK, CO), WIDE),
+            ((NB // 8 * BLK, CO), WIDE),
+            ((7, 128), WIDE),
+            ((2, CO), WIDE),
+            ((PIX, CO), LOW),
+        ],
+        [SMEM] * 3 + [VMEM] * 12,
         scratch=[
-            pltpu.VMEM((28, CI, CO), LOW),
-            pltpu.VMEM((PIX, CO), WIDE),
-            pltpu.VMEM((CI, CO), LOW),
+            pltpu.VMEM((2, SLOTS + 1, CI, CO), LOW),
+            pltpu.VMEM((2, CO), WIDE),
+            pltpu.VMEM((64, 128), WIDE),
         ],
         flops=2 * 28 * 512 * 256 * 256,
         moved=16 << 20,
-    )(at, block_order, factor, views, natural, master_rows, *halves, *peers)
-    return (update_rows, new_master, new_row, new_col, next_output)
+        room=16,
+    )(at, block_order, decay_rate, col_moment, views, natural, master_rows, *halves, *peers)
+    return (update_rows, new_master, new_row.reshape(-1), new_col, next_output)
 
 
 def solution(mesh):

time: 172 us -> 113 us (0.66)
  waiting for transfers between devices: 69.2 us -> 44.1 us
  local copies, waits for them, and re-layouts: 27.1 us -> 8.4 us
  starting transfers between devices: 47.3 us -> 38.1 us
  Pallas kernels: 23.3 us -> 19.6 us
    ppermute x39 -> x32, waiting for transfers between devices: 69.2 us -> 44.1 us  [swap(): return lax.ppermute(value, AXES, [(at, at ^ mask) for at in range(32)])]
    unnamed x45 -> x18, local copies, waits for them, and re-layouts: 17.4 us -> 4.33 us
    ppermute x39 -> x32, starting transfers between devices: 47.3 us -> 38.1 us  [swap(): return lax.ppermute(value, AXES, [(at, at ^ mask) for at in range(32)])]
    gather x6 -> x0, local copies, waits for them, and re-layouts: 2.34 us -> none  [the longest x2 0.6 us: shards(): rows = rows[:, :, jnp.arange(4) ^ axis_z].reshape(2, 4, 4, SLOTS, 16)]
    pallas_call x4 -> x5, Pallas kernels: 3.62 us -> 3.48 us  [the longest x1 0.87 us: shards(): call(pack_kernel, [((SLOTS + 1, 16, CO), LOW)], [SMEM, HBM, VMEM], scratc...]
  transfers between devices with their start and end apart: 39 -> 32, of which waited for: 14 -> 14; matrix products, arithmetic and copies ran while one was open for 8% -> 7% of each run, Pallas kernels for 10% -> 10%
where the time goes in v2:
time: 113 us
  waiting for transfers between devices  44.1 us (39%)
  starting transfers between devices  38.1 us (34%)
  Pallas kernels  19.6 us (17%)
  local copies, waits for them, and re-layouts  8.4 us (7%)
  between operations  1.76 us (2%)
    ppermute x32, waiting for transfers between devices, swap(): return lax.ppermute(value, AXES, [(at, at ^ mask) for at in range(32)])  44.1 us
    ppermute x32, starting transfers between devices, swap(): return lax.ppermute(value, AXES, [(at, at ^ mask) for at in range(32)])  38.1 us
    pallas_call x1, Pallas kernels, shards(): call(term_kernel, [(part_a, LOW), (part_a, LOW), (part_b, LOW), (part_b,...  8.66 us
    pallas_call x1, Pallas kernels, shards(): call(finish_kernel, [((NB // 8 * BLK, CO), WIDE), ((NB // 8 * BLK, CO), W...  4.9 us
    unnamed x18, local copies, waits for them, and re-layouts  4.33 us
  transfers between devices with their start and end apart: 32, of which 14 were waited for; matrix products, arithmetic and copies ran while one was open for 7% of the time, Pallas kernels for 10%

profile of v2, /device:TPU:0, one launch (start us, length us, event | category | flops | bytes accessed | tf_op | source)
XLA Modules:
  0.0 112.9 jit_solution(971531229983519047)
XLA Ops:
  0.7 1.2 %copy-done = f32[896,256]{1,0:T(8,128)S(1)} copy-done((f32[896,256]{1,0:T(8,128)S(1)}, f32[896,256]{1,0:T(8,128)}, u32[]{:S(2)}) %copy-start) | copy-done | bytes 917528
  2.6 0.9 shard_map.141.own
  3.5 5.1 %collective-permute-start.9 = (bf16[15,16,256]{2,1,0:T(8,128)(2,1)S(1)}, bf16[15,16,256]{2,1,0:T(8,128)(2,1)S(1)}, u32[]{:S(2)}, u32[]{:S(2)}) collective-permute-start(bf16[15,16,256]{2,1,0:T(8,128)(2,1)S(1)} %shard_map.141.own), channel_id=1, source_target_pairs={{0,6},{1,7},{2,4},{3,5},{4,2},{5,3},{6,0},{7,1},{8,14},{9,15},{10,... | collective-permute-start | bytes 368648 | tf_op jit(solution)/shard_map/ppermute | solution.py:132
  9.8 1.3 %scatter_custom_fusion = s32[224]{0:T(256)S(1)} fusion(s32[224]{0:T(256)S(1)} %compare_select_fusion.1, s32[224]{0:T(256)S(1)} %iota.11, s32[]{:T(128)} %constant.88.clone.1), kind=kCustom, calls=%fused_computation.24 | custom fusion | bytes 900 | tf_op jit(solution)/shard_map/scatter | solution.py:442
  11.1 1.2 %copy.44 = bf16[1,4,18,18,256]{4,3,2,1,0:T(8,128)(2,1)S(1)} copy(bf16[1,4,18,18,256]{4,1,3,2,0:T(4,128)(2,1)} %param.12) | data formatting | bytes 1327104 | tf_op args[2]
  13.3 8.7 %shard_map.138 = (bf16[7,128,256]{2,1,0:T(8,128)(2,1)S(1)}, bf16[7,128,256]{2,1,0:T(8,128)(2,1)}, bf16[7,128,256]{2,1,0:T(8,128)(2,1)S(1)}, bf16[7,128,256]{2,1,0:T(8,128)(2,1)S(1)}) custom-call(s32[4]{0:T(128)S(1)} %pad_add_fusion.at, bf16[4,18,18,256]{3,2,1,0:T(8,128)(2,1)S(1)} %bitcast.26, bf16[4,18,18,256]{3,2,1,0:T(8,128)(2,1)S(1)} %bitcast.27, ...), custom_call_target="tpu_custom_call" | custom-call | flops 1879048192 | bytes 6291456 | tf_op jit(solution)/shard_map/pallas_call | solution.py:412
  21.9 1.7 %collective-permute-start.3 = (bf16[7,128,256]{2,1,0:T(8,128)(2,1)}, bf16[7,128,256]{2,1,0:T(8,128)(2,1)S(1)}, u32[]{:S(2)}, u32[]{:S(2)}) collective-permute-start(bf16[7,128,256]{2,1,0:T(8,128)(2,1)} %get-tuple-element.27), channel_id=1, source_target_pairs={{0,8},{1,9},{2,10},{3,11},{4,12},{5,13},{6,14},{7,15},{8,0},{9,1},... | collective-permute-start | bytes 1376264 | tf_op jit(solution)/shard_map/ppermute | solution.py:132
  23.6 1.5 %collective-permute-start.4 = (bf16[7,128,256]{2,1,0:T(8,128)(2,1)S(1)}, bf16[7,128,256]{2,1,0:T(8,128)(2,1)S(1)}, u32[]{:S(2)}, u32[]{:S(2)}) collective-permute-start(bf16[7,128,256]{2,1,0:T(8,128)(2,1)S(1)} %get-tuple-element.29), channel_id=1, source_target_pairs={{0,16},{1,17},{2,18},{3,19},{4,20},{5,21},{6,22},{7,23},{8,24},{9,... | collective-permute-start | bytes 1376264 | tf_op jit(solution)/shard_map/ppermute | solution.py:132
  25.6 9.2 %collective-permute-done.3.got_a = bf16[7,128,256]{2,1,0:T(8,128)(2,1)S(1)} collective-permute-done((bf16[7,128,256]{2,1,0:T(8,128)(2,1)}, bf16[7,128,256]{2,1,0:T(8,128)(2,1)S(1)}, u32[]{:S(2)}, u32[]{:S(2)}) %collective-permute-start.3) | collective-permute-done | bytes 458784 | tf_op jit(solution)/shard_map/ppermute | solution.py:132
  34.9 1.2 %collective-permute-done.4.got_b = bf16[7,128,256]{2,1,0:T(8,128)(2,1)S(1)} collective-permute-done((bf16[7,128,256]{2,1,0:T(8,128)(2,1)S(1)}, bf16[7,128,256]{2,1,0:T(8,128)(2,1)S(1)}, u32[]{:S(2)}, u32[]{:S(2)}) %collective-permute-start.4) | collective-permute-done | bytes 458784 | tf_op jit(solution)/shard_map/ppermute | solution.py:132
  36.8 1.6 %collective-permute-start.5 = (bf16[7,64,256]{2,1,0:T(8,128)(2,1)S(1)}, bf16[7,64,256]{2,1,0:T(8,128)(2,1)S(1)}, u32[]{:S(2)}, u32[]{:S(2)}) collective-permute-start(bf16[7,64,256]{2,1,0:T(8,128)(2,1)S(1)} %get-tuple-element.31), channel_id=1, source_target_pairs={{0,16},{1,17},{2,18},{3,19},{4,20},{5,21},{6,22},{7,23},{8,24},{9,... | collective-permute-start | bytes 688136 | tf_op jit(solution)/shard_map/ppermute | solution.py:132
  40.2 3.3 %collective-permute-done.5.got_a = bf16[7,64,256]{2,1,0:T(8,128)(2,1)S(1)} collective-permute-done((bf16[7,64,256]{2,1,0:T(8,128)(2,1)S(1)}, bf16[7,64,256]{2,1,0:T(8,128)(2,1)S(1)}, u32[]{:S(2)}, u32[]{:S(2)}) %collective-permute-start.5) | collective-permute-done | bytes 229408 | tf_op jit(solution)/shard_map/ppermute | solution.py:132
  43.5 1.2 %collective-permute-done.6.got_b = bf16[7,64,256]{2,1,0:T(8,128)(2,1)S(1)} collective-permute-done((bf16[7,64,256]{2,1,0:T(8,128)(2,1)S(1)}, bf16[7,64,256]{2,1,0:T(8,128)(2,1)S(1)}, u32[]{:S(2)}, u32[]{:S(2)}) %collective-permute-start.6) | collective-permute-done | bytes 229408 | tf_op jit(solution)/shard_map/ppermute | solution.py:132
  46.8 1.5 %collective-permute-start.11 = (bf16[4,224,256]{2,1,0:T(8,128)(2,1)S(1)}, bf16[4,224,256]{2,1,0:T(8,128)(2,1)S(1)}, u32[]{:S(2)}, u32[]{:S(2)}) collective-permute-start(bf16[4,224,256]{2,1,0:T(8,128)(2,1)S(1)} %shard_map.142.refs_0_), channel_id=1, source_target_pairs={{0,16},{1,17},{2,18},{3,19},{4,20},{5,21},{6,22},{7,23},{8,24},{9,... | collective-permute-start | bytes 1376264 | tf_op jit(solution)/shard_map/ppermute | solution.py:132
  48.4 1.2 %collective-permute-start.10 = (bf16[4,224,256]{2,1,0:T(8,128)(2,1)S(1)}, bf16[4,224,256]{2,1,0:T(8,128)(2,1)S(1)}, u32[]{:S(2)}, u32[]{:S(2)}) collective-permute-start(bf16[4,224,256]{2,1,0:T(8,128)(2,1)S(1)} %shard_map.142.refs_0_), channel_id=1, source_target_pairs={{0,8},{1,9},{2,10},{3,11},{4,12},{5,13},{6,14},{7,15},{8,0},{9,1},... | collective-permute-start | bytes 1376264 | tf_op jit(solution)/shard_map/ppermute | solution.py:132
  49.6 1.2 %collective-permute-start.17 = (bf16[14,16,256]{2,1,0:T(8,128)(2,1)S(1)}, bf16[14,16,256]{2,1,0:T(8,128)(2,1)S(1)}, u32[]{:S(2)}, u32[]{:S(2)}) collective-permute-start(bf16[14,16,256]{2,1,0:T(8,128)(2,1)S(1)} %get-tuple-element.35), channel_id=1, source_target_pairs={{0,2},{1,3},{2,0},{3,1},{4,6},{5,7},{6,4},{7,5},{8,10},{9,11},{10,... | collective-permute-start | bytes 344072 | tf_op jit(solution)/shard_map/ppermute | solution.py:132
  50.8 2.9 %collective-permute-start.18 = (bf16[14,16,256]{2,1,0:T(8,128)(2,1)S(1)}, bf16[14,16,256]{2,1,0:T(8,128)(2,1)S(1)}, u32[]{:S(2)}, u32[]{:S(2)}) collective-permute-start(bf16[14,16,256]{2,1,0:T(8,128)(2,1)S(1)} %get-tuple-element.36), channel_id=1, source_target_pairs={{0,4},{1,5},{2,6},{3,7},{4,0},{5,1},{6,2},{7,3},{8,12},{9,13},{10,... | collective-permute-start | bytes 344072 | tf_op jit(solution)/shard_map/ppermute | solution.py:132
  56.5 4.2 %collective-permute-start.19 = (bf16[14,16,256]{2,1,0:T(8,128)(2,1)S(1)}, bf16[14,16,256]{2,1,0:T(8,128)(2,1)S(1)}, u32[]{:S(2)}, u32[]{:S(2)}) collective-permute-start(bf16[14,16,256]{2,1,0:T(8,128)(2,1)S(1)} %get-tuple-element.37), channel_id=1, source_target_pairs={{0,6},{1,7},{2,4},{3,5},{4,2},{5,3},{6,0},{7,1},{8,14},{9,15},{10,... | collective-permute-start | bytes 344072 | tf_op jit(solution)/shard_map/ppermute | solution.py:132
  60.9 2.6 %collective-permute-done.19.three = bf16[14,16,256]{2,1,0:T(8,128)(2,1)S(1)} collective-permute-done((bf16[14,16,256]{2,1,0:T(8,128)(2,1)S(1)}, bf16[14,16,256]{2,1,0:T(8,128)(2,1)S(1)}, u32[]{:S(2)}, u32[]{:S(2)}) %collective-permute-start.19) | collective-permute-done | bytes 114720 | tf_op jit(solution)/shard_map/ppermute | solution.py:132
  64.4 3.9 %collective-permute-start.23 = (bf16[15,16,256]{2,1,0:T(8,128)(2,1)S(1)}, bf16[15,16,256]{2,1,0:T(8,128)(2,1)S(1)}, u32[]{:S(2)}, u32[]{:S(2)}) collective-permute-start(bf16[15,16,256]{2,1,0:T(8,128)(2,1)S(1)} %shard_map.144.own), channel_id=1, source_target_pairs={{0,6},{1,7},{2,4},{3,5},{4,2},{5,3},{6,0},{7,1},{8,14},{9,15},{10,... | collective-permute-start | bytes 368648 | tf_op jit(solution)/shard_map/ppermute | solution.py:132
  68.3 3.2 %collective-permute-done.23.three = bf16[15,16,256]{2,1,0:T(8,128)(2,1)S(1)} collective-permute-done((bf16[15,16,256]{2,1,0:T(8,128)(2,1)S(1)}, bf16[15,16,256]{2,1,0:T(8,128)(2,1)S(1)}, u32[]{:S(2)}, u32[]{:S(2)}) %collective-permute-start.23) | collective-permute-done | bytes 122912 | tf_op jit(solution)/shard_map/ppermute | solution.py:132
  71.5 2.2 %collective-permute-start.22 = (bf16[15,16,256]{2,1,0:T(8,128)(2,1)S(1)}, bf16[15,16,256]{2,1,0:T(8,128)(2,1)S(1)}, u32[]{:S(2)}, u32[]{:S(2)}) collective-permute-start(bf16[15,16,256]{2,1,0:T(8,128)(2,1)S(1)} %shard_map.144.own), channel_id=1, source_target_pairs={{0,4},{1,5},{2,6},{3,7},{4,0},{5,1},{6,2},{7,3},{8,12},{9,13},{10,... | collective-permute-start | bytes 368648 | tf_op jit(solution)/shard_map/ppermute | solution.py:132
  74.3 3.0 %collective-permute-done.22.two = bf16[15,16,256]{2,1,0:T(8,128)(2,1)S(1)} collective-permute-done((bf16[15,16,256]{2,1,0:T(8,128)(2,1)S(1)}, bf16[15,16,256]{2,1,0:T(8,128)(2,1)S(1)}, u32[]{:S(2)}, u32[]{:S(2)}) %collective-permute-start.22) | collective-permute-done | bytes 122912 | tf_op jit(solution)/shard_map/ppermute | solution.py:132
  77.2 4.3 %collective-permute-start.21 = (bf16[15,16,256]{2,1,0:T(8,128)(2,1)S(1)}, bf16[15,16,256]{2,1,0:T(8,128)(2,1)S(1)}, u32[]{:S(2)}, u32[]{:S(2)}) collective-permute-start(bf16[15,16,256]{2,1,0:T(8,128)(2,1)S(1)} %shard_map.144.own), channel_id=1, source_target_pairs={{0,2},{1,3},{2,0},{3,1},{4,6},{5,7},{6,4},{7,5},{8,10},{9,11},{10,... | collective-permute-start | bytes 368648 | tf_op jit(solution)/shard_map/ppermute | solution.py:132
  81.5 1.2 %copy.45 = bf16[1,4,18,18,256]{4,3,2,1,0:T(8,128)(2,1)S(1)} copy(bf16[1,4,18,18,256]{4,1,3,2,0:T(4,128)(2,1)} %param.19) | data formatting | bytes 1327104 | tf_op args[9]
  83.0 1.4 %collective-permute-done.21.one = bf16[15,16,256]{2,1,0:T(8,128)(2,1)S(1)} collective-permute-done((bf16[15,16,256]{2,1,0:T(8,128)(2,1)S(1)}, bf16[15,16,256]{2,1,0:T(8,128)(2,1)S(1)}, u32[]{:S(2)}, u32[]{:S(2)}) %collective-permute-start.21) | collective-permute-done | bytes 122912 | tf_op jit(solution)/shard_map/ppermute | solution.py:132
  85.0 1.8 %collective-permute-start.25 = (bf16[8,64,256]{2,1,0:T(8,128)(2,1)S(1)}, bf16[8,64,256]{2,1,0:T(8,128)(2,1)S(1)}, u32[]{:S(2)}, u32[]{:S(2)}) collective-permute-start(bf16[8,64,256]{2,1,0:T(8,128)(2,1)S(1)} %get-tuple-element.39.mine_b), channel_id=1, source_target_pairs={{0,8},{1,9},{2,10},{3,11},{4,12},{5,13},{6,14},{7,15},{8,0},{9,1},... | collective-permute-start | bytes 786440 | tf_op jit(solution)/shard_map/ppermute | solution.py:132
  87.3 0.9 shard_map.143.after.natural
  88.2 6.6 %collective-permute-done.24.got_a = bf16[7,64,256]{2,1,0:T(8,128)(2,1)S(1)} collective-permute-done((bf16[7,64,256]{2,1,0:T(8,128)(2,1)S(1)}, bf16[7,64,256]{2,1,0:T(8,128)(2,1)S(1)}, u32[]{:S(2)}, u32[]{:S(2)}) %collective-permute-start.24) | collective-permute-done | bytes 229408 | tf_op jit(solution)/shard_map/ppermute | solution.py:132
  96.0 8.7 %collective-permute-done.27.got_b = bf16[8,128,256]{2,1,0:T(8,128)(2,1)S(1)} collective-permute-done((bf16[8,128,256]{2,1,0:T(8,128)(2,1)S(1)}, bf16[8,128,256]{2,1,0:T(8,128)(2,1)S(1)}, u32[]{:S(2)}, u32[]{:S(2)}) %collective-permute-start.27) | collective-permute-done | bytes 524320 | tf_op jit(solution)/shard_map/ppermute | solution.py:132
  105.2 2.0 %collective-permute-done.28.peer_a = bf16[7,128,256]{2,1,0:T(8,128)(2,1)S(1)} collective-permute-done((bf16[7,128,256]{2,1,0:T(8,128)(2,1)S(1)}, bf16[7,128,256]{2,1,0:T(8,128)(2,1)S(1)}, u32[]{:S(2)}, u32[]{:S(2)}) %collective-permute-start.28) | collective-permute-done | bytes 458784 | tf_op jit(solution)/shard_map/ppermute | solution.py:132
  108.0 4.9 %shard_map.147 = (f32[896,256]{1,0:T(8,128)}, f32[896,256]{1,0:T(8,128)}, f32[7,128]{1,0:T(8,128)}, f32[2,256]{1,0:T(2,128)}, bf16[512,256]{1,0:T(8,128)(2,1)}) custom-call(s32[4]{0:T(128)S(1)} %pad_add_fusion.at, s32[224]{0:T(256)S(1)} %copy-done.2, f32[1]{0:T(128)S(6)} %sub.12.rate, f32[2,256]{1,0:T(2,128)S(1)} %copy-done.4, ...), custom_call_target="tpu_custom_call" | custom-call | flops 1879048192 | bytes 16777216 | tf_op jit(solution)/shard_map/pallas_call | solution.py:493
  (95 shorter events, 15.2 us)
Async XLA Ops:
  3.5 22.1 %collective-permute-start.9 = (bf16[15,16,256]{2,1,0:T(8,128)(2,1)S(1)}, bf16[15,16,256]{2,1,0:T(8,128)(2,1)S(1)}, u32[]{:S(2)}, u32[]{:S(2)}) collective-permute-start(bf16[15,16,256]{2,1,0:T(8,128)(2,1)S(1)} %shard_map.141.own), channel_id=1, source_target_pairs={{0,6},{1,7},{2,4},{3,5},{4,2},{5,3},{6,0},{7,1},{8,14},{9,15},{10,... | collective-permute-start | bytes 368648 | tf_op jit(solution)/shard_map/ppermute | solution.py:132
  8.6 17.0 %collective-permute-start.8 = (bf16[15,16,256]{2,1,0:T(8,128)(2,1)S(1)}, bf16[15,16,256]{2,1,0:T(8,128)(2,1)S(1)}, u32[]{:S(2)}, u32[]{:S(2)}) collective-permute-start(bf16[15,16,256]{2,1,0:T(8,128)(2,1)S(1)} %shard_map.141.own), channel_id=1, source_target_pairs={{0,4},{1,5},{2,6},{3,7},{4,0},{5,1},{6,2},{7,3},{8,12},{9,13},{10,... | collective-permute-start | bytes 368648 | tf_op jit(solution)/shard_map/ppermute | solution.py:132
  8.6 4.6 %collective-permute-start.1 = (bf16[512,256]{1,0:T(8,128)(2,1)}, bf16[512,256]{1,0:T(8,128)(2,1)S(1)}, u32[]{:S(2)}, u32[]{:S(2)}) collective-permute-start(bf16[512,256]{1,0:T(8,128)(2,1)} %pre.1), channel_id=1, source_target_pairs={{0,1},{1,0},{2,3},{3,2},{4,5},{5,4},{6,7},{7,6},{8,9},{9,8},{10,11... | collective-permute-start | bytes 786440 | tf_op jit(solution)/shard_map/ppermute | solution.py:132
  8.6 4.6 %collective-permute-start.2 = (bf16[512,256]{1,0:T(8,128)(2,1)}, bf16[512,256]{1,0:T(8,128)(2,1)S(1)}, u32[]{:S(2)}, u32[]{:S(2)}) collective-permute-start(bf16[512,256]{1,0:T(8,128)(2,1)} %grad.1), channel_id=1, source_target_pairs={{0,1},{1,0},{2,3},{3,2},{4,5},{5,4},{6,7},{7,6},{8,9},{9,8},{10,11... | collective-permute-start | bytes 786440 | tf_op jit(solution)/shard_map/ppermute | solution.py:132
  9.1 3.3 %collective-permute-start = (bf16[1,4,18,18,256]{4,1,3,2,0:T(4,128)(2,1)}, bf16[1,4,18,18,256]{4,1,3,2,0:T(4,128)(2,1)S(1)}, u32[]{:S(2)}, u32[]{:S(2)}) collective-permute-start(bf16[1,4,18,18,256]{4,1,3,2,0:T(4,128)(2,1)} %param.12), channel_id=1, source_target_pairs={{0,1},{1,0},{2,3},{3,2},{4,5},{5,4},{6,7},{7,6},{8,9},{9,8},{10,11... | collective-permute-start | bytes 1990664 | tf_op jit(solution)/shard_map/ppermute | solution.py:132
  12.4 13.2 %collective-permute-start.7 = (bf16[15,16,256]{2,1,0:T(8,128)(2,1)S(1)}, bf16[15,16,256]{2,1,0:T(8,128)(2,1)S(1)}, u32[]{:S(2)}, u32[]{:S(2)}) collective-permute-start(bf16[15,16,256]{2,1,0:T(8,128)(2,1)S(1)} %shard_map.141.own), channel_id=1, source_target_pairs={{0,2},{1,3},{2,0},{3,1},{4,6},{5,7},{6,4},{7,5},{8,10},{9,11},{10,... | collective-permute-start | bytes 368648 | tf_op jit(solution)/shard_map/ppermute | solution.py:132
  21.9 12.9 %collective-permute-start.3 = (bf16[7,128,256]{2,1,0:T(8,128)(2,1)}, bf16[7,128,256]{2,1,0:T(8,128)(2,1)S(1)}, u32[]{:S(2)}, u32[]{:S(2)}) collective-permute-start(bf16[7,128,256]{2,1,0:T(8,128)(2,1)} %get-tuple-element.27), channel_id=1, source_target_pairs={{0,8},{1,9},{2,10},{3,11},{4,12},{5,13},{6,14},{7,15},{8,0},{9,1},... | collective-permute-start | bytes 1376264 | tf_op jit(solution)/shard_map/ppermute | solution.py:132
  23.6 12.4 %collective-permute-start.4 = (bf16[7,128,256]{2,1,0:T(8,128)(2,1)S(1)}, bf16[7,128,256]{2,1,0:T(8,128)(2,1)S(1)}, u32[]{:S(2)}, u32[]{:S(2)}) collective-permute-start(bf16[7,128,256]{2,1,0:T(8,128)(2,1)S(1)} %get-tuple-element.29), channel_id=1, source_target_pairs={{0,16},{1,17},{2,18},{3,19},{4,20},{5,21},{6,22},{7,23},{8,24},{9,... | collective-permute-start | bytes 1376264 | tf_op jit(solution)/shard_map/ppermute | solution.py:132
  36.8 6.7 %collective-permute-start.5 = (bf16[7,64,256]{2,1,0:T(8,128)(2,1)S(1)}, bf16[7,64,256]{2,1,0:T(8,128)(2,1)S(1)}, u32[]{:S(2)}, u32[]{:S(2)}) collective-permute-start(bf16[7,64,256]{2,1,0:T(8,128)(2,1)S(1)} %get-tuple-element.31), channel_id=1, source_target_pairs={{0,16},{1,17},{2,18},{3,19},{4,20},{5,21},{6,22},{7,23},{8,24},{9,... | collective-permute-start | bytes 688136 | tf_op jit(solution)/shard_map/ppermute | solution.py:132
  38.4 6.4 %collective-permute-start.6 = (bf16[7,64,256]{2,1,0:T(8,128)(2,1)S(1)}, bf16[7,64,256]{2,1,0:T(8,128)(2,1)S(1)}, u32[]{:S(2)}, u32[]{:S(2)}) collective-permute-start(bf16[7,64,256]{2,1,0:T(8,128)(2,1)S(1)} %get-tuple-element.33), channel_id=1, source_target_pairs={{0,8},{1,9},{2,10},{3,11},{4,12},{5,13},{6,14},{7,15},{8,0},{9,1},... | collective-permute-start | bytes 688136 | tf_op jit(solution)/shard_map/ppermute | solution.py:132
  38.9 1.3 %collective-permute-start.20 = (bf16[4,16,256]{2,1,0:T(8,128)(2,1)S(1)}, bf16[4,16,256]{2,1,0:T(8,128)(2,1)S(1)}, u32[]{:S(2)}, u32[]{:S(2)}) collective-permute-start(bf16[4,16,256]{2,1,0:T(8,128)(2,1)S(1)} %get-tuple-element.48), channel_id=1, source_target_pairs={{0,1},{1,0},{2,3},{3,2},{4,5},{5,4},{6,7},{7,6},{8,9},{9,8},{10,11... | collective-permute-start | bytes 98312 | tf_op jit(solution)/shard_map/ppermute | solution.py:132
  46.0 27.6 %collective-permute-start.12 = (bf16[4,224,256]{2,1,0:T(8,128)(2,1)S(1)}, bf16[4,224,256]{2,1,0:T(8,128)(2,1)S(1)}, u32[]{:S(2)}, u32[]{:S(2)}) collective-permute-start(bf16[4,224,256]{2,1,0:T(8,128)(2,1)S(1)} %shard_map.142.refs_0_), channel_id=1, source_target_pairs={{0,24},{1,25},{2,26},{3,27},{4,28},{5,29},{6,30},{7,31},{8,16},{9,... | collective-permute-start | bytes 1376264 | tf_op jit(solution)/shard_map/ppermute | solution.py:132
  46.8 26.8 %collective-permute-start.11 = (bf16[4,224,256]{2,1,0:T(8,128)(2,1)S(1)}, bf16[4,224,256]{2,1,0:T(8,128)(2,1)S(1)}, u32[]{:S(2)}, u32[]{:S(2)}) collective-permute-start(bf16[4,224,256]{2,1,0:T(8,128)(2,1)S(1)} %shard_map.142.refs_0_), channel_id=1, source_target_pairs={{0,16},{1,17},{2,18},{3,19},{4,20},{5,21},{6,22},{7,23},{8,24},{9,... | collective-permute-start | bytes 1376264 | tf_op jit(solution)/shard_map/ppermute | solution.py:132
  48.4 25.8 %collective-permute-start.10 = (bf16[4,224,256]{2,1,0:T(8,128)(2,1)S(1)}, bf16[4,224,256]{2,1,0:T(8,128)(2,1)S(1)}, u32[]{:S(2)}, u32[]{:S(2)}) collective-permute-start(bf16[4,224,256]{2,1,0:T(8,128)(2,1)S(1)} %shard_map.142.refs_0_), channel_id=1, source_target_pairs={{0,8},{1,9},{2,10},{3,11},{4,12},{5,13},{6,14},{7,15},{8,0},{9,1},... | collective-permute-start | bytes 1376264 | tf_op jit(solution)/shard_map/ppermute | solution.py:132
  49.6 6.3 %collective-permute-start.17 = (bf16[14,16,256]{2,1,0:T(8,128)(2,1)S(1)}, bf16[14,16,256]{2,1,0:T(8,128)(2,1)S(1)}, u32[]{:S(2)}, u32[]{:S(2)}) collective-permute-start(bf16[14,16,256]{2,1,0:T(8,128)(2,1)S(1)} %get-tuple-element.35), channel_id=1, source_target_pairs={{0,2},{1,3},{2,0},{3,1},{4,6},{5,7},{6,4},{7,5},{8,10},{9,11},{10,... | collective-permute-start | bytes 344072 | tf_op jit(solution)/shard_map/ppermute | solution.py:132
  50.8 5.7 %collective-permute-start.18 = (bf16[14,16,256]{2,1,0:T(8,128)(2,1)S(1)}, bf16[14,16,256]{2,1,0:T(8,128)(2,1)S(1)}, u32[]{:S(2)}, u32[]{:S(2)}) collective-permute-start(bf16[14,16,256]{2,1,0:T(8,128)(2,1)S(1)} %get-tuple-element.36), channel_id=1, source_target_pairs={{0,4},{1,5},{2,6},{3,7},{4,0},{5,1},{6,2},{7,3},{8,12},{9,13},{10,... | collective-permute-start | bytes 344072 | tf_op jit(solution)/shard_map/ppermute | solution.py:132
  55.9 30.9 %collective-permute-start.13 = (bf16[4,224,256]{2,1,0:T(8,128)(2,1)S(1)}, bf16[4,224,256]{2,1,0:T(8,128)(2,1)S(1)}, u32[]{:S(2)}, u32[]{:S(2)}) collective-permute-start(bf16[4,224,256]{2,1,0:T(8,128)(2,1)S(1)} %shard_map.142.refs_0_), channel_id=1, source_target_pairs={{0,1},{1,0},{2,3},{3,2},{4,5},{5,4},{6,7},{7,6},{8,9},{9,8},{10,11... | collective-permute-start | bytes 1376264 | tf_op jit(solution)/shard_map/ppermute | solution.py:132
  56.5 7.0 %collective-permute-start.19 = (bf16[14,16,256]{2,1,0:T(8,128)(2,1)S(1)}, bf16[14,16,256]{2,1,0:T(8,128)(2,1)S(1)}, u32[]{:S(2)}, u32[]{:S(2)}) collective-permute-start(bf16[14,16,256]{2,1,0:T(8,128)(2,1)S(1)} %get-tuple-element.37), channel_id=1, source_target_pairs={{0,6},{1,7},{2,4},{3,5},{4,2},{5,3},{6,0},{7,1},{8,14},{9,15},{10,... | collective-permute-start | bytes 344072 | tf_op jit(solution)/shard_map/ppermute | solution.py:132
  64.4 7.1 %collective-permute-start.23 = (bf16[15,16,256]{2,1,0:T(8,128)(2,1)S(1)}, bf16[15,16,256]{2,1,0:T(8,128)(2,1)S(1)}, u32[]{:S(2)}, u32[]{:S(2)}) collective-permute-start(bf16[15,16,256]{2,1,0:T(8,128)(2,1)S(1)} %shard_map.144.own), channel_id=1, source_target_pairs={{0,6},{1,7},{2,4},{3,5},{4,2},{5,3},{6,0},{7,1},{8,14},{9,15},{10,... | collective-permute-start | bytes 368648 | tf_op jit(solution)/shard_map/ppermute | solution.py:132
  71.5 5.8 %collective-permute-start.22 = (bf16[15,16,256]{2,1,0:T(8,128)(2,1)S(1)}, bf16[15,16,256]{2,1,0:T(8,128)(2,1)S(1)}, u32[]{:S(2)}, u32[]{:S(2)}) collective-permute-start(bf16[15,16,256]{2,1,0:T(8,128)(2,1)S(1)} %shard_map.144.own), channel_id=1, source_target_pairs={{0,4},{1,5},{2,6},{3,7},{4,0},{5,1},{6,2},{7,3},{8,12},{9,13},{10,... | collective-permute-start | bytes 368648 | tf_op jit(solution)/shard_map/ppermute | solution.py:132
  73.7 13.6 %collective-permute-start.16 = (bf16[4,224,256]{2,1,0:T(8,128)(2,1)S(1)}, bf16[4,224,256]{2,1,0:T(8,128)(2,1)S(1)}, u32[]{:S(2)}, u32[]{:S(2)}) collective-permute-start(bf16[4,224,256]{2,1,0:T(8,128)(2,1)S(1)} %collective-permute-done.12.refs_3_), channel_id=1, source_target_pairs={{0,1},{1,0},{2,3},{3,2},{4,5},{5,4},{6,7},{7,6},{8,9},{9,8},{10,11... | collective-permute-start | bytes 1376264 | tf_op jit(solution)/shard_map/ppermute | solution.py:132
  73.7 13.6 %collective-permute-start.15 = (bf16[4,224,256]{2,1,0:T(8,128)(2,1)S(1)}, bf16[4,224,256]{2,1,0:T(8,128)(2,1)S(1)}, u32[]{:S(2)}, u32[]{:S(2)}) collective-permute-start(bf16[4,224,256]{2,1,0:T(8,128)(2,1)S(1)} %collective-permute-done.11.refs_2_), channel_id=1, source_target_pairs={{0,1},{1,0},{2,3},{3,2},{4,5},{5,4},{6,7},{7,6},{8,9},{9,8},{10,11... | collective-permute-start | bytes 1376264 | tf_op jit(solution)/shard_map/ppermute | solution.py:132
  74.2 13.1 %collective-permute-start.14 = (bf16[4,224,256]{2,1,0:T(8,128)(2,1)S(1)}, bf16[4,224,256]{2,1,0:T(8,128)(2,1)S(1)}, u32[]{:S(2)}, u32[]{:S(2)}) collective-permute-start(bf16[4,224,256]{2,1,0:T(8,128)(2,1)S(1)} %collective-permute-done.10.refs_1_), channel_id=1, source_target_pairs={{0,1},{1,0},{2,3},{3,2},{4,5},{5,4},{6,7},{7,6},{8,9},{9,8},{10,11... | collective-permute-start | bytes 1376264 | tf_op jit(solution)/shard_map/ppermute | solution.py:132
  77.2 7.1 %collective-permute-start.21 = (bf16[15,16,256]{2,1,0:T(8,128)(2,1)S(1)}, bf16[15,16,256]{2,1,0:T(8,128)(2,1)S(1)}, u32[]{:S(2)}, u32[]{:S(2)}) collective-permute-start(bf16[15,16,256]{2,1,0:T(8,128)(2,1)S(1)} %shard_map.144.own), channel_id=1, source_target_pairs={{0,2},{1,3},{2,0},{3,1},{4,6},{5,7},{6,4},{7,5},{8,10},{9,11},{10,... | collective-permute-start | bytes 368648 | tf_op jit(solution)/shard_map/ppermute | solution.py:132
  85.0 9.9 %collective-permute-start.25 = (bf16[8,64,256]{2,1,0:T(8,128)(2,1)S(1)}, bf16[8,64,256]{2,1,0:T(8,128)(2,1)S(1)}, u32[]{:S(2)}, u32[]{:S(2)}) collective-permute-start(bf16[8,64,256]{2,1,0:T(8,128)(2,1)S(1)} %get-tuple-element.39.mine_b), channel_id=1, source_target_pairs={{0,8},{1,9},{2,10},{3,11},{4,12},{5,13},{6,14},{7,15},{8,0},{9,1},... | collective-permute-start | bytes 786440 | tf_op jit(solution)/shard_map/ppermute | solution.py:132
  86.8 8.0 %collective-permute-start.24 = (bf16[7,64,256]{2,1,0:T(8,128)(2,1)S(1)}, bf16[7,64,256]{2,1,0:T(8,128)(2,1)S(1)}, u32[]{:S(2)}, u32[]{:S(2)}) collective-permute-start(bf16[7,64,256]{2,1,0:T(8,128)(2,1)S(1)} %get-tuple-element.38.mine_a), channel_id=1, source_target_pairs={{0,16},{1,17},{2,18},{3,19},{4,20},{5,21},{6,22},{7,23},{8,24},{9,... | collective-permute-start | bytes 688136 | tf_op jit(solution)/shard_map/ppermute | solution.py:132
  95.5 9.2 %collective-permute-start.27 = (bf16[8,128,256]{2,1,0:T(8,128)(2,1)S(1)}, bf16[8,128,256]{2,1,0:T(8,128)(2,1)S(1)}, u32[]{:S(2)}, u32[]{:S(2)}) collective-permute-start(bf16[8,128,256]{2,1,0:T(8,128)(2,1)S(1)} %get-tuple-element.41.mine_b), channel_id=1, source_target_pairs={{0,16},{1,17},{2,18},{3,19},{4,20},{5,21},{6,22},{7,23},{8,24},{9,... | collective-permute-start | bytes 1572872 | tf_op jit(solution)/shard_map/ppermute | solution.py:132
  96.0 9.2 %collective-permute-start.26 = (bf16[7,128,256]{2,1,0:T(8,128)(2,1)S(1)}, bf16[7,128,256]{2,1,0:T(8,128)(2,1)S(1)}, u32[]{:S(2)}, u32[]{:S(2)}) collective-permute-start(bf16[7,128,256]{2,1,0:T(8,128)(2,1)S(1)} %get-tuple-element.40.mine_a), channel_id=1, source_target_pairs={{0,8},{1,9},{2,10},{3,11},{4,12},{5,13},{6,14},{7,15},{8,0},{9,1},... | collective-permute-start | bytes 1376264 | tf_op jit(solution)/shard_map/ppermute | solution.py:132
  96.0 11.3 %collective-permute-start.30 = (bf16[8,128,256]{2,1,0:T(8,128)(2,1)S(1)}, bf16[8,128,256]{2,1,0:T(8,128)(2,1)S(1)}, u32[]{:S(2)}, u32[]{:S(2)}) collective-permute-start(bf16[8,128,256]{2,1,0:T(8,128)(2,1)S(1)} %get-tuple-element.41.mine_b), channel_id=1, source_target_pairs={{0,1},{1,0},{2,3},{3,2},{4,5},{5,4},{6,7},{7,6},{8,9},{9,8},{10,11... | collective-permute-start | bytes 1572872 | tf_op jit(solution)/shard_map/ppermute | solution.py:132
  104.7 3.2 %collective-permute-start.31 = (bf16[8,128,256]{2,1,0:T(8,128)(2,1)S(1)}, bf16[8,128,256]{2,1,0:T(8,128)(2,1)S(1)}, u32[]{:S(2)}, u32[]{:S(2)}) collective-permute-start(bf16[8,128,256]{2,1,0:T(8,128)(2,1)S(1)} %collective-permute-done.27.got_b), channel_id=1, source_target_pairs={{0,1},{1,0},{2,3},{3,2},{4,5},{5,4},{6,7},{7,6},{8,9},{9,8},{10,11... | collective-permute-start | bytes 1572872 | tf_op jit(solution)/shard_map/ppermute | solution.py:132
  104.7 2.6 %collective-permute-start.28 = (bf16[7,128,256]{2,1,0:T(8,128)(2,1)S(1)}, bf16[7,128,256]{2,1,0:T(8,128)(2,1)S(1)}, u32[]{:S(2)}, u32[]{:S(2)}) collective-permute-start(bf16[7,128,256]{2,1,0:T(8,128)(2,1)S(1)} %get-tuple-element.40.mine_a), channel_id=1, source_target_pairs={{0,1},{1,0},{2,3},{3,2},{4,5},{5,4},{6,7},{7,6},{8,9},{9,8},{10,11... | collective-permute-start | bytes 1376264 | tf_op jit(solution)/shard_map/ppermute | solution.py:132
  105.2 2.7 %collective-permute-start.29 = (bf16[7,128,256]{2,1,0:T(8,128)(2,1)S(1)}, bf16[7,128,256]{2,1,0:T(8,128)(2,1)S(1)}, u32[]{:S(2)}, u32[]{:S(2)}) collective-permute-start(bf16[7,128,256]{2,1,0:T(8,128)(2,1)S(1)} %collective-permute-done.26.got_a), channel_id=1, source_target_pairs={{0,1},{1,0},{2,3},{3,2},{4,5},{5,4},{6,7},{7,6},{8,9},{9,8},{10,11... | collective-permute-start | bytes 1376264 | tf_op jit(solution)/shard_map/ppermute | solution.py:132
  (8 other events, 104.7 us)

commit v3 on v2

v3 whole, which is shorter than its diff:
```python
import functools
import jax
import jax.numpy as jnp
from jax import lax
from jax.experimental import pallas as pl
from jax.experimental.pallas import tpu as pltpu
from jax.sharding import PartitionSpec as P

CI = 256
CO = 256
BLK = 32
FR = 2
HW = 16
NB3 = 216
NB = 224


learn_rate = 0.002
decay_power = 0.8


def silu_slope(values):
    sigma = jax.nn.sigmoid(values)
    return sigma * (1.0 + values * (1.0 - sigma))


def tap_views(frames):
    views = []
    for frame_off in range(3):
        for row_off in range(3):
            for col_off in range(3):
                window = frames[
                    frame_off : frame_off + FR, row_off : row_off + HW, col_off : col_off + HW, :
                ]
                views.append(window.reshape(FR * HW * HW, CI))
    return views


def contract_rows(left, right):
    return lax.dot_general(
        left, right, (((0,), (0,)), ((), ())), preferred_element_type=jnp.float32
    )


def kernel_sums(values, is_small):
    large_part = jnp.sum(jnp.where(is_small[:, None], 0.0, values), axis=0)
    small_part = jnp.sum(jnp.where(is_small[:, None], values, 0.0), axis=0)
    return jnp.stack([large_part, small_part])


def general_shards(
    step_count,
    block_order,
    saved_tiles,
    pre_act,
    grad_output,
    pointwise_live,
    master_rows,
    row_moment,
    col_moment,
    next_tiles,
):
    pre_float = pre_act.astype(jnp.float32)
    activation = jax.nn.silu(pre_float).astype(jnp.bfloat16)
    grad_act = lax.dot_general(
        grad_output, pointwise_live, (((1,), (1,)), ((), ())), preferred_element_type=jnp.float32
    )
    grad_pre = (grad_act * silu_slope(pre_float)).astype(jnp.bfloat16)
    pieces = [contract_rows(view, grad_pre) for view in tap_views(saved_tiles[0])]
    pieces.append(contract_rows(activation, grad_output))
    own_term = jnp.concatenate(pieces, axis=0).astype(jnp.bfloat16)
    total_rows = NB * BLK
    stored = jnp.take(own_term.reshape(NB, BLK, CO), block_order, axis=0).reshape(total_rows, CO)
    own_rows = master_rows.shape[0]
    partial_value = lax.psum_scatter(stored, "shard", scatter_dimension=0, tiled=True).astype(
        jnp.float32
    )
    gradient = lax.psum(partial_value, "group")
    owner = lax.axis_index("shard")
    own_count = own_rows // BLK
    own_blocks = lax.dynamic_slice_in_dim(block_order, owner * own_count, own_count)
    is_small = jnp.repeat(own_blocks >= NB3, BLK, total_repeat_length=own_rows)
    decay_rate = 1.0 - step_count.astype(jnp.float32)[0] ** (-decay_power)
    counts = jnp.array([27 * CI, CO], jnp.float32)
    squares = gradient * gradient
    new_row = decay_rate * row_moment + (1.0 - decay_rate) * jnp.mean(squares, axis=1)
    col_part = kernel_sums(squares, is_small)
    row_part = kernel_sums(new_row[:, None], is_small)[:, 0]
    weighted = kernel_sums(squares / new_row[:, None], is_small)
    col_total, weight_total, row_total = lax.psum((col_part, weighted, row_part), "shard")
    new_col = decay_rate * col_moment + (1.0 - decay_rate) * col_total / counts[:, None]
    row_mean = row_total / counts
    col_rows = jnp.where(is_small[:, None], new_col[1], new_col[0])
    mean_rows = jnp.where(is_small, row_mean[1], row_mean[0])
    scaled = gradient / jnp.sqrt(new_row[:, None] * col_rows / mean_rows[:, None])
    square_total = row_mean * jnp.sum(weight_total / new_col, axis=1)
    clip_factor = jnp.maximum(1.0, jnp.sqrt(square_total / (counts * CO)))
    update_rows = scaled / jnp.where(is_small, clip_factor[1], clip_factor[0])[:, None]
    new_master = master_rows - learn_rate * update_rows
    weights_low = new_master.astype(jnp.bfloat16)
    gathered = lax.all_gather(weights_low, "shard", axis=0, tiled=True)
    inverse = jnp.zeros((NB,), jnp.int32).at[block_order].set(jnp.arange(NB, dtype=jnp.int32))
    natural = jnp.take(gathered.reshape(NB, BLK, CO), inverse, axis=0).reshape(total_rows, CO)
    spatial = natural[: 27 * CI].reshape(27, CI, CO)
    pointwise = natural[27 * CI :]
    hidden_sum = jnp.zeros((FR * HW * HW, CO), jnp.float32)
    for index_tap, view in enumerate(tap_views(next_tiles[0])):
        hidden_sum = hidden_sum + jnp.dot(
            view, spatial[index_tap], preferred_element_type=jnp.float32
        )
    hidden_act = jax.nn.silu(hidden_sum).astype(jnp.bfloat16)
    next_output = jnp.dot(hidden_act, pointwise, preferred_element_type=jnp.float32).astype(
        jnp.bfloat16
    )
    return (update_rows, new_master, new_row, new_col, next_output)


AXES = ("group", "shard")
SLOTS = 14
PIX = FR * HW * HW
SHIFTED = (FR + 2) * (HW + 2) * HW
LOW = jnp.bfloat16
WIDE = jnp.float32
VMEM = pl.BlockSpec(memory_space=pltpu.VMEM)
SMEM = pl.BlockSpec(memory_space=pltpu.SMEM)
HBM = pl.BlockSpec(memory_space=pl.ANY)
MASK_CORE, MASK_NEAR, MASK_FAR, MASK_X, MASK_Y = 1, 2, 4, 8, 16
PARTS = ((0, 5, (0, 1, 2)), (5, 5, (1, 2, 0)), (10, 4, (2, 0, 1)))
MASKS = (MASK_X, MASK_Y, MASK_NEAR)


def swap(value, mask):
    return lax.ppermute(value, AXES, [(at, at ^ mask) for at in range(32)])


def call(kernel, outs, in_specs, scratch=(), flops=0, moved=0, room=8):
    return pl.pallas_call(
        kernel,
        out_shape=[jax.ShapeDtypeStruct(shape, dtype) for shape, dtype in outs],
        in_specs=in_specs,
        out_specs=[VMEM] * len(outs),
        scratch_shapes=list(scratch),
        compiler_params=pltpu.CompilerParams(vmem_limit_bytes=room << 20),
        cost_estimate=pl.CostEstimate(flops=flops, bytes_accessed=moved, transcendentals=0),
    )


def store_shifted(tile, out):
    for col_off in range(3):
        out[col_off] = tile[:, :, col_off : col_off + HW, :].reshape(SHIFTED, CI)


def shift_kernel(tile, out):
    store_shifted(tile, out)


def slope_of(pre, grad, pointwise):
    grad_act = lax.dot_general(
        grad, pointwise, (((1,), (1,)), ((), ())), preferred_element_type=WIDE
    )
    return (grad_act * silu_slope(pre.astype(WIDE))).astype(LOW)


def own_kernel(tile, pre, grad, pointwise, views, slopes, acts):
    store_shifted(tile, views)
    slopes[...] = slope_of(pre[...], grad[...], pointwise[...])
    acts[...] = jax.nn.silu(pre[...].astype(WIDE)).astype(LOW)


def term_kernel(
    at, views, slopes, acts, grad, tile_peer, pre_peer, grad_peer, pointwise,
    keep_one, send_one, keep_two, send_two, keep_three, send_three,
    views_peer, both_slopes, both_acts, both_grads, staged,
):
    core = at[4]
    store_shifted(tile_peer, views_peer)
    both_slopes[:PIX] = slopes[...]
    both_slopes[PIX:] = slope_of(pre_peer[...], grad_peer[...], pointwise[...])
    outs = ((keep_one, send_one), (keep_two, send_two), (keep_three, send_three))

    def put(slot, total):
        value = total.astype(LOW)
        for (first, count, order), (keep, send) in zip(PARTS, outs):
            if first <= slot < first + count:
                for mine in range(2):

                    @pl.when(at[order[0]] == mine)
                    def _():
                        keep[slot - first] = value[mine * 128 : mine * 128 + 128]
                        send[slot - first] = value[128 - mine * 128 : 256 - mine * 128]

    def tap_rows(tap):
        frame_off, row_off, col_off = tap // 9, lax.rem(tap // 3, 3), lax.rem(tap, 3)
        parts = []
        for ref in (views, views_peer):
            for frame in range(FR):
                start = pl.multiple_of(((frame + frame_off) * (HW + 2) + row_off) * HW, HW)
                parts.append(ref[col_off, pl.ds(start, HW * HW), :])
        return jnp.concatenate(parts, axis=0)

    for slot in range(SLOTS - 1):
        put(slot, contract_rows(tap_rows(core * SLOTS + slot), both_slopes[...]))

    @pl.when(core == 0)
    def _():
        staged[...] = contract_rows(tap_rows(SLOTS - 1), both_slopes[...])

    @pl.when(core == 1)
    def _():
        both_acts[:PIX] = acts[...]
        both_acts[PIX:] = jax.nn.silu(pre_peer[...].astype(WIDE)).astype(LOW)
        both_grads[:PIX] = grad[...]
        both_grads[PIX:] = grad_peer[...]
        staged[...] = contract_rows(both_acts[...], both_grads[...])

    put(SLOTS - 1, staged[...])


def fold_kernel(step, at, after, *refs):
    size = 256 >> (step + 1)
    ins, outs = refs[:6], refs[6:]
    for part, (first, count, order) in enumerate(PARTS):
        keep, got = ins[2 * part], ins[2 * part + 1]
        mine = at[order[step] if step < 3 else 3]
        for which, out in ((mine, 0), (1 - mine, 1)):
            rows = pl.ds(pl.multiple_of(which * size, size), size)
            value = (keep[:, rows].astype(WIDE) + got[:, rows].astype(WIDE)).astype(LOW)
            if step < 3:
                outs[2 * part + out][...] = value
            else:
                outs[out][first : first + count] = value


def moment_kernel(at, rate, own, got, row_moment, scaled):
    total = (own[...].astype(WIDE) + got[...].astype(WIDE)).reshape(SLOTS * 16, CO)
    squares = total * total
    decay = rate[0]
    mean = jnp.sum(squares, axis=1, keepdims=True) * (1.0 / CO)
    new_row = decay * row_moment[...] + (1.0 - decay) * mean
    scaled[:SLOTS] = (total * lax.rsqrt(new_row)).astype(LOW).reshape(SLOTS, 16, CO)
    weighted = squares / new_row
    cut = (SLOTS - 1) * 16
    last_small = at[4] == 1
    rows = []
    for values in (squares, weighted, jnp.broadcast_to(new_row, (SLOTS * 16, CO))):
        large = jnp.sum(values[:cut], axis=0, keepdims=True)
        last = jnp.sum(values[cut:], axis=0, keepdims=True)
        rows.append(large + jnp.where(last_small, 0.0, last))
        rows.append(jnp.where(last_small, last, 0.0))
    spread = jnp.broadcast_to(new_row, (SLOTS * 16, 128))
    spread = jnp.concatenate([spread, jnp.zeros((32, 128), WIDE)], axis=0)
    rows.append(jnp.transpose(spread)[:1])
    rows.append(jnp.zeros((1, CO), WIDE))
    message = jnp.concatenate(rows, axis=0)
    high = message.astype(LOW).astype(WIDE)
    scaled[SLOTS] = jnp.concatenate([high, message - high], axis=0).astype(LOW)


def store_factors(total, decay, col_moment, new_col, factor):
    for kernel in range(2):
        count = 27.0 * CI if kernel == 0 else float(CO)
        col = decay * col_moment[kernel : kernel + 1] + (1.0 - decay) * (
            total[kernel : kernel + 1] / count
        )
        row_mean = total[4 + kernel : 5 + kernel] / count
        square = row_mean * jnp.sum(
            total[2 + kernel : 3 + kernel] / col, axis=1, keepdims=True
        )
        clip = jnp.maximum(1.0, jnp.sqrt(square / (count * CO)))
        new_col[kernel : kernel + 1] = col
        factor[kernel : kernel + 1] = 1.0 / (jnp.sqrt(col / row_mean) * clip)


def stack_kernel(at, own, got, out):
    out[at[2]] = own[...]
    out[1 - at[2]] = got[...]


def line_kernel(at, after, own, got, out_a, out_b):
    for which, piece in ((at[3], own), (1 - at[3], got)):
        for near in range(2):
            rows = piece[near, :SLOTS].reshape(SLOTS * 16, CO)
            out_a[which * 2 + near] = rows[: 3 * BLK]
            out_b[which * 2 + near] = rows[3 * BLK :]


def double_kernel(after, own_a, got_a, own_b, got_b, out_a, out_b):
    out_a[0], out_a[1] = own_a[...], got_a[...]
    out_b[0], out_b[1] = own_b[...], got_b[...]


def order_kernel(at, block_order, *refs):
    pieces, out = refs[:-1], refs[-1]
    count = NB // 8
    quarters = count // 4
    for index, piece in enumerate(pieces):
        flip_core, kind = divmod(index, 4)
        core = at[4] ^ flip_core
        first, blocks = ((0, 3), (0, 3), (3, 4), (3, 4))[kind]
        for away in range(2):
            flip_x = away if kind < 2 else kind - 2
            flip_y = kind if kind < 2 else away
            quarter = (at[1] ^ flip_y) * 2 + (at[0] ^ flip_x)
            for line in range(4):
                for local in range(blocks):
                    block = block_order[
                        (line * 2 + core) * count + quarter * quarters + first + local
                    ]
                    to = pl.ds(pl.multiple_of(block * BLK, BLK), BLK)
                    out[to, :] = piece[away, line, local * BLK : local * BLK + BLK]


def widen_kernel(step, at, after, *refs):
    size = 256 >> (step + 1)
    if step == 3:
        (own, got), outs = refs[:2], refs[2:]
    else:
        ins, outs = refs[:6], refs[6:]
    for part, (first, _, order) in enumerate(PARTS):
        mine = at[order[step] if step < 3 else 3]
        for index, which in enumerate((mine, 1 - mine)):
            rows = pl.ds(pl.multiple_of(which * size, size), size)
            if step == 3:
                value = (own, got)[index][first : first + 5]
            else:
                value = ins[2 * part + index][...]
            outs[part][:, rows] = value
            if step == 1:
                outs[3][first : first + 5, rows] = value


def finish_kernel(
    at, block_order, rate, col_moment, views, natural, master,
    mine, got_one, got_two, got_three, peer, peer_one, peer_two, peer_three,
    update_rows, new_master, new_row, new_col, next_output, scaled, factor, row_table,
):
    core = at[4]
    gots = ((got_one, got_two, got_three), (peer_one, peer_two, peer_three))
    for index, own in enumerate((mine, peer)):
        side = core ^ index
        for (first, _, order), got in zip(PARTS, gots[index]):
            which = at[order[0]]
            rows = pl.ds(pl.multiple_of(which * 128, 128), 128)
            scaled[side, first : first + 5, rows] = own[first : first + 5]
            rows = pl.ds(pl.multiple_of(128 - which * 128, 128), 128)
            scaled[side, first : first + 5, rows] = got[...]
    message = scaled[:, SLOTS].astype(WIDE).reshape(32, 2, 8, CO)
    message = message[:, 0] + message[:, 1]
    store_factors(jnp.sum(message, axis=0), rate[0], col_moment, new_col, factor)
    for index in range(32):
        for half in range(2):
            row_table[index * 2 + half : index * 2 + half + 1] = message[
                index, 6:7, half * 128 : half * 128 + 128
            ]
    large = learn_rate * factor[0:1]
    total = jnp.zeros((PIX, CO), WIDE)
    for tap in range(27):
        frame_off, row_off, col_off = tap // 9, tap // 3 % 3, tap % 3
        step = scaled[tap // SLOTS, tap % SLOTS].astype(WIDE) * large
        weights = natural[tap * CI : tap * CI + CI].astype(WIDE) - step
        starts = [((frame + frame_off) * (HW + 2) + row_off) * HW for frame in range(FR)]
        window = jnp.concatenate(
            [views[col_off, start : start + HW * HW, :] for start in starts], axis=0
        )
        total = total + jnp.dot(window, weights.astype(LOW), preferred_element_type=WIDE)
    small = learn_rate * factor[1:2]
    weights = natural[27 * CI :].astype(WIDE) - scaled[1, SLOTS - 1].astype(WIDE) * small
    next_act = jax.nn.silu(total).astype(LOW)
    next_output[...] = jnp.dot(
        next_act, weights.astype(LOW), preferred_element_type=WIDE
    ).astype(LOW)

    owner = at[3] * 4 + at[2] * 2 + core
    lane = lax.broadcasted_iota(jnp.int32, (1, 128), 1)
    for line in range(7):
        values = jnp.zeros((1, 128), WIDE)
        for part in range(4):
            local = line * 4 + part
            block = block_order[owner * (NB // 8) + local]
            side, slot, place = block // (8 * SLOTS), lax.rem(block // 8, SLOTS), lax.rem(block, 8)
            one, two, three = place // 4, lax.rem(place // 2, 2), lax.rem(place, 2)
            sender = jnp.where(
                slot < 5,
                three * 8 + one * 4 + two * 2,
                jnp.where(slot < 10, two * 8 + three * 4 + one * 2, place * 2),
            )
            chosen = jnp.where(block >= NB3, factor[1:2], factor[0:1])
            rows = slice(local * BLK, local * BLK + BLK)
            start = pl.multiple_of(place * BLK, BLK)
            update = scaled[side, slot, pl.ds(start, BLK), :].astype(WIDE) * chosen
            update_rows[rows, :] = update
            new_master[rows, :] = master[rows, :] - learn_rate * update
            for half in range(2):
                at_row = (side * 16 + sender + half) * 2 + slot // 8
                to = part * 32 + half * 16
                turn = lax.rem(128 + to - lax.rem(slot, 8) * 16, 128)
                turned = pltpu.roll(row_table[pl.ds(at_row, 1), :], turn, 1)
                values = jnp.where((lane >= to) & (lane < to + 16), turned, values)
        new_row[line : line + 1] = values


def shards(
    step_count,
    block_order,
    saved_tiles,
    pre_act,
    grad_output,
    pointwise_live,
    master_rows,
    row_moment,
    col_moment,
    next_tiles,
):
    group, shard = lax.axis_index("group"), lax.axis_index("shard")
    axis_y, axis_x = group // 2, group % 2
    far, near, core = shard // 4, shard // 2 % 2, shard % 2
    at = jnp.stack([axis_x, axis_y, near, far, core]).astype(jnp.int32)
    decay_rate = 1.0 - step_count.astype(WIDE) ** (-decay_power)

    tile_peer = swap(saved_tiles, MASK_CORE)
    pre_peer = swap(pre_act, MASK_CORE)
    grad_peer = swap(grad_output, MASK_CORE)
    own_views, slopes, acts = call(
        own_kernel,
        [((3, SHIFTED, CI), LOW), ((PIX, CO), LOW), ((PIX, CO), LOW)],
        [VMEM] * 4,
        moved=4 << 20,
    )(saved_tiles[0], pre_act, grad_output, pointwise_live)

    quarter = lax.dynamic_slice_in_dim(master_rows, group * (SLOTS * 16), SLOTS * 16)
    values = jnp.pad(row_moment.reshape(7, 128), ((0, 9), (0, 0)))
    high = lax.reduce_precision(values, 8, 7)
    values = jnp.concatenate([high, values - high], axis=1)
    packed = jnp.concatenate([quarter, values], axis=0).astype(LOW).reshape(SLOTS + 1, 16, CO)
    pair = call(stack_kernel, [((2, SLOTS + 1, 16, CO), LOW)], [SMEM] + [VMEM] * 2)(
        at, packed, swap(packed, MASK_NEAR)
    )[0]
    pair_far = swap(pair, MASK_FAR)
    moment_line = jnp.stack([pair[:, SLOTS], pair_far[:, SLOTS]])
    moment_all = jnp.stack([moment_line, swap(moment_line, MASK_CORE)])[:, :, :, :7].astype(WIDE)
    moment_all = (moment_all[..., :128] + moment_all[..., 128:]).reshape(2, 2, 2, 896)
    moment_stored = moment_all[jnp.arange(2) ^ core][:, jnp.arange(2) ^ far]
    moment_stored = jnp.transpose(moment_stored, (1, 2, 0, 3)).reshape(NB, BLK)
    inverse = jnp.zeros((NB,), jnp.int32).at[block_order].set(jnp.arange(NB, dtype=jnp.int32))
    moment_natural = jnp.take(moment_stored, inverse, axis=0).reshape(2, SLOTS, 16, 16)
    moment_natural = lax.dynamic_index_in_dim(moment_natural, core, 0, False)
    place = (axis_x, axis_y, near)
    own_moment = [
        lax.dynamic_index_in_dim(
            moment_natural[first : first + count],
            place[order[0]] * 8 + place[order[1]] * 4 + place[order[2]] * 2 + far,
            1,
            False,
        )
        for first, count, order in PARTS
    ]
    own_moment = jnp.concatenate(own_moment, axis=0).reshape(SLOTS * 16, 1)
    views = call(shift_kernel, [((3, SHIFTED, CI), LOW)], [VMEM], moved=3 << 20)(next_tiles[0])[0]

    sums = call(
        term_kernel,
        [((count, 128, CO), LOW) for _, count, _ in PARTS for _ in range(2)],
        [SMEM] + [VMEM] * 8,
        scratch=[
            pltpu.VMEM((3, SHIFTED, CI), LOW),
            pltpu.VMEM((2 * PIX, CO), LOW),
            pltpu.VMEM((2 * PIX, CO), LOW),
            pltpu.VMEM((2 * PIX, CO), LOW),
            pltpu.VMEM((CI, CO), WIDE),
        ],
        flops=2 * 14 * 1024 * 256 * 256,
        moved=6 << 20,
        room=12,
    )(at, own_views, slopes, acts, grad_output, tile_peer[0], pre_peer, grad_peer, pointwise_live)
    for step in range(1, 4):
        arrived = []
        for part, (_, _, order) in enumerate(PARTS):
            arrived += [sums[2 * part], swap(sums[2 * part + 1], MASKS[order[step - 1]])]
        size = 256 >> (step + 1)
        outs = [((count, size, CO), LOW) for _, count, _ in PARTS for _ in range(2)]
        if step == 3:
            outs = [((SLOTS, size, CO), LOW)] * 2
        after = (pair_far, pair_far, views)[step - 1]
        sums = call(
            functools.partial(fold_kernel, step), outs, [SMEM, HBM] + [VMEM] * 6, moved=1 << 20
        )(at, after, *arrived)

    line_a, line_b = call(
        line_kernel,
        [((4, 3 * BLK, CO), LOW), ((4, 4 * BLK, CO), LOW)],
        [SMEM, HBM] + [VMEM] * 2,
        moved=1 << 20,
    )(at, sums[0], pair, pair_far)
    line_got_a, line_got_b = swap(line_a, MASK_X), swap(line_b, MASK_Y)
    scaled = call(moment_kernel, [((SLOTS + 1, 16, CO), LOW)], [SMEM] * 2 + [VMEM] * 3)(
        at, decay_rate, sums[0], swap(sums[1], MASK_FAR), own_moment
    )[0]
    plane_a, plane_b = call(
        double_kernel,
        [((2, 4, 3 * BLK, CO), LOW), ((2, 4, 4 * BLK, CO), LOW)],
        [HBM] + [VMEM] * 4,
        moved=2 << 20,
    )(scaled, line_a, line_got_a, line_b, line_got_b)
    planes = [plane_a, swap(plane_a, MASK_Y), plane_b, swap(plane_b, MASK_X)]
    planes = planes + [swap(plane, MASK_CORE) for plane in planes]
    natural = call(
        order_kernel, [((NB * BLK, CO), LOW)], [SMEM] * 2 + [VMEM] * 8, moved=8 << 20
    )(at, block_order, *planes)[0]

    pieces = [scaled, swap(scaled, MASK_FAR)]
    for step in range(3, 0, -1):
        size = 256 >> step
        outs = [((5, size, CO), LOW)] * 3
        if step == 1:
            outs = outs + [((SLOTS + 1, size, CO), LOW)]
        after = (natural, at, at)[step - 1]
        joined = call(
            functools.partial(widen_kernel, step), outs, [SMEM, HBM] + [VMEM] * len(pieces)
        )(at, after, *pieces)
        pieces = []
        for part, (_, _, order) in enumerate(PARTS):
            pieces += [joined[part], swap(joined[part], MASKS[order[step - 1]])]
    halves = [joined[3], pieces[1], pieces[3], pieces[5]]
    peers = [swap(half, MASK_CORE) for half in halves]

    update_rows, new_master, new_row, new_col, next_output = call(
        finish_kernel,
        [
            ((NB // 8 * BLK, CO), WIDE),
            ((NB // 8 * BLK, CO), WIDE),
            ((7, 128), WIDE),
            ((2, CO), WIDE),
            ((PIX, CO), LOW),
        ],
        [SMEM] * 3 + [VMEM] * 12,
        scratch=[
            pltpu.VMEM((2, SLOTS + 1, CI, CO), LOW),
            pltpu.VMEM((2, CO), WIDE),
            pltpu.VMEM((64, 128), WIDE),
        ],
        flops=2 * 28 * 512 * 256 * 256,
        moved=16 << 20,
        room=16,
    )(at, block_order, decay_rate, col_moment, views, natural, master_rows, *halves, *peers)
    return (update_rows, new_master, new_row.reshape(-1), new_col, next_output)


def solution(mesh):
    in_specs = (
        P(),
        P(),
        P(("group", "shard"), None, None, None, None),
        P(("group", "shard"), None),
        P(("group", "shard"), None),
        P(),
        P("shard", None),
        P("shard"),
        P(),
        P(("group", "shard"), None, None, None, None),
    )
    out_specs = (P("shard", None), P("shard", None), P("shard"), P(), P(("group", "shard"), None))
    body = shards if (mesh.shape["group"], mesh.shape["shard"]) == (4, 8) else general_shards
    return jax.shard_map(body, mesh=mesh, in_specs=in_specs, out_specs=out_specs, check_vma=False)
```

time: 113 us -> 133 us (1.18)
  waiting for transfers between devices: 44.1 us -> 60.3 us
  starting transfers between devices: 38.1 us -> 33.3 us
  local copies, waits for them, and re-layouts: 8.4 us -> 11.9 us
  other arithmetic: 0.92 us -> 3.6 us
  Pallas kernels: 19.6 us -> 22.1 us
    ppermute x32 -> x38, waiting for transfers between devices: 44.1 us -> 60.3 us  [swap(): return lax.ppermute(value, AXES, [(at, at ^ mask) for at in range(32)])]
    ppermute x32 -> x38, starting transfers between devices: 38.1 us -> 33.3 us  [swap(): return lax.ppermute(value, AXES, [(at, at ^ mask) for at in range(32)])]
    pallas_call x8 -> x12, Pallas kernels: 13.5 us -> 15.8 us  [the longest x1 8.85 us: shards(): call(term_kernel, [((count, 128, CO), LOW) for _, count, _ in PARTS for _...]
    gather x2, local copies, waits for them, and re-layouts: 0.81 us -> 2.32 us  [shards(): jnp.take(moment_stored, inverse, axis=0).reshape(2, SLOTS, 16, 16)]
    another operation x2, other arithmetic: 0.09 us -> 1.43 us  [the longest x1 0.08 us: shards(): at = jnp.stack([axis_x, axis_y, axis_z, core]).astype(jnp.int32)]
    unnamed x18 -> x32, local copies, waits for them, and re-layouts: 4.33 us -> 4.09 us
  transfers between devices with their start and end apart: 32 -> 38, of which waited for: 14 -> 27; matrix products, arithmetic and copies ran while one was open for 7% -> 7% of each run, Pallas kernels for 10% -> 3%
where the time goes in v3:
time: 133 us
  waiting for transfers between devices  60.3 us (45%)
  starting transfers between devices  33.3 us (25%)
  Pallas kernels  22.1 us (17%)
  local copies, waits for them, and re-layouts  11.9 us (9%)
  other arithmetic  3.6 us (3%)
  between operations  1.86 us (1%)
    ppermute x38, waiting for transfers between devices, swap(): return lax.ppermute(value, AXES, [(at, at ^ mask) for at in range(32)])  60.3 us
    ppermute x38, starting transfers between devices, swap(): return lax.ppermute(value, AXES, [(at, at ^ mask) for at in range(32)])  33.3 us
    pallas_call x1, Pallas kernels, shards(): call(term_kernel, [((count, 128, CO), LOW) for _, count, _ in PARTS for _...  8.85 us
    pallas_call x1, Pallas kernels, shards(): call(finish_kernel, [((NB // 8 * BLK, CO), WIDE), ((NB // 8 * BLK, CO), W...  5.23 us
    unnamed x32, local copies, waits for them, and re-layouts  4.09 us
  transfers between devices with their start and end apart: 38, of which 27 were waited for; matrix products, arithmetic and copies ran while one was open for 7% of the time, Pallas kernels for 3%

profile of v3, /device:TPU:0, one launch (start us, length us, event | category | flops | bytes accessed | tf_op | source)
XLA Modules:
  0.0 133.1 jit_solution(14041583904830712466)
XLA Ops:
  2.4 3.1 %collective-permute-start = (bf16[15,16,256]{2,1,0:T(8,128)(2,1)S(1)}, bf16[15,16,256]{2,1,0:T(8,128)(2,1)S(1)}, u32[]{:S(2)}, u32[]{:S(2)}) collective-permute-start(bf16[15,16,256]{2,1,0:T(8,128)(2,1)S(1)} %bitcast.44), channel_id=1, source_target_pairs={{0,2},{1,3},{2,0},{3,1},{4,6},{5,7},{6,4},{7,5},{8,10},{9,11},{10,... | collective-permute-start | bytes 368648 | tf_op jit(solution)/shard_map/ppermute | solution.py:133
  9.4 2.8 %collective-permute-start.1 = (bf16[2,15,16,256]{3,2,1,0:T(8,128)(2,1)S(1)}, bf16[2,15,16,256]{3,2,1,0:T(8,128)(2,1)S(1)}, u32[]{:S(2)}, u32[]{:S(2)}) collective-permute-start(bf16[2,15,16,256]{3,2,1,0:T(8,128)(2,1)S(1)} %shard_map.138.own), channel_id=1, source_target_pairs={{0,4},{1,5},{2,6},{3,7},{4,0},{5,1},{6,2},{7,3},{8,12},{9,13},{10,... | collective-permute-start | bytes 737288 | tf_op jit(solution)/shard_map/ppermute | solution.py:133
  13.2 10.2 %collective-permute-done.1.after.got = bf16[2,15,16,256]{3,2,1,0:T(8,128)(2,1)S(1)} collective-permute-done((bf16[2,15,16,256]{3,2,1,0:T(8,128)(2,1)S(1)}, bf16[2,15,16,256]{3,2,1,0:T(8,128)(2,1)S(1)}, u32[]{:S(2)}, u32[]{:S(2)}) %collective-permute-start.1) | collective-permute-done | bytes 245792 | tf_op jit(solution)/shard_map/ppermute | solution.py:133
  29.4 8.8 %shard_map.140 = (bf16[5,128,256]{2,1,0:T(8,128)(2,1)S(1)}, bf16[5,128,256]{2,1,0:T(8,128)(2,1)}, bf16[5,128,256]{2,1,0:T(8,128)(2,1)S(1)}, bf16[5,128,256]{2,1,...) custom-call(s32[5]{0:T(128)S(1)} %stack.35.at.after, ...), custom_call_target="tpu_custom_call" | custom-call | flops 1879048192 | bytes 6291456 | tf_op jit(solution)/shard_map/pallas_call | solution.py:460
  39.6 1.5 %collective-permute-start.5 = (bf16[5,128,256]{2,1,0:T(8,128)(2,1)}, bf16[5,128,256]{2,1,0:T(8,128)(2,1)S(1)}, u32[]{:S(2)}, u32[]{:S(2)}) collective-permute-start(bf16[5,128,256]{2,1,0:T(8,128)(2,1)} %get-tuple-element.51), channel_id=1, source_target_pairs={{0,8},{1,9},{2,10},{3,11},{4,12},{5,13},{6,14},{7,15},{8,0},{9,1},... | collective-permute-start | bytes 983048 | tf_op jit(solution)/shard_map/ppermute | solution.py:133
  41.2 1.5 %collective-permute-start.6 = (bf16[5,128,256]{2,1,0:T(8,128)(2,1)}, bf16[5,128,256]{2,1,0:T(8,128)(2,1)}, u32[]{:S(2)}, u32[]{:S(2)}) collective-permute-start(bf16[5,128,256]{2,1,0:T(8,128)(2,1)} %get-tuple-element.53), channel_id=1, source_target_pairs={{0,16},{1,17},{2,18},{3,19},{4,20},{5,21},{6,22},{7,23},{8,24},{9,... | collective-permute-start | bytes 983048 | tf_op jit(solution)/shard_map/ppermute | solution.py:133
  46.6 2.1 %collective-permute-done.7.refs_5_ = bf16[4,128,256]{2,1,0:T(8,128)(2,1)} collective-permute-done((bf16[4,128,256]{2,1,0:T(8,128)(2,1)}, bf16[4,128,256]{2,1,0:T(8,128)(2,1)}, u32[]{:S(2)}, u32[]{:S(2)}) %collective-permute-start.7) | collective-permute-done | bytes 262176 | tf_op jit(solution)/shard_map/ppermute | solution.py:133
  50.0 1.3 %collective-permute-done.6.refs_3_ = bf16[5,128,256]{2,1,0:T(8,128)(2,1)} collective-permute-done((bf16[5,128,256]{2,1,0:T(8,128)(2,1)}, bf16[5,128,256]{2,1,0:T(8,128)(2,1)}, u32[]{:S(2)}, u32[]{:S(2)}) %collective-permute-start.6) | collective-permute-done | bytes 327712 | tf_op jit(solution)/shard_map/ppermute | solution.py:133
  54.1 1.5 %collective-permute-start.8 = (bf16[5,64,256]{2,1,0:T(8,128)(2,1)S(1)}, bf16[5,64,256]{2,1,0:T(8,128)(2,1)S(1)}, u32[]{:S(2)}, u32[]{:S(2)}) collective-permute-start(bf16[5,64,256]{2,1,0:T(8,128)(2,1)S(1)} %get-tuple-element.57), channel_id=1, source_target_pairs={{0,16},{1,17},{2,18},{3,19},{4,20},{5,21},{6,22},{7,23},{8,24},{9,... | collective-permute-start | bytes 491528 | tf_op jit(solution)/shard_map/ppermute | solution.py:133
  55.7 1.7 %collective-permute-start.9 = (bf16[5,64,256]{2,1,0:T(8,128)(2,1)S(1)}, bf16[5,64,256]{2,1,0:T(8,128)(2,1)S(1)}, u32[]{:S(2)}, u32[]{:S(2)}) collective-permute-start(bf16[5,64,256]{2,1,0:T(8,128)(2,1)S(1)} %get-tuple-element.59), channel_id=1, source_target_pairs={{0,2},{1,3},{2,0},{3,1},{4,6},{5,7},{6,4},{7,5},{8,10},{9,11},{10,... | collective-permute-start | bytes 491528 | tf_op jit(solution)/shard_map/ppermute | solution.py:133
  59.5 1.5 %collective-permute-done.9.refs_3_ = bf16[5,64,256]{2,1,0:T(8,128)(2,1)S(1)} collective-permute-done((bf16[5,64,256]{2,1,0:T(8,128)(2,1)S(1)}, bf16[5,64,256]{2,1,0:T(8,128)(2,1)S(1)}, u32[]{:S(2)}, u32[]{:S(2)}) %collective-permute-start.9) | collective-permute-done | bytes 163872 | tf_op jit(solution)/shard_map/ppermute | solution.py:133
  62.2 1.7 %collective-permute-start.11 = (bf16[5,32,256]{2,1,0:T(8,128)(2,1)S(1)}, bf16[5,32,256]{2,1,0:T(8,128)(2,1)S(1)}, u32[]{:S(2)}, u32[]{:S(2)}) collective-permute-start(bf16[5,32,256]{2,1,0:T(8,128)(2,1)S(1)} %get-tuple-element.63), channel_id=1, source_target_pairs={{0,2},{1,3},{2,0},{3,1},{4,6},{5,7},{6,4},{7,5},{8,10},{9,11},{10,... | collective-permute-start | bytes 245768 | tf_op jit(solution)/shard_map/ppermute | solution.py:133
  64.0 1.5 %collective-permute-start.12 = (bf16[5,32,256]{2,1,0:T(8,128)(2,1)S(1)}, bf16[5,32,256]{2,1,0:T(8,128)(2,1)S(1)}, u32[]{:S(2)}, u32[]{:S(2)}) collective-permute-start(bf16[5,32,256]{2,1,0:T(8,128)(2,1)S(1)} %get-tuple-element.65), channel_id=1, source_target_pairs={{0,8},{1,9},{2,10},{3,11},{4,12},{5,13},{6,14},{7,15},{8,0},{9,1},... | collective-permute-start | bytes 245768 | tf_op jit(solution)/shard_map/ppermute | solution.py:133
  66.7 1.7 %collective-permute-done.12.refs_3_ = bf16[5,32,256]{2,1,0:T(8,128)(2,1)S(1)} collective-permute-done((bf16[5,32,256]{2,1,0:T(8,128)(2,1)S(1)}, bf16[5,32,256]{2,1,0:T(8,128)(2,1)S(1)}, u32[]{:S(2)}, u32[]{:S(2)}) %collective-permute-start.12) | collective-permute-done | bytes 81952 | tf_op jit(solution)/shard_map/ppermute | solution.py:133
  69.6 1.6 %collective-permute-start.17 = (bf16[4,128,256]{2,1,0:T(8,128)(2,1)S(1)}, bf16[4,128,256]{2,1,0:T(8,128)(2,1)S(1)}, u32[]{:S(2)}, u32[]{:S(2)}) collective-permute-start(bf16[4,128,256]{2,1,0:T(8,128)(2,1)S(1)} %get-tuple-element.71.own_b), channel_id=1, source_target_pairs={{0,16},{1,17},{2,18},{3,19},{4,20},{5,21},{6,22},{7,23},{8,24},{9,... | collective-permute-start | bytes 786440 | tf_op jit(solution)/shard_map/ppermute | solution.py:133
  71.2 1.7 %collective-permute-start.14 = (bf16[14,16,256]{2,1,0:T(8,128)(2,1)S(1)}, bf16[14,16,256]{2,1,0:T(8,128)(2,1)S(1)}, u32[]{:S(2)}, u32[]{:S(2)}) collective-permute-start(bf16[14,16,256]{2,1,0:T(8,128)(2,1)S(1)} %get-tuple-element.69), channel_id=1, source_target_pairs={{0,4},{1,5},{2,6},{3,7},{4,0},{5,1},{6,2},{7,3},{8,12},{9,13},{10,... | collective-permute-start | bytes 344072 | tf_op jit(solution)/shard_map/ppermute | solution.py:133
  72.9 1.5 %collective-permute-start.16 = (bf16[4,96,256]{2,1,0:T(8,128)(2,1)S(1)}, bf16[4,96,256]{2,1,0:T(8,128)(2,1)S(1)}, u32[]{:S(2)}, u32[]{:S(2)}) collective-permute-start(bf16[4,96,256]{2,1,0:T(8,128)(2,1)S(1)} %get-tuple-element.70.own_a), channel_id=1, source_target_pairs={{0,8},{1,9},{2,10},{3,11},{4,12},{5,13},{6,14},{7,15},{8,0},{9,1},... | collective-permute-start | bytes 589832 | tf_op jit(solution)/shard_map/ppermute | solution.py:133
  74.6 3.5 %collective-permute-done.14.got = bf16[14,16,256]{2,1,0:T(8,128)(2,1)S(1)} collective-permute-done((bf16[14,16,256]{2,1,0:T(8,128)(2,1)S(1)}, bf16[14,16,256]{2,1,0:T(8,128)(2,1)S(1)}, u32[]{:S(2)}, u32[]{:S(2)}) %collective-permute-start.14) | collective-permute-done | bytes 114720 | tf_op jit(solution)/shard_map/ppermute | solution.py:133
  78.9 1.5 %collective-permute-done.16.got_a = bf16[4,96,256]{2,1,0:T(8,128)(2,1)S(1)} collective-permute-done((bf16[4,96,256]{2,1,0:T(8,128)(2,1)S(1)}, bf16[4,96,256]{2,1,0:T(8,128)(2,1)S(1)}, u32[]{:S(2)}, u32[]{:S(2)}) %collective-permute-start.16) | collective-permute-done | bytes 196640 | tf_op jit(solution)/shard_map/ppermute | solution.py:133
  80.5 1.7 %collective-permute-start.19 = (bf16[2,4,128,256]{3,2,1,0:T(8,128)(2,1)S(1)}, bf16[2,4,128,256]{3,2,1,0:T(8,128)(2,1)S(1)}, u32[]{:S(2)}, u32[]{:S(2)}) collective-permute-start(bf16[2,4,128,256]{3,2,1,0:T(8,128)(2,1)S(1)} %get-tuple-element.73.refs_2_), channel_id=1, source_target_pairs={{0,8},{1,9},{2,10},{3,11},{4,12},{5,13},{6,14},{7,15},{8,0},{9,1},... | collective-permute-start | bytes 1572872 | tf_op jit(solution)/shard_map/ppermute | solution.py:133
  84.6 5.2 %collective-permute-done.19.refs_3_ = bf16[2,4,128,256]{3,2,1,0:T(8,128)(2,1)S(1)} collective-permute-done((bf16[2,4,128,256]{3,2,1,0:T(8,128)(2,1)S(1)}, bf16[2,4,128,256]{3,2,1,0:T(8,128)(2,1)S(1)}, u32[]{:S(2)}, u32[]{:S(2)}) %collective-permute-start.19) | collective-permute-done | bytes 524320 | tf_op jit(solution)/shard_map/ppermute | solution.py:133
  89.8 2.3 %collective-permute-done.24.refs_1_ = bf16[15,16,256]{2,1,0:T(8,128)(2,1)S(1)} collective-permute-done((bf16[15,16,256]{2,1,0:T(8,128)(2,1)S(1)}, bf16[15,16,256]{2,1,0:T(8,128)(2,1)S(1)}, u32[]{:S(2)}, u32[]{:S(2)}) %collective-permute-start.24) | collective-permute-done | bytes 122912 | tf_op jit(solution)/shard_map/ppermute | solution.py:133
  92.8 4.3 %collective-permute-done.25.refs_1_ = bf16[5,32,256]{2,1,0:T(8,128)(2,1)S(1)} collective-permute-done((bf16[5,32,256]{2,1,0:T(8,128)(2,1)S(1)}, bf16[5,32,256]{2,1,0:T(8,128)(2,1)S(1)}, u32[]{:S(2)}, u32[]{:S(2)}) %collective-permute-start.25) | collective-permute-done | bytes 81952 | tf_op jit(solution)/shard_map/ppermute | solution.py:133
  97.6 4.0 %collective-permute-done.26.refs_3_ = bf16[5,32,256]{2,1,0:T(8,128)(2,1)S(1)} collective-permute-done((bf16[5,32,256]{2,1,0:T(8,128)(2,1)S(1)}, bf16[5,32,256]{2,1,0:T(8,128)(2,1)S(1)}, u32[]{:S(2)}, u32[]{:S(2)}) %collective-permute-start.26) | collective-permute-done | bytes 81952 | tf_op jit(solution)/shard_map/ppermute | solution.py:133
  101.6 1.4 %collective-permute-start.27 = (bf16[5,32,256]{2,1,0:T(8,128)(2,1)S(1)}, bf16[5,32,256]{2,1,0:T(8,128)(2,1)S(1)}, u32[]{:S(2)}, u32[]{:S(2)}) collective-permute-start(bf16[5,32,256]{2,1,0:T(8,128)(2,1)S(1)} %get-tuple-element.76.refs_4_), channel_id=1, source_target_pairs={{0,16},{1,17},{2,18},{3,19},{4,20},{5,21},{6,22},{7,23},{8,24},{9,... | collective-permute-start | bytes 245768 | tf_op jit(solution)/shard_map/ppermute | solution.py:133
  103.0 3.9 %collective-permute-done.27.refs_5_ = bf16[5,32,256]{2,1,0:T(8,128)(2,1)S(1)} collective-permute-done((bf16[5,32,256]{2,1,0:T(8,128)(2,1)S(1)}, bf16[5,32,256]{2,1,0:T(8,128)(2,1)S(1)}, u32[]{:S(2)}, u32[]{:S(2)}) %collective-permute-start.27) | collective-permute-done | bytes 81952 | tf_op jit(solution)/shard_map/ppermute | solution.py:133
  107.5 1.5 %collective-permute-start.28 = (bf16[5,64,256]{2,1,0:T(8,128)(2,1)S(1)}, bf16[5,64,256]{2,1,0:T(8,128)(2,1)S(1)}, u32[]{:S(2)}, u32[]{:S(2)}) collective-permute-start(bf16[5,64,256]{2,1,0:T(8,128)(2,1)S(1)} %get-tuple-element.77.refs_0_), channel_id=1, source_target_pairs={{0,16},{1,17},{2,18},{3,19},{4,20},{5,21},{6,22},{7,23},{8,24},{9,... | collective-permute-start | bytes 491528 | tf_op jit(solution)/shard_map/ppermute | solution.py:133
  110.4 2.5 %collective-permute-done.28.refs_1_ = bf16[5,64,256]{2,1,0:T(8,128)(2,1)S(1)} collective-permute-done((bf16[5,64,256]{2,1,0:T(8,128)(2,1)S(1)}, bf16[5,64,256]{2,1,0:T(8,128)(2,1)S(1)}, u32[]{:S(2)}, u32[]{:S(2)}) %collective-permute-start.28) | collective-permute-done | bytes 163872 | tf_op jit(solution)/shard_map/ppermute | solution.py:133
  112.9 1.4 %collective-permute-done.29.refs_3_ = bf16[5,64,256]{2,1,0:T(8,128)(2,1)S(1)} collective-permute-done((bf16[5,64,256]{2,1,0:T(8,128)(2,1)S(1)}, bf16[5,64,256]{2,1,0:T(8,128)(2,1)S(1)}, u32[]{:S(2)}, u32[]{:S(2)}) %collective-permute-start.29) | collective-permute-done | bytes 163872 | tf_op jit(solution)/shard_map/ppermute | solution.py:133
  116.5 1.6 %collective-permute-start.33 = (bf16[5,128,256]{2,1,0:T(8,128)(2,1)S(1)}, bf16[5,128,256]{2,1,0:T(8,128)(2,1)S(1)}, u32[]{:S(2)}, u32[]{:S(2)}) collective-permute-start(bf16[5,128,256]{2,1,0:T(8,128)(2,1)S(1)} %get-tuple-element.83), channel_id=1, source_target_pairs={{0,2},{1,3},{2,0},{3,1},{4,6},{5,7},{6,4},{7,5},{8,10},{9,11},{10,... | collective-permute-start | bytes 983048 | tf_op jit(solution)/shard_map/ppermute | solution.py:133
  118.0 7.2 %collective-permute-done.31.got_one = bf16[5,128,256]{2,1,0:T(8,128)(2,1)S(1)} collective-permute-done((bf16[5,128,256]{2,1,0:T(8,128)(2,1)S(1)}, bf16[5,128,256]{2,1,0:T(8,128)(2,1)S(1)}, u32[]{:S(2)}, u32[]{:S(2)}) %collective-permute-start.31) | collective-permute-done | bytes 327712 | tf_op jit(solution)/shard_map/ppermute | solution.py:133
  127.8 5.2 %shard_map.151 = (f32[896,256]{1,0:T(8,128)}, f32[896,256]{1,0:T(8,128)}, f32[7,128]{1,0:T(8,128)}, f32[2,256]{1,0:T(2,128)}, bf16[512,256]{1,0:T(8,128)(2,1)}) custom-call(s32[5]{0:T(128)S(1)} %stack.35.at.after, s32[224]{0:T(256)S(1)} %copy-done.10, f32[1]{0:T(128)S(6)} %sub.19.rate, f32[2,256]{1,0:T(2,128)S(1)} %copy-done.11, ...), custom_call_target="tpu_custom_call" | custom-call | flops 1879048192 | bytes 16777216 | tf_op jit(solution)/shard_map/pallas_call | solution.py:526
  (131 shorter events, 37.8 us)
Async XLA Ops:
  2.4 6.4 %collective-permute-start = (bf16[15,16,256]{2,1,0:T(8,128)(2,1)S(1)}, bf16[15,16,256]{2,1,0:T(8,128)(2,1)S(1)}, u32[]{:S(2)}, u32[]{:S(2)}) collective-permute-start(bf16[15,16,256]{2,1,0:T(8,128)(2,1)S(1)} %bitcast.44), channel_id=1, source_target_pairs={{0,2},{1,3},{2,0},{3,1},{4,6},{5,7},{6,4},{7,5},{8,10},{9,11},{10,... | collective-permute-start | bytes 368648 | tf_op jit(solution)/shard_map/ppermute | solution.py:133
  5.5 23.8 %collective-permute-start.3 = (bf16[512,256]{1,0:T(8,128)(2,1)}, bf16[512,256]{1,0:T(8,128)(2,1)}, u32[]{:S(2)}, u32[]{:S(2)}) collective-permute-start(bf16[512,256]{1,0:T(8,128)(2,1)} %pre.1), channel_id=1, source_target_pairs={{0,1},{1,0},{2,3},{3,2},{4,5},{5,4},{6,7},{7,6},{8,9},{9,8},{10,11... | collective-permute-start | bytes 786440 | tf_op jit(solution)/shard_map/ppermute | solution.py:133
  5.5 23.8 %collective-permute-start.4 = (bf16[512,256]{1,0:T(8,128)(2,1)}, bf16[512,256]{1,0:T(8,128)(2,1)}, u32[]{:S(2)}, u32[]{:S(2)}) collective-permute-start(bf16[512,256]{1,0:T(8,128)(2,1)} %grad.3), channel_id=1, source_target_pairs={{0,1},{1,0},{2,3},{3,2},{4,5},{5,4},{6,7},{7,6},{8,9},{9,8},{10,11... | collective-permute-start | bytes 786440 | tf_op jit(solution)/shard_map/ppermute | solution.py:133
  6.0 22.1 %collective-permute-start.2 = (bf16[1,4,18,18,256]{4,1,3,2,0:T(4,128)(2,1)}, bf16[1,4,18,18,256]{4,1,3,2,0:T(4,128)(2,1)}, u32[]{:S(2)}, u32[]{:S(2)}) collective-permute-start(bf16[1,4,18,18,256]{4,1,3,2,0:T(4,128)(2,1)} %param.12), channel_id=1, source_target_pairs={{0,1},{1,0},{2,3},{3,2},{4,5},{5,4},{6,7},{7,6},{8,9},{9,8},{10,11... | collective-permute-start | bytes 1990664 | tf_op jit(solution)/shard_map/ppermute | solution.py:133
  9.4 14.0 %collective-permute-start.1 = (bf16[2,15,16,256]{3,2,1,0:T(8,128)(2,1)S(1)}, bf16[2,15,16,256]{3,2,1,0:T(8,128)(2,1)S(1)}, u32[]{:S(2)}, u32[]{:S(2)}) collective-permute-start(bf16[2,15,16,256]{3,2,1,0:T(8,128)(2,1)S(1)} %shard_map.138.own), channel_id=1, source_target_pairs={{0,4},{1,5},{2,6},{3,7},{4,0},{5,1},{6,2},{7,3},{8,12},{9,13},{10,... | collective-permute-start | bytes 737288 | tf_op jit(solution)/shard_map/ppermute | solution.py:133
  39.6 9.0 %collective-permute-start.7 = (bf16[4,128,256]{2,1,0:T(8,128)(2,1)}, bf16[4,128,256]{2,1,0:T(8,128)(2,1)}, u32[]{:S(2)}, u32[]{:S(2)}) collective-permute-start(bf16[4,128,256]{2,1,0:T(8,128)(2,1)} %get-tuple-element.55), channel_id=1, source_target_pairs={{0,2},{1,3},{2,0},{3,1},{4,6},{5,7},{6,4},{7,5},{8,10},{9,11},{10,... | collective-permute-start | bytes 786440 | tf_op jit(solution)/shard_map/ppermute | solution.py:133
  39.6 10.3 %collective-permute-start.5 = (bf16[5,128,256]{2,1,0:T(8,128)(2,1)}, bf16[5,128,256]{2,1,0:T(8,128)(2,1)S(1)}, u32[]{:S(2)}, u32[]{:S(2)}) collective-permute-start(bf16[5,128,256]{2,1,0:T(8,128)(2,1)} %get-tuple-element.51), channel_id=1, source_target_pairs={{0,8},{1,9},{2,10},{3,11},{4,12},{5,13},{6,14},{7,15},{8,0},{9,1},... | collective-permute-start | bytes 983048 | tf_op jit(solution)/shard_map/ppermute | solution.py:133
  41.2 10.2 %collective-permute-start.6 = (bf16[5,128,256]{2,1,0:T(8,128)(2,1)}, bf16[5,128,256]{2,1,0:T(8,128)(2,1)}, u32[]{:S(2)}, u32[]{:S(2)}) collective-permute-start(bf16[5,128,256]{2,1,0:T(8,128)(2,1)} %get-tuple-element.53), channel_id=1, source_target_pairs={{0,16},{1,17},{2,18},{3,19},{4,20},{5,21},{6,22},{7,23},{8,24},{9,... | collective-permute-start | bytes 983048 | tf_op jit(solution)/shard_map/ppermute | solution.py:133
  53.6 5.0 %collective-permute-start.10 = (bf16[4,64,256]{2,1,0:T(8,128)(2,1)S(1)}, bf16[4,64,256]{2,1,0:T(8,128)(2,1)S(1)}, u32[]{:S(2)}, u32[]{:S(2)}) collective-permute-start(bf16[4,64,256]{2,1,0:T(8,128)(2,1)S(1)} %get-tuple-element.61), channel_id=1, source_target_pairs={{0,8},{1,9},{2,10},{3,11},{4,12},{5,13},{6,14},{7,15},{8,0},{9,1},... | collective-permute-start | bytes 393224 | tf_op jit(solution)/shard_map/ppermute | solution.py:133
  54.1 5.3 %collective-permute-start.8 = (bf16[5,64,256]{2,1,0:T(8,128)(2,1)S(1)}, bf16[5,64,256]{2,1,0:T(8,128)(2,1)S(1)}, u32[]{:S(2)}, u32[]{:S(2)}) collective-permute-start(bf16[5,64,256]{2,1,0:T(8,128)(2,1)S(1)} %get-tuple-element.57), channel_id=1, source_target_pairs={{0,16},{1,17},{2,18},{3,19},{4,20},{5,21},{6,22},{7,23},{8,24},{9,... | collective-permute-start | bytes 491528 | tf_op jit(solution)/shard_map/ppermute | solution.py:133
  55.7 5.3 %collective-permute-start.9 = (bf16[5,64,256]{2,1,0:T(8,128)(2,1)S(1)}, bf16[5,64,256]{2,1,0:T(8,128)(2,1)S(1)}, u32[]{:S(2)}, u32[]{:S(2)}) collective-permute-start(bf16[5,64,256]{2,1,0:T(8,128)(2,1)S(1)} %get-tuple-element.59), channel_id=1, source_target_pairs={{0,2},{1,3},{2,0},{3,1},{4,6},{5,7},{6,4},{7,5},{8,10},{9,11},{10,... | collective-permute-start | bytes 491528 | tf_op jit(solution)/shard_map/ppermute | solution.py:133
  62.2 4.4 %collective-permute-start.11 = (bf16[5,32,256]{2,1,0:T(8,128)(2,1)S(1)}, bf16[5,32,256]{2,1,0:T(8,128)(2,1)S(1)}, u32[]{:S(2)}, u32[]{:S(2)}) collective-permute-start(bf16[5,32,256]{2,1,0:T(8,128)(2,1)S(1)} %get-tuple-element.63), channel_id=1, source_target_pairs={{0,2},{1,3},{2,0},{3,1},{4,6},{5,7},{6,4},{7,5},{8,10},{9,11},{10,... | collective-permute-start | bytes 245768 | tf_op jit(solution)/shard_map/ppermute | solution.py:133
  69.6 10.9 %collective-permute-start.17 = (bf16[4,128,256]{2,1,0:T(8,128)(2,1)S(1)}, bf16[4,128,256]{2,1,0:T(8,128)(2,1)S(1)}, u32[]{:S(2)}, u32[]{:S(2)}) collective-permute-start(bf16[4,128,256]{2,1,0:T(8,128)(2,1)S(1)} %get-tuple-element.71.own_b), channel_id=1, source_target_pairs={{0,16},{1,17},{2,18},{3,19},{4,20},{5,21},{6,22},{7,23},{8,24},{9,... | collective-permute-start | bytes 786440 | tf_op jit(solution)/shard_map/ppermute | solution.py:133
  71.2 6.9 %collective-permute-start.14 = (bf16[14,16,256]{2,1,0:T(8,128)(2,1)S(1)}, bf16[14,16,256]{2,1,0:T(8,128)(2,1)S(1)}, u32[]{:S(2)}, u32[]{:S(2)}) collective-permute-start(bf16[14,16,256]{2,1,0:T(8,128)(2,1)S(1)} %get-tuple-element.69), channel_id=1, source_target_pairs={{0,4},{1,5},{2,6},{3,7},{4,0},{5,1},{6,2},{7,3},{8,12},{9,13},{10,... | collective-permute-start | bytes 344072 | tf_op jit(solution)/shard_map/ppermute | solution.py:133
  72.9 7.5 %collective-permute-start.16 = (bf16[4,96,256]{2,1,0:T(8,128)(2,1)S(1)}, bf16[4,96,256]{2,1,0:T(8,128)(2,1)S(1)}, u32[]{:S(2)}, u32[]{:S(2)}) collective-permute-start(bf16[4,96,256]{2,1,0:T(8,128)(2,1)S(1)} %get-tuple-element.70.own_a), channel_id=1, source_target_pairs={{0,8},{1,9},{2,10},{3,11},{4,12},{5,13},{6,14},{7,15},{8,0},{9,1},... | collective-permute-start | bytes 589832 | tf_op jit(solution)/shard_map/ppermute | solution.py:133
  80.5 9.3 %collective-permute-start.19 = (bf16[2,4,128,256]{3,2,1,0:T(8,128)(2,1)S(1)}, bf16[2,4,128,256]{3,2,1,0:T(8,128)(2,1)S(1)}, u32[]{:S(2)}, u32[]{:S(2)}) collective-permute-start(bf16[2,4,128,256]{3,2,1,0:T(8,128)(2,1)S(1)} %get-tuple-element.73.refs_2_), channel_id=1, source_target_pairs={{0,8},{1,9},{2,10},{3,11},{4,12},{5,13},{6,14},{7,15},{8,0},{9,1},... | collective-permute-start | bytes 1572872 | tf_op jit(solution)/shard_map/ppermute | solution.py:133
  82.2 10.6 %collective-permute-start.18 = (bf16[2,4,96,256]{3,2,1,0:T(8,128)(2,1)S(1)}, bf16[2,4,96,256]{3,2,1,0:T(8,128)(2,1)S(1)}, u32[]{:S(2)}, u32[]{:S(2)}) collective-permute-start(bf16[2,4,96,256]{3,2,1,0:T(8,128)(2,1)S(1)} %get-tuple-element.72.refs_0_), channel_id=1, source_target_pairs={{0,16},{1,17},{2,18},{3,19},{4,20},{5,21},{6,22},{7,23},{8,24},{9,... | collective-permute-start | bytes 1179656 | tf_op jit(solution)/shard_map/ppermute | solution.py:133
  82.8 26.2 %collective-permute-start.22 = (bf16[2,4,128,256]{3,2,1,0:T(8,128)(2,1)S(1)}, bf16[2,4,128,256]{3,2,1,0:T(8,128)(2,1)S(1)}, u32[]{:S(2)}, u32[]{:S(2)}) collective-permute-start(bf16[2,4,128,256]{3,2,1,0:T(8,128)(2,1)S(1)} %get-tuple-element.73.refs_2_), channel_id=1, source_target_pairs={{0,1},{1,0},{2,3},{3,2},{4,5},{5,4},{6,7},{7,6},{8,9},{9,8},{10,11... | collective-permute-start | bytes 1572872 | tf_op jit(solution)/shard_map/ppermute | solution.py:133
  82.8 26.2 %collective-permute-start.20 = (bf16[2,4,96,256]{3,2,1,0:T(8,128)(2,1)S(1)}, bf16[2,4,96,256]{3,2,1,0:T(8,128)(2,1)S(1)}, u32[]{:S(2)}, u32[]{:S(2)}) collective-permute-start(bf16[2,4,96,256]{3,2,1,0:T(8,128)(2,1)S(1)} %get-tuple-element.72.refs_0_), channel_id=1, source_target_pairs={{0,1},{1,0},{2,3},{3,2},{4,5},{5,4},{6,7},{7,6},{8,9},{9,8},{10,11... | collective-permute-start | bytes 1179656 | tf_op jit(solution)/shard_map/ppermute | solution.py:133
  83.3 8.8 %collective-permute-start.24 = (bf16[15,16,256]{2,1,0:T(8,128)(2,1)S(1)}, bf16[15,16,256]{2,1,0:T(8,128)(2,1)S(1)}, u32[]{:S(2)}, u32[]{:S(2)}) collective-permute-start(bf16[15,16,256]{2,1,0:T(8,128)(2,1)S(1)} %shard_map.144.after.refs_0_), channel_id=1, source_target_pairs={{0,4},{1,5},{2,6},{3,7},{4,0},{5,1},{6,2},{7,3},{8,12},{9,13},{10,... | collective-permute-start | bytes 368648 | tf_op jit(solution)/shard_map/ppermute | solution.py:133
  89.8 19.7 %collective-permute-start.23 = (bf16[2,4,128,256]{3,2,1,0:T(8,128)(2,1)S(1)}, bf16[2,4,128,256]{3,2,1,0:T(8,128)(2,1)S(1)}, u32[]{:S(2)}, u32[]{:S(2)}) collective-permute-start(bf16[2,4,128,256]{3,2,1,0:T(8,128)(2,1)S(1)} %collective-permute-done.19.refs_3_), channel_id=1, source_target_pairs={{0,1},{1,0},{2,3},{3,2},{4,5},{5,4},{6,7},{7,6},{8,9},{9,8},{10,11... | collective-permute-start | bytes 1572872 | tf_op jit(solution)/shard_map/ppermute | solution.py:133
  92.7 4.5 %collective-permute-start.25 = (bf16[5,32,256]{2,1,0:T(8,128)(2,1)S(1)}, bf16[5,32,256]{2,1,0:T(8,128)(2,1)S(1)}, u32[]{:S(2)}, u32[]{:S(2)}) collective-permute-start(bf16[5,32,256]{2,1,0:T(8,128)(2,1)S(1)} %get-tuple-element.74.refs_0_), channel_id=1, source_target_pairs={{0,2},{1,3},{2,0},{3,1},{4,6},{5,7},{6,4},{7,5},{8,10},{9,11},{10,... | collective-permute-start | bytes 245768 | tf_op jit(solution)/shard_map/ppermute | solution.py:133
  92.8 16.7 %collective-permute-start.21 = (bf16[2,4,96,256]{3,2,1,0:T(8,128)(2,1)S(1)}, bf16[2,4,96,256]{3,2,1,0:T(8,128)(2,1)S(1)}, u32[]{:S(2)}, u32[]{:S(2)}) collective-permute-start(bf16[2,4,96,256]{3,2,1,0:T(8,128)(2,1)S(1)} %collective-permute-done.18.refs_1_), channel_id=1, source_target_pairs={{0,1},{1,0},{2,3},{3,2},{4,5},{5,4},{6,7},{7,6},{8,9},{9,8},{10,11... | collective-permute-start | bytes 1179656 | tf_op jit(solution)/shard_map/ppermute | solution.py:133
  97.2 4.4 %collective-permute-start.26 = (bf16[5,32,256]{2,1,0:T(8,128)(2,1)S(1)}, bf16[5,32,256]{2,1,0:T(8,128)(2,1)S(1)}, u32[]{:S(2)}, u32[]{:S(2)}) collective-permute-start(bf16[5,32,256]{2,1,0:T(8,128)(2,1)S(1)} %get-tuple-element.75.refs_2_), channel_id=1, source_target_pairs={{0,8},{1,9},{2,10},{3,11},{4,12},{5,13},{6,14},{7,15},{8,0},{9,1},... | collective-permute-start | bytes 245768 | tf_op jit(solution)/shard_map/ppermute | solution.py:133
  101.6 5.3 %collective-permute-start.27 = (bf16[5,32,256]{2,1,0:T(8,128)(2,1)S(1)}, bf16[5,32,256]{2,1,0:T(8,128)(2,1)S(1)}, u32[]{:S(2)}, u32[]{:S(2)}) collective-permute-start(bf16[5,32,256]{2,1,0:T(8,128)(2,1)S(1)} %get-tuple-element.76.refs_4_), channel_id=1, source_target_pairs={{0,16},{1,17},{2,18},{3,19},{4,20},{5,21},{6,22},{7,23},{8,24},{9,... | collective-permute-start | bytes 245768 | tf_op jit(solution)/shard_map/ppermute | solution.py:133
  107.5 5.4 %collective-permute-start.28 = (bf16[5,64,256]{2,1,0:T(8,128)(2,1)S(1)}, bf16[5,64,256]{2,1,0:T(8,128)(2,1)S(1)}, u32[]{:S(2)}, u32[]{:S(2)}) collective-permute-start(bf16[5,64,256]{2,1,0:T(8,128)(2,1)S(1)} %get-tuple-element.77.refs_0_), channel_id=1, source_target_pairs={{0,16},{1,17},{2,18},{3,19},{4,20},{5,21},{6,22},{7,23},{8,24},{9,... | collective-permute-start | bytes 491528 | tf_op jit(solution)/shard_map/ppermute | solution.py:133
  109.0 5.3 %collective-permute-start.29 = (bf16[5,64,256]{2,1,0:T(8,128)(2,1)S(1)}, bf16[5,64,256]{2,1,0:T(8,128)(2,1)S(1)}, u32[]{:S(2)}, u32[]{:S(2)}) collective-permute-start(bf16[5,64,256]{2,1,0:T(8,128)(2,1)S(1)} %get-tuple-element.78.refs_2_), channel_id=1, source_target_pairs={{0,2},{1,3},{2,0},{3,1},{4,6},{5,7},{6,4},{7,5},{8,10},{9,11},{10,... | collective-permute-start | bytes 491528 | tf_op jit(solution)/shard_map/ppermute | solution.py:133
  109.0 5.4 %collective-permute-start.30 = (bf16[5,64,256]{2,1,0:T(8,128)(2,1)S(1)}, bf16[5,64,256]{2,1,0:T(8,128)(2,1)S(1)}, u32[]{:S(2)}, u32[]{:S(2)}) collective-permute-start(bf16[5,64,256]{2,1,0:T(8,128)(2,1)S(1)} %get-tuple-element.79.refs_4_), channel_id=1, source_target_pairs={{0,8},{1,9},{2,10},{3,11},{4,12},{5,13},{6,14},{7,15},{8,0},{9,1},... | collective-permute-start | bytes 491528 | tf_op jit(solution)/shard_map/ppermute | solution.py:133
  115.1 12.8 %collective-permute-start.34 = (bf16[15,128,256]{2,1,0:T(8,128)(2,1)S(1)}, bf16[15,128,256]{2,1,0:T(8,128)(2,1)S(1)}, u32[]{:S(2)}, u32[]{:S(2)}) collective-permute-start(bf16[15,128,256]{2,1,0:T(8,128)(2,1)S(1)} %get-tuple-element.80.mine), channel_id=1, source_target_pairs={{0,1},{1,0},{2,3},{3,2},{4,5},{5,4},{6,7},{7,6},{8,9},{9,8},{10,11... | collective-permute-start | bytes 2949128 | tf_op jit(solution)/shard_map/ppermute | solution.py:133
  115.1 10.1 %collective-permute-start.31 = (bf16[5,128,256]{2,1,0:T(8,128)(2,1)S(1)}, bf16[5,128,256]{2,1,0:T(8,128)(2,1)S(1)}, u32[]{:S(2)}, u32[]{:S(2)}) collective-permute-start(bf16[5,128,256]{2,1,0:T(8,128)(2,1)S(1)} %get-tuple-element.81), channel_id=1, source_target_pairs={{0,8},{1,9},{2,10},{3,11},{4,12},{5,13},{6,14},{7,15},{8,0},{9,1},... | collective-permute-start | bytes 983048 | tf_op jit(solution)/shard_map/ppermute | solution.py:133
  115.6 9.8 %collective-permute-start.32 = (bf16[5,128,256]{2,1,0:T(8,128)(2,1)S(1)}, bf16[5,128,256]{2,1,0:T(8,128)(2,1)S(1)}, u32[]{:S(2)}, u32[]{:S(2)}) collective-permute-start(bf16[5,128,256]{2,1,0:T(8,128)(2,1)S(1)} %get-tuple-element.82), channel_id=1, source_target_pairs={{0,16},{1,17},{2,18},{3,19},{4,20},{5,21},{6,22},{7,23},{8,24},{9,... | collective-permute-start | bytes 983048 | tf_op jit(solution)/shard_map/ppermute | solution.py:133
  116.5 9.5 %collective-permute-start.33 = (bf16[5,128,256]{2,1,0:T(8,128)(2,1)S(1)}, bf16[5,128,256]{2,1,0:T(8,128)(2,1)S(1)}, u32[]{:S(2)}, u32[]{:S(2)}) collective-permute-start(bf16[5,128,256]{2,1,0:T(8,128)(2,1)S(1)} %get-tuple-element.83), channel_id=1, source_target_pairs={{0,2},{1,3},{2,0},{3,1},{4,6},{5,7},{6,4},{7,5},{8,10},{9,11},{10,... | collective-permute-start | bytes 983048 | tf_op jit(solution)/shard_map/ppermute | solution.py:133
  (20 other events, 162.7 us)

commit v4 on v3

v4 whole, which is shorter than its diff:
```python
import functools
import jax
import jax.numpy as jnp
from jax import lax
from jax.experimental import pallas as pl
from jax.experimental.pallas import tpu as pltpu
from jax.sharding import PartitionSpec as P

CI = 256
CO = 256
BLK = 32
FR = 2
HW = 16
NB3 = 216
NB = 224


learn_rate = 0.002
decay_power = 0.8


def silu_slope(values):
    sigma = jax.nn.sigmoid(values)
    return sigma * (1.0 + values * (1.0 - sigma))


def tap_views(frames):
    views = []
    for frame_off in range(3):
        for row_off in range(3):
            for col_off in range(3):
                window = frames[
                    frame_off : frame_off + FR, row_off : row_off + HW, col_off : col_off + HW, :
                ]
                views.append(window.reshape(FR * HW * HW, CI))
    return views


def contract_rows(left, right):
    return lax.dot_general(
        left, right, (((0,), (0,)), ((), ())), preferred_element_type=jnp.float32
    )


def kernel_sums(values, is_small):
    large_part = jnp.sum(jnp.where(is_small[:, None], 0.0, values), axis=0)
    small_part = jnp.sum(jnp.where(is_small[:, None], values, 0.0), axis=0)
    return jnp.stack([large_part, small_part])


def general_shards(
    step_count,
    block_order,
    saved_tiles,
    pre_act,
    grad_output,
    pointwise_live,
    master_rows,
    row_moment,
    col_moment,
    next_tiles,
):
    pre_float = pre_act.astype(jnp.float32)
    activation = jax.nn.silu(pre_float).astype(jnp.bfloat16)
    grad_act = lax.dot_general(
        grad_output, pointwise_live, (((1,), (1,)), ((), ())), preferred_element_type=jnp.float32
    )
    grad_pre = (grad_act * silu_slope(pre_float)).astype(jnp.bfloat16)
    pieces = [contract_rows(view, grad_pre) for view in tap_views(saved_tiles[0])]
    pieces.append(contract_rows(activation, grad_output))
    own_term = jnp.concatenate(pieces, axis=0).astype(jnp.bfloat16)
    total_rows = NB * BLK
    stored = jnp.take(own_term.reshape(NB, BLK, CO), block_order, axis=0).reshape(total_rows, CO)
    own_rows = master_rows.shape[0]
    partial_value = lax.psum_scatter(stored, "shard", scatter_dimension=0, tiled=True).astype(
        jnp.float32
    )
    gradient = lax.psum(partial_value, "group")
    owner = lax.axis_index("shard")
    own_count = own_rows // BLK
    own_blocks = lax.dynamic_slice_in_dim(block_order, owner * own_count, own_count)
    is_small = jnp.repeat(own_blocks >= NB3, BLK, total_repeat_length=own_rows)
    decay_rate = 1.0 - step_count.astype(jnp.float32)[0] ** (-decay_power)
    counts = jnp.array([27 * CI, CO], jnp.float32)
    squares = gradient * gradient
    new_row = decay_rate * row_moment + (1.0 - decay_rate) * jnp.mean(squares, axis=1)
    col_part = kernel_sums(squares, is_small)
    row_part = kernel_sums(new_row[:, None], is_small)[:, 0]
    weighted = kernel_sums(squares / new_row[:, None], is_small)
    col_total, weight_total, row_total = lax.psum((col_part, weighted, row_part), "shard")
    new_col = decay_rate * col_moment + (1.0 - decay_rate) * col_total / counts[:, None]
    row_mean = row_total / counts
    col_rows = jnp.where(is_small[:, None], new_col[1], new_col[0])
    mean_rows = jnp.where(is_small, row_mean[1], row_mean[0])
    scaled = gradient / jnp.sqrt(new_row[:, None] * col_rows / mean_rows[:, None])
    square_total = row_mean * jnp.sum(weight_total / new_col, axis=1)
    clip_factor = jnp.maximum(1.0, jnp.sqrt(square_total / (counts * CO)))
    update_rows = scaled / jnp.where(is_small, clip_factor[1], clip_factor[0])[:, None]
    new_master = master_rows - learn_rate * update_rows
    weights_low = new_master.astype(jnp.bfloat16)
    gathered = lax.all_gather(weights_low, "shard", axis=0, tiled=True)
    inverse = jnp.zeros((NB,), jnp.int32).at[block_order].set(jnp.arange(NB, dtype=jnp.int32))
    natural = jnp.take(gathered.reshape(NB, BLK, CO), inverse, axis=0).reshape(total_rows, CO)
    spatial = natural[: 27 * CI].reshape(27, CI, CO)
    pointwise = natural[27 * CI :]
    hidden_sum = jnp.zeros((FR * HW * HW, CO), jnp.float32)
    for index_tap, view in enumerate(tap_views(next_tiles[0])):
        hidden_sum = hidden_sum + jnp.dot(
            view, spatial[index_tap], preferred_element_type=jnp.float32
        )
    hidden_act = jax.nn.silu(hidden_sum).astype(jnp.bfloat16)
    next_output = jnp.dot(hidden_act, pointwise, preferred_element_type=jnp.float32).astype(
        jnp.bfloat16
    )
    return (update_rows, new_master, new_row, new_col, next_output)


AXES = ("group", "shard")
SLOTS = 14
PIX = FR * HW * HW
SHIFTED = (FR + 2) * (HW + 2) * HW
SLOPES = 3 * SHIFTED
ACTS = SLOPES + PIX
BROUGHT = ACTS + PIX
LOW = jnp.bfloat16
WIDE = jnp.float32
VMEM = pl.BlockSpec(memory_space=pltpu.VMEM)
SMEM = pl.BlockSpec(memory_space=pltpu.SMEM)
HBM = pl.BlockSpec(memory_space=pl.ANY)
MASK_CORE, MASK_NEAR, MASK_FAR, MASK_X, MASK_Y = 1, 2, 4, 8, 16
PARTS = ((0, 5, (0, 1, 2)), (5, 5, (1, 2, 0)), (10, 4, (2, 0, 1)))
MASKS = (MASK_X, MASK_Y, MASK_NEAR)


def swap(value, mask):
    return lax.ppermute(value, AXES, [(at, at ^ mask) for at in range(32)])


def call(kernel, outs, in_specs, scratch=(), flops=0, moved=0, room=8, pin=True):
    return pl.pallas_call(
        kernel,
        out_shape=[(pltpu.VMEM if pin else jax.ShapeDtypeStruct)(*out) for out in outs],
        in_specs=in_specs,
        out_specs=[VMEM] * len(outs),
        scratch_shapes=list(scratch),
        compiler_params=pltpu.CompilerParams(vmem_limit_bytes=room << 20),
        cost_estimate=pl.CostEstimate(flops=flops, bytes_accessed=moved, transcendentals=0),
    )


def far_away(array):
    return pltpu.with_memory_space_constraint(array, pltpu.HBM)


def store_shifted(tile, out):
    for col_off in range(3):
        out[col_off * SHIFTED : (col_off + 1) * SHIFTED] = tile[
            :, :, col_off : col_off + HW, :
        ].reshape(SHIFTED, CI)


def shift_kernel(tile, out):
    store_shifted(tile, out)


def slope_of(pre, grad, pointwise):
    grad_act = lax.dot_general(
        grad, pointwise, (((1,), (1,)), ((), ())), preferred_element_type=WIDE
    )
    return (grad_act * silu_slope(pre.astype(WIDE))).astype(LOW)


def fetch(pairs, arrived):
    copies = [
        pltpu.make_async_copy(source, target, arrived.at[index])
        for index, (source, target) in enumerate(pairs)
    ]
    for copy in copies:
        copy.start()
    return copies


def own_kernel(at, tile, pre_far, grad_far, pointwise_far, brought, pre, grad, pointwise, arrived):
    copies = fetch(((pre_far, pre), (grad_far, grad), (pointwise_far, pointwise)), arrived)
    store_shifted(tile, brought)
    for copy in copies:
        copy.wait()
    brought[SLOPES:ACTS] = slope_of(pre[...], grad[...], pointwise[...])
    brought[ACTS:] = jax.nn.silu(pre[...].astype(WIDE)).astype(LOW)


def pack_kernel(at, after, master_far, row_moment_far, packed, master, row_moment, arrived):
    quarter = pl.multiple_of((at[1] * 2 + at[0]) * (SLOTS * 16), SLOTS * 16)
    row_moment[...] = jnp.zeros((16, 128), WIDE)
    copies = fetch(
        (
            (master_far.at[pl.ds(quarter, SLOTS * 16), :], master),
            (row_moment_far, row_moment.at[pl.ds(0, 7), :]),
        ),
        arrived,
    )
    for copy in copies:
        copy.wait()
    packed[:SLOTS] = master[...].astype(LOW).reshape(SLOTS, 16, CO)
    high = row_moment[...].astype(LOW).astype(WIDE)
    packed[SLOTS] = jnp.concatenate([high, row_moment[...] - high], axis=1).astype(LOW)


def term_kernel(
    at, own, tile_peer, pre_peer, grad_peer, grad_far, pointwise_far,
    keep, send_one, send_two, send_three, peer, rights, pointwise, arrived,
):
    core = at[4]
    copies = fetch(((grad_far, rights.at[1, pl.ds(0, PIX), :]), (pointwise_far, pointwise)), arrived)
    store_shifted(tile_peer, peer)
    peer[ACTS:] = jax.nn.silu(pre_peer[...].astype(WIDE)).astype(LOW)
    for copy in copies:
        copy.wait()
    peer[SLOPES:ACTS] = slope_of(pre_peer[...], grad_peer[...], pointwise[...])
    rights[0, :PIX] = own[SLOPES:ACTS]
    rights[0, PIX:] = peer[SLOPES:ACTS]
    rights[1, PIX:] = grad_peer[...]
    for slot in range(SLOTS):
        tap = core * SLOTS + slot
        frame_off, row_off, col_off = tap // 9, lax.rem(tap // 3, 3), lax.rem(tap, 3)
        pieces = []
        for ref in (own, peer):
            for frame in range(FR):
                start = col_off * SHIFTED + ((frame + frame_off) * (HW + 2) + row_off) * HW
                if slot == SLOTS - 1:
                    start = jnp.where(core == 0, start, ACTS + frame * HW * HW)
                pieces.append(ref[pl.ds(pl.multiple_of(start, HW), HW * HW), :])
        right = rights[core] if slot == SLOTS - 1 else rights[0]
        total = contract_rows(jnp.concatenate(pieces, axis=0), right)
        for (first, count, order), send in zip(PARTS, (send_one, send_two, send_three)):
            if first <= slot < first + count:
                low, high, at_low = total[:128], total[128:], at[order[0]] == 0
                keep[slot] = jnp.where(at_low, low, high).astype(LOW)
                send[slot - first] = jnp.where(at_low, high, low).astype(LOW)


def fold_kernel(step, skip, at, *refs):
    size = 256 >> (step + 1)
    refs = refs[skip:]
    keep, gots, stay, sends = refs[0], refs[1:4], refs[4], refs[5:]
    for part, (first, count, order) in enumerate(PARTS):
        mine = at[order[step] if step < 3 else 3]
        here = slice(first, first + count)
        for which, out in ((mine, 0), (1 - mine, 1)):
            rows = pl.ds(pl.multiple_of(which * size, size), size)
            value = keep[here, rows] + gots[part][:, rows]
            if out == 0:
                stay[here] = value
            elif step < 3:
                sends[part][...] = value
            else:
                sends[0][here] = value


def moment_kernel(at, rate, own, got, moments, scaled):
    total = (own[...].astype(WIDE) + got[...].astype(WIDE)).reshape(SLOTS * 16, CO)
    squares = total * total
    decay = rate[0]
    mean = jnp.sum(squares, axis=1, keepdims=True) * (1.0 / CO)
    row_moment = jnp.concatenate([moments[:, slot : slot + 1] for slot in range(SLOTS)], axis=0)
    new_row = decay * row_moment + (1.0 - decay) * mean
    scaled[:SLOTS] = (total * lax.rsqrt(new_row)).astype(LOW).reshape(SLOTS, 16, CO)
    weighted = squares / new_row
    cut = (SLOTS - 1) * 16
    last_small = at[4] == 1
    rows = []
    for values in (squares, weighted, jnp.broadcast_to(new_row, (SLOTS * 16, CO))):
        large = jnp.sum(values[:cut], axis=0, keepdims=True)
        last = jnp.sum(values[cut:], axis=0, keepdims=True)
        rows.append(large + jnp.where(last_small, 0.0, last))
        rows.append(jnp.where(last_small, last, 0.0))
    spread = jnp.broadcast_to(new_row, (SLOTS * 16, 128))
    spread = jnp.concatenate([spread, jnp.zeros((32, 128), WIDE)], axis=0)
    rows.append(jnp.transpose(spread)[:1])
    rows.append(jnp.zeros((1, CO), WIDE))
    message = jnp.concatenate(rows, axis=0)
    high = message.astype(LOW).astype(WIDE)
    scaled[SLOTS] = jnp.concatenate([high, message - high], axis=0).astype(LOW)


def store_factors(total, decay, col_moment, new_col, factor):
    for kernel in range(2):
        count = 27.0 * CI if kernel == 0 else float(CO)
        col = decay * col_moment[kernel : kernel + 1] + (1.0 - decay) * (
            total[kernel : kernel + 1] / count
        )
        row_mean = total[4 + kernel : 5 + kernel] / count
        square = row_mean * jnp.sum(
            total[2 + kernel : 3 + kernel] / col, axis=1, keepdims=True
        )
        clip = jnp.maximum(1.0, jnp.sqrt(square / (count * CO)))
        new_col[kernel : kernel + 1] = col
        factor[kernel : kernel + 1] = 1.0 / (jnp.sqrt(col / row_mean) * clip)


def stack_kernel(at, after, own, got, out):
    out[at[2]] = own[...]
    out[1 - at[2]] = got[...]


def line_kernel(at, after, own, got, out_a, out_b):
    for which, piece in ((at[3], own), (1 - at[3], got)):
        for near in range(2):
            rows = piece[near, :SLOTS].reshape(SLOTS * 16, CO)
            out_a[which * 2 + near] = rows[: 3 * BLK]
            out_b[which * 2 + near] = rows[3 * BLK :]


def gather_moments_kernel(at, own, got, out):
    for which, piece in ((at[3], own), (1 - at[3], got)):
        for near in range(2):
            out[which * 2 + near] = piece[near, SLOTS]


def moments_kernel(at, block_order, mine, peer, out, table, rows, inverse):
    core = at[4]
    for side, ref in enumerate((mine, peer)):
        for line in range(4):
            values = ref[line].astype(WIDE)
            values = values[:, :128] + values[:, 128:]
            table[pl.ds(pl.multiple_of((line * 2 + (core ^ side)) * 8, 8), 8), :] = values[:8]

    def invert(stored, carry):
        inverse[block_order[stored]] = stored
        return carry

    lax.fori_loop(0, NB, invert, 0, unroll=8)
    rows[...] = jnp.zeros((128, 128), WIDE)
    for first, count, order in PARTS:
        place = at[order[0]] * 4 + at[order[1]] * 2 + at[order[2]]
        for slot in range(first, first + count):
            stored = inverse[(core * SLOTS + slot) * 8 + place]
            owner, local = stored // (NB // 8), lax.rem(stored, NB // 8)
            row = table[pl.ds(owner * 8 + local // 4, 1), :]
            turn = lax.rem(128 - lax.rem(local, 4) * BLK - at[3] * 16, 128)
            rows[slot : slot + 1] = pltpu.roll(row, turn, 1)
    out[...] = jnp.transpose(rows[...])[:16]


def double_kernel(after, own_a, got_a, own_b, got_b, out_a, out_b):
    out_a[0], out_a[1] = own_a[...], got_a[...]
    out_b[0], out_b[1] = own_b[...], got_b[...]


def merge_kernel(after, *refs):
    pieces, out = refs[:-1], refs[-1]
    first = 0
    for kind, piece in enumerate(pieces):
        count = piece.shape[2]
        out[kind % 2, :, :, first : first + count] = piece[...]
        first += count * (kind % 2)


def order_kernel(at, block_order, mine, peer, out):
    count = NB // 8
    quarters = count // 4
    for flip_core, piece in enumerate((mine, peer)):
        core = at[4] ^ flip_core
        for kind in range(2):
            for away in range(2):
                for local in range(quarters):
                    in_a = local < 3
                    flip_x, flip_y = (away, kind) if in_a else (kind, away)
                    quarter = (at[1] ^ flip_y) * 2 + (at[0] ^ flip_x)
                    for line in range(4):
                        block = block_order[(line * 2 + core) * count + quarter * quarters + local]
                        to = pl.ds(pl.multiple_of(block * BLK, BLK), BLK)
                        out[to, :] = piece[kind, away, line, local * BLK : local * BLK + BLK]


def widen_kernel(step, at, after, *refs):
    size = 256 >> (step + 1)
    if step == 3:
        (own, got), outs = refs[:2], refs[2:]
    else:
        ins, outs = refs[:6], refs[6:]
    for part, (first, _, order) in enumerate(PARTS):
        mine = at[order[step] if step < 3 else 3]
        for index, which in enumerate((mine, 1 - mine)):
            rows = pl.ds(pl.multiple_of(which * size, size), size)
            if step == 3:
                value = (own, got)[index][first : first + 5]
            else:
                value = ins[2 * part + index][...]
            if step == 0:
                outs[0][first : first + 5, rows] = value
            else:
                outs[part][:, rows] = value


def window(views, tap):
    frame_off, row_off, col_off = tap // 9, lax.rem(tap // 3, 3), lax.rem(tap, 3)
    parts = []
    for frame in range(FR):
        start = col_off * SHIFTED + ((frame + frame_off) * (HW + 2) + row_off) * HW
        parts.append(views[pl.ds(pl.multiple_of(start, HW), HW * HW), :])
    return jnp.concatenate(parts, axis=0)


def old_hidden_kernel(views, natural, hidden):
    total = jnp.zeros((PIX, CO), WIDE)
    for tap in range(27):
        weights = natural[tap * CI : tap * CI + CI]
        total = total + jnp.dot(window(views, tap), weights, preferred_element_type=WIDE)
    hidden[...] = total


def add_taps(views, scaled, core):
    total = jnp.zeros((PIX, CO), WIDE)
    for slot in range(SLOTS):
        tap = jnp.minimum(core * SLOTS + slot, 26)
        weights = scaled[slot]
        if slot == SLOTS - 1:
            weights = jnp.where(core == 0, weights.astype(WIDE), 0.0).astype(LOW)
        total = total + jnp.dot(window(views, tap), weights, preferred_element_type=WIDE)
    return total


def half_hidden_kernel(at, views, scaled, hidden):
    hidden[...] = add_taps(views, scaled, at[4])


def finish_kernel(
    at, block_order, rate, col_moment, views, natural, master, mine, peer, old, own_part,
    update_rows, new_master, new_row, new_col, next_output, factor, row_table,
):
    core = at[4]
    total = jnp.zeros((8, CO), WIDE)
    for side, piece in enumerate((mine, peer)):
        message = piece[SLOTS].astype(WIDE).reshape(16, 2, 8, CO)
        message = message[:, 0] + message[:, 1]
        total = total + jnp.sum(message, axis=0)
        for index in range(16):
            for half in range(2):
                to = (side * 16 + index) * 2 + half
                row_table[to : to + 1] = message[index, 6:7, half * 128 : half * 128 + 128]
    store_factors(total, rate[0], col_moment, new_col, factor)
    change = own_part[...] + add_taps(views, peer, 1 - core)
    hidden = old[...] - (learn_rate * factor[0:1]) * change
    small = jnp.where(core == 1, mine[SLOTS - 1].astype(WIDE), peer[SLOTS - 1].astype(WIDE))
    weights = natural[27 * CI :].astype(WIDE) - small * (learn_rate * factor[1:2])
    next_output[...] = jnp.dot(
        jax.nn.silu(hidden).astype(LOW), weights.astype(LOW), preferred_element_type=WIDE
    ).astype(LOW)

    owner = at[3] * 4 + at[2] * 2 + core
    lane = lax.broadcasted_iota(jnp.int32, (1, 128), 1)
    for line in range(7):
        values = jnp.zeros((1, 128), WIDE)
        for part in range(4):
            local = line * 4 + part
            block = block_order[owner * (NB // 8) + local]
            side = (block // (8 * SLOTS)) ^ core
            slot, place = lax.rem(block // 8, SLOTS), lax.rem(block, 8)
            one, two, three = place // 4, lax.rem(place // 2, 2), lax.rem(place, 2)
            sender = jnp.where(
                slot < 5,
                three * 8 + one * 4 + two * 2,
                jnp.where(slot < 10, two * 8 + three * 4 + one * 2, place * 2),
            )
            chosen = jnp.where(block >= NB3, factor[1:2], factor[0:1])
            rows = slice(local * BLK, local * BLK + BLK)
            there = pl.ds(pl.multiple_of(place * BLK, BLK), BLK)
            value = jnp.where(
                side == 0, mine[slot, there, :].astype(WIDE), peer[slot, there, :].astype(WIDE)
            )
            update = value * chosen
            update_rows[rows, :] = update
            new_master[rows, :] = master[rows, :] - learn_rate * update
            for half in range(2):
                at_row = (side * 16 + sender + half) * 2 + slot // 8
                to = part * 32 + half * 16
                turn = lax.rem(128 + to - lax.rem(slot, 8) * 16, 128)
                turned = pltpu.roll(row_table[pl.ds(at_row, 1), :], turn, 1)
                values = jnp.where((lane >= to) & (lane < to + 16), turned, values)
        new_row[line : line + 1] = values


def shards(
    step_count,
    block_order,
    saved_tiles,
    pre_act,
    grad_output,
    pointwise_live,
    master_rows,
    row_moment,
    col_moment,
    next_tiles,
):
    group, shard = lax.axis_index("group"), lax.axis_index("shard")
    axis_y, axis_x = group // 2, group % 2
    far, near, core = shard // 4, shard // 2 % 2, shard % 2
    at = jnp.stack([axis_x, axis_y, near, far, core]).astype(jnp.int32)
    decay_rate = 1.0 - step_count.astype(WIDE) ** (-decay_power)

    tile_peer = swap(saved_tiles, MASK_CORE)
    pre_peer = swap(pre_act, MASK_CORE)
    grad_peer = swap(grad_output, MASK_CORE)
    rows_far = [far_away(array) for array in (pre_act, grad_output, pointwise_live)]
    brought = call(
        own_kernel,
        [((BROUGHT, CI), LOW)],
        [SMEM, VMEM] + [HBM] * 3,
        scratch=[
            pltpu.VMEM((PIX, CO), LOW),
            pltpu.VMEM((PIX, CO), LOW),
            pltpu.VMEM((CO, CO), LOW),
            pltpu.SemaphoreType.DMA((3,)),
        ],
        moved=4 << 20,
    )(at, saved_tiles[0], *rows_far)[0]

    keep, *sends = call(
        term_kernel,
        [((SLOTS, 128, CO), LOW)] + [((count, 128, CO), LOW) for _, count, _ in PARTS],
        [SMEM] + [VMEM] * 4 + [HBM] * 2,
        scratch=[
            pltpu.VMEM((BROUGHT, CI), LOW),
            pltpu.VMEM((2, 2 * PIX, CO), LOW),
            pltpu.VMEM((CO, CO), LOW),
            pltpu.SemaphoreType.DMA((2,)),
        ],
        flops=2 * 14 * 1024 * 256 * 256,
        moved=6 << 20,
        room=12,
    )(at, brought, tile_peer[0], pre_peer, grad_peer, *rows_far[1:])

    packed = call(
        pack_kernel,
        [((SLOTS + 1, 16, CO), LOW)],
        [SMEM] + [HBM] * 3,
        scratch=[
            pltpu.VMEM((SLOTS * 16, CO), WIDE),
            pltpu.VMEM((16, 128), WIDE),
            pltpu.SemaphoreType.DMA((2,)),
        ],
    )(at, keep, far_away(master_rows), far_away(row_moment.reshape(7, 128)))[0]
    packed_near = swap(packed, MASK_NEAR)
    views = call(shift_kernel, [((3 * SHIFTED, CI), LOW)], [VMEM], moved=3 << 20)(next_tiles[0])[0]

    for step in range(1, 4):
        gots = [
            swap(send, MASKS[order[step - 1]]) for send, (_, _, order) in zip(sends, PARTS)
        ]
        if step == 1:
            pair = call(
                stack_kernel,
                [((2, SLOTS + 1, 16, CO), LOW)],
                [SMEM, HBM] + [VMEM] * 2,
                moved=1 << 20,
            )(at, gots[2], packed, packed_near)[0]
            pair_far = swap(pair, MASK_FAR)
        size = 256 >> (step + 1)
        outs = [((SLOTS, size, CO), LOW)] + [((count, size, CO), LOW) for _, count, _ in PARTS]
        if step == 3:
            outs = outs[:1] * 2
        after = ([], [pair_far], [line_a, line_b, views] if step == 3 else [])[step - 1]
        keep, *sends = call(
            functools.partial(fold_kernel, step, len(after)),
            outs,
            [SMEM] + [HBM] * len(after) + [VMEM] * 4,
            moved=1 << 20,
        )(at, *after, keep, *gots)
        if step == 2:
            line_a, line_b = call(
                line_kernel,
                [((4, 3 * BLK, CO), LOW), ((4, 4 * BLK, CO), LOW)],
                [SMEM, HBM] + [VMEM] * 2,
                moved=1 << 20,
            )(at, keep, pair, pair_far)
    line_got_a, line_got_b = swap(line_a, MASK_X), swap(line_b, MASK_Y)
    moments = call(gather_moments_kernel, [((4, 16, CO), LOW)], [SMEM] + [VMEM] * 2)(
        at, pair, pair_far
    )[0]
    own_moment = call(
        moments_kernel,
        [((16, 128), WIDE)],
        [SMEM] * 2 + [VMEM] * 2,
        scratch=[
            pltpu.VMEM((64, 128), WIDE),
            pltpu.VMEM((128, 128), WIDE),
            pltpu.SMEM((NB,), jnp.int32),
        ],
    )(at, block_order, moments, swap(moments, MASK_CORE))[0]
    scaled = call(moment_kernel, [((SLOTS + 1, 16, CO), LOW)], [SMEM] * 2 + [VMEM] * 3)(
        at, decay_rate, keep, swap(sends[0], MASK_FAR), own_moment
    )[0]
    plane_a, plane_b = call(
        double_kernel,
        [((2, 4, 3 * BLK, CO), LOW), ((2, 4, 4 * BLK, CO), LOW)],
        [HBM] + [VMEM] * 4,
        moved=2 << 20,
    )(keep, line_a, line_got_a, line_b, line_got_b)
    planes = [plane_a, swap(plane_a, MASK_Y), plane_b, swap(plane_b, MASK_X)]

    pieces = [scaled, swap(scaled, MASK_FAR)]
    after = at
    for step in range(3, -1, -1):
        size = 256 >> step
        outs = [((5, size, CO), LOW)] * 3 if step > 0 else [((SLOTS + 1, size, CO), LOW)]
        joined = call(
            functools.partial(widen_kernel, step), outs, [SMEM, HBM] + [VMEM] * len(pieces)
        )(at, after, *pieces)
        if step == 2:
            merged = call(
                merge_kernel, [((2, 2, 4, 7 * BLK, CO), LOW)], [HBM] + [VMEM] * 4, moved=4 << 20
            )(joined[0], *planes)[0]
            natural = call(
                order_kernel, [((NB * BLK, CO), LOW)], [SMEM] * 2 + [VMEM] * 2, moved=8 << 20
            )(at, block_order, merged, swap(merged, MASK_CORE))[0]
        after = natural if step == 1 else at
        if step > 0:
            pieces = []
            for part, (_, _, order) in enumerate(PARTS):
                pieces += [joined[part], swap(joined[part], MASKS[order[step - 1]])]
    mine = joined[0]
    peer = swap(mine, MASK_CORE)
    old = call(
        old_hidden_kernel,
        [((PIX, CO), WIDE)],
        [VMEM] * 2,
        flops=2 * 27 * 512 * 256 * 256,
        moved=6 << 20,
    )(views, natural)[0]
    half = call(
        half_hidden_kernel,
        [((PIX, CO), WIDE)],
        [SMEM] + [VMEM] * 2,
        flops=2 * 14 * 512 * 256 * 256,
        moved=4 << 20,
    )(at, views, mine)[0]

    update_rows, new_master, new_row, new_col, next_output = call(
        finish_kernel,
        [
            ((NB // 8 * BLK, CO), WIDE),
            ((NB // 8 * BLK, CO), WIDE),
            ((7, 128), WIDE),
            ((2, CO), WIDE),
            ((PIX, CO), LOW),
        ],
        [SMEM] * 3 + [VMEM] * 8,
        scratch=[
            pltpu.VMEM((2, CO), WIDE),
            pltpu.VMEM((64, 128), WIDE),
        ],
        pin=False,
        flops=2 * 16 * 512 * 256 * 256,
        moved=16 << 20,
        room=16,
    )(at, block_order, decay_rate, col_moment, views, natural, master_rows, mine, peer, old, half)
    return (update_rows, new_master, new_row.reshape(-1), new_col, next_output)


def solution(mesh):
    in_specs = (
        P(),
        P(),
        P(("group", "shard"), None, None, None, None),
        P(("group", "shard"), None),
        P(("group", "shard"), None),
        P(),
        P("shard", None),
        P("shard"),
        P(),
        P(("group", "shard"), None, None, None, None),
    )
    out_specs = (P("shard", None), P("shard", None), P("shard"), P(), P(("group", "shard"), None))
    body = shards if (mesh.shape["group"], mesh.shape["shard"]) == (4, 8) else general_shards
    return jax.shard_map(body, mesh=mesh, in_specs=in_specs, out_specs=out_specs, check_vma=False)
```

time: 133 us -> 101 us (0.76)
  waiting for transfers between devices: 60.3 us -> 40.5 us
  local copies, waits for them, and re-layouts: 11.9 us -> 1.58 us
  other arithmetic: 3.6 us -> 0 us
  Pallas kernels: 22.1 us -> 24.7 us
    ppermute x38 -> x32, waiting for transfers between devices: 60.3 us -> 40.5 us  [swap(): return lax.ppermute(value, AXES, [(at, at ^ mask) for at in range(32)])]
    gather x4 -> x0, local copies, waits for them, and re-layouts: 3.61 us -> none  [the longest x2 2.32 us: shards(): jnp.take(moment_stored, inverse, axis=0).reshape(2, SLOTS, 16, 16)]
    pallas_call x8 -> x14, Pallas kernels: 13.6 us -> 16.8 us  [the longest x1 4 us: shards(): call(term_kernel, [((SLOTS, 128, CO), LOW)] + [((count, 128, CO), LOW) fo...]
    unnamed x32 -> x10, local copies, waits for them, and re-layouts: 4.09 us -> 1.37 us
    another operation x2 -> x0, other arithmetic: 1.43 us -> none
    ppermute x38 -> x32, starting transfers between devices: 33.3 us -> 32 us  [swap(): return lax.ppermute(value, AXES, [(at, at ^ mask) for at in range(32)])]
  transfers between devices with their start and end apart: 38 -> 32, of which waited for: 27 -> 18; matrix products, arithmetic and copies ran while one was open for 7% -> 2% of each run, Pallas kernels for 3% -> 15%
where the time goes in v4:
time: 101 us
  waiting for transfers between devices  40.5 us (40%)
  starting transfers between devices  32 us (32%)
  Pallas kernels  24.7 us (24%)
  between operations  1.69 us (2%)
  local copies, waits for them, and re-layouts  1.58 us (2%)
    ppermute x32, waiting for transfers between devices, swap(): return lax.ppermute(value, AXES, [(at, at ^ mask) for at in range(32)])  40.5 us
    ppermute x32, starting transfers between devices, swap(): return lax.ppermute(value, AXES, [(at, at ^ mask) for at in range(32)])  32 us
    pallas_call x1, Pallas kernels, shards(): call(finish_kernel, [((NB // 8 * BLK, CO), WIDE), ((NB // 8 * BLK, CO), W...  4.02 us
    pallas_call x1, Pallas kernels, shards(): call(term_kernel, [((SLOTS, 128, CO), LOW)] + [((count, 128, CO), LOW) fo...  4 us
    pallas_call x4, Pallas kernels, shards(): call(functools.partial(widen_kernel, step), outs, [SMEM, HBM] + [VMEM] *...  2.41 us
  transfers between devices with their start and end apart: 32, of which 18 were waited for; matrix products, arithmetic and copies ran while one was open for 2% of the time, Pallas kernels for 15%

profile of v4, /device:TPU:0, one launch (start us, length us, event | category | flops | bytes accessed | tf_op | source)
XLA Modules:
  0.0 100.6 jit_solution(883124579069870559)
XLA Ops:
  3.0 1.9 %shard_map.138.own = bf16[4480,256]{1,0:T(8,128)(2,1)S(1)} custom-call(s32[5]{0:T(128)S(1)} %stack.23.at.after, bf16[4,18,18,256]{3,2,1,0:T(8,128)(2,1)S(1)} %bitcast.16, bf16[512,256]{1,0:T(8,128)(2,1)} %pre_far.1, bf16[512,256]{1,0:T(8,128)(2,1)} %grad_far.3, bf16[256,256]{1,0:T(8,128)(2,1)} %pointwise_far.3), custom_call_target="tpu_custom_call" | custom-call | bytes 4194304 | tf_op jit(solution)/shard_map/pallas_call | solution.py:506
  5.1 4.0 %shard_map.139 = (bf16[14,128,256]{2,1,0:T(8,128)(2,1)S(1)}, bf16[5,128,256]{2,1,0:T(8,128)(2,1)S(1)}, bf16[5,128,256]{2,1,0:T(8,128)(2,1)S(1)}, bf16[4,128,256]{2,1,0:T(8,128)(2,1)S(1)}) custom-call(s32[5]{0:T(128)S(1)} %stack.23.at.after, bf16[4480,256]{1,0:T(8,128)(2,1)S(1)} %shard_map.138.own, bf16[4,18,18,256]{3,2,1,0:T(8,128)(2,1)S(1)} %bitcast.18, ...), custom_call_target="tpu_custom_call" | custom-call | flops 1879048192 | bytes 6291456 | tf_op jit(solution)/shard_map/pallas_call | solution.py:519
  9.1 2.7 %collective-permute-start.3 = (bf16[4,128,256]{2,1,0:T(8,128)(2,1)S(1)}, bf16[4,128,256]{2,1,0:T(8,128)(2,1)S(1)}, u32[]{:S(2)}, u32[]{:S(2)}) collective-permute-start(bf16[4,128,256]{2,1,0:T(8,128)(2,1)S(1)} %get-tuple-element.37), channel_id=1, source_target_pairs={{0,2},{1,3},{2,0},{3,1},{4,6},{5,7},{6,4},{7,5},{8,10},{9,11},{10,... | collective-permute-start | bytes 786440 | tf_op jit(solution)/shard_map/ppermute | solution.py:136
  11.8 1.5 %collective-permute-start.6 = (bf16[5,128,256]{2,1,0:T(8,128)(2,1)S(1)}, bf16[5,128,256]{2,1,0:T(8,128)(2,1)S(1)}, u32[]{:S(2)}, u32[]{:S(2)}) collective-permute-start(bf16[5,128,256]{2,1,0:T(8,128)(2,1)S(1)} %get-tuple-element.39), channel_id=1, source_target_pairs={{0,8},{1,9},{2,10},{3,11},{4,12},{5,13},{6,14},{7,15},{8,0},{9,1},... | collective-permute-start | bytes 983048 | tf_op jit(solution)/shard_map/ppermute | solution.py:136
  13.3 1.5 %collective-permute-start.7 = (bf16[5,128,256]{2,1,0:T(8,128)(2,1)S(1)}, bf16[5,128,256]{2,1,0:T(8,128)(2,1)S(1)}, u32[]{:S(2)}, u32[]{:S(2)}) collective-permute-start(bf16[5,128,256]{2,1,0:T(8,128)(2,1)S(1)} %get-tuple-element.40), channel_id=1, source_target_pairs={{0,16},{1,17},{2,18},{3,19},{4,20},{5,21},{6,22},{7,23},{8,24},{9,... | collective-permute-start | bytes 983048 | tf_op jit(solution)/shard_map/ppermute | solution.py:136
  14.8 1.5 %shard_map.140.own = bf16[15,16,256]{2,1,0:T(8,128)(2,1)S(1)} custom-call(s32[5]{0:T(128)S(1)} %stack.23.at.after, bf16[14,128,256]{2,1,0:T(8,128)(2,1)S(1)} %get-tuple-element.38.after.refs_0_, f32[896,256]{1,0:T(8,128)} %master.1, f32[7,128]{1,0:T(8,128)} %bitcast.19), custom_call_target="tpu_custom_call" | custom-call | tf_op jit(solution)/shard_map/pallas_call | solution.py:534
  16.9 4.5 %collective-permute-done.4.got = bf16[15,16,256]{2,1,0:T(8,128)(2,1)S(1)} collective-permute-done((bf16[15,16,256]{2,1,0:T(8,128)(2,1)S(1)}, bf16[15,16,256]{2,1,0:T(8,128)(2,1)S(1)}, u32[]{:S(2)}, u32[]{:S(2)}) %collective-permute-start.4) | collective-permute-done | bytes 122912 | tf_op jit(solution)/shard_map/ppermute | solution.py:136
  21.9 2.8 %collective-permute-start.5 = (bf16[2,15,16,256]{3,2,1,0:T(8,128)(2,1)S(1)}, bf16[2,15,16,256]{3,2,1,0:T(8,128)(2,1)S(1)}, u32[]{:S(2)}, u32[]{:S(2)}) collective-permute-start(bf16[2,15,16,256]{3,2,1,0:T(8,128)(2,1)S(1)} %shard_map.141.own), channel_id=1, source_target_pairs={{0,4},{1,5},{2,6},{3,7},{4,0},{5,1},{6,2},{7,3},{8,12},{9,13},{10,... | collective-permute-start | bytes 737288 | tf_op jit(solution)/shard_map/ppermute | solution.py:136
  25.4 1.6 %collective-permute-start.8 = (bf16[5,64,256]{2,1,0:T(8,128)(2,1)S(1)}, bf16[5,64,256]{2,1,0:T(8,128)(2,1)S(1)}, u32[]{:S(2)}, u32[]{:S(2)}) collective-permute-start(bf16[5,64,256]{2,1,0:T(8,128)(2,1)S(1)} %get-tuple-element.42), channel_id=1, source_target_pairs={{0,16},{1,17},{2,18},{3,19},{4,20},{5,21},{6,22},{7,23},{8,24},{9,... | collective-permute-start | bytes 491528 | tf_op jit(solution)/shard_map/ppermute | solution.py:136
  27.0 1.6 %collective-permute-start.9 = (bf16[5,64,256]{2,1,0:T(8,128)(2,1)S(1)}, bf16[5,64,256]{2,1,0:T(8,128)(2,1)S(1)}, u32[]{:S(2)}, u32[]{:S(2)}) collective-permute-start(bf16[5,64,256]{2,1,0:T(8,128)(2,1)S(1)} %get-tuple-element.43), channel_id=1, source_target_pairs={{0,2},{1,3},{2,0},{3,1},{4,6},{5,7},{6,4},{7,5},{8,10},{9,11},{10,... | collective-permute-start | bytes 491528 | tf_op jit(solution)/shard_map/ppermute | solution.py:136
  28.6 1.5 %collective-permute-start.10 = (bf16[4,64,256]{2,1,0:T(8,128)(2,1)S(1)}, bf16[4,64,256]{2,1,0:T(8,128)(2,1)S(1)}, u32[]{:S(2)}, u32[]{:S(2)}) collective-permute-start(bf16[4,64,256]{2,1,0:T(8,128)(2,1)S(1)} %get-tuple-element.44), channel_id=1, source_target_pairs={{0,8},{1,9},{2,10},{3,11},{4,12},{5,13},{6,14},{7,15},{8,0},{9,1},... | collective-permute-start | bytes 393224 | tf_op jit(solution)/shard_map/ppermute | solution.py:136
  30.1 3.5 %collective-permute-done.10.refs_4_ = bf16[4,64,256]{2,1,0:T(8,128)(2,1)S(1)} collective-permute-done((bf16[4,64,256]{2,1,0:T(8,128)(2,1)S(1)}, bf16[4,64,256]{2,1,0:T(8,128)(2,1)S(1)}, u32[]{:S(2)}, u32[]{:S(2)}) %collective-permute-start.10) | collective-permute-done | bytes 131104 | tf_op jit(solution)/shard_map/ppermute | solution.py:136
  33.6 2.1 %collective-permute-done.9.refs_3_ = bf16[5,64,256]{2,1,0:T(8,128)(2,1)S(1)} collective-permute-done((bf16[5,64,256]{2,1,0:T(8,128)(2,1)S(1)}, bf16[5,64,256]{2,1,0:T(8,128)(2,1)S(1)}, u32[]{:S(2)}, u32[]{:S(2)}) %collective-permute-start.9) | collective-permute-done | bytes 163872 | tf_op jit(solution)/shard_map/ppermute | solution.py:136
  36.9 1.8 %collective-permute-start.21 = (bf16[4,128,256]{2,1,0:T(8,128)(2,1)S(1)}, bf16[4,128,256]{2,1,0:T(8,128)(2,1)S(1)}, u32[]{:S(2)}, u32[]{:S(2)}) collective-permute-start(bf16[4,128,256]{2,1,0:T(8,128)(2,1)S(1)} %get-tuple-element.47.refs_1_.own_b), channel_id=1, source_target_pairs={{0,16},{1,17},{2,18},{3,19},{4,20},{5,21},{6,22},{7,23},{8,24},{9,... | collective-permute-start | bytes 786440 | tf_op jit(solution)/shard_map/ppermute | solution.py:136
  38.6 1.5 %collective-permute-start.20 = (bf16[4,96,256]{2,1,0:T(8,128)(2,1)S(1)}, bf16[4,96,256]{2,1,0:T(8,128)(2,1)S(1)}, u32[]{:S(2)}, u32[]{:S(2)}) collective-permute-start(bf16[4,96,256]{2,1,0:T(8,128)(2,1)S(1)} %get-tuple-element.46.refs_0_.own_a), channel_id=1, source_target_pairs={{0,8},{1,9},{2,10},{3,11},{4,12},{5,13},{6,14},{7,15},{8,0},{9,1},... | collective-permute-start | bytes 589832 | tf_op jit(solution)/shard_map/ppermute | solution.py:136
  41.8 3.8 %collective-permute-done.13.refs_6_ = bf16[4,32,256]{2,1,0:T(8,128)(2,1)S(1)} collective-permute-done((bf16[4,32,256]{2,1,0:T(8,128)(2,1)S(1)}, bf16[4,32,256]{2,1,0:T(8,128)(2,1)S(1)}, u32[]{:S(2)}, u32[]{:S(2)}) %collective-permute-start.13) | collective-permute-done | bytes 65568 | tf_op jit(solution)/shard_map/ppermute | solution.py:136
  46.7 1.4 %collective-permute-start.23 = (bf16[2,4,128,256]{3,2,1,0:T(8,128)(2,1)S(1)}, bf16[2,4,128,256]{3,2,1,0:T(8,128)(2,1)S(1)}, u32[]{:S(2)}, u32[]{:S(2)}) collective-permute-start(bf16[2,4,128,256]{3,2,1,0:T(8,128)(2,1)S(1)} %get-tuple-element.58.refs_2_), channel_id=1, source_target_pairs={{0,8},{1,9},{2,10},{3,11},{4,12},{5,13},{6,14},{7,15},{8,0},{9,1},... | collective-permute-start | bytes 1572872 | tf_op jit(solution)/shard_map/ppermute | solution.py:136
  48.1 1.3 %collective-permute-start.22 = (bf16[2,4,96,256]{3,2,1,0:T(8,128)(2,1)S(1)}, bf16[2,4,96,256]{3,2,1,0:T(8,128)(2,1)S(1)}, u32[]{:S(2)}, u32[]{:S(2)}) collective-permute-start(bf16[2,4,96,256]{3,2,1,0:T(8,128)(2,1)S(1)} %get-tuple-element.57.refs_0_), channel_id=1, source_target_pairs={{0,16},{1,17},{2,18},{3,19},{4,20},{5,21},{6,22},{7,23},{8,24},{9,... | collective-permute-start | bytes 1179656 | tf_op jit(solution)/shard_map/ppermute | solution.py:136
  49.4 2.3 %collective-permute-start.14 = (bf16[14,16,256]{2,1,0:T(8,128)(2,1)S(1)}, bf16[14,16,256]{2,1,0:T(8,128)(2,1)S(1)}, u32[]{:S(2)}, u32[]{:S(2)}) collective-permute-start(bf16[14,16,256]{2,1,0:T(8,128)(2,1)S(1)} %get-tuple-element.52), channel_id=1, source_target_pairs={{0,4},{1,5},{2,6},{3,7},{4,0},{5,1},{6,2},{7,3},{8,12},{9,13},{10,... | collective-permute-start | bytes 344072 | tf_op jit(solution)/shard_map/ppermute | solution.py:136
  53.5 1.4 %shard_map.147.moments = f32[16,128]{1,0:T(8,128)S(1)} custom-call(s32[5]{0:T(128)S(1)} %stack.23.at.after, s32[224]{0:T(256)S(1)} %copy-done.1, bf16[4,16,256]{2,1,0:T(8,128)(2,1)S(1)} %shard_map.146.mine, bf16[4,16,256]{2,1,0:T(8,128)(2,1)S(1)} %collective-permute-done.15.peer), custom_call_target="tpu_custom_call" | custom-call | tf_op jit(solution)/shard_map/pallas_call | solution.py:581
  54.9 2.2 %collective-permute-done.14.got = bf16[14,16,256]{2,1,0:T(8,128)(2,1)S(1)} collective-permute-done((bf16[14,16,256]{2,1,0:T(8,128)(2,1)S(1)}, bf16[14,16,256]{2,1,0:T(8,128)(2,1)S(1)}, u32[]{:S(2)}, u32[]{:S(2)}) %collective-permute-start.14) | collective-permute-done | bytes 114720 | tf_op jit(solution)/shard_map/ppermute | solution.py:136
  58.4 7.4 %collective-permute-done.16.refs_1_ = bf16[15,16,256]{2,1,0:T(8,128)(2,1)S(1)} collective-permute-done((bf16[15,16,256]{2,1,0:T(8,128)(2,1)S(1)}, bf16[15,16,256]{2,1,0:T(8,128)(2,1)S(1)}, u32[]{:S(2)}, u32[]{:S(2)}) %collective-permute-start.16) | collective-permute-done | bytes 122912 | tf_op jit(solution)/shard_map/ppermute | solution.py:136
  67.7 3.1 %collective-permute-done.17.refs_1_ = bf16[5,32,256]{2,1,0:T(8,128)(2,1)S(1)} collective-permute-done((bf16[5,32,256]{2,1,0:T(8,128)(2,1)S(1)}, bf16[5,32,256]{2,1,0:T(8,128)(2,1)S(1)}, u32[]{:S(2)}, u32[]{:S(2)}) %collective-permute-start.17) | collective-permute-done | bytes 81952 | tf_op jit(solution)/shard_map/ppermute | solution.py:136
  72.3 2.0 %collective-permute-start.26 = (bf16[5,64,256]{2,1,0:T(8,128)(2,1)S(1)}, bf16[5,64,256]{2,1,0:T(8,128)(2,1)S(1)}, u32[]{:S(2)}, u32[]{:S(2)}) collective-permute-start(bf16[5,64,256]{2,1,0:T(8,128)(2,1)S(1)} %get-tuple-element.59.refs_2_), channel_id=1, source_target_pairs={{0,2},{1,3},{2,0},{3,1},{4,6},{5,7},{6,4},{7,5},{8,10},{9,11},{10,... | collective-permute-start | bytes 491528 | tf_op jit(solution)/shard_map/ppermute | solution.py:136
  74.3 1.5 %collective-permute-start.27 = (bf16[5,64,256]{2,1,0:T(8,128)(2,1)S(1)}, bf16[5,64,256]{2,1,0:T(8,128)(2,1)S(1)}, u32[]{:S(2)}, u32[]{:S(2)}) collective-permute-start(bf16[5,64,256]{2,1,0:T(8,128)(2,1)S(1)} %get-tuple-element.60.refs_4_), channel_id=1, source_target_pairs={{0,8},{1,9},{2,10},{3,11},{4,12},{5,13},{6,14},{7,15},{8,0},{9,1},... | collective-permute-start | bytes 491528 | tf_op jit(solution)/shard_map/ppermute | solution.py:136
  76.5 2.6 %collective-permute-done.26.refs_3_ = bf16[5,64,256]{2,1,0:T(8,128)(2,1)S(1)} collective-permute-done((bf16[5,64,256]{2,1,0:T(8,128)(2,1)S(1)}, bf16[5,64,256]{2,1,0:T(8,128)(2,1)S(1)}, u32[]{:S(2)}, u32[]{:S(2)}) %collective-permute-start.26) | collective-permute-done | bytes 163872 | tf_op jit(solution)/shard_map/ppermute | solution.py:136
  79.1 1.5 %collective-permute-done.27.refs_5_ = bf16[5,64,256]{2,1,0:T(8,128)(2,1)S(1)} collective-permute-done((bf16[5,64,256]{2,1,0:T(8,128)(2,1)S(1)}, bf16[5,64,256]{2,1,0:T(8,128)(2,1)S(1)}, u32[]{:S(2)}, u32[]{:S(2)}) %collective-permute-start.27) | collective-permute-done | bytes 163872 | tf_op jit(solution)/shard_map/ppermute | solution.py:136
  80.5 1.2 %collective-permute-done.25.refs_1_ = bf16[5,64,256]{2,1,0:T(8,128)(2,1)S(1)} collective-permute-done((bf16[5,64,256]{2,1,0:T(8,128)(2,1)S(1)}, bf16[5,64,256]{2,1,0:T(8,128)(2,1)S(1)}, u32[]{:S(2)}, u32[]{:S(2)}) %collective-permute-start.25) | collective-permute-done | bytes 163872 | tf_op jit(solution)/shard_map/ppermute | solution.py:136
  84.9 6.2 %collective-permute-done.28.refs_1_ = bf16[5,128,256]{2,1,0:T(8,128)(2,1)S(1)} collective-permute-done((bf16[5,128,256]{2,1,0:T(8,128)(2,1)S(1)}, bf16[5,128,256]{2,1,0:T(8,128)(2,1)S(1)}, u32[]{:S(2)}, u32[]{:S(2)}) %collective-permute-start.28) | collective-permute-done | bytes 327712 | tf_op jit(solution)/shard_map/ppermute | solution.py:136
  92.6 1.7 %shard_map.157.own_part = f32[512,256]{1,0:T(8,128)S(1)} custom-call(s32[5]{0:T(128)S(1)} %stack.23.at.after, bf16[3456,256]{1,0:T(8,128)(2,1)S(1)} %shard_map.137.refs_2_.views, bf16[15,256,256]{2,1,0:T(8,128)(2,1)S(1)} %shard_map.155.scaled.mine), custom_call_target="tpu_custom_call" | custom-call | flops 939524096 | bytes 4194304 | tf_op jit(solution)/shard_map/pallas_call | solution.py:631
  94.3 2.0 %shard_map.156.old = f32[512,256]{1,0:T(8,128)S(1)} custom-call(bf16[3456,256]{1,0:T(8,128)(2,1)S(1)} %shard_map.137.refs_2_.views, bf16[7168,256]{1,0:T(8,128)(2,1)S(1)} %shard_map.153.after.natural), custom_call_target="tpu_custom_call" | custom-call | flops 1811939328 | bytes 6291456 | tf_op jit(solution)/shard_map/pallas_call | solution.py:624
  96.5 4.0 %shard_map.158 = (f32[896,256]{1,0:T(8,128)}, f32[896,256]{1,0:T(8,128)}, f32[7,128]{1,0:T(8,128)}, f32[2,256]{1,0:T(2,128)}, bf16[512,256]{1,0:T(8,128)(2,1)}) custom-call(s32[5]{0:T(128)S(1)} %stack.23.at.after, s32[224]{0:T(256)S(1)} %copy-done.1, f32[1]{0:T(128)S(6)} %sub.16.rate, f32[2,256]{1,0:T(2,128)S(1)} %copy-done.2, ...), custom_call_target="tpu_custom_call" | custom-call | flops 1073741824 | bytes 16777216 | tf_op jit(solution)/shard_map/pallas_call | solution.py:639
  (66 shorter events, 19.4 us)
Async XLA Ops:
  0.6 4.3 %collective-permute-start = (bf16[1,4,18,18,256]{4,1,3,2,0:T(4,128)(2,1)}, bf16[1,4,18,18,256]{4,1,3,2,0:T(4,128)(2,1)S(1)}, u32[]{:S(2)}, u32[]{:S(2)}) collective-permute-start(bf16[1,4,18,18,256]{4,1,3,2,0:T(4,128)(2,1)} %param.12), channel_id=1, source_target_pairs={{0,1},{1,0},{2,3},{3,2},{4,5},{5,4},{6,7},{7,6},{8,9},{9,8},{10,11... | collective-permute-start | bytes 1990664 | tf_op jit(solution)/shard_map/ppermute | solution.py:136
  1.1 3.9 %collective-permute-start.1 = (bf16[512,256]{1,0:T(8,128)(2,1)}, bf16[512,256]{1,0:T(8,128)(2,1)S(1)}, u32[]{:S(2)}, u32[]{:S(2)}) collective-permute-start(bf16[512,256]{1,0:T(8,128)(2,1)} %pre_far.1), channel_id=1, source_target_pairs={{0,1},{1,0},{2,3},{3,2},{4,5},{5,4},{6,7},{7,6},{8,9},{9,8},{10,11... | collective-permute-start | bytes 786440 | tf_op jit(solution)/shard_map/ppermute | solution.py:136
  1.2 3.9 %collective-permute-start.2 = (bf16[512,256]{1,0:T(8,128)(2,1)}, bf16[512,256]{1,0:T(8,128)(2,1)S(1)}, u32[]{:S(2)}, u32[]{:S(2)}) collective-permute-start(bf16[512,256]{1,0:T(8,128)(2,1)} %grad_far.3), channel_id=1, source_target_pairs={{0,1},{1,0},{2,3},{3,2},{4,5},{5,4},{6,7},{7,6},{8,9},{9,8},{10,11... | collective-permute-start | bytes 786440 | tf_op jit(solution)/shard_map/ppermute | solution.py:136
  9.1 12.2 %collective-permute-start.3 = (bf16[4,128,256]{2,1,0:T(8,128)(2,1)S(1)}, bf16[4,128,256]{2,1,0:T(8,128)(2,1)S(1)}, u32[]{:S(2)}, u32[]{:S(2)}) collective-permute-start(bf16[4,128,256]{2,1,0:T(8,128)(2,1)S(1)} %get-tuple-element.37), channel_id=1, source_target_pairs={{0,2},{1,3},{2,0},{3,1},{4,6},{5,7},{6,4},{7,5},{8,10},{9,11},{10,... | collective-permute-start | bytes 786440 | tf_op jit(solution)/shard_map/ppermute | solution.py:136
  11.8 12.9 %collective-permute-start.6 = (bf16[5,128,256]{2,1,0:T(8,128)(2,1)S(1)}, bf16[5,128,256]{2,1,0:T(8,128)(2,1)S(1)}, u32[]{:S(2)}, u32[]{:S(2)}) collective-permute-start(bf16[5,128,256]{2,1,0:T(8,128)(2,1)S(1)} %get-tuple-element.39), channel_id=1, source_target_pairs={{0,8},{1,9},{2,10},{3,11},{4,12},{5,13},{6,14},{7,15},{8,0},{9,1},... | collective-permute-start | bytes 983048 | tf_op jit(solution)/shard_map/ppermute | solution.py:136
  13.3 11.5 %collective-permute-start.7 = (bf16[5,128,256]{2,1,0:T(8,128)(2,1)S(1)}, bf16[5,128,256]{2,1,0:T(8,128)(2,1)S(1)}, u32[]{:S(2)}, u32[]{:S(2)}) collective-permute-start(bf16[5,128,256]{2,1,0:T(8,128)(2,1)S(1)} %get-tuple-element.40), channel_id=1, source_target_pairs={{0,16},{1,17},{2,18},{3,19},{4,20},{5,21},{6,22},{7,23},{8,24},{9,... | collective-permute-start | bytes 983048 | tf_op jit(solution)/shard_map/ppermute | solution.py:136
  16.4 5.0 %collective-permute-start.4 = (bf16[15,16,256]{2,1,0:T(8,128)(2,1)S(1)}, bf16[15,16,256]{2,1,0:T(8,128)(2,1)S(1)}, u32[]{:S(2)}, u32[]{:S(2)}) collective-permute-start(bf16[15,16,256]{2,1,0:T(8,128)(2,1)S(1)} %shard_map.140.own), channel_id=1, source_target_pairs={{0,2},{1,3},{2,0},{3,1},{4,6},{5,7},{6,4},{7,5},{8,10},{9,11},{10,... | collective-permute-start | bytes 368648 | tf_op jit(solution)/shard_map/ppermute | solution.py:136
  21.9 13.7 %collective-permute-start.5 = (bf16[2,15,16,256]{3,2,1,0:T(8,128)(2,1)S(1)}, bf16[2,15,16,256]{3,2,1,0:T(8,128)(2,1)S(1)}, u32[]{:S(2)}, u32[]{:S(2)}) collective-permute-start(bf16[2,15,16,256]{3,2,1,0:T(8,128)(2,1)S(1)} %shard_map.141.own), channel_id=1, source_target_pairs={{0,4},{1,5},{2,6},{3,7},{4,0},{5,1},{6,2},{7,3},{8,12},{9,13},{10,... | collective-permute-start | bytes 737288 | tf_op jit(solution)/shard_map/ppermute | solution.py:136
  25.4 8.1 %collective-permute-start.8 = (bf16[5,64,256]{2,1,0:T(8,128)(2,1)S(1)}, bf16[5,64,256]{2,1,0:T(8,128)(2,1)S(1)}, u32[]{:S(2)}, u32[]{:S(2)}) collective-permute-start(bf16[5,64,256]{2,1,0:T(8,128)(2,1)S(1)} %get-tuple-element.42), channel_id=1, source_target_pairs={{0,16},{1,17},{2,18},{3,19},{4,20},{5,21},{6,22},{7,23},{8,24},{9,... | collective-permute-start | bytes 491528 | tf_op jit(solution)/shard_map/ppermute | solution.py:136
  27.0 8.7 %collective-permute-start.9 = (bf16[5,64,256]{2,1,0:T(8,128)(2,1)S(1)}, bf16[5,64,256]{2,1,0:T(8,128)(2,1)S(1)}, u32[]{:S(2)}, u32[]{:S(2)}) collective-permute-start(bf16[5,64,256]{2,1,0:T(8,128)(2,1)S(1)} %get-tuple-element.43), channel_id=1, source_target_pairs={{0,2},{1,3},{2,0},{3,1},{4,6},{5,7},{6,4},{7,5},{8,10},{9,11},{10,... | collective-permute-start | bytes 491528 | tf_op jit(solution)/shard_map/ppermute | solution.py:136
  28.6 5.0 %collective-permute-start.10 = (bf16[4,64,256]{2,1,0:T(8,128)(2,1)S(1)}, bf16[4,64,256]{2,1,0:T(8,128)(2,1)S(1)}, u32[]{:S(2)}, u32[]{:S(2)}) collective-permute-start(bf16[4,64,256]{2,1,0:T(8,128)(2,1)S(1)} %get-tuple-element.44), channel_id=1, source_target_pairs={{0,8},{1,9},{2,10},{3,11},{4,12},{5,13},{6,14},{7,15},{8,0},{9,1},... | collective-permute-start | bytes 393224 | tf_op jit(solution)/shard_map/ppermute | solution.py:136
  36.9 9.8 %collective-permute-start.21 = (bf16[4,128,256]{2,1,0:T(8,128)(2,1)S(1)}, bf16[4,128,256]{2,1,0:T(8,128)(2,1)S(1)}, u32[]{:S(2)}, u32[]{:S(2)}) collective-permute-start(bf16[4,128,256]{2,1,0:T(8,128)(2,1)S(1)} %get-tuple-element.47.refs_1_.own_b), channel_id=1, source_target_pairs={{0,16},{1,17},{2,18},{3,19},{4,20},{5,21},{6,22},{7,23},{8,24},{9,... | collective-permute-start | bytes 786440 | tf_op jit(solution)/shard_map/ppermute | solution.py:136
  38.6 8.0 %collective-permute-start.20 = (bf16[4,96,256]{2,1,0:T(8,128)(2,1)S(1)}, bf16[4,96,256]{2,1,0:T(8,128)(2,1)S(1)}, u32[]{:S(2)}, u32[]{:S(2)}) collective-permute-start(bf16[4,96,256]{2,1,0:T(8,128)(2,1)S(1)} %get-tuple-element.46.refs_0_.own_a), channel_id=1, source_target_pairs={{0,8},{1,9},{2,10},{3,11},{4,12},{5,13},{6,14},{7,15},{8,0},{9,1},... | collective-permute-start | bytes 589832 | tf_op jit(solution)/shard_map/ppermute | solution.py:136
  40.1 5.5 %collective-permute-start.11 = (bf16[5,32,256]{2,1,0:T(8,128)(2,1)S(1)}, bf16[5,32,256]{2,1,0:T(8,128)(2,1)S(1)}, u32[]{:S(2)}, u32[]{:S(2)}) collective-permute-start(bf16[5,32,256]{2,1,0:T(8,128)(2,1)S(1)} %get-tuple-element.48), channel_id=1, source_target_pairs={{0,2},{1,3},{2,0},{3,1},{4,6},{5,7},{6,4},{7,5},{8,10},{9,11},{10,... | collective-permute-start | bytes 245768 | tf_op jit(solution)/shard_map/ppermute | solution.py:136
  40.8 5.3 %collective-permute-start.12 = (bf16[5,32,256]{2,1,0:T(8,128)(2,1)S(1)}, bf16[5,32,256]{2,1,0:T(8,128)(2,1)S(1)}, u32[]{:S(2)}, u32[]{:S(2)}) collective-permute-start(bf16[5,32,256]{2,1,0:T(8,128)(2,1)S(1)} %get-tuple-element.49), channel_id=1, source_target_pairs={{0,8},{1,9},{2,10},{3,11},{4,12},{5,13},{6,14},{7,15},{8,0},{9,1},... | collective-permute-start | bytes 245768 | tf_op jit(solution)/shard_map/ppermute | solution.py:136
  41.3 4.3 %collective-permute-start.13 = (bf16[4,32,256]{2,1,0:T(8,128)(2,1)S(1)}, bf16[4,32,256]{2,1,0:T(8,128)(2,1)S(1)}, u32[]{:S(2)}, u32[]{:S(2)}) collective-permute-start(bf16[4,32,256]{2,1,0:T(8,128)(2,1)S(1)} %get-tuple-element.50), channel_id=1, source_target_pairs={{0,16},{1,17},{2,18},{3,19},{4,20},{5,21},{6,22},{7,23},{8,24},{9,... | collective-permute-start | bytes 196616 | tf_op jit(solution)/shard_map/ppermute | solution.py:136
  46.7 25.3 %collective-permute-start.23 = (bf16[2,4,128,256]{3,2,1,0:T(8,128)(2,1)S(1)}, bf16[2,4,128,256]{3,2,1,0:T(8,128)(2,1)S(1)}, u32[]{:S(2)}, u32[]{:S(2)}) collective-permute-start(bf16[2,4,128,256]{3,2,1,0:T(8,128)(2,1)S(1)} %get-tuple-element.58.refs_2_), channel_id=1, source_target_pairs={{0,8},{1,9},{2,10},{3,11},{4,12},{5,13},{6,14},{7,15},{8,0},{9,1},... | collective-permute-start | bytes 1572872 | tf_op jit(solution)/shard_map/ppermute | solution.py:136
  48.1 23.9 %collective-permute-start.22 = (bf16[2,4,96,256]{3,2,1,0:T(8,128)(2,1)S(1)}, bf16[2,4,96,256]{3,2,1,0:T(8,128)(2,1)S(1)}, u32[]{:S(2)}, u32[]{:S(2)}) collective-permute-start(bf16[2,4,96,256]{3,2,1,0:T(8,128)(2,1)S(1)} %get-tuple-element.57.refs_0_), channel_id=1, source_target_pairs={{0,16},{1,17},{2,18},{3,19},{4,20},{5,21},{6,22},{7,23},{8,24},{9,... | collective-permute-start | bytes 1179656 | tf_op jit(solution)/shard_map/ppermute | solution.py:136
  49.4 7.7 %collective-permute-start.14 = (bf16[14,16,256]{2,1,0:T(8,128)(2,1)S(1)}, bf16[14,16,256]{2,1,0:T(8,128)(2,1)S(1)}, u32[]{:S(2)}, u32[]{:S(2)}) collective-permute-start(bf16[14,16,256]{2,1,0:T(8,128)(2,1)S(1)} %get-tuple-element.52), channel_id=1, source_target_pairs={{0,4},{1,5},{2,6},{3,7},{4,0},{5,1},{6,2},{7,3},{8,12},{9,13},{10,... | collective-permute-start | bytes 344072 | tf_op jit(solution)/shard_map/ppermute | solution.py:136
  52.3 1.3 %collective-permute-start.15 = (bf16[4,16,256]{2,1,0:T(8,128)(2,1)S(1)}, bf16[4,16,256]{2,1,0:T(8,128)(2,1)S(1)}, u32[]{:S(2)}, u32[]{:S(2)}) collective-permute-start(bf16[4,16,256]{2,1,0:T(8,128)(2,1)S(1)} %shard_map.146.mine), channel_id=1, source_target_pairs={{0,1},{1,0},{2,3},{3,2},{4,5},{5,4},{6,7},{7,6},{8,9},{9,8},{10,11... | collective-permute-start | bytes 98312 | tf_op jit(solution)/shard_map/ppermute | solution.py:136
  58.0 7.8 %collective-permute-start.16 = (bf16[15,16,256]{2,1,0:T(8,128)(2,1)S(1)}, bf16[15,16,256]{2,1,0:T(8,128)(2,1)S(1)}, u32[]{:S(2)}, u32[]{:S(2)}) collective-permute-start(bf16[15,16,256]{2,1,0:T(8,128)(2,1)S(1)} %shard_map.148.refs_0_), channel_id=1, source_target_pairs={{0,4},{1,5},{2,6},{3,7},{4,0},{5,1},{6,2},{7,3},{8,12},{9,13},{10,... | collective-permute-start | bytes 368648 | tf_op jit(solution)/shard_map/ppermute | solution.py:136
  66.3 4.5 %collective-permute-start.17 = (bf16[5,32,256]{2,1,0:T(8,128)(2,1)S(1)}, bf16[5,32,256]{2,1,0:T(8,128)(2,1)S(1)}, u32[]{:S(2)}, u32[]{:S(2)}) collective-permute-start(bf16[5,32,256]{2,1,0:T(8,128)(2,1)S(1)} %get-tuple-element.53.refs_0_), channel_id=1, source_target_pairs={{0,2},{1,3},{2,0},{3,1},{4,6},{5,7},{6,4},{7,5},{8,10},{9,11},{10,... | collective-permute-start | bytes 245768 | tf_op jit(solution)/shard_map/ppermute | solution.py:136
  66.4 4.5 %collective-permute-start.18 = (bf16[5,32,256]{2,1,0:T(8,128)(2,1)S(1)}, bf16[5,32,256]{2,1,0:T(8,128)(2,1)S(1)}, u32[]{:S(2)}, u32[]{:S(2)}) collective-permute-start(bf16[5,32,256]{2,1,0:T(8,128)(2,1)S(1)} %get-tuple-element.54.refs_2_), channel_id=1, source_target_pairs={{0,8},{1,9},{2,10},{3,11},{4,12},{5,13},{6,14},{7,15},{8,0},{9,1},... | collective-permute-start | bytes 245768 | tf_op jit(solution)/shard_map/ppermute | solution.py:136
  67.0 4.4 %collective-permute-start.19 = (bf16[5,32,256]{2,1,0:T(8,128)(2,1)S(1)}, bf16[5,32,256]{2,1,0:T(8,128)(2,1)S(1)}, u32[]{:S(2)}, u32[]{:S(2)}) collective-permute-start(bf16[5,32,256]{2,1,0:T(8,128)(2,1)S(1)} %get-tuple-element.55.refs_4_), channel_id=1, source_target_pairs={{0,16},{1,17},{2,18},{3,19},{4,20},{5,21},{6,22},{7,23},{8,24},{9,... | collective-permute-start | bytes 245768 | tf_op jit(solution)/shard_map/ppermute | solution.py:136
  72.2 11.8 %collective-permute-start.24 = (bf16[2,2,4,224,256]{4,3,2,1,0:T(8,128)(2,1)S(1)}, bf16[2,2,4,224,256]{4,3,2,1,0:T(8,128)(2,1)S(1)}, u32[]{:S(2)}, u32[]{:S(2)}) collective-permute-start(bf16[2,2,4,224,256]{4,3,2,1,0:T(8,128)(2,1)S(1)} %shard_map.152.mine), channel_id=1, source_target_pairs={{0,1},{1,0},{2,3},{3,2},{4,5},{5,4},{6,7},{7,6},{8,9},{9,8},{10,11... | collective-permute-start | bytes 5505032 | tf_op jit(solution)/shard_map/ppermute | solution.py:136
  72.3 6.8 %collective-permute-start.26 = (bf16[5,64,256]{2,1,0:T(8,128)(2,1)S(1)}, bf16[5,64,256]{2,1,0:T(8,128)(2,1)S(1)}, u32[]{:S(2)}, u32[]{:S(2)}) collective-permute-start(bf16[5,64,256]{2,1,0:T(8,128)(2,1)S(1)} %get-tuple-element.59.refs_2_), channel_id=1, source_target_pairs={{0,2},{1,3},{2,0},{3,1},{4,6},{5,7},{6,4},{7,5},{8,10},{9,11},{10,... | collective-permute-start | bytes 491528 | tf_op jit(solution)/shard_map/ppermute | solution.py:136
  74.3 6.3 %collective-permute-start.27 = (bf16[5,64,256]{2,1,0:T(8,128)(2,1)S(1)}, bf16[5,64,256]{2,1,0:T(8,128)(2,1)S(1)}, u32[]{:S(2)}, u32[]{:S(2)}) collective-permute-start(bf16[5,64,256]{2,1,0:T(8,128)(2,1)S(1)} %get-tuple-element.60.refs_4_), channel_id=1, source_target_pairs={{0,8},{1,9},{2,10},{3,11},{4,12},{5,13},{6,14},{7,15},{8,0},{9,1},... | collective-permute-start | bytes 491528 | tf_op jit(solution)/shard_map/ppermute | solution.py:136
  75.8 6.0 %collective-permute-start.25 = (bf16[5,64,256]{2,1,0:T(8,128)(2,1)S(1)}, bf16[5,64,256]{2,1,0:T(8,128)(2,1)S(1)}, u32[]{:S(2)}, u32[]{:S(2)}) collective-permute-start(bf16[5,64,256]{2,1,0:T(8,128)(2,1)S(1)} %get-tuple-element.56.after.refs_0_), channel_id=1, source_target_pairs={{0,16},{1,17},{2,18},{3,19},{4,20},{5,21},{6,22},{7,23},{8,24},{9,... | collective-permute-start | bytes 491528 | tf_op jit(solution)/shard_map/ppermute | solution.py:136
  82.4 8.7 %collective-permute-start.28 = (bf16[5,128,256]{2,1,0:T(8,128)(2,1)S(1)}, bf16[5,128,256]{2,1,0:T(8,128)(2,1)S(1)}, u32[]{:S(2)}, u32[]{:S(2)}) collective-permute-start(bf16[5,128,256]{2,1,0:T(8,128)(2,1)S(1)} %get-tuple-element.61.refs_0_), channel_id=1, source_target_pairs={{0,8},{1,9},{2,10},{3,11},{4,12},{5,13},{6,14},{7,15},{8,0},{9,1},... | collective-permute-start | bytes 983048 | tf_op jit(solution)/shard_map/ppermute | solution.py:136
  83.0 8.4 %collective-permute-start.29 = (bf16[5,128,256]{2,1,0:T(8,128)(2,1)S(1)}, bf16[5,128,256]{2,1,0:T(8,128)(2,1)S(1)}, u32[]{:S(2)}, u32[]{:S(2)}) collective-permute-start(bf16[5,128,256]{2,1,0:T(8,128)(2,1)S(1)} %get-tuple-element.62.refs_2_), channel_id=1, source_target_pairs={{0,16},{1,17},{2,18},{3,19},{4,20},{5,21},{6,22},{7,23},{8,24},{9,... | collective-permute-start | bytes 983048 | tf_op jit(solution)/shard_map/ppermute | solution.py:136
  83.7 8.2 %collective-permute-start.30 = (bf16[5,128,256]{2,1,0:T(8,128)(2,1)S(1)}, bf16[5,128,256]{2,1,0:T(8,128)(2,1)S(1)}, u32[]{:S(2)}, u32[]{:S(2)}) collective-permute-start(bf16[5,128,256]{2,1,0:T(8,128)(2,1)S(1)} %get-tuple-element.63.refs_4_), channel_id=1, source_target_pairs={{0,2},{1,3},{2,0},{3,1},{4,6},{5,7},{6,4},{7,5},{8,10},{9,11},{10,... | collective-permute-start | bytes 983048 | tf_op jit(solution)/shard_map/ppermute | solution.py:136
  92.5 4.0 %collective-permute-start.31 = (bf16[15,256,256]{2,1,0:T(8,128)(2,1)S(1)}, bf16[15,256,256]{2,1,0:T(8,128)(2,1)S(1)}, u32[]{:S(2)}, u32[]{:S(2)}) collective-permute-start(bf16[15,256,256]{2,1,0:T(8,128)(2,1)S(1)} %shard_map.155.scaled.mine), channel_id=1, source_target_pairs={{0,1},{1,0},{2,3},{3,2},{4,5},{5,4},{6,7},{7,6},{8,9},{9,8},{10,11... | collective-permute-start | bytes 5898248 | tf_op jit(solution)/shard_map/ppermute | solution.py:136
  (4 other events, 35.7 us)

commit v5 on v4

--- a/solution.py
+++ b/solution.py
@@ -128,12 +128,34 @@
 SMEM = pl.BlockSpec(memory_space=pltpu.SMEM)
 HBM = pl.BlockSpec(memory_space=pl.ANY)
 MASK_CORE, MASK_NEAR, MASK_FAR, MASK_X, MASK_Y = 1, 2, 4, 8, 16
-PARTS = ((0, 5, (0, 1, 2)), (5, 5, (1, 2, 0)), (10, 4, (2, 0, 1)))
+PARTS = ((0, 9), (9, 5))
+ORDERS = (((0, 1, 2), (1, 2, 0)), ((2, 0, 1), (2, 0, 1)))
+MESSAGE = 9
+GATHERED = ((0, 10), (10, 5))
 MASKS = (MASK_X, MASK_Y, MASK_NEAR)
 
 
 def swap(value, mask):
     return lax.ppermute(value, AXES, [(at, at ^ mask) for at in range(32)])
+
+
+def swap_mixed(value, masks):
+    return lax.ppermute(value, AXES, [(at, at ^ masks[at & 1]) for at in range(32)])
+
+
+def swap_part(value, part, step):
+    return swap_mixed(value, [MASKS[ORDERS[part][core][step]] for core in range(2)])
+
+
+def place_of(at, part, step):
+    if step == 3:
+        return at[3]
+    zero, one = (ORDERS[part][core][step] for core in range(2))
+    return at[zero] if zero == one else jnp.where(at[4] == 0, at[zero], at[one])
+
+
+def gathered_at(slot):
+    return slot + (slot >= MESSAGE) * 1
 
 
 def call(kernel, outs, in_specs, scratch=(), flops=0, moved=0, room=8, pin=True):
@@ -208,7 +230,7 @@
 
 def term_kernel(
     at, own, tile_peer, pre_peer, grad_peer, grad_far, pointwise_far,
-    keep, send_one, send_two, send_three, peer, rights, pointwise, arrived,
+    keep, send_one, send_two, peer, rights, pointwise, arrived,
 ):
     core = at[4]
     copies = fetch(((grad_far, rights.at[1, pl.ds(0, PIX), :]), (pointwise_far, pointwise)), arrived)
@@ -232,19 +254,21 @@
                 pieces.append(ref[pl.ds(pl.multiple_of(start, HW), HW * HW), :])
         right = rights[core] if slot == SLOTS - 1 else rights[0]
         total = contract_rows(jnp.concatenate(pieces, axis=0), right)
-        for (first, count, order), send in zip(PARTS, (send_one, send_two, send_three)):
+        for part, ((first, count), send) in enumerate(zip(PARTS, (send_one, send_two))):
             if first <= slot < first + count:
-                low, high, at_low = total[:128], total[128:], at[order[0]] == 0
+                low, high, at_low = total[:128], total[128:], place_of(at, part, 0) == 0
                 keep[slot] = jnp.where(at_low, low, high).astype(LOW)
                 send[slot - first] = jnp.where(at_low, high, low).astype(LOW)
 
 
-def fold_kernel(step, skip, at, *refs):
+def fold_kernel(step, at, *refs):
     size = 256 >> (step + 1)
-    refs = refs[skip:]
-    keep, gots, stay, sends = refs[0], refs[1:4], refs[4], refs[5:]
-    for part, (first, count, order) in enumerate(PARTS):
-        mine = at[order[step] if step < 3 else 3]
+    extra = 0 if step == 2 else 2
+    own, got = refs[:extra] or (None, None)
+    refs = refs[extra:]
+    keep, gots, stay, sends = refs[0], refs[1:3], refs[3], refs[4:]
+    for part, (first, count) in enumerate(PARTS):
+        mine = place_of(at, part, step)
         here = slice(first, first + count)
         for which, out in ((mine, 0), (1 - mine, 1)):
             rows = pl.ds(pl.multiple_of(which * size, size), size)
@@ -255,16 +279,29 @@
                 sends[part][...] = value
             else:
                 sends[0][here] = value
-
-
-def moment_kernel(at, rate, own, got, moments, scaled):
+    if step == 1:
+        pair = sends[2]
+        pair[at[2]] = own[...]
+        pair[1 - at[2]] = got[...]
+    if step == 3:
+        line, moments = sends[1:]
+        for which, piece in ((at[3], own), (1 - at[3], got)):
+            for near in range(2):
+                line[which * 2 + near] = piece[near, :SLOTS].reshape(SLOTS * 16, CO)
+                moments[which * 2 + near] = piece[near, SLOTS]
+
+
+def moment_kernel(at, rate, own, got, moments, line, line_got, scaled, plane):
+    plane[0], plane[1] = line[...], line_got[...]
     total = (own[...].astype(WIDE) + got[...].astype(WIDE)).reshape(SLOTS * 16, CO)
     squares = total * total
     decay = rate[0]
     mean = jnp.sum(squares, axis=1, keepdims=True) * (1.0 / CO)
     row_moment = jnp.concatenate([moments[:, slot : slot + 1] for slot in range(SLOTS)], axis=0)
     new_row = decay * row_moment + (1.0 - decay) * mean
-    scaled[:SLOTS] = (total * lax.rsqrt(new_row)).astype(LOW).reshape(SLOTS, 16, CO)
+    value = (total * lax.rsqrt(new_row)).astype(LOW).reshape(SLOTS, 16, CO)
+    scaled[:MESSAGE] = value[:MESSAGE]
+    scaled[MESSAGE + 1 :] = value[MESSAGE:]
     weighted = squares / new_row
     cut = (SLOTS - 1) * 16
     last_small = at[4] == 1
@@ -280,7 +317,7 @@
     rows.append(jnp.zeros((1, CO), WIDE))
     message = jnp.concatenate(rows, axis=0)
     high = message.astype(LOW).astype(WIDE)
-    scaled[SLOTS] = jnp.concatenate([high, message - high], axis=0).astype(LOW)
+    scaled[MESSAGE] = jnp.concatenate([high, message - high], axis=0).astype(LOW)
 
 
 def store_factors(total, decay, col_moment, new_col, factor):
@@ -298,25 +335,6 @@
         factor[kernel : kernel + 1] = 1.0 / (jnp.sqrt(col / row_mean) * clip)
 
 
-def stack_kernel(at, after, own, got, out):
-    out[at[2]] = own[...]
-    out[1 - at[2]] = got[...]
-
-
-def line_kernel(at, after, own, got, out_a, out_b):
-    for which, piece in ((at[3], own), (1 - at[3], got)):
-        for near in range(2):
-            rows = piece[near, :SLOTS].reshape(SLOTS * 16, CO)
-            out_a[which * 2 + near] = rows[: 3 * BLK]
-            out_b[which * 2 + near] = rows[3 * BLK :]
-
-
-def gather_moments_kernel(at, own, got, out):
-    for which, piece in ((at[3], own), (1 - at[3], got)):
-        for near in range(2):
-            out[which * 2 + near] = piece[near, SLOTS]
-
-
 def moments_kernel(at, block_order, mine, peer, out, table, rows, inverse):
     core = at[4]
     for side, ref in enumerate((mine, peer)):
@@ -331,8 +349,8 @@
 
     lax.fori_loop(0, NB, invert, 0, unroll=8)
     rows[...] = jnp.zeros((128, 128), WIDE)
-    for first, count, order in PARTS:
-        place = at[order[0]] * 4 + at[order[1]] * 2 + at[order[2]]
+    for part, (first, count) in enumerate(PARTS):
+        place = place_of(at, part, 0) * 4 + place_of(at, part, 1) * 2 + place_of(at, part, 2)
         for slot in range(first, first + count):
             stored = inverse[(core * SLOTS + slot) * 8 + place]
             owner, local = stored // (NB // 8), lax.rem(stored, NB // 8)
@@ -342,53 +360,33 @@
     out[...] = jnp.transpose(rows[...])[:16]
 
 
-def double_kernel(after, own_a, got_a, own_b, got_b, out_a, out_b):
-    out_a[0], out_a[1] = own_a[...], got_a[...]
-    out_b[0], out_b[1] = own_b[...], got_b[...]
-
-
-def merge_kernel(after, *refs):
-    pieces, out = refs[:-1], refs[-1]
-    first = 0
-    for kind, piece in enumerate(pieces):
-        count = piece.shape[2]
-        out[kind % 2, :, :, first : first + count] = piece[...]
-        first += count * (kind % 2)
-
-
-def order_kernel(at, block_order, mine, peer, out):
+def order_kernel(at, block_order, mine, mine_got, peer, peer_got, out):
     count = NB // 8
     quarters = count // 4
-    for flip_core, piece in enumerate((mine, peer)):
+    for flip_core, pieces in enumerate(((mine, mine_got), (peer, peer_got))):
         core = at[4] ^ flip_core
-        for kind in range(2):
-            for away in range(2):
+        for second, piece in enumerate(pieces):
+            for first in range(2):
+                flip_x = jnp.where(core == 0, first, second)
+                quarter = (at[1] ^ first ^ second ^ flip_x) * 2 + (at[0] ^ flip_x)
                 for local in range(quarters):
-                    in_a = local < 3
-                    flip_x, flip_y = (away, kind) if in_a else (kind, away)
-                    quarter = (at[1] ^ flip_y) * 2 + (at[0] ^ flip_x)
                     for line in range(4):
                         block = block_order[(line * 2 + core) * count + quarter * quarters + local]
                         to = pl.ds(pl.multiple_of(block * BLK, BLK), BLK)
-                        out[to, :] = piece[kind, away, line, local * BLK : local * BLK + BLK]
+                        out[to, :] = piece[first, line, local * BLK : local * BLK + BLK]
 
 
 def widen_kernel(step, at, after, *refs):
     size = 256 >> (step + 1)
-    if step == 3:
-        (own, got), outs = refs[:2], refs[2:]
-    else:
-        ins, outs = refs[:6], refs[6:]
-    for part, (first, _, order) in enumerate(PARTS):
-        mine = at[order[step] if step < 3 else 3]
+    ins, outs = (refs[:2], refs[2:]) if step == 3 else (refs[:4], refs[4:])
+    for part, (first, count) in enumerate(GATHERED):
+        mine = place_of(at, part, step)
+        here = slice(first, first + count)
         for index, which in enumerate((mine, 1 - mine)):
             rows = pl.ds(pl.multiple_of(which * size, size), size)
-            if step == 3:
-                value = (own, got)[index][first : first + 5]
-            else:
-                value = ins[2 * part + index][...]
+            value = ins[index][here] if step == 3 else ins[2 * part + index][...]
             if step == 0:
-                outs[0][first : first + 5, rows] = value
+                outs[0][here, rows] = value
             else:
                 outs[part][:, rows] = value
 
@@ -414,7 +412,7 @@
     total = jnp.zeros((PIX, CO), WIDE)
     for slot in range(SLOTS):
         tap = jnp.minimum(core * SLOTS + slot, 26)
-        weights = scaled[slot]
+        weights = scaled[gathered_at(slot)]
         if slot == SLOTS - 1:
             weights = jnp.where(core == 0, weights.astype(WIDE), 0.0).astype(LOW)
         total = total + jnp.dot(window(views, tap), weights, preferred_element_type=WIDE)
@@ -432,7 +430,7 @@
     core = at[4]
     total = jnp.zeros((8, CO), WIDE)
     for side, piece in enumerate((mine, peer)):
-        message = piece[SLOTS].astype(WIDE).reshape(16, 2, 8, CO)
+        message = piece[MESSAGE].astype(WIDE).reshape(16, 2, 8, CO)
         message = message[:, 0] + message[:, 1]
         total = total + jnp.sum(message, axis=0)
         for index in range(16):
@@ -442,7 +440,7 @@
     store_factors(total, rate[0], col_moment, new_col, factor)
     change = own_part[...] + add_taps(views, peer, 1 - core)
     hidden = old[...] - (learn_rate * factor[0:1]) * change
-    small = jnp.where(core == 1, mine[SLOTS - 1].astype(WIDE), peer[SLOTS - 1].astype(WIDE))
+    small = jnp.where(core == 1, mine[SLOTS].astype(WIDE), peer[SLOTS].astype(WIDE))
     weights = natural[27 * CI :].astype(WIDE) - small * (learn_rate * factor[1:2])
     next_output[...] = jnp.dot(
         jax.nn.silu(hidden).astype(LOW), weights.astype(LOW), preferred_element_type=WIDE
@@ -457,17 +455,15 @@
             block = block_order[owner * (NB // 8) + local]
             side = (block // (8 * SLOTS)) ^ core
             slot, place = lax.rem(block // 8, SLOTS), lax.rem(block, 8)
-            one, two, three = place // 4, lax.rem(place // 2, 2), lax.rem(place, 2)
-            sender = jnp.where(
-                slot < 5,
-                three * 8 + one * 4 + two * 2,
-                jnp.where(slot < 10, two * 8 + three * 4 + one * 2, place * 2),
-            )
+            near, x, y = place // 4, lax.rem(place // 2, 2), lax.rem(place, 2)
+            other = jnp.where(side == core, x * 8 + y * 4 + near * 2, y * 8 + near * 4 + x * 2)
+            sender = jnp.where(slot < MESSAGE, place * 2, other)
+            index = gathered_at(slot)
             chosen = jnp.where(block >= NB3, factor[1:2], factor[0:1])
             rows = slice(local * BLK, local * BLK + BLK)
             there = pl.ds(pl.multiple_of(place * BLK, BLK), BLK)
             value = jnp.where(
-                side == 0, mine[slot, there, :].astype(WIDE), peer[slot, there, :].astype(WIDE)
+                side == 0, mine[index, there, :].astype(WIDE), peer[index, there, :].astype(WIDE)
             )
             update = value * chosen
             update_rows[rows, :] = update
@@ -518,7 +514,7 @@
 
     keep, *sends = call(
         term_kernel,
-        [((SLOTS, 128, CO), LOW)] + [((count, 128, CO), LOW) for _, count, _ in PARTS],
+        [((SLOTS, 128, CO), LOW)] + [((count, 128, CO), LOW) for _, count in PARTS],
         [SMEM] + [VMEM] * 4 + [HBM] * 2,
         scratch=[
             pltpu.VMEM((BROUGHT, CI), LOW),
@@ -545,39 +541,28 @@
     views = call(shift_kernel, [((3 * SHIFTED, CI), LOW)], [VMEM], moved=3 << 20)(next_tiles[0])[0]
 
     for step in range(1, 4):
-        gots = [
-            swap(send, MASKS[order[step - 1]]) for send, (_, _, order) in zip(sends, PARTS)
-        ]
+        gots = [swap_part(send, part, step - 1) for part, send in enumerate(sends)]
+        size = 256 >> (step + 1)
+        outs = [((SLOTS, size, CO), LOW)] + [((count, size, CO), LOW) for _, count in PARTS]
         if step == 1:
-            pair = call(
-                stack_kernel,
-                [((2, SLOTS + 1, 16, CO), LOW)],
-                [SMEM, HBM] + [VMEM] * 2,
-                moved=1 << 20,
-            )(at, gots[2], packed, packed_near)[0]
+            extra = [packed, packed_near]
+            outs = outs + [((2, SLOTS + 1, 16, CO), LOW)]
+        elif step == 2:
+            extra = []
+        else:
+            extra = [pair, pair_far]
+            outs = outs[:1] * 2 + [((4, SLOTS * 16, CO), LOW), ((4, 16, CO), LOW)]
+        keep, *sends = call(
+            functools.partial(fold_kernel, step),
+            outs,
+            [SMEM] + [VMEM] * (len(extra) + 3),
+            moved=1 << 20,
+        )(at, *extra, keep, *gots)
+        if step == 1:
+            pair = sends.pop()
             pair_far = swap(pair, MASK_FAR)
-        size = 256 >> (step + 1)
-        outs = [((SLOTS, size, CO), LOW)] + [((count, size, CO), LOW) for _, count, _ in PARTS]
-        if step == 3:
-            outs = outs[:1] * 2
-        after = ([], [pair_far], [line_a, line_b, views] if step == 3 else [])[step - 1]
-        keep, *sends = call(
-            functools.partial(fold_kernel, step, len(after)),
-            outs,
-            [SMEM] + [HBM] * len(after) + [VMEM] * 4,
-            moved=1 << 20,
-        )(at, *after, keep, *gots)
-        if step == 2:
-            line_a, line_b = call(
-                line_kernel,
-                [((4, 3 * BLK, CO), LOW), ((4, 4 * BLK, CO), LOW)],
-                [SMEM, HBM] + [VMEM] * 2,
-                moved=1 << 20,
-            )(at, keep, pair, pair_far)
-    line_got_a, line_got_b = swap(line_a, MASK_X), swap(line_b, MASK_Y)
-    moments = call(gather_moments_kernel, [((4, 16, CO), LOW)], [SMEM] + [VMEM] * 2)(
-        at, pair, pair_far
-    )[0]
+    _, line, moments = sends
+    line_got = swap_mixed(line, (MASK_X, MASK_Y))
     own_moment = call(
         moments_kernel,
         [((16, 128), WIDE)],
@@ -588,37 +573,31 @@
             pltpu.SMEM((NB,), jnp.int32),
         ],
     )(at, block_order, moments, swap(moments, MASK_CORE))[0]
-    scaled = call(moment_kernel, [((SLOTS + 1, 16, CO), LOW)], [SMEM] * 2 + [VMEM] * 3)(
-        at, decay_rate, keep, swap(sends[0], MASK_FAR), own_moment
-    )[0]
-    plane_a, plane_b = call(
-        double_kernel,
-        [((2, 4, 3 * BLK, CO), LOW), ((2, 4, 4 * BLK, CO), LOW)],
-        [HBM] + [VMEM] * 4,
+    scaled, plane = call(
+        moment_kernel,
+        [((SLOTS + 1, 16, CO), LOW), ((2, 4, SLOTS * 16, CO), LOW)],
+        [SMEM] * 2 + [VMEM] * 5,
         moved=2 << 20,
-    )(keep, line_a, line_got_a, line_b, line_got_b)
-    planes = [plane_a, swap(plane_a, MASK_Y), plane_b, swap(plane_b, MASK_X)]
+    )(at, decay_rate, keep, swap(sends[0], MASK_FAR), own_moment, line, line_got)
+    plane_got = swap_mixed(plane, (MASK_Y, MASK_X))
+    natural = call(
+        order_kernel, [((NB * BLK, CO), LOW)], [SMEM] * 2 + [VMEM] * 4, moved=8 << 20
+    )(at, block_order, plane, plane_got, swap(plane, MASK_CORE), swap(plane_got, MASK_CORE))[0]
 
     pieces = [scaled, swap(scaled, MASK_FAR)]
-    after = at
     for step in range(3, -1, -1):
+        after = (natural, at, plane_got, views)[step]
         size = 256 >> step
-        outs = [((5, size, CO), LOW)] * 3 if step > 0 else [((SLOTS + 1, size, CO), LOW)]
+        outs = [((count, size, CO), LOW) for _, count in GATHERED]
+        if step == 0:
+            outs = [((SLOTS + 1, size, CO), LOW)]
         joined = call(
             functools.partial(widen_kernel, step), outs, [SMEM, HBM] + [VMEM] * len(pieces)
         )(at, after, *pieces)
-        if step == 2:
-            merged = call(
-                merge_kernel, [((2, 2, 4, 7 * BLK, CO), LOW)], [HBM] + [VMEM] * 4, moved=4 << 20
-            )(joined[0], *planes)[0]
-            natural = call(
-                order_kernel, [((NB * BLK, CO), LOW)], [SMEM] * 2 + [VMEM] * 2, moved=8 << 20
-            )(at, block_order, merged, swap(merged, MASK_CORE))[0]
-        after = natural if step == 1 else at
         if step > 0:
             pieces = []
-            for part, (_, _, order) in enumerate(PARTS):
-                pieces += [joined[part], swap(joined[part], MASKS[order[step - 1]])]
+            for part, value in enumerate(joined):
+                pieces += [value, swap_part(value, part, step - 1)]
     mine = joined[0]
     peer = swap(mine, MASK_CORE)
     old = call(

time: 101 us -> 95.3 us (0.944)
  starting transfers between devices: 32 us -> 20.7 us
  waiting for transfers between devices: 40.5 us -> 48.4 us
  Pallas kernels: 24.7 us -> 22.8 us
    ppermute x32 -> x11, starting transfers between devices: 32 us -> 7.84 us  [swap(): return lax.ppermute(value, AXES, [(at, at ^ mask) for at in range(32)])]
    ppermute x0 -> x14, waiting for transfers between devices: none -> 24 us  [swap_mixed(): lax.ppermute(value, AXES, [(at, at ^ masks[at & 1]) for at in range(32)])]
    ppermute x32 -> x11, waiting for transfers between devices: 40.5 us -> 24.4 us  [swap(): return lax.ppermute(value, AXES, [(at, at ^ mask) for at in range(32)])]
    ppermute x0 -> x14, starting transfers between devices: none -> 12.9 us  [swap_mixed(): lax.ppermute(value, AXES, [(at, at ^ masks[at & 1]) for at in range(32)])]
    pallas_call x10 -> x5, Pallas kernels: 5.49 us -> 3.68 us  [the longest x3 1.86 us: shards(): call(functools.partial(fold_kernel, step), outs, [SMEM] + [VMEM] * (len(e...]
  transfers between devices with their start and end apart: 32 -> 25, of which waited for: 18 -> 13; matrix products, arithmetic and copies ran while one was open for 2% -> 2% of each run, Pallas kernels for 15% -> 12%
where the time goes in v5:
time: 95.3 us; the launch traced here: 95.1 us
  waiting for transfers between devices  48.4 us (51%)
  Pallas kernels  22.8 us (24%)
  starting transfers between devices  20.7 us (22%)
  between operations  1.6 us (2%)
  local copies, waits for them, and re-layouts  1.58 us (2%)
    ppermute x11, waiting for transfers between devices, swap(): return lax.ppermute(value, AXES, [(at, at ^ mask) for at in range(32)])  24.4 us
    ppermute x14, waiting for transfers between devices, swap_mixed(): lax.ppermute(value, AXES, [(at, at ^ masks[at & 1]) for at in range(32)])  24 us
    ppermute x14, starting transfers between devices, swap_mixed(): lax.ppermute(value, AXES, [(at, at ^ masks[at & 1]) for at in range(32)])  12.9 us
    ppermute x11, starting transfers between devices, swap(): return lax.ppermute(value, AXES, [(at, at ^ mask) for at in range(32)])  7.84 us
    pallas_call x1, Pallas kernels, shards(): call(finish_kernel, [((NB // 8 * BLK, CO), WIDE), ((NB // 8 * BLK, CO), W...  4.05 us
    pallas_call x1, Pallas kernels, shards(): call(term_kernel, [((SLOTS, 128, CO), LOW)] + [((count, 128, CO), LOW) fo...  4 us
    pallas_call x4, Pallas kernels, shards(): call(functools.partial(widen_kernel, step), outs, [SMEM, HBM] + [VMEM] *...  2.42 us
    pallas_call x1, Pallas kernels, shards(): call(old_hidden_kernel, [((PIX, CO), WIDE)], [VMEM] * 2, flops=2 * 27 * 5...  2 us
  transfers between devices with their start and end apart: 25, of which 13 were waited for; matrix products, arithmetic and copies ran while one was open for 2% of the time, Pallas kernels for 12%

profile of v5, /device:TPU:0, one launch (start us, length us, event | category | flops | bytes accessed | tf_op | source)
XLA Modules:
  0.0 95.1 jit_solution(7178589535812430186)
XLA Ops:
  1.7 1.2 %copy.25 = bf16[1,4,18,18,256]{4,3,2,1,0:T(8,128)(2,1)S(1)} copy(bf16[1,4,18,18,256]{4,1,3,2,0:T(4,128)(2,1)} %param.12) | data formatting | bytes 1327104 | tf_op args[2]
  3.0 1.9 %shard_map.138.own = bf16[4480,256]{1,0:T(8,128)(2,1)S(1)} custom-call(s32[5]{0:T(128)S(1)} %stack.23.at.after, bf16[4,18,18,256]{3,2,1,0:T(8,128)(2,1)S(1)} %bitcast.16, bf16[512,256]{1,0:T(8,128)(2,1)} %pre_far.1, bf16[512,256]{1,0:T(8,128)(2,1)} %grad_far.3, bf16[256,256]{1,0:T(8,128)(2,1)} %pointwise_far.3), custom_call_target="tpu_custom_call" | custom-call | bytes 4194304 | tf_op jit(solution)/shard_map/pallas_call | solution.py:502
  5.1 4.0 %shard_map.139 = (bf16[14,128,256]{2,1,0:T(8,128)(2,1)S(1)}, bf16[9,128,256]{2,1,0:T(8,128)(2,1)S(1)}, bf16[5,128,256]{2,1,0:T(8,128)(2,1)S(1)}) custom-call(s32[5]{0:T(128)S(1)} %stack.23.at.after, bf16[4480,256]{1,0:T(8,128)(2,1)S(1)} %shard_map.138.own, bf16[4,18,18,256]{3,2,1,0:T(8,128)(2,1)S(1)} %bitcast.18, ...), custom_call_target="tpu_custom_call" | custom-call | flops 1879048192 | bytes 6291456 | tf_op jit(solution)/shard_map/pallas_call | solution.py:515
  9.1 2.6 %collective-permute-start.4 = (bf16[9,128,256]{2,1,0:T(8,128)(2,1)S(1)}, bf16[9,128,256]{2,1,0:T(8,128)(2,1)S(1)}, u32[]{:S(2)}, u32[]{:S(2)}) collective-permute-start(bf16[9,128,256]{2,1,0:T(8,128)(2,1)S(1)} %get-tuple-element.33), channel_id=1, source_target_pairs={{0,8},{1,17},{2,10},{3,19},{4,12},{5,21},{6,14},{7,23},{8,0},{9,25... | collective-permute-start | bytes 1769480 | tf_op jit(solution)/shard_map/ppermute | solution.py:143
  11.7 1.6 %collective-permute-start.5 = (bf16[5,128,256]{2,1,0:T(8,128)(2,1)S(1)}, bf16[5,128,256]{2,1,0:T(8,128)(2,1)S(1)}, u32[]{:S(2)}, u32[]{:S(2)}) collective-permute-start(bf16[5,128,256]{2,1,0:T(8,128)(2,1)S(1)} %get-tuple-element.34), channel_id=1, source_target_pairs={{0,2},{1,3},{2,0},{3,1},{4,6},{5,7},{6,4},{7,5},{8,10},{9,11},{10,... | collective-permute-start | bytes 983048 | tf_op jit(solution)/shard_map/ppermute | solution.py:143
  13.3 1.5 %shard_map.140.refs_0_ = bf16[15,16,256]{2,1,0:T(8,128)(2,1)S(1)} custom-call(s32[5]{0:T(128)S(1)} %stack.23.at.after, bf16[14,128,256]{2,1,0:T(8,128)(2,1)S(1)} %get-tuple-element.32.after.refs_2_, f32[896,256]{1,0:T(8,128)} %master.1, f32[7,128]{1,0:T(8,128)} %bitcast.19), custom_call_target="tpu_custom_call" | custom-call | tf_op jit(solution)/shard_map/pallas_call | solution.py:530
  15.4 8.8 %collective-permute-done.3.refs_1_ = bf16[15,16,256]{2,1,0:T(8,128)(2,1)S(1)} collective-permute-done((bf16[15,16,256]{2,1,0:T(8,128)(2,1)S(1)}, bf16[15,16,256]{2,1,0:T(8,128)(2,1)S(1)}, u32[]{:S(2)}, u32[]{:S(2)}) %collective-permute-start.3) | collective-permute-done | bytes 122912 | tf_op jit(solution)/shard_map/ppermute | solution.py:139
  24.2 0.7 shard_map.141
  25.3 1.6 %collective-permute-start.8 = (bf16[5,64,256]{2,1,0:T(8,128)(2,1)S(1)}, bf16[5,64,256]{2,1,0:T(8,128)(2,1)S(1)}, u32[]{:S(2)}, u32[]{:S(2)}) collective-permute-start(bf16[5,64,256]{2,1,0:T(8,128)(2,1)S(1)} %get-tuple-element.38), channel_id=1, source_target_pairs={{0,8},{1,9},{2,10},{3,11},{4,12},{5,13},{6,14},{7,15},{8,0},{9,1},... | collective-permute-start | bytes 491528 | tf_op jit(solution)/shard_map/ppermute | solution.py:143
  26.9 2.6 %collective-permute-start.6 = (bf16[2,15,16,256]{3,2,1,0:T(8,128)(2,1)S(1)}, bf16[2,15,16,256]{3,2,1,0:T(8,128)(2,1)S(1)}, u32[]{:S(2)}, u32[]{:S(2)}) collective-permute-start(bf16[2,15,16,256]{3,2,1,0:T(8,128)(2,1)S(1)} %get-tuple-element.35.refs_0_), channel_id=1, source_target_pairs={{0,4},{1,5},{2,6},{3,7},{4,0},{5,1},{6,2},{7,3},{8,12},{9,13},{10,... | collective-permute-start | bytes 737288 | tf_op jit(solution)/shard_map/ppermute | solution.py:139
  29.5 2.4 %collective-permute-done.8.refs_2_ = bf16[5,64,256]{2,1,0:T(8,128)(2,1)S(1)} collective-permute-done((bf16[5,64,256]{2,1,0:T(8,128)(2,1)S(1)}, bf16[5,64,256]{2,1,0:T(8,128)(2,1)S(1)}, u32[]{:S(2)}, u32[]{:S(2)}) %collective-permute-start.8) | collective-permute-done | bytes 163872 | tf_op jit(solution)/shard_map/ppermute | solution.py:143
  32.5 1.4 %collective-permute-start.9 = (bf16[9,32,256]{2,1,0:T(8,128)(2,1)S(1)}, bf16[9,32,256]{2,1,0:T(8,128)(2,1)S(1)}, u32[]{:S(2)}, u32[]{:S(2)}) collective-permute-start(bf16[9,32,256]{2,1,0:T(8,128)(2,1)S(1)} %get-tuple-element.40), channel_id=1, source_target_pairs={{0,2},{1,9},{2,0},{3,11},{4,6},{5,13},{6,4},{7,15},{8,10},{9,1},{1... | collective-permute-start | bytes 442376 | tf_op jit(solution)/shard_map/ppermute | solution.py:143
  34.5 6.9 %collective-permute-done.6.refs_1_ = bf16[2,15,16,256]{3,2,1,0:T(8,128)(2,1)S(1)} collective-permute-done((bf16[2,15,16,256]{3,2,1,0:T(8,128)(2,1)S(1)}, bf16[2,15,16,256]{3,2,1,0:T(8,128)(2,1)S(1)}, u32[]{:S(2)}, u32[]{:S(2)}) %collective-permute-start.6) | collective-permute-done | bytes 245792 | tf_op jit(solution)/shard_map/ppermute | solution.py:139
  42.3 2.0 %collective-permute-start.11 = (bf16[14,16,256]{2,1,0:T(8,128)(2,1)S(1)}, bf16[14,16,256]{2,1,0:T(8,128)(2,1)S(1)}, u32[]{:S(2)}, u32[]{:S(2)}) collective-permute-start(bf16[14,16,256]{2,1,0:T(8,128)(2,1)S(1)} %get-tuple-element.43), channel_id=1, source_target_pairs={{0,4},{1,5},{2,6},{3,7},{4,0},{5,1},{6,2},{7,3},{8,12},{9,13},{10,... | collective-permute-start | bytes 344072 | tf_op jit(solution)/shard_map/ppermute | solution.py:139
  45.5 1.2 %shard_map.144.moments = f32[16,128]{1,0:T(8,128)S(1)} custom-call(s32[5]{0:T(128)S(1)} %stack.23.at.after, s32[224]{0:T(256)S(1)} %copy-done.1, bf16[4,16,256]{2,1,0:T(8,128)(2,1)S(1)} %get-tuple-element.44.mine, bf16[4,16,256]{2,1,0:T(8,128)(2,1)S(1)} %collective-permute-done.12.peer), custom_call_target="tpu_custom_call" | custom-call | tf_op jit(solution)/shard_map/pallas_call | solution.py:566
  46.8 2.6 %collective-permute-done.11.got = bf16[14,16,256]{2,1,0:T(8,128)(2,1)S(1)} collective-permute-done((bf16[14,16,256]{2,1,0:T(8,128)(2,1)S(1)}, bf16[14,16,256]{2,1,0:T(8,128)(2,1)S(1)}, u32[]{:S(2)}, u32[]{:S(2)}) %collective-permute-start.11) | collective-permute-done | bytes 114720 | tf_op jit(solution)/shard_map/ppermute | solution.py:139
  49.3 1.3 %collective-permute-done.13.line_got = bf16[4,224,256]{2,1,0:T(8,128)(2,1)S(1)} collective-permute-done((bf16[4,224,256]{2,1,0:T(8,128)(2,1)S(1)}, bf16[4,224,256]{2,1,0:T(8,128)(2,1)S(1)}, u32[]{:S(2)}, u32[]{:S(2)}) %collective-permute-start.13) | collective-permute-done | bytes 458784 | tf_op jit(solution)/shard_map/ppermute | solution.py:143
  50.7 0.9 shard_map.145
  51.5 1.0 %collective-permute-start.14 = (bf16[2,4,224,256]{3,2,1,0:T(8,128)(2,1)S(1)}, bf16[2,4,224,256]{3,2,1,0:T(8,128)(2,1)S(1)}, u32[]{:S(2)}, u32[]{:S(2)}) collective-permute-start(bf16[2,4,224,256]{3,2,1,0:T(8,128)(2,1)S(1)} %get-tuple-element.46.mine), channel_id=1, source_target_pairs={{0,16},{1,9},{2,18},{3,11},{4,20},{5,13},{6,22},{7,15},{8,24},{9,1... | collective-permute-start | bytes 2752520 | tf_op jit(solution)/shard_map/ppermute | solution.py:143
  52.6 1.1 %collective-permute-start.17 = (bf16[15,16,256]{2,1,0:T(8,128)(2,1)S(1)}, bf16[15,16,256]{2,1,0:T(8,128)(2,1)S(1)}, u32[]{:S(2)}, u32[]{:S(2)}) collective-permute-start(bf16[15,16,256]{2,1,0:T(8,128)(2,1)S(1)} %get-tuple-element.47.refs_0_), channel_id=1, source_target_pairs={{0,4},{1,5},{2,6},{3,7},{4,0},{5,1},{6,2},{7,3},{8,12},{9,13},{10,... | collective-permute-start | bytes 368648 | tf_op jit(solution)/shard_map/ppermute | solution.py:139
  54.1 5.5 %collective-permute-done.17.refs_1_ = bf16[15,16,256]{2,1,0:T(8,128)(2,1)S(1)} collective-permute-done((bf16[15,16,256]{2,1,0:T(8,128)(2,1)S(1)}, bf16[15,16,256]{2,1,0:T(8,128)(2,1)S(1)}, u32[]{:S(2)}, u32[]{:S(2)}) %collective-permute-start.17) | collective-permute-done | bytes 122912 | tf_op jit(solution)/shard_map/ppermute | solution.py:139
  60.2 1.3 %collective-permute-start.19 = (bf16[5,32,256]{2,1,0:T(8,128)(2,1)S(1)}, bf16[5,32,256]{2,1,0:T(8,128)(2,1)S(1)}, u32[]{:S(2)}, u32[]{:S(2)}) collective-permute-start(bf16[5,32,256]{2,1,0:T(8,128)(2,1)S(1)} %get-tuple-element.49.refs_2_), channel_id=1, source_target_pairs={{0,16},{1,17},{2,18},{3,19},{4,20},{5,21},{6,22},{7,23},{8,24},{9,... | collective-permute-start | bytes 245768 | tf_op jit(solution)/shard_map/ppermute | solution.py:143
  61.5 5.2 %collective-permute-done.19.refs_3_ = bf16[5,32,256]{2,1,0:T(8,128)(2,1)S(1)} collective-permute-done((bf16[5,32,256]{2,1,0:T(8,128)(2,1)S(1)}, bf16[5,32,256]{2,1,0:T(8,128)(2,1)S(1)}, u32[]{:S(2)}, u32[]{:S(2)}) %collective-permute-start.19) | collective-permute-done | bytes 81952 | tf_op jit(solution)/shard_map/ppermute | solution.py:143
  67.4 1.0 %collective-permute-start.20 = (bf16[10,64,256]{2,1,0:T(8,128)(2,1)S(1)}, bf16[10,64,256]{2,1,0:T(8,128)(2,1)S(1)}, u32[]{:S(2)}, u32[]{:S(2)}) collective-permute-start(bf16[10,64,256]{2,1,0:T(8,128)(2,1)S(1)} %get-tuple-element.50.refs_0_), channel_id=1, source_target_pairs={{0,16},{1,3},{2,18},{3,1},{4,20},{5,7},{6,22},{7,5},{8,24},{9,11},... | collective-permute-start | bytes 983048 | tf_op jit(solution)/shard_map/ppermute | solution.py:143
  69.2 5.8 %collective-permute-done.21.refs_3_ = bf16[5,64,256]{2,1,0:T(8,128)(2,1)S(1)} collective-permute-done((bf16[5,64,256]{2,1,0:T(8,128)(2,1)S(1)}, bf16[5,64,256]{2,1,0:T(8,128)(2,1)S(1)}, u32[]{:S(2)}, u32[]{:S(2)}) %collective-permute-start.21) | collective-permute-done | bytes 163872 | tf_op jit(solution)/shard_map/ppermute | solution.py:143
  76.3 1.0 %shard_map.146.after.natural = bf16[7168,256]{1,0:T(8,128)(2,1)S(1)} custom-call(s32[5]{0:T(128)S(1)} %stack.23.at.after, s32[224]{0:T(256)S(1)} %copy-done.1, bf16[2,4,224,256]{3,2,1,0:T(8,128)(2,1)S(1)} %get-tuple-element.46.mine, bf16[2,4,224,256]{3,2,1,0:T(8,128)(2,1)S(1)} %collective-permute-done.14.mine_got.after, ...), custom_call_target="tpu_custom_call" | custom-call | bytes 8388608 | tf_op jit(solution)/shard_map/pallas_call | solution.py:583
  77.2 8.0 %collective-permute-done.23.refs_3_ = bf16[5,128,256]{2,1,0:T(8,128)(2,1)S(1)} collective-permute-done((bf16[5,128,256]{2,1,0:T(8,128)(2,1)S(1)}, bf16[5,128,256]{2,1,0:T(8,128)(2,1)S(1)}, u32[]{:S(2)}, u32[]{:S(2)}) %collective-permute-start.23) | collective-permute-done | bytes 327712 | tf_op jit(solution)/shard_map/ppermute | solution.py:143
  85.2 1.1 %collective-permute-done.22.refs_1_ = bf16[10,128,256]{2,1,0:T(8,128)(2,1)S(1)} collective-permute-done((bf16[10,128,256]{2,1,0:T(8,128)(2,1)S(1)}, bf16[10,128,256]{2,1,0:T(8,128)(2,1)S(1)}, u32[]{:S(2)}, u32[]{:S(2)}) %collective-permute-start.22) | collective-permute-done | bytes 655392 | tf_op jit(solution)/shard_map/ppermute | solution.py:143
  86.3 0.7 shard_map.150.scaled.mine
  87.1 2.0 %shard_map.151.old = f32[512,256]{1,0:T(8,128)S(1)} custom-call(bf16[3456,256]{1,0:T(8,128)(2,1)S(1)} %shard_map.137.after.views, bf16[7168,256]{1,0:T(8,128)(2,1)S(1)} %shard_map.146.after.natural), custom_call_target="tpu_custom_call" | custom-call | flops 1811939328 | bytes 6291456 | tf_op jit(solution)/shard_map/pallas_call | solution.py:603
  89.1 1.7 %shard_map.152.own_part = f32[512,256]{1,0:T(8,128)S(1)} custom-call(s32[5]{0:T(128)S(1)} %stack.23.at.after, bf16[3456,256]{1,0:T(8,128)(2,1)S(1)} %shard_map.137.after.views, bf16[15,256,256]{2,1,0:T(8,128)(2,1)S(1)} %shard_map.150.scaled.mine), custom_call_target="tpu_custom_call" | custom-call | flops 939524096 | bytes 4194304 | tf_op jit(solution)/shard_map/pallas_call | solution.py:610
  91.0 4.1 %shard_map.153 = (f32[896,256]{1,0:T(8,128)}, f32[896,256]{1,0:T(8,128)}, f32[7,128]{1,0:T(8,128)}, f32[2,256]{1,0:T(2,128)}, bf16[512,256]{1,0:T(8,128)(2,1)}) custom-call(s32[5]{0:T(128)S(1)} %stack.23.at.after, s32[224]{0:T(256)S(1)} %copy-done.1, f32[1]{0:T(128)S(6)} %sub.16.rate, f32[2,256]{1,0:T(2,128)S(1)} %copy-done.2, ...), custom_call_target="tpu_custom_call" | custom-call | flops 1073741824 | bytes 16777216 | tf_op jit(solution)/shard_map/pallas_call | solution.py:618
  (47 shorter events, 8.9 us)
Async XLA Ops:
  0.6 4.3 %collective-permute-start = (bf16[1,4,18,18,256]{4,1,3,2,0:T(4,128)(2,1)}, bf16[1,4,18,18,256]{4,1,3,2,0:T(4,128)(2,1)S(1)}, u32[]{:S(2)}, u32[]{:S(2)}) collective-permute-start(bf16[1,4,18,18,256]{4,1,3,2,0:T(4,128)(2,1)} %param.12), channel_id=1, source_target_pairs={{0,1},{1,0},{2,3},{3,2},{4,5},{5,4},{6,7},{7,6},{8,9},{9,8},{10,11... | collective-permute-start | bytes 1990664 | tf_op jit(solution)/shard_map/ppermute | solution.py:139
  1.1 3.9 %collective-permute-start.1 = (bf16[512,256]{1,0:T(8,128)(2,1)}, bf16[512,256]{1,0:T(8,128)(2,1)S(1)}, u32[]{:S(2)}, u32[]{:S(2)}) collective-permute-start(bf16[512,256]{1,0:T(8,128)(2,1)} %pre_far.1), channel_id=1, source_target_pairs={{0,1},{1,0},{2,3},{3,2},{4,5},{5,4},{6,7},{7,6},{8,9},{9,8},{10,11... | collective-permute-start | bytes 786440 | tf_op jit(solution)/shard_map/ppermute | solution.py:139
  1.2 3.9 %collective-permute-start.2 = (bf16[512,256]{1,0:T(8,128)(2,1)}, bf16[512,256]{1,0:T(8,128)(2,1)S(1)}, u32[]{:S(2)}, u32[]{:S(2)}) collective-permute-start(bf16[512,256]{1,0:T(8,128)(2,1)} %grad_far.3), channel_id=1, source_target_pairs={{0,1},{1,0},{2,3},{3,2},{4,5},{5,4},{6,7},{7,6},{8,9},{9,8},{10,11... | collective-permute-start | bytes 786440 | tf_op jit(solution)/shard_map/ppermute | solution.py:139
  9.1 15.1 %collective-permute-start.4 = (bf16[9,128,256]{2,1,0:T(8,128)(2,1)S(1)}, bf16[9,128,256]{2,1,0:T(8,128)(2,1)S(1)}, u32[]{:S(2)}, u32[]{:S(2)}) collective-permute-start(bf16[9,128,256]{2,1,0:T(8,128)(2,1)S(1)} %get-tuple-element.33), channel_id=1, source_target_pairs={{0,8},{1,17},{2,10},{3,19},{4,12},{5,21},{6,14},{7,23},{8,0},{9,25... | collective-permute-start | bytes 1769480 | tf_op jit(solution)/shard_map/ppermute | solution.py:143
  11.7 12.4 %collective-permute-start.5 = (bf16[5,128,256]{2,1,0:T(8,128)(2,1)S(1)}, bf16[5,128,256]{2,1,0:T(8,128)(2,1)S(1)}, u32[]{:S(2)}, u32[]{:S(2)}) collective-permute-start(bf16[5,128,256]{2,1,0:T(8,128)(2,1)S(1)} %get-tuple-element.34), channel_id=1, source_target_pairs={{0,2},{1,3},{2,0},{3,1},{4,6},{5,7},{6,4},{7,5},{8,10},{9,11},{10,... | collective-permute-start | bytes 983048 | tf_op jit(solution)/shard_map/ppermute | solution.py:143
  14.9 30.7 %copy-start.1 = (s32[224]{0:T(256)S(1)}, s32[224]{0:T(256)}, u32[]{:S(2)}) copy-start(s32[224]{0:T(256)} %block_order.5) | copy-start | bytes 2692
  14.9 9.3 %collective-permute-start.3 = (bf16[15,16,256]{2,1,0:T(8,128)(2,1)S(1)}, bf16[15,16,256]{2,1,0:T(8,128)(2,1)S(1)}, u32[]{:S(2)}, u32[]{:S(2)}) collective-permute-start(bf16[15,16,256]{2,1,0:T(8,128)(2,1)S(1)} %shard_map.140.refs_0_), channel_id=1, source_target_pairs={{0,2},{1,3},{2,0},{3,1},{4,6},{5,7},{6,4},{7,5},{8,10},{9,11},{10,... | collective-permute-start | bytes 368648 | tf_op jit(solution)/shard_map/ppermute | solution.py:139
  24.8 28.9 %copy-start.3 = (bf16[1,4,18,18,256]{4,1,3,2,0:T(4,128)(2,1)S(1)}, bf16[1,4,18,18,256]{4,1,3,2,0:T(4,128)(2,1)}, u32[]{:S(2)}) copy-start(bf16[1,4,18,18,256]{4,1,3,2,0:T(4,128)(2,1)} %param.19) | copy-start | bytes 1990660
  24.8 7.0 %collective-permute-start.7 = (bf16[9,64,256]{2,1,0:T(8,128)(2,1)S(1)}, bf16[9,64,256]{2,1,0:T(8,128)(2,1)S(1)}, u32[]{:S(2)}, u32[]{:S(2)}) collective-permute-start(bf16[9,64,256]{2,1,0:T(8,128)(2,1)S(1)} %get-tuple-element.37), channel_id=1, source_target_pairs={{0,16},{1,3},{2,18},{3,1},{4,20},{5,7},{6,22},{7,5},{8,24},{9,11},... | collective-permute-start | bytes 884744 | tf_op jit(solution)/shard_map/ppermute | solution.py:143
  25.3 6.6 %collective-permute-start.8 = (bf16[5,64,256]{2,1,0:T(8,128)(2,1)S(1)}, bf16[5,64,256]{2,1,0:T(8,128)(2,1)S(1)}, u32[]{:S(2)}, u32[]{:S(2)}) collective-permute-start(bf16[5,64,256]{2,1,0:T(8,128)(2,1)S(1)} %get-tuple-element.38), channel_id=1, source_target_pairs={{0,8},{1,9},{2,10},{3,11},{4,12},{5,13},{6,14},{7,15},{8,0},{9,1},... | collective-permute-start | bytes 491528 | tf_op jit(solution)/shard_map/ppermute | solution.py:143
  26.9 14.4 %collective-permute-start.6 = (bf16[2,15,16,256]{3,2,1,0:T(8,128)(2,1)S(1)}, bf16[2,15,16,256]{3,2,1,0:T(8,128)(2,1)S(1)}, u32[]{:S(2)}, u32[]{:S(2)}) collective-permute-start(bf16[2,15,16,256]{3,2,1,0:T(8,128)(2,1)S(1)} %get-tuple-element.35.refs_0_), channel_id=1, source_target_pairs={{0,4},{1,5},{2,6},{3,7},{4,0},{5,1},{6,2},{7,3},{8,12},{9,13},{10,... | collective-permute-start | bytes 737288 | tf_op jit(solution)/shard_map/ppermute | solution.py:139
  32.5 9.1 %collective-permute-start.9 = (bf16[9,32,256]{2,1,0:T(8,128)(2,1)S(1)}, bf16[9,32,256]{2,1,0:T(8,128)(2,1)S(1)}, u32[]{:S(2)}, u32[]{:S(2)}) collective-permute-start(bf16[9,32,256]{2,1,0:T(8,128)(2,1)S(1)} %get-tuple-element.40), channel_id=1, source_target_pairs={{0,2},{1,9},{2,0},{3,11},{4,6},{5,13},{6,4},{7,15},{8,10},{9,1},{1... | collective-permute-start | bytes 442376 | tf_op jit(solution)/shard_map/ppermute | solution.py:143
  33.9 7.5 %collective-permute-start.10 = (bf16[5,32,256]{2,1,0:T(8,128)(2,1)S(1)}, bf16[5,32,256]{2,1,0:T(8,128)(2,1)S(1)}, u32[]{:S(2)}, u32[]{:S(2)}) collective-permute-start(bf16[5,32,256]{2,1,0:T(8,128)(2,1)S(1)} %get-tuple-element.41), channel_id=1, source_target_pairs={{0,16},{1,17},{2,18},{3,19},{4,20},{5,21},{6,22},{7,23},{8,24},{9,... | collective-permute-start | bytes 245768 | tf_op jit(solution)/shard_map/ppermute | solution.py:143
  42.1 8.5 %collective-permute-start.13 = (bf16[4,224,256]{2,1,0:T(8,128)(2,1)S(1)}, bf16[4,224,256]{2,1,0:T(8,128)(2,1)S(1)}, u32[]{:S(2)}, u32[]{:S(2)}) collective-permute-start(bf16[4,224,256]{2,1,0:T(8,128)(2,1)S(1)} %get-tuple-element.45.line), channel_id=1, source_target_pairs={{0,8},{1,17},{2,10},{3,19},{4,12},{5,21},{6,14},{7,23},{8,0},{9,25... | collective-permute-start | bytes 1376264 | tf_op jit(solution)/shard_map/ppermute | solution.py:143
  42.3 7.0 %collective-permute-start.11 = (bf16[14,16,256]{2,1,0:T(8,128)(2,1)S(1)}, bf16[14,16,256]{2,1,0:T(8,128)(2,1)S(1)}, u32[]{:S(2)}, u32[]{:S(2)}) collective-permute-start(bf16[14,16,256]{2,1,0:T(8,128)(2,1)S(1)} %get-tuple-element.43), channel_id=1, source_target_pairs={{0,4},{1,5},{2,6},{3,7},{4,0},{5,1},{6,2},{7,3},{8,12},{9,13},{10,... | collective-permute-start | bytes 344072 | tf_op jit(solution)/shard_map/ppermute | solution.py:139
  44.3 1.2 %collective-permute-start.12 = (bf16[4,16,256]{2,1,0:T(8,128)(2,1)S(1)}, bf16[4,16,256]{2,1,0:T(8,128)(2,1)S(1)}, u32[]{:S(2)}, u32[]{:S(2)}) collective-permute-start(bf16[4,16,256]{2,1,0:T(8,128)(2,1)S(1)} %get-tuple-element.44.mine), channel_id=1, source_target_pairs={{0,1},{1,0},{2,3},{3,2},{4,5},{5,4},{6,7},{7,6},{8,9},{9,8},{10,11... | collective-permute-start | bytes 98312 | tf_op jit(solution)/shard_map/ppermute | solution.py:139
  51.5 15.2 %collective-permute-start.14 = (bf16[2,4,224,256]{3,2,1,0:T(8,128)(2,1)S(1)}, bf16[2,4,224,256]{3,2,1,0:T(8,128)(2,1)S(1)}, u32[]{:S(2)}, u32[]{:S(2)}) collective-permute-start(bf16[2,4,224,256]{3,2,1,0:T(8,128)(2,1)S(1)} %get-tuple-element.46.mine), channel_id=1, source_target_pairs={{0,16},{1,9},{2,18},{3,11},{4,20},{5,13},{6,22},{7,15},{8,24},{9,1... | collective-permute-start | bytes 2752520 | tf_op jit(solution)/shard_map/ppermute | solution.py:143
  52.6 7.0 %collective-permute-start.17 = (bf16[15,16,256]{2,1,0:T(8,128)(2,1)S(1)}, bf16[15,16,256]{2,1,0:T(8,128)(2,1)S(1)}, u32[]{:S(2)}, u32[]{:S(2)}) collective-permute-start(bf16[15,16,256]{2,1,0:T(8,128)(2,1)S(1)} %get-tuple-element.47.refs_0_), channel_id=1, source_target_pairs={{0,4},{1,5},{2,6},{3,7},{4,0},{5,1},{6,2},{7,3},{8,12},{9,13},{10,... | collective-permute-start | bytes 368648 | tf_op jit(solution)/shard_map/ppermute | solution.py:139
  60.2 6.6 %collective-permute-start.18 = (bf16[10,32,256]{2,1,0:T(8,128)(2,1)S(1)}, bf16[10,32,256]{2,1,0:T(8,128)(2,1)S(1)}, u32[]{:S(2)}, u32[]{:S(2)}) collective-permute-start(bf16[10,32,256]{2,1,0:T(8,128)(2,1)S(1)} %get-tuple-element.48.refs_0_), channel_id=1, source_target_pairs={{0,2},{1,9},{2,0},{3,11},{4,6},{5,13},{6,4},{7,15},{8,10},{9,1},{1... | collective-permute-start | bytes 491528 | tf_op jit(solution)/shard_map/ppermute | solution.py:143
  60.2 6.5 %collective-permute-start.19 = (bf16[5,32,256]{2,1,0:T(8,128)(2,1)S(1)}, bf16[5,32,256]{2,1,0:T(8,128)(2,1)S(1)}, u32[]{:S(2)}, u32[]{:S(2)}) collective-permute-start(bf16[5,32,256]{2,1,0:T(8,128)(2,1)S(1)} %get-tuple-element.49.refs_2_), channel_id=1, source_target_pairs={{0,16},{1,17},{2,18},{3,19},{4,20},{5,21},{6,22},{7,23},{8,24},{9,... | collective-permute-start | bytes 245768 | tf_op jit(solution)/shard_map/ppermute | solution.py:143
  67.4 7.7 %collective-permute-start.20 = (bf16[10,64,256]{2,1,0:T(8,128)(2,1)S(1)}, bf16[10,64,256]{2,1,0:T(8,128)(2,1)S(1)}, u32[]{:S(2)}, u32[]{:S(2)}) collective-permute-start(bf16[10,64,256]{2,1,0:T(8,128)(2,1)S(1)} %get-tuple-element.50.refs_0_), channel_id=1, source_target_pairs={{0,16},{1,3},{2,18},{3,1},{4,20},{5,7},{6,22},{7,5},{8,24},{9,11},... | collective-permute-start | bytes 983048 | tf_op jit(solution)/shard_map/ppermute | solution.py:143
  68.4 7.9 %collective-permute-start.15 = (bf16[2,4,224,256]{3,2,1,0:T(8,128)(2,1)S(1)}, bf16[2,4,224,256]{3,2,1,0:T(8,128)(2,1)S(1)}, u32[]{:S(2)}, u32[]{:S(2)}) collective-permute-start(bf16[2,4,224,256]{3,2,1,0:T(8,128)(2,1)S(1)} %get-tuple-element.46.mine), channel_id=1, source_target_pairs={{0,1},{1,0},{2,3},{3,2},{4,5},{5,4},{6,7},{7,6},{8,9},{9,8},{10,11... | collective-permute-start | bytes 2752520 | tf_op jit(solution)/shard_map/ppermute | solution.py:139
  68.4 7.9 %collective-permute-start.16 = (bf16[2,4,224,256]{3,2,1,0:T(8,128)(2,1)S(1)}, bf16[2,4,224,256]{3,2,1,0:T(8,128)(2,1)S(1)}, u32[]{:S(2)}, u32[]{:S(2)}) collective-permute-start(bf16[2,4,224,256]{3,2,1,0:T(8,128)(2,1)S(1)} %collective-permute-done.14.mine_got.after), channel_id=1, source_target_pairs={{0,1},{1,0},{2,3},{3,2},{4,5},{5,4},{6,7},{7,6},{8,9},{9,8},{10,11... | collective-permute-start | bytes 2752520 | tf_op jit(solution)/shard_map/ppermute | solution.py:139
  68.9 6.1 %collective-permute-start.21 = (bf16[5,64,256]{2,1,0:T(8,128)(2,1)S(1)}, bf16[5,64,256]{2,1,0:T(8,128)(2,1)S(1)}, u32[]{:S(2)}, u32[]{:S(2)}) collective-permute-start(bf16[5,64,256]{2,1,0:T(8,128)(2,1)S(1)} %get-tuple-element.51.refs_2_), channel_id=1, source_target_pairs={{0,8},{1,9},{2,10},{3,11},{4,12},{5,13},{6,14},{7,15},{8,0},{9,1},... | collective-permute-start | bytes 491528 | tf_op jit(solution)/shard_map/ppermute | solution.py:143
  75.6 10.7 %collective-permute-start.22 = (bf16[10,128,256]{2,1,0:T(8,128)(2,1)S(1)}, bf16[10,128,256]{2,1,0:T(8,128)(2,1)S(1)}, u32[]{:S(2)}, u32[]{:S(2)}) collective-permute-start(bf16[10,128,256]{2,1,0:T(8,128)(2,1)S(1)} %get-tuple-element.52.refs_0_), channel_id=1, source_target_pairs={{0,8},{1,17},{2,10},{3,19},{4,12},{5,21},{6,14},{7,23},{8,0},{9,25... | collective-permute-start | bytes 1966088 | tf_op jit(solution)/shard_map/ppermute | solution.py:143
  76.0 9.2 %collective-permute-start.23 = (bf16[5,128,256]{2,1,0:T(8,128)(2,1)S(1)}, bf16[5,128,256]{2,1,0:T(8,128)(2,1)S(1)}, u32[]{:S(2)}, u32[]{:S(2)}) collective-permute-start(bf16[5,128,256]{2,1,0:T(8,128)(2,1)S(1)} %get-tuple-element.53.refs_2_), channel_id=1, source_target_pairs={{0,2},{1,3},{2,0},{3,1},{4,6},{5,7},{6,4},{7,5},{8,10},{9,11},{10,... | collective-permute-start | bytes 983048 | tf_op jit(solution)/shard_map/ppermute | solution.py:143
  87.0 4.0 %collective-permute-start.24 = (bf16[15,256,256]{2,1,0:T(8,128)(2,1)S(1)}, bf16[15,256,256]{2,1,0:T(8,128)(2,1)S(1)}, u32[]{:S(2)}, u32[]{:S(2)}) collective-permute-start(bf16[15,256,256]{2,1,0:T(8,128)(2,1)S(1)} %shard_map.150.scaled.mine), channel_id=1, source_target_pairs={{0,1},{1,0},{2,3},{3,2},{4,5},{5,4},{6,7},{7,6},{8,9},{9,8},{10,11... | collective-permute-start | bytes 5898248 | tf_op jit(solution)/shard_map/ppermute | solution.py:139
  89.1 2.0 %copy-start = (f32[896,256]{1,0:T(8,128)S(1)}, f32[896,256]{1,0:T(8,128)}, u32[]{:S(2)}) copy-start(f32[896,256]{1,0:T(8,128)} %master.1) | copy-start | bytes 2752516
  89.1 1.9 %copy-start.2 = (f32[2,256]{1,0:T(2,128)S(1)}, f32[2,256]{1,0:T(2,128)}, u32[]{:S(2)}) copy-start(f32[2,256]{1,0:T(2,128)} %col_moment.1) | copy-start | bytes 6148

commit v6 on v5

--- a/solution.py
+++ b/solution.py
@@ -128,9 +128,9 @@
 SMEM = pl.BlockSpec(memory_space=pltpu.SMEM)
 HBM = pl.BlockSpec(memory_space=pl.ANY)
 MASK_CORE, MASK_NEAR, MASK_FAR, MASK_X, MASK_Y = 1, 2, 4, 8, 16
-PARTS = ((0, 9), (9, 5))
+PARTS = ((0, 10), (10, 4))
 ORDERS = (((0, 1, 2), (1, 2, 0)), ((2, 0, 1), (2, 0, 1)))
-MESSAGE = 9
+MESSAGE = SLOTS
 GATHERED = ((0, 10), (10, 5))
 MASKS = (MASK_X, MASK_Y, MASK_NEAR)
 
@@ -148,22 +148,16 @@
 
 
 def place_of(at, part, step):
-    if step == 3:
-        return at[3]
     zero, one = (ORDERS[part][core][step] for core in range(2))
     return at[zero] if zero == one else jnp.where(at[4] == 0, at[zero], at[one])
 
 
-def gathered_at(slot):
-    return slot + (slot >= MESSAGE) * 1
-
-
-def call(kernel, outs, in_specs, scratch=(), flops=0, moved=0, room=8, pin=True):
+def call(kernel, outs, in_specs, out_specs=None, scratch=(), flops=0, moved=0, room=8, pin=True):
     return pl.pallas_call(
         kernel,
         out_shape=[(pltpu.VMEM if pin else jax.ShapeDtypeStruct)(*out) for out in outs],
         in_specs=in_specs,
-        out_specs=[VMEM] * len(outs),
+        out_specs=out_specs or [VMEM] * len(outs),
         scratch_shapes=list(scratch),
         compiler_params=pltpu.CompilerParams(vmem_limit_bytes=room << 20),
         cost_estimate=pl.CostEstimate(flops=flops, bytes_accessed=moved, transcendentals=0),
@@ -190,6 +184,17 @@
         grad, pointwise, (((1,), (1,)), ((), ())), preferred_element_type=WIDE
     )
     return (grad_act * silu_slope(pre.astype(WIDE))).astype(LOW)
+
+
+def view_start(tap, frame):
+    frame_off, row_off, col_off = tap // 9, tap // 3 % 3, tap % 3
+    return col_off * SHIFTED + ((frame + frame_off) * (HW + 2) + row_off) * HW
+
+
+def core_start(core, slot, frame):
+    return pl.multiple_of(
+        jnp.where(core == 0, view_start(slot, frame), view_start(min(SLOTS + slot, 26), frame)), HW
+    )
 
 
 def fetch(pairs, arrived):
@@ -243,12 +248,10 @@
     rights[0, PIX:] = peer[SLOPES:ACTS]
     rights[1, PIX:] = grad_peer[...]
     for slot in range(SLOTS):
-        tap = core * SLOTS + slot
-        frame_off, row_off, col_off = tap // 9, lax.rem(tap // 3, 3), lax.rem(tap, 3)
         pieces = []
         for ref in (own, peer):
             for frame in range(FR):
-                start = col_off * SHIFTED + ((frame + frame_off) * (HW + 2) + row_off) * HW
+                start = core_start(core, slot, frame)
                 if slot == SLOTS - 1:
                     start = jnp.where(core == 0, start, ACTS + frame * HW * HW)
                 pieces.append(ref[pl.ds(pl.multiple_of(start, HW), HW * HW), :])
@@ -268,56 +271,62 @@
     refs = refs[extra:]
     keep, gots, stay, sends = refs[0], refs[1:3], refs[3], refs[4:]
     for part, (first, count) in enumerate(PARTS):
+        here = slice(first, first + count)
+        if step == 3:
+            stay[here] = keep[here] + gots[part][...]
+            continue
         mine = place_of(at, part, step)
-        here = slice(first, first + count)
         for which, out in ((mine, 0), (1 - mine, 1)):
             rows = pl.ds(pl.multiple_of(which * size, size), size)
             value = keep[here, rows] + gots[part][:, rows]
             if out == 0:
                 stay[here] = value
-            elif step < 3:
+            else:
                 sends[part][...] = value
-            else:
-                sends[0][here] = value
     if step == 1:
         pair = sends[2]
-        pair[at[2]] = own[...]
-        pair[1 - at[2]] = got[...]
+        pair[at[3]] = own[...]
+        pair[1 - at[3]] = got[...]
     if step == 3:
-        line, moments = sends[1:]
-        for which, piece in ((at[3], own), (1 - at[3], got)):
-            for near in range(2):
-                line[which * 2 + near] = piece[near, :SLOTS].reshape(SLOTS * 16, CO)
-                moments[which * 2 + near] = piece[near, SLOTS]
-
-
-def moment_kernel(at, rate, own, got, moments, line, line_got, scaled, plane):
-    plane[0], plane[1] = line[...], line_got[...]
-    total = (own[...].astype(WIDE) + got[...].astype(WIDE)).reshape(SLOTS * 16, CO)
+        line, moments = sends
+        for which, piece in ((at[2], own), (1 - at[2], got)):
+            for far in range(2):
+                line[far * 2 + which] = piece[far, :SLOTS].reshape(SLOTS * 16, CO)
+                moments[far * 2 + which] = piece[far, SLOTS]
+
+
+def moment_kernel(
+    at, rate, own, got, moments, line, line_one, line_two, scaled_one, scaled_two, lines,
+):
+    for index, piece in enumerate((line, line_one, line_two)):
+        lines[index] = piece[...]
+    count = SLOTS * BLK
+    total = (own[...].astype(WIDE) + got[...].astype(WIDE)).reshape(count, CO)
     squares = total * total
     decay = rate[0]
     mean = jnp.sum(squares, axis=1, keepdims=True) * (1.0 / CO)
     row_moment = jnp.concatenate([moments[:, slot : slot + 1] for slot in range(SLOTS)], axis=0)
     new_row = decay * row_moment + (1.0 - decay) * mean
-    value = (total * lax.rsqrt(new_row)).astype(LOW).reshape(SLOTS, 16, CO)
-    scaled[:MESSAGE] = value[:MESSAGE]
-    scaled[MESSAGE + 1 :] = value[MESSAGE:]
+    value = (total * lax.rsqrt(new_row)).astype(LOW).reshape(SLOTS, BLK, CO)
+    split = PARTS[0][1]
+    scaled_one[...] = value[:split]
+    scaled_two[: SLOTS - split] = value[split:]
     weighted = squares / new_row
-    cut = (SLOTS - 1) * 16
+    cut = count - BLK
     last_small = at[4] == 1
     rows = []
-    for values in (squares, weighted, jnp.broadcast_to(new_row, (SLOTS * 16, CO))):
+    for values in (squares, weighted, jnp.broadcast_to(new_row, (count, CO))):
         large = jnp.sum(values[:cut], axis=0, keepdims=True)
         last = jnp.sum(values[cut:], axis=0, keepdims=True)
         rows.append(large + jnp.where(last_small, 0.0, last))
         rows.append(jnp.where(last_small, last, 0.0))
-    spread = jnp.broadcast_to(new_row, (SLOTS * 16, 128))
-    spread = jnp.concatenate([spread, jnp.zeros((32, 128), WIDE)], axis=0)
-    rows.append(jnp.transpose(spread)[:1])
-    rows.append(jnp.zeros((1, CO), WIDE))
+    spread = jnp.broadcast_to(new_row, (count, 128))
+    spread = jnp.concatenate([spread, jnp.zeros((512 - count, 128), WIDE)], axis=0)
+    rows += [jnp.transpose(spread[:CO])[:1], jnp.transpose(spread[CO:])[:1]]
     message = jnp.concatenate(rows, axis=0)
     high = message.astype(LOW).astype(WIDE)
-    scaled[MESSAGE] = jnp.concatenate([high, message - high], axis=0).astype(LOW)
+    message = jnp.concatenate([high, message - high, jnp.zeros((16, CO), WIDE)], axis=0)
+    scaled_two[SLOTS - split] = message.astype(LOW)
 
 
 def store_factors(total, decay, col_moment, new_col, factor):
@@ -335,8 +344,27 @@
         factor[kernel : kernel + 1] = 1.0 / (jnp.sqrt(col / row_mean) * clip)
 
 
-def moments_kernel(at, block_order, mine, peer, out, table, rows, inverse):
+def moments_kernel(at, block_order, mine, peer, out, plan, table, rows, inverse):
     core = at[4]
+    owner = at[3] * 4 + at[2] * 2 + core
+
+    def place_block(local, carry):
+        block = block_order[owner * (NB // 8) + local]
+        half = (block >= 8 * SLOTS).astype(jnp.int32)
+        slot, place = (block - half * (8 * SLOTS)) // 8, lax.rem(block, 8)
+        high, middle, low = place // 4, lax.rem(place // 2, 2), lax.rem(place, 2)
+        other = jnp.where(half == 0, low * 4 + high * 2 + middle, middle * 4 + low * 2 + high)
+        sender = jnp.where(slot < PARTS[1][0], other, place)
+        side = half ^ core
+        plan[local * 8] = side
+        plan[local * 8 + 1] = slot
+        plan[local * 8 + 2] = place * BLK
+        plan[local * 8 + 3] = (block >= NB3).astype(jnp.int32)
+        plan[local * 8 + 4] = (side * 8 + sender) * 4 + slot // 4
+        plan[local * 8 + 5] = lax.rem(128 + (lax.rem(local, 4) - lax.rem(slot, 4)) * BLK, 128)
+        return carry
+
+    lax.fori_loop(0, NB // 8, place_block, 0, unroll=4)
     for side, ref in enumerate((mine, peer)):
         for line in range(4):
             values = ref[line].astype(WIDE)
@@ -355,67 +383,60 @@
             stored = inverse[(core * SLOTS + slot) * 8 + place]
             owner, local = stored // (NB // 8), lax.rem(stored, NB // 8)
             row = table[pl.ds(owner * 8 + local // 4, 1), :]
-            turn = lax.rem(128 - lax.rem(local, 4) * BLK - at[3] * 16, 128)
+            turn = lax.rem(128 - lax.rem(local, 4) * BLK, 128)
             rows[slot : slot + 1] = pltpu.roll(row, turn, 1)
-    out[...] = jnp.transpose(rows[...])[:16]
-
-
-def order_kernel(at, block_order, mine, mine_got, peer, peer_got, out):
+    out[...] = jnp.transpose(rows[...])[:BLK]
+
+
+def order_kernel(at, block_order, mine, mine_far, peer, peer_far, out):
     count = NB // 8
     quarters = count // 4
-    for flip_core, pieces in enumerate(((mine, mine_got), (peer, peer_got))):
+    for flip_core, (pieces, far) in enumerate(((mine, mine_far), (peer, peer_far))):
         core = at[4] ^ flip_core
-        for second, piece in enumerate(pieces):
-            for first in range(2):
-                flip_x = jnp.where(core == 0, first, second)
-                quarter = (at[1] ^ first ^ second ^ flip_x) * 2 + (at[0] ^ flip_x)
-                for local in range(quarters):
-                    for line in range(4):
-                        block = block_order[(line * 2 + core) * count + quarter * quarters + local]
-                        to = pl.ds(pl.multiple_of(block * BLK, BLK), BLK)
-                        out[to, :] = piece[first, line, local * BLK : local * BLK + BLK]
+        for index, piece in enumerate((pieces.at[0], pieces.at[1], pieces.at[2], far)):
+            quarter = (at[1] ^ (index % 2)) * 2 + (at[0] ^ (index // 2))
+            for local in range(quarters):
+                for line in range(4):
+                    block = block_order[(line * 2 + core) * count + quarter * quarters + local]
+                    to = pl.ds(pl.multiple_of(block * BLK, BLK), BLK)
+                    out[to, :] = piece[line, local * BLK : local * BLK + BLK]
 
 
 def widen_kernel(step, at, after, *refs):
     size = 256 >> (step + 1)
-    ins, outs = (refs[:2], refs[2:]) if step == 3 else (refs[:4], refs[4:])
+    ins, outs = refs[:4], refs[4:]
     for part, (first, count) in enumerate(GATHERED):
         mine = place_of(at, part, step)
-        here = slice(first, first + count)
         for index, which in enumerate((mine, 1 - mine)):
             rows = pl.ds(pl.multiple_of(which * size, size), size)
-            value = ins[index][here] if step == 3 else ins[2 * part + index][...]
+            value = ins[2 * part + index][...]
             if step == 0:
-                outs[0][here, rows] = value
+                outs[0][first : first + count, rows] = value
             else:
                 outs[part][:, rows] = value
 
 
-def window(views, tap):
-    frame_off, row_off, col_off = tap // 9, lax.rem(tap // 3, 3), lax.rem(tap, 3)
-    parts = []
-    for frame in range(FR):
-        start = col_off * SHIFTED + ((frame + frame_off) * (HW + 2) + row_off) * HW
-        parts.append(views[pl.ds(pl.multiple_of(start, HW), HW * HW), :])
-    return jnp.concatenate(parts, axis=0)
+def window(views, starts):
+    return jnp.concatenate([views[pl.ds(start, HW * HW), :] for start in starts], axis=0)
 
 
 def old_hidden_kernel(views, natural, hidden):
     total = jnp.zeros((PIX, CO), WIDE)
     for tap in range(27):
         weights = natural[tap * CI : tap * CI + CI]
-        total = total + jnp.dot(window(views, tap), weights, preferred_element_type=WIDE)
+        starts = [view_start(tap, frame) for frame in range(FR)]
+        total = total + jnp.dot(window(views, starts), weights, preferred_element_type=WIDE)
     hidden[...] = total
 
 
 def add_taps(views, scaled, core):
     total = jnp.zeros((PIX, CO), WIDE)
     for slot in range(SLOTS):
-        tap = jnp.minimum(core * SLOTS + slot, 26)
-        weights = scaled[gathered_at(slot)]
+        starts = [core_start(core, slot, frame) for frame in range(FR)]
+        weights = scaled[slot]
         if slot == SLOTS - 1:
             weights = jnp.where(core == 0, weights.astype(WIDE), 0.0).astype(LOW)
-        total = total + jnp.dot(window(views, tap), weights, preferred_element_type=WIDE)
+        total = total + jnp.dot(window(views, starts), weights, preferred_element_type=WIDE)
     return total
 
 
@@ -424,57 +445,53 @@
 
 
 def finish_kernel(
-    at, block_order, rate, col_moment, views, natural, master, mine, peer, old, own_part,
-    update_rows, new_master, new_row, new_col, next_output, factor, row_table,
+    at, plan, rate, col_moment, views, natural, master, mine, peer, old, own_part,
+    update_far, master_far, new_row, new_col, next_output,
+    factor, row_table, update_rows, new_master, stored,
 ):
     core = at[4]
     total = jnp.zeros((8, CO), WIDE)
     for side, piece in enumerate((mine, peer)):
-        message = piece[MESSAGE].astype(WIDE).reshape(16, 2, 8, CO)
-        message = message[:, 0] + message[:, 1]
-        total = total + jnp.sum(message, axis=0)
-        for index in range(16):
-            for half in range(2):
-                to = (side * 16 + index) * 2 + half
-                row_table[to : to + 1] = message[index, 6:7, half * 128 : half * 128 + 128]
+        for sender in range(8):
+            message = piece[MESSAGE, sender * BLK : sender * BLK + 16].astype(WIDE)
+            message = message[:8] + message[8:]
+            total = total + message
+            for line in range(4):
+                to = (side * 8 + sender) * 4 + line
+                row_table[to : to + 1] = message[
+                    6 + line // 2 : 7 + line // 2, line % 2 * 128 : line % 2 * 128 + 128
+                ]
     store_factors(total, rate[0], col_moment, new_col, factor)
-    change = own_part[...] + add_taps(views, peer, 1 - core)
-    hidden = old[...] - (learn_rate * factor[0:1]) * change
-    small = jnp.where(core == 1, mine[SLOTS].astype(WIDE), peer[SLOTS].astype(WIDE))
-    weights = natural[27 * CI :].astype(WIDE) - small * (learn_rate * factor[1:2])
-    next_output[...] = jnp.dot(
-        jax.nn.silu(hidden).astype(LOW), weights.astype(LOW), preferred_element_type=WIDE
-    ).astype(LOW)
-
-    owner = at[3] * 4 + at[2] * 2 + core
+
     lane = lax.broadcasted_iota(jnp.int32, (1, 128), 1)
     for line in range(7):
         values = jnp.zeros((1, 128), WIDE)
         for part in range(4):
             local = line * 4 + part
-            block = block_order[owner * (NB // 8) + local]
-            side = (block // (8 * SLOTS)) ^ core
-            slot, place = lax.rem(block // 8, SLOTS), lax.rem(block, 8)
-            near, x, y = place // 4, lax.rem(place // 2, 2), lax.rem(place, 2)
-            other = jnp.where(side == core, x * 8 + y * 4 + near * 2, y * 8 + near * 4 + x * 2)
-            sender = jnp.where(slot < MESSAGE, place * 2, other)
-            index = gathered_at(slot)
-            chosen = jnp.where(block >= NB3, factor[1:2], factor[0:1])
+            side, slot, first, kernel, from_row, turn = (plan[local * 8 + item] for item in range(6))
             rows = slice(local * BLK, local * BLK + BLK)
-            there = pl.ds(pl.multiple_of(place * BLK, BLK), BLK)
+            there = pl.ds(pl.multiple_of(first, BLK), BLK)
             value = jnp.where(
-                side == 0, mine[index, there, :].astype(WIDE), peer[index, there, :].astype(WIDE)
+                side == 0, mine[slot, there, :].astype(WIDE), peer[slot, there, :].astype(WIDE)
             )
-            update = value * chosen
+            update = value * factor[pl.ds(kernel, 1), :]
             update_rows[rows, :] = update
             new_master[rows, :] = master[rows, :] - learn_rate * update
-            for half in range(2):
-                at_row = (side * 16 + sender + half) * 2 + slot // 8
-                to = part * 32 + half * 16
-                turn = lax.rem(128 + to - lax.rem(slot, 8) * 16, 128)
-                turned = pltpu.roll(row_table[pl.ds(at_row, 1), :], turn, 1)
-                values = jnp.where((lane >= to) & (lane < to + 16), turned, values)
+            here = (lane >= part * BLK) & (lane < part * BLK + BLK)
+            turned = pltpu.roll(row_table[pl.ds(from_row, 1), :], turn, 1)
+            values = jnp.where(here, turned, values)
         new_row[line : line + 1] = values
+    copies = fetch(((update_rows, update_far), (new_master, master_far)), stored)
+
+    change = own_part[...] + add_taps(views, peer, 1 - core)
+    hidden = old[...] - (learn_rate * factor[0:1]) * change
+    small = jnp.where(core == 1, mine[SLOTS - 1].astype(WIDE), peer[SLOTS - 1].astype(WIDE))
+    weights = natural[27 * CI :].astype(WIDE) - small * (learn_rate * factor[1:2])
+    next_output[...] = jnp.dot(
+        jax.nn.silu(hidden).astype(LOW), weights.astype(LOW), preferred_element_type=WIDE
+    ).astype(LOW)
+    for copy in copies:
+        copy.wait()
 
 
 def shards(
@@ -537,7 +554,7 @@
             pltpu.SemaphoreType.DMA((2,)),
         ],
     )(at, keep, far_away(master_rows), far_away(row_moment.reshape(7, 128)))[0]
-    packed_near = swap(packed, MASK_NEAR)
+    packed_far = swap(packed, MASK_FAR)
     views = call(shift_kernel, [((3 * SHIFTED, CI), LOW)], [VMEM], moved=3 << 20)(next_tiles[0])[0]
 
     for step in range(1, 4):
@@ -545,13 +562,13 @@
         size = 256 >> (step + 1)
         outs = [((SLOTS, size, CO), LOW)] + [((count, size, CO), LOW) for _, count in PARTS]
         if step == 1:
-            extra = [packed, packed_near]
+            extra = [packed, packed_far]
             outs = outs + [((2, SLOTS + 1, 16, CO), LOW)]
         elif step == 2:
             extra = []
         else:
-            extra = [pair, pair_far]
-            outs = outs[:1] * 2 + [((4, SLOTS * 16, CO), LOW), ((4, 16, CO), LOW)]
+            extra = [pair, pair_near]
+            outs = [((SLOTS, BLK, CO), LOW), ((4, SLOTS * 16, CO), LOW), ((4, 16, CO), LOW)]
         keep, *sends = call(
             functools.partial(fold_kernel, step),
             outs,
@@ -560,44 +577,44 @@
         )(at, *extra, keep, *gots)
         if step == 1:
             pair = sends.pop()
-            pair_far = swap(pair, MASK_FAR)
-    _, line, moments = sends
-    line_got = swap_mixed(line, (MASK_X, MASK_Y))
-    own_moment = call(
+            pair_near = swap(pair, MASK_NEAR)
+    line, moments = sends
+    line_one, line_two = swap(line, MASK_Y), swap(line, MASK_X)
+    own_moment, plan = call(
         moments_kernel,
-        [((16, 128), WIDE)],
+        [((BLK, 128), WIDE), ((NB,), jnp.int32)],
         [SMEM] * 2 + [VMEM] * 2,
+        out_specs=[VMEM, SMEM],
+        pin=False,
         scratch=[
             pltpu.VMEM((64, 128), WIDE),
             pltpu.VMEM((128, 128), WIDE),
             pltpu.SMEM((NB,), jnp.int32),
         ],
-    )(at, block_order, moments, swap(moments, MASK_CORE))[0]
-    scaled, plane = call(
+    )(at, block_order, moments, swap(moments, MASK_CORE))
+    *scaled, lines = call(
         moment_kernel,
-        [((SLOTS + 1, 16, CO), LOW), ((2, 4, SLOTS * 16, CO), LOW)],
-        [SMEM] * 2 + [VMEM] * 5,
+        [((count, BLK, CO), LOW) for _, count in GATHERED] + [((3, 4, SLOTS * 16, CO), LOW)],
+        [SMEM] * 2 + [VMEM] * 6,
         moved=2 << 20,
-    )(at, decay_rate, keep, swap(sends[0], MASK_FAR), own_moment, line, line_got)
-    plane_got = swap_mixed(plane, (MASK_Y, MASK_X))
+    )(at, decay_rate, keep, swap(keep, MASK_FAR), own_moment, line, line_one, line_two)
+    line_far = swap(line_one, MASK_X)
     natural = call(
         order_kernel, [((NB * BLK, CO), LOW)], [SMEM] * 2 + [VMEM] * 4, moved=8 << 20
-    )(at, block_order, plane, plane_got, swap(plane, MASK_CORE), swap(plane_got, MASK_CORE))[0]
-
-    pieces = [scaled, swap(scaled, MASK_FAR)]
-    for step in range(3, -1, -1):
-        after = (natural, at, plane_got, views)[step]
+    )(at, block_order, lines, line_far, swap(lines, MASK_CORE), swap(line_far, MASK_CORE))[0]
+
+    joined = scaled
+    for step in range(2, -1, -1):
+        pieces = []
+        for part, value in enumerate(joined):
+            pieces += [value, swap_part(value, part, step)]
         size = 256 >> step
         outs = [((count, size, CO), LOW) for _, count in GATHERED]
         if step == 0:
             outs = [((SLOTS + 1, size, CO), LOW)]
         joined = call(
             functools.partial(widen_kernel, step), outs, [SMEM, HBM] + [VMEM] * len(pieces)
-        )(at, after, *pieces)
-        if step > 0:
-            pieces = []
-            for part, value in enumerate(joined):
-                pieces += [value, swap_part(value, part, step - 1)]
+        )(at, (natural, line_far, views)[step], *pieces)
     mine = joined[0]
     peer = swap(mine, MASK_CORE)
     old = call(
@@ -615,25 +632,30 @@
         moved=4 << 20,
     )(at, views, mine)[0]
 
+    outs = [
+        ((NB // 8 * BLK, CO), WIDE),
+        ((NB // 8 * BLK, CO), WIDE),
+        ((7, 128), WIDE),
+        ((2, CO), WIDE),
+        ((PIX, CO), LOW),
+    ]
     update_rows, new_master, new_row, new_col, next_output = call(
         finish_kernel,
-        [
-            ((NB // 8 * BLK, CO), WIDE),
-            ((NB // 8 * BLK, CO), WIDE),
-            ((7, 128), WIDE),
-            ((2, CO), WIDE),
-            ((PIX, CO), LOW),
-        ],
+        outs,
         [SMEM] * 3 + [VMEM] * 8,
+        out_specs=[HBM] * 2 + [VMEM] * 3,
         scratch=[
             pltpu.VMEM((2, CO), WIDE),
             pltpu.VMEM((64, 128), WIDE),
+            pltpu.VMEM((NB // 8 * BLK, CO), WIDE),
+            pltpu.VMEM((NB // 8 * BLK, CO), WIDE),
+            pltpu.SemaphoreType.DMA((2,)),
         ],
         pin=False,
         flops=2 * 16 * 512 * 256 * 256,
         moved=16 << 20,
         room=16,
-    )(at, block_order, decay_rate, col_moment, views, natural, master_rows, mine, peer, old, half)
+    )(at, plan, decay_rate, col_moment, views, natural, master_rows, mine, peer, old, half)
     return (update_rows, new_master, new_row.reshape(-1), new_col, next_output)
 
 

time: 95.3 us -> 91.9 us (0.964)
  waiting for transfers between devices: 48.4 us -> 38 us
  starting transfers between devices: 20.7 us -> 26.9 us
    ppermute x11 -> x13, waiting for transfers between devices: 24.4 us -> 12.9 us  [swap(): return lax.ppermute(value, AXES, [(at, at ^ mask) for at in range(32)])]
    ppermute x11 -> x13, starting transfers between devices: 7.84 us -> 12 us  [swap(): return lax.ppermute(value, AXES, [(at, at ^ mask) for at in range(32)])]
    ppermute x14 -> x12, starting transfers between devices: 12.9 us -> 14.9 us  [swap_mixed(): lax.ppermute(value, AXES, [(at, at ^ masks[at & 1]) for at in range(32)])]
    pallas_call x3, Pallas kernels: 6.15 us -> 7.59 us  [the longest x1 3.91 us: shards(): call(finish_kernel, outs, [SMEM] * 3 + [VMEM] * 8, out_specs=[HBM] * 2 +...]
    ppermute x14 -> x12, waiting for transfers between devices: 24 us -> 25.2 us  [swap_mixed(): lax.ppermute(value, AXES, [(at, at ^ masks[at & 1]) for at in range(32)])]
    pallas_call x4 -> x3, Pallas kernels: 2.42 us -> 1.86 us  [shards(): call(functools.partial(widen_kernel, step), outs, [SMEM, HBM] + [VMEM] *...]
  transfers between devices with their start and end apart: 25 -> 25, of which waited for: 13 -> 13; matrix products, arithmetic and copies ran while one was open for 2% -> 2% of each run, Pallas kernels for 12% -> 14%
where the time goes in v6:
time: 91.9 us; the launch traced here: 91.7 us
  waiting for transfers between devices  38 us (41%)
  starting transfers between devices  26.9 us (29%)
  Pallas kernels  23.6 us (26%)
  between operations  1.61 us (2%)
  local copies, waits for them, and re-layouts  1.58 us (2%)
    ppermute x12, waiting for transfers between devices, swap_mixed(): lax.ppermute(value, AXES, [(at, at ^ masks[at & 1]) for at in range(32)])  25.2 us
    ppermute x12, starting transfers between devices, swap_mixed(): lax.ppermute(value, AXES, [(at, at ^ masks[at & 1]) for at in range(32)])  14.9 us
    ppermute x13, waiting for transfers between devices, swap(): return lax.ppermute(value, AXES, [(at, at ^ mask) for at in range(32)])  12.9 us
    ppermute x13, starting transfers between devices, swap(): return lax.ppermute(value, AXES, [(at, at ^ mask) for at in range(32)])  12 us
    pallas_call x1, Pallas kernels, shards(): call(term_kernel, [((SLOTS, 128, CO), LOW)] + [((count, 128, CO), LOW) fo...  3.92 us
    pallas_call x1, Pallas kernels, shards(): call(finish_kernel, outs, [SMEM] * 3 + [VMEM] * 8, out_specs=[HBM] * 2 +...  3.91 us
    pallas_call x1, Pallas kernels, shards(): call(moments_kernel, [((BLK, 128), WIDE), ((NB,), jnp.int32)], [SMEM] * 2...  2.69 us
    pallas_call x1, Pallas kernels, shards(): call(old_hidden_kernel, [((PIX, CO), WIDE)], [VMEM] * 2, flops=2 * 27 * 5...  2 us
  transfers between devices with their start and end apart: 25, of which 13 were waited for; matrix products, arithmetic and copies ran while one was open for 2% of the time, Pallas kernels for 14%

profile of v6, /device:TPU:0, one launch (start us, length us, event | category | flops | bytes accessed | tf_op | source)
XLA Modules:
  0.0 91.7 jit_solution(7566889531286456416)
XLA Ops:
  1.7 1.2 %copy.26 = bf16[1,4,18,18,256]{4,3,2,1,0:T(8,128)(2,1)S(1)} copy(bf16[1,4,18,18,256]{4,1,3,2,0:T(4,128)(2,1)} %param.12) | data formatting | bytes 1327104 | tf_op args[2]
  3.0 1.9 %shard_map.137.own = bf16[4480,256]{1,0:T(8,128)(2,1)S(1)} custom-call(s32[5]{0:T(128)S(1)} %stack.23.at, bf16[4,18,18,256]{3,2,1,0:T(8,128)(2,1)S(1)} %bitcast.16, bf16[512,256]{1,0:T(8,128)(2,1)} %pre_far.1, bf16[512,256]{1,0:T(8,128)(2,1)} %grad_far.3, bf16[256,256]{1,0:T(8,128)(2,1)} %pointwise_far.3), custom_call_target="tpu_custom_call" | custom-call | bytes 4194304 | tf_op jit(solution)/shard_map/pallas_call | solution.py:519
  5.1 3.9 %shard_map.138 = (bf16[14,128,256]{2,1,0:T(8,128)(2,1)S(1)}, bf16[10,128,256]{2,1,0:T(8,128)(2,1)S(1)}, bf16[4,128,256]{2,1,0:T(8,128)(2,1)S(1)}) custom-call(s32[5]{0:T(128)S(1)} %stack.23.at, bf16[4480,256]{1,0:T(8,128)(2,1)S(1)} %shard_map.137.own, bf16[4,18,18,256]{3,2,1,0:T(8,128)(2,1)S(1)} %bitcast.18, ...), custom_call_target="tpu_custom_call" | custom-call | flops 1879048192 | bytes 6291456 | tf_op jit(solution)/shard_map/pallas_call | solution.py:532
  9.0 2.6 %collective-permute-start.4 = (bf16[10,128,256]{2,1,0:T(8,128)(2,1)S(1)}, bf16[10,128,256]{2,1,0:T(8,128)(2,1)S(1)}, u32[]{:S(2)}, u32[]{:S(2)}) collective-permute-start(bf16[10,128,256]{2,1,0:T(8,128)(2,1)S(1)} %get-tuple-element.33), channel_id=1, source_target_pairs={{0,8},{1,17},{2,10},{3,19},{4,12},{5,21},{6,14},{7,23},{8,0},{9,25... | collective-permute-start | bytes 1966088 | tf_op jit(solution)/shard_map/ppermute | solution.py:143
  11.7 1.6 %collective-permute-start.5 = (bf16[4,128,256]{2,1,0:T(8,128)(2,1)S(1)}, bf16[4,128,256]{2,1,0:T(8,128)(2,1)S(1)}, u32[]{:S(2)}, u32[]{:S(2)}) collective-permute-start(bf16[4,128,256]{2,1,0:T(8,128)(2,1)S(1)} %get-tuple-element.34), channel_id=1, source_target_pairs={{0,2},{1,3},{2,0},{3,1},{4,6},{5,7},{6,4},{7,5},{8,10},{9,11},{10,... | collective-permute-start | bytes 786440 | tf_op jit(solution)/shard_map/ppermute | solution.py:143
  13.2 1.5 %shard_map.139.refs_0_ = bf16[15,16,256]{2,1,0:T(8,128)(2,1)S(1)} custom-call(s32[5]{0:T(128)S(1)} %stack.23.at, bf16[14,128,256]{2,1,0:T(8,128)(2,1)S(1)} %get-tuple-element.32.after.refs_2_, f32[896,256]{1,0:T(8,128)} %master.1, f32[7,128]{1,0:T(8,128)} %bitcast.19), custom_call_target="tpu_custom_call" | custom-call | tf_op jit(solution)/shard_map/pallas_call | solution.py:547
  14.8 2.6 %collective-permute-start.3 = (bf16[15,16,256]{2,1,0:T(8,128)(2,1)S(1)}, bf16[15,16,256]{2,1,0:T(8,128)(2,1)S(1)}, u32[]{:S(2)}, u32[]{:S(2)}) collective-permute-start(bf16[15,16,256]{2,1,0:T(8,128)(2,1)S(1)} %shard_map.139.refs_0_), channel_id=1, source_target_pairs={{0,4},{1,5},{2,6},{3,7},{4,0},{5,1},{6,2},{7,3},{8,12},{9,13},{10,... | collective-permute-start | bytes 368648 | tf_op jit(solution)/shard_map/ppermute | solution.py:139
  17.4 4.3 %collective-permute-done.3.refs_1_ = bf16[15,16,256]{2,1,0:T(8,128)(2,1)S(1)} collective-permute-done((bf16[15,16,256]{2,1,0:T(8,128)(2,1)S(1)}, bf16[15,16,256]{2,1,0:T(8,128)(2,1)S(1)}, u32[]{:S(2)}, u32[]{:S(2)}) %collective-permute-start.3) | collective-permute-done | bytes 122912 | tf_op jit(solution)/shard_map/ppermute | solution.py:139
  21.8 0.9 collective-permute-done.5.refs_4_
  24.1 1.3 %collective-permute-start.8 = (bf16[4,64,256]{2,1,0:T(8,128)(2,1)S(1)}, bf16[4,64,256]{2,1,0:T(8,128)(2,1)S(1)}, u32[]{:S(2)}, u32[]{:S(2)}) collective-permute-start(bf16[4,64,256]{2,1,0:T(8,128)(2,1)S(1)} %get-tuple-element.38), channel_id=1, source_target_pairs={{0,8},{1,9},{2,10},{3,11},{4,12},{5,13},{6,14},{7,15},{8,0},{9,1},... | collective-permute-start | bytes 393224 | tf_op jit(solution)/shard_map/ppermute | solution.py:143
  25.4 2.6 %collective-permute-start.6 = (bf16[2,15,16,256]{3,2,1,0:T(8,128)(2,1)S(1)}, bf16[2,15,16,256]{3,2,1,0:T(8,128)(2,1)S(1)}, u32[]{:S(2)}, u32[]{:S(2)}) collective-permute-start(bf16[2,15,16,256]{3,2,1,0:T(8,128)(2,1)S(1)} %get-tuple-element.35.refs_0_), channel_id=1, source_target_pairs={{0,2},{1,3},{2,0},{3,1},{4,6},{5,7},{6,4},{7,5},{8,10},{9,11},{10,... | collective-permute-start | bytes 737288 | tf_op jit(solution)/shard_map/ppermute | solution.py:139
  28.0 2.3 %collective-permute-done.8.refs_2_ = bf16[4,64,256]{2,1,0:T(8,128)(2,1)S(1)} collective-permute-done((bf16[4,64,256]{2,1,0:T(8,128)(2,1)S(1)}, bf16[4,64,256]{2,1,0:T(8,128)(2,1)S(1)}, u32[]{:S(2)}, u32[]{:S(2)}) %collective-permute-start.8) | collective-permute-done | bytes 131104 | tf_op jit(solution)/shard_map/ppermute | solution.py:143
  31.1 2.7 %collective-permute-start.9 = (bf16[10,32,256]{2,1,0:T(8,128)(2,1)S(1)}, bf16[10,32,256]{2,1,0:T(8,128)(2,1)S(1)}, u32[]{:S(2)}, u32[]{:S(2)}) collective-permute-start(bf16[10,32,256]{2,1,0:T(8,128)(2,1)S(1)} %get-tuple-element.40), channel_id=1, source_target_pairs={{0,2},{1,9},{2,0},{3,11},{4,6},{5,13},{6,4},{7,15},{8,10},{9,1},{1... | collective-permute-start | bytes 491528 | tf_op jit(solution)/shard_map/ppermute | solution.py:143
  34.9 3.1 %collective-permute-done.10.refs_4_ = bf16[4,32,256]{2,1,0:T(8,128)(2,1)S(1)} collective-permute-done((bf16[4,32,256]{2,1,0:T(8,128)(2,1)S(1)}, bf16[4,32,256]{2,1,0:T(8,128)(2,1)S(1)}, u32[]{:S(2)}, u32[]{:S(2)}) %collective-permute-start.10) | collective-permute-done | bytes 65568 | tf_op jit(solution)/shard_map/ppermute | solution.py:143
  38.6 1.3 %collective-permute-start.14 = (bf16[4,224,256]{2,1,0:T(8,128)(2,1)S(1)}, bf16[4,224,256]{2,1,0:T(8,128)(2,1)S(1)}, u32[]{:S(2)}, u32[]{:S(2)}) collective-permute-start(bf16[4,224,256]{2,1,0:T(8,128)(2,1)S(1)} %get-tuple-element.46.line), channel_id=1, source_target_pairs={{0,8},{1,9},{2,10},{3,11},{4,12},{5,13},{6,14},{7,15},{8,0},{9,1},... | collective-permute-start | bytes 1376264 | tf_op jit(solution)/shard_map/ppermute | solution.py:139
  40.7 1.6 %collective-permute-start.12 = (bf16[14,32,256]{2,1,0:T(8,128)(2,1)S(1)}, bf16[14,32,256]{2,1,0:T(8,128)(2,1)S(1)}, u32[]{:S(2)}, u32[]{:S(2)}) collective-permute-start(bf16[14,32,256]{2,1,0:T(8,128)(2,1)S(1)} %get-tuple-element.44.own), channel_id=1, source_target_pairs={{0,4},{1,5},{2,6},{3,7},{4,0},{5,1},{6,2},{7,3},{8,12},{9,13},{10,... | collective-permute-start | bytes 688136 | tf_op jit(solution)/shard_map/ppermute | solution.py:139
  43.5 2.7 %shard_map.143 = (f32[32,128]{1,0:T(8,128)S(1)}, s32[224]{0:T(256)S(1)}) custom-call(s32[5]{0:T(128)S(1)} %stack.23.at, s32[224]{0:T(256)S(1)} %copy-done.1, bf16[4,16,256]{2,1,0:T(8,128)(2,1)S(1)} %get-tuple-element.42.mine, bf16[4,16,256]{2,1,0:T(8,128)(2,1)S(1)} %collective-permute-done.11.peer), custom_call_target="tpu_custom_call" | custom-call | tf_op jit(solution)/shard_map/pallas_call | solution.py:583
  46.2 6.0 %collective-permute-done.12.got = bf16[14,32,256]{2,1,0:T(8,128)(2,1)S(1)} collective-permute-done((bf16[14,32,256]{2,1,0:T(8,128)(2,1)S(1)}, bf16[14,32,256]{2,1,0:T(8,128)(2,1)S(1)}, u32[]{:S(2)}, u32[]{:S(2)}) %collective-permute-start.12) | collective-permute-done | bytes 229408 | tf_op jit(solution)/shard_map/ppermute | solution.py:139
  52.2 1.0 %shard_map.145 = (bf16[10,32,256]{2,1,0:T(8,128)(2,1)S(1)}, bf16[5,32,256]{2,1,0:T(8,128)(2,1)S(1)}, bf16[3,4,224,256]{3,2,1,0:T(8,128)(2,1)S(1)}) custom-call(s32[5]{0:T(128)S(1)} %stack.23.at, f32[1]{0:T(128)S(6)} %sub.16.rate, bf16[14,32,256]{2,1,0:T(8,128)(2,1)S(1)} %get-tuple-element.44.own, bf16[14,32,256]{2,1,0:T(8,128)(2,1)S(1)} %collective-permute-done.12.got, ...), custom_call_target="tpu_custom_call" | custom-call | bytes 2097152 | tf_op jit(solution)/shard_map/pallas_call | solution.py:595
  53.9 1.0 %collective-permute-start.15 = (bf16[4,224,256]{2,1,0:T(8,128)(2,1)S(1)}, bf16[4,224,256]{2,1,0:T(8,128)(2,1)S(1)}, u32[]{:S(2)}, u32[]{:S(2)}) collective-permute-start(bf16[4,224,256]{2,1,0:T(8,128)(2,1)S(1)} %collective-permute-done.13.line_one), channel_id=1, source_target_pairs={{0,8},{1,9},{2,10},{3,11},{4,12},{5,13},{6,14},{7,15},{8,0},{9,1},... | collective-permute-start | bytes 1376264 | tf_op jit(solution)/shard_map/ppermute | solution.py:139
  54.9 0.9 %collective-permute-start.19 = (bf16[5,32,256]{2,1,0:T(8,128)(2,1)S(1)}, bf16[5,32,256]{2,1,0:T(8,128)(2,1)S(1)}, u32[]{:S(2)}, u32[]{:S(2)}) collective-permute-start(bf16[5,32,256]{2,1,0:T(8,128)(2,1)S(1)} %get-tuple-element.49.refs_2_), channel_id=1, source_target_pairs={{0,16},{1,17},{2,18},{3,19},{4,20},{5,21},{6,22},{7,23},{8,24},{9,... | collective-permute-start | bytes 245768 | tf_op jit(solution)/shard_map/ppermute | solution.py:143
  56.3 3.3 %collective-permute-done.19.refs_3_ = bf16[5,32,256]{2,1,0:T(8,128)(2,1)S(1)} collective-permute-done((bf16[5,32,256]{2,1,0:T(8,128)(2,1)S(1)}, bf16[5,32,256]{2,1,0:T(8,128)(2,1)S(1)}, u32[]{:S(2)}, u32[]{:S(2)}) %collective-permute-start.19) | collective-permute-done | bytes 81952 | tf_op jit(solution)/shard_map/ppermute | solution.py:143
  60.1 1.5 %collective-permute-start.20 = (bf16[10,64,256]{2,1,0:T(8,128)(2,1)S(1)}, bf16[10,64,256]{2,1,0:T(8,128)(2,1)S(1)}, u32[]{:S(2)}, u32[]{:S(2)}) collective-permute-start(bf16[10,64,256]{2,1,0:T(8,128)(2,1)S(1)} %get-tuple-element.50.refs_0_), channel_id=1, source_target_pairs={{0,16},{1,3},{2,18},{3,1},{4,20},{5,7},{6,22},{7,5},{8,24},{9,11},... | collective-permute-start | bytes 983048 | tf_op jit(solution)/shard_map/ppermute | solution.py:143
  61.6 1.0 %collective-permute-start.21 = (bf16[5,64,256]{2,1,0:T(8,128)(2,1)S(1)}, bf16[5,64,256]{2,1,0:T(8,128)(2,1)S(1)}, u32[]{:S(2)}, u32[]{:S(2)}) collective-permute-start(bf16[5,64,256]{2,1,0:T(8,128)(2,1)S(1)} %get-tuple-element.51.refs_2_), channel_id=1, source_target_pairs={{0,8},{1,9},{2,10},{3,11},{4,12},{5,13},{6,14},{7,15},{8,0},{9,1},... | collective-permute-start | bytes 491528 | tf_op jit(solution)/shard_map/ppermute | solution.py:143
  62.7 8.1 %collective-permute-done.21.refs_3_ = bf16[5,64,256]{2,1,0:T(8,128)(2,1)S(1)} collective-permute-done((bf16[5,64,256]{2,1,0:T(8,128)(2,1)S(1)}, bf16[5,64,256]{2,1,0:T(8,128)(2,1)S(1)}, u32[]{:S(2)}, u32[]{:S(2)}) %collective-permute-start.21) | collective-permute-done | bytes 163872 | tf_op jit(solution)/shard_map/ppermute | solution.py:143
  71.4 1.1 %collective-permute-start.22 = (bf16[10,128,256]{2,1,0:T(8,128)(2,1)S(1)}, bf16[10,128,256]{2,1,0:T(8,128)(2,1)S(1)}, u32[]{:S(2)}, u32[]{:S(2)}) collective-permute-start(bf16[10,128,256]{2,1,0:T(8,128)(2,1)S(1)} %get-tuple-element.52.refs_0_), channel_id=1, source_target_pairs={{0,8},{1,17},{2,10},{3,19},{4,12},{5,21},{6,14},{7,23},{8,0},{9,25... | collective-permute-start | bytes 1966088 | tf_op jit(solution)/shard_map/ppermute | solution.py:143
  73.7 1.2 %collective-permute-done.17.peer_far = bf16[4,224,256]{2,1,0:T(8,128)(2,1)S(1)} collective-permute-done((bf16[4,224,256]{2,1,0:T(8,128)(2,1)S(1)}, bf16[4,224,256]{2,1,0:T(8,128)(2,1)S(1)}, u32[]{:S(2)}, u32[]{:S(2)}) %collective-permute-start.17) | collective-permute-done | bytes 458784 | tf_op jit(solution)/shard_map/ppermute | solution.py:139
  74.9 1.0 %shard_map.146.after.natural = bf16[7168,256]{1,0:T(8,128)(2,1)S(1)} custom-call(s32[5]{0:T(128)S(1)} %stack.23.at, s32[224]{0:T(256)S(1)} %copy-done.1, bf16[3,4,224,256]{3,2,1,0:T(8,128)(2,1)S(1)} %get-tuple-element.47.mine, bf16[4,224,256]{2,1,0:T(8,128)(2,1)S(1)} %collective-permute-done.15.mine_far.after, ...), custom_call_target="tpu_custom_call" | custom-call | bytes 8388608 | tf_op jit(solution)/shard_map/pallas_call | solution.py:602
  75.8 7.2 %collective-permute-done.23.refs_3_ = bf16[5,128,256]{2,1,0:T(8,128)(2,1)S(1)} collective-permute-done((bf16[5,128,256]{2,1,0:T(8,128)(2,1)S(1)}, bf16[5,128,256]{2,1,0:T(8,128)(2,1)S(1)}, u32[]{:S(2)}, u32[]{:S(2)}) %collective-permute-start.23) | collective-permute-done | bytes 327712 | tf_op jit(solution)/shard_map/ppermute | solution.py:143
  83.8 1.7 %shard_map.151.own_part = f32[512,256]{1,0:T(8,128)S(1)} custom-call(s32[5]{0:T(128)S(1)} %stack.23.at, bf16[3456,256]{1,0:T(8,128)(2,1)S(1)} %shard_map.144.after.views, bf16[15,256,256]{2,1,0:T(8,128)(2,1)S(1)} %shard_map.149.scaled.mine), custom_call_target="tpu_custom_call" | custom-call | flops 939524096 | bytes 4194304 | tf_op jit(solution)/shard_map/pallas_call | solution.py:627
  85.5 2.0 %shard_map.150.old = f32[512,256]{1,0:T(8,128)S(1)} custom-call(bf16[3456,256]{1,0:T(8,128)(2,1)S(1)} %shard_map.144.after.views, bf16[7168,256]{1,0:T(8,128)(2,1)S(1)} %shard_map.146.after.natural), custom_call_target="tpu_custom_call" | custom-call | flops 1811939328 | bytes 6291456 | tf_op jit(solution)/shard_map/pallas_call | solution.py:620
  87.8 3.9 %shard_map.152 = (f32[896,256]{1,0:T(8,128)}, f32[896,256]{1,0:T(8,128)}, f32[7,128]{1,0:T(8,128)}, f32[2,256]{1,0:T(2,128)}, bf16[512,256]{1,0:T(8,128)(2,1)}) custom-call(s32[5]{0:T(128)S(1)} %stack.23.at, s32[224]{0:T(256)S(1)} %get-tuple-element.43.plan, f32[1]{0:T(128)S(6)} %sub.16.rate, f32[2,256]{1,0:T(2,128)S(1)} %copy-done.2, ...), custom_call_target="tpu_custom_call" | custom-call | flops 1073741824 | bytes 16777216 | tf_op jit(solution)/shard_map/pallas_call | solution.py:642
  (46 shorter events, 11.0 us)
Async XLA Ops:
  0.6 4.3 %collective-permute-start = (bf16[1,4,18,18,256]{4,1,3,2,0:T(4,128)(2,1)}, bf16[1,4,18,18,256]{4,1,3,2,0:T(4,128)(2,1)S(1)}, u32[]{:S(2)}, u32[]{:S(2)}) collective-permute-start(bf16[1,4,18,18,256]{4,1,3,2,0:T(4,128)(2,1)} %param.12), channel_id=1, source_target_pairs={{0,1},{1,0},{2,3},{3,2},{4,5},{5,4},{6,7},{7,6},{8,9},{9,8},{10,11... | collective-permute-start | bytes 1990664 | tf_op jit(solution)/shard_map/ppermute | solution.py:139
  1.1 3.9 %collective-permute-start.1 = (bf16[512,256]{1,0:T(8,128)(2,1)}, bf16[512,256]{1,0:T(8,128)(2,1)S(1)}, u32[]{:S(2)}, u32[]{:S(2)}) collective-permute-start(bf16[512,256]{1,0:T(8,128)(2,1)} %pre_far.1), channel_id=1, source_target_pairs={{0,1},{1,0},{2,3},{3,2},{4,5},{5,4},{6,7},{7,6},{8,9},{9,8},{10,11... | collective-permute-start | bytes 786440 | tf_op jit(solution)/shard_map/ppermute | solution.py:139
  1.2 3.9 %collective-permute-start.2 = (bf16[512,256]{1,0:T(8,128)(2,1)}, bf16[512,256]{1,0:T(8,128)(2,1)S(1)}, u32[]{:S(2)}, u32[]{:S(2)}) collective-permute-start(bf16[512,256]{1,0:T(8,128)(2,1)} %grad_far.3), channel_id=1, source_target_pairs={{0,1},{1,0},{2,3},{3,2},{4,5},{5,4},{6,7},{7,6},{8,9},{9,8},{10,11... | collective-permute-start | bytes 786440 | tf_op jit(solution)/shard_map/ppermute | solution.py:139
  9.0 13.6 %collective-permute-start.4 = (bf16[10,128,256]{2,1,0:T(8,128)(2,1)S(1)}, bf16[10,128,256]{2,1,0:T(8,128)(2,1)S(1)}, u32[]{:S(2)}, u32[]{:S(2)}) collective-permute-start(bf16[10,128,256]{2,1,0:T(8,128)(2,1)S(1)} %get-tuple-element.33), channel_id=1, source_target_pairs={{0,8},{1,17},{2,10},{3,19},{4,12},{5,21},{6,14},{7,23},{8,0},{9,25... | collective-permute-start | bytes 1966088 | tf_op jit(solution)/shard_map/ppermute | solution.py:143
  11.7 11.0 %collective-permute-start.5 = (bf16[4,128,256]{2,1,0:T(8,128)(2,1)S(1)}, bf16[4,128,256]{2,1,0:T(8,128)(2,1)S(1)}, u32[]{:S(2)}, u32[]{:S(2)}) collective-permute-start(bf16[4,128,256]{2,1,0:T(8,128)(2,1)S(1)} %get-tuple-element.34), channel_id=1, source_target_pairs={{0,2},{1,3},{2,0},{3,1},{4,6},{5,7},{6,4},{7,5},{8,10},{9,11},{10,... | collective-permute-start | bytes 786440 | tf_op jit(solution)/shard_map/ppermute | solution.py:143
  14.8 28.7 %copy-start.1 = (s32[224]{0:T(256)S(1)}, s32[224]{0:T(256)}, u32[]{:S(2)}) copy-start(s32[224]{0:T(256)} %block_order.3) | copy-start | bytes 2692
  14.8 7.0 %collective-permute-start.3 = (bf16[15,16,256]{2,1,0:T(8,128)(2,1)S(1)}, bf16[15,16,256]{2,1,0:T(8,128)(2,1)S(1)}, u32[]{:S(2)}, u32[]{:S(2)}) collective-permute-start(bf16[15,16,256]{2,1,0:T(8,128)(2,1)S(1)} %shard_map.139.refs_0_), channel_id=1, source_target_pairs={{0,4},{1,5},{2,6},{3,7},{4,0},{5,1},{6,2},{7,3},{8,12},{9,13},{10,... | collective-permute-start | bytes 368648 | tf_op jit(solution)/shard_map/ppermute | solution.py:139
  23.3 32.5 %copy-start.3 = (bf16[1,4,18,18,256]{4,1,3,2,0:T(4,128)(2,1)S(1)}, bf16[1,4,18,18,256]{4,1,3,2,0:T(4,128)(2,1)}, u32[]{:S(2)}) copy-start(bf16[1,4,18,18,256]{4,1,3,2,0:T(4,128)(2,1)} %param.19) | copy-start | bytes 1990660
  23.3 7.1 %collective-permute-start.7 = (bf16[10,64,256]{2,1,0:T(8,128)(2,1)S(1)}, bf16[10,64,256]{2,1,0:T(8,128)(2,1)S(1)}, u32[]{:S(2)}, u32[]{:S(2)}) collective-permute-start(bf16[10,64,256]{2,1,0:T(8,128)(2,1)S(1)} %get-tuple-element.37), channel_id=1, source_target_pairs={{0,16},{1,3},{2,18},{3,1},{4,20},{5,7},{6,22},{7,5},{8,24},{9,11},... | collective-permute-start | bytes 983048 | tf_op jit(solution)/shard_map/ppermute | solution.py:143
  24.1 6.2 %collective-permute-start.8 = (bf16[4,64,256]{2,1,0:T(8,128)(2,1)S(1)}, bf16[4,64,256]{2,1,0:T(8,128)(2,1)S(1)}, u32[]{:S(2)}, u32[]{:S(2)}) collective-permute-start(bf16[4,64,256]{2,1,0:T(8,128)(2,1)S(1)} %get-tuple-element.38), channel_id=1, source_target_pairs={{0,8},{1,9},{2,10},{3,11},{4,12},{5,13},{6,14},{7,15},{8,0},{9,1},... | collective-permute-start | bytes 393224 | tf_op jit(solution)/shard_map/ppermute | solution.py:143
  25.4 9.5 %collective-permute-start.6 = (bf16[2,15,16,256]{3,2,1,0:T(8,128)(2,1)S(1)}, bf16[2,15,16,256]{3,2,1,0:T(8,128)(2,1)S(1)}, u32[]{:S(2)}, u32[]{:S(2)}) collective-permute-start(bf16[2,15,16,256]{3,2,1,0:T(8,128)(2,1)S(1)} %get-tuple-element.35.refs_0_), channel_id=1, source_target_pairs={{0,2},{1,3},{2,0},{3,1},{4,6},{5,7},{6,4},{7,5},{8,10},{9,11},{10,... | collective-permute-start | bytes 737288 | tf_op jit(solution)/shard_map/ppermute | solution.py:139
  31.1 6.9 %collective-permute-start.9 = (bf16[10,32,256]{2,1,0:T(8,128)(2,1)S(1)}, bf16[10,32,256]{2,1,0:T(8,128)(2,1)S(1)}, u32[]{:S(2)}, u32[]{:S(2)}) collective-permute-start(bf16[10,32,256]{2,1,0:T(8,128)(2,1)S(1)} %get-tuple-element.40), channel_id=1, source_target_pairs={{0,2},{1,9},{2,0},{3,11},{4,6},{5,13},{6,4},{7,15},{8,10},{9,1},{1... | collective-permute-start | bytes 491528 | tf_op jit(solution)/shard_map/ppermute | solution.py:143
  33.7 4.3 %collective-permute-start.10 = (bf16[4,32,256]{2,1,0:T(8,128)(2,1)S(1)}, bf16[4,32,256]{2,1,0:T(8,128)(2,1)S(1)}, u32[]{:S(2)}, u32[]{:S(2)}) collective-permute-start(bf16[4,32,256]{2,1,0:T(8,128)(2,1)S(1)} %get-tuple-element.41), channel_id=1, source_target_pairs={{0,16},{1,17},{2,18},{3,19},{4,20},{5,21},{6,22},{7,23},{8,24},{9,... | collective-permute-start | bytes 196616 | tf_op jit(solution)/shard_map/ppermute | solution.py:143
  38.6 13.5 %collective-permute-start.14 = (bf16[4,224,256]{2,1,0:T(8,128)(2,1)S(1)}, bf16[4,224,256]{2,1,0:T(8,128)(2,1)S(1)}, u32[]{:S(2)}, u32[]{:S(2)}) collective-permute-start(bf16[4,224,256]{2,1,0:T(8,128)(2,1)S(1)} %get-tuple-element.46.line), channel_id=1, source_target_pairs={{0,8},{1,9},{2,10},{3,11},{4,12},{5,13},{6,14},{7,15},{8,0},{9,1},... | collective-permute-start | bytes 1376264 | tf_op jit(solution)/shard_map/ppermute | solution.py:139
  39.9 12.3 %collective-permute-start.13 = (bf16[4,224,256]{2,1,0:T(8,128)(2,1)S(1)}, bf16[4,224,256]{2,1,0:T(8,128)(2,1)S(1)}, u32[]{:S(2)}, u32[]{:S(2)}) collective-permute-start(bf16[4,224,256]{2,1,0:T(8,128)(2,1)S(1)} %get-tuple-element.46.line), channel_id=1, source_target_pairs={{0,16},{1,17},{2,18},{3,19},{4,20},{5,21},{6,22},{7,23},{8,24},{9,... | collective-permute-start | bytes 1376264 | tf_op jit(solution)/shard_map/ppermute | solution.py:139
  40.7 11.5 %collective-permute-start.12 = (bf16[14,32,256]{2,1,0:T(8,128)(2,1)S(1)}, bf16[14,32,256]{2,1,0:T(8,128)(2,1)S(1)}, u32[]{:S(2)}, u32[]{:S(2)}) collective-permute-start(bf16[14,32,256]{2,1,0:T(8,128)(2,1)S(1)} %get-tuple-element.44.own), channel_id=1, source_target_pairs={{0,4},{1,5},{2,6},{3,7},{4,0},{5,1},{6,2},{7,3},{8,12},{9,13},{10,... | collective-permute-start | bytes 688136 | tf_op jit(solution)/shard_map/ppermute | solution.py:139
  42.3 1.2 %collective-permute-start.11 = (bf16[4,16,256]{2,1,0:T(8,128)(2,1)S(1)}, bf16[4,16,256]{2,1,0:T(8,128)(2,1)S(1)}, u32[]{:S(2)}, u32[]{:S(2)}) collective-permute-start(bf16[4,16,256]{2,1,0:T(8,128)(2,1)S(1)} %get-tuple-element.42.mine), channel_id=1, source_target_pairs={{0,1},{1,0},{2,3},{3,2},{4,5},{5,4},{6,7},{7,6},{8,9},{9,8},{10,11... | collective-permute-start | bytes 98312 | tf_op jit(solution)/shard_map/ppermute | solution.py:139
  53.2 21.7 %collective-permute-start.16 = (bf16[3,4,224,256]{3,2,1,0:T(8,128)(2,1)S(1)}, bf16[3,4,224,256]{3,2,1,0:T(8,128)(2,1)S(1)}, u32[]{:S(2)}, u32[]{:S(2)}) collective-permute-start(bf16[3,4,224,256]{3,2,1,0:T(8,128)(2,1)S(1)} %get-tuple-element.47.mine), channel_id=1, source_target_pairs={{0,1},{1,0},{2,3},{3,2},{4,5},{5,4},{6,7},{7,6},{8,9},{9,8},{10,11... | collective-permute-start | bytes 4128776 | tf_op jit(solution)/shard_map/ppermute | solution.py:139
  53.2 6.3 %collective-permute-start.18 = (bf16[10,32,256]{2,1,0:T(8,128)(2,1)S(1)}, bf16[10,32,256]{2,1,0:T(8,128)(2,1)S(1)}, u32[]{:S(2)}, u32[]{:S(2)}) collective-permute-start(bf16[10,32,256]{2,1,0:T(8,128)(2,1)S(1)} %get-tuple-element.48.refs_0_), channel_id=1, source_target_pairs={{0,2},{1,9},{2,0},{3,11},{4,6},{5,13},{6,4},{7,15},{8,10},{9,1},{1... | collective-permute-start | bytes 491528 | tf_op jit(solution)/shard_map/ppermute | solution.py:143
  53.9 16.9 %collective-permute-start.15 = (bf16[4,224,256]{2,1,0:T(8,128)(2,1)S(1)}, bf16[4,224,256]{2,1,0:T(8,128)(2,1)S(1)}, u32[]{:S(2)}, u32[]{:S(2)}) collective-permute-start(bf16[4,224,256]{2,1,0:T(8,128)(2,1)S(1)} %collective-permute-done.13.line_one), channel_id=1, source_target_pairs={{0,8},{1,9},{2,10},{3,11},{4,12},{5,13},{6,14},{7,15},{8,0},{9,1},... | collective-permute-start | bytes 1376264 | tf_op jit(solution)/shard_map/ppermute | solution.py:139
  54.9 4.7 %collective-permute-start.19 = (bf16[5,32,256]{2,1,0:T(8,128)(2,1)S(1)}, bf16[5,32,256]{2,1,0:T(8,128)(2,1)S(1)}, u32[]{:S(2)}, u32[]{:S(2)}) collective-permute-start(bf16[5,32,256]{2,1,0:T(8,128)(2,1)S(1)} %get-tuple-element.49.refs_2_), channel_id=1, source_target_pairs={{0,16},{1,17},{2,18},{3,19},{4,20},{5,21},{6,22},{7,23},{8,24},{9,... | collective-permute-start | bytes 245768 | tf_op jit(solution)/shard_map/ppermute | solution.py:143
  60.1 10.6 %collective-permute-start.20 = (bf16[10,64,256]{2,1,0:T(8,128)(2,1)S(1)}, bf16[10,64,256]{2,1,0:T(8,128)(2,1)S(1)}, u32[]{:S(2)}, u32[]{:S(2)}) collective-permute-start(bf16[10,64,256]{2,1,0:T(8,128)(2,1)S(1)} %get-tuple-element.50.refs_0_), channel_id=1, source_target_pairs={{0,16},{1,3},{2,18},{3,1},{4,20},{5,7},{6,22},{7,5},{8,24},{9,11},... | collective-permute-start | bytes 983048 | tf_op jit(solution)/shard_map/ppermute | solution.py:143
  61.6 9.1 %collective-permute-start.21 = (bf16[5,64,256]{2,1,0:T(8,128)(2,1)S(1)}, bf16[5,64,256]{2,1,0:T(8,128)(2,1)S(1)}, u32[]{:S(2)}, u32[]{:S(2)}) collective-permute-start(bf16[5,64,256]{2,1,0:T(8,128)(2,1)S(1)} %get-tuple-element.51.refs_2_), channel_id=1, source_target_pairs={{0,8},{1,9},{2,10},{3,11},{4,12},{5,13},{6,14},{7,15},{8,0},{9,1},... | collective-permute-start | bytes 491528 | tf_op jit(solution)/shard_map/ppermute | solution.py:143
  71.4 11.6 %collective-permute-start.22 = (bf16[10,128,256]{2,1,0:T(8,128)(2,1)S(1)}, bf16[10,128,256]{2,1,0:T(8,128)(2,1)S(1)}, u32[]{:S(2)}, u32[]{:S(2)}) collective-permute-start(bf16[10,128,256]{2,1,0:T(8,128)(2,1)S(1)} %get-tuple-element.52.refs_0_), channel_id=1, source_target_pairs={{0,8},{1,17},{2,10},{3,19},{4,12},{5,21},{6,14},{7,23},{8,0},{9,25... | collective-permute-start | bytes 1966088 | tf_op jit(solution)/shard_map/ppermute | solution.py:143
  72.5 2.3 %collective-permute-start.17 = (bf16[4,224,256]{2,1,0:T(8,128)(2,1)S(1)}, bf16[4,224,256]{2,1,0:T(8,128)(2,1)S(1)}, u32[]{:S(2)}, u32[]{:S(2)}) collective-permute-start(bf16[4,224,256]{2,1,0:T(8,128)(2,1)S(1)} %collective-permute-done.15.mine_far.after), channel_id=1, source_target_pairs={{0,1},{1,0},{2,3},{3,2},{4,5},{5,4},{6,7},{7,6},{8,9},{9,8},{10,11... | collective-permute-start | bytes 1376264 | tf_op jit(solution)/shard_map/ppermute | solution.py:139
  73.4 9.6 %collective-permute-start.23 = (bf16[5,128,256]{2,1,0:T(8,128)(2,1)S(1)}, bf16[5,128,256]{2,1,0:T(8,128)(2,1)S(1)}, u32[]{:S(2)}, u32[]{:S(2)}) collective-permute-start(bf16[5,128,256]{2,1,0:T(8,128)(2,1)S(1)} %get-tuple-element.53.refs_2_), channel_id=1, source_target_pairs={{0,2},{1,3},{2,0},{3,1},{4,6},{5,7},{6,4},{7,5},{8,10},{9,11},{10,... | collective-permute-start | bytes 983048 | tf_op jit(solution)/shard_map/ppermute | solution.py:143
  83.7 4.0 %collective-permute-start.24 = (bf16[15,256,256]{2,1,0:T(8,128)(2,1)S(1)}, bf16[15,256,256]{2,1,0:T(8,128)(2,1)S(1)}, u32[]{:S(2)}, u32[]{:S(2)}) collective-permute-start(bf16[15,256,256]{2,1,0:T(8,128)(2,1)S(1)} %shard_map.149.scaled.mine), channel_id=1, source_target_pairs={{0,1},{1,0},{2,3},{3,2},{4,5},{5,4},{6,7},{7,6},{8,9},{9,8},{10,11... | collective-permute-start | bytes 5898248 | tf_op jit(solution)/shard_map/ppermute | solution.py:139
  85.5 2.3 %copy-start = (f32[896,256]{1,0:T(8,128)S(1)}, f32[896,256]{1,0:T(8,128)}, u32[]{:S(2)}) copy-start(f32[896,256]{1,0:T(8,128)} %master.1) | copy-start | bytes 2752516
  85.5 2.3 %copy-start.2 = (f32[2,256]{1,0:T(2,128)S(1)}, f32[2,256]{1,0:T(2,128)}, u32[]{:S(2)}) copy-start(f32[2,256]{1,0:T(2,128)} %col_moment.1) | copy-start | bytes 6148

commit v7 on v6

--- a/solution.py
+++ b/solution.py
@@ -129,7 +129,7 @@
 HBM = pl.BlockSpec(memory_space=pl.ANY)
 MASK_CORE, MASK_NEAR, MASK_FAR, MASK_X, MASK_Y = 1, 2, 4, 8, 16
 PARTS = ((0, 10), (10, 4))
-ORDERS = (((0, 1, 2), (1, 2, 0)), ((2, 0, 1), (2, 0, 1)))
+ORDERS = (((0, 1, 2), (1, 2, 0)), ((2, 0, 1), (2, 1, 0)))
 MESSAGE = SLOTS
 GATHERED = ((0, 10), (10, 5))
 MASKS = (MASK_X, MASK_Y, MASK_NEAR)
@@ -179,11 +179,14 @@
     store_shifted(tile, out)
 
 
-def slope_of(pre, grad, pointwise):
+def store_factors_of(pre, grad, pointwise, out):
+    values = pre[...].astype(WIDE)
+    sigma = jax.nn.sigmoid(values)
     grad_act = lax.dot_general(
-        grad, pointwise, (((1,), (1,)), ((), ())), preferred_element_type=WIDE
-    )
-    return (grad_act * silu_slope(pre.astype(WIDE))).astype(LOW)
+        grad[...], pointwise[...], (((1,), (1,)), ((), ())), preferred_element_type=WIDE
+    )
+    out[SLOPES:ACTS] = (grad_act * (sigma * (1.0 + values * (1.0 - sigma)))).astype(LOW)
+    out[ACTS:] = (values * sigma).astype(LOW)
 
 
 def view_start(tap, frame):
@@ -207,13 +210,14 @@
     return copies
 
 
-def own_kernel(at, tile, pre_far, grad_far, pointwise_far, brought, pre, grad, pointwise, arrived):
+def own_kernel(
+    at, tile, pre_far, grad_far, pointwise_far, brought, grad, pointwise, pre, arrived
+):
     copies = fetch(((pre_far, pre), (grad_far, grad), (pointwise_far, pointwise)), arrived)
     store_shifted(tile, brought)
     for copy in copies:
         copy.wait()
-    brought[SLOPES:ACTS] = slope_of(pre[...], grad[...], pointwise[...])
-    brought[ACTS:] = jax.nn.silu(pre[...].astype(WIDE)).astype(LOW)
+    store_factors_of(pre, grad, pointwise, brought)
 
 
 def pack_kernel(at, after, master_far, row_moment_far, packed, master, row_moment, arrived):
@@ -234,18 +238,14 @@
 
 
 def term_kernel(
-    at, own, tile_peer, pre_peer, grad_peer, grad_far, pointwise_far,
-    keep, send_one, send_two, peer, rights, pointwise, arrived,
+    at, own, tile_peer, pre_peer, grad_peer, grad, pointwise, keep, send_one, send_two, peer, rights
 ):
     core = at[4]
-    copies = fetch(((grad_far, rights.at[1, pl.ds(0, PIX), :]), (pointwise_far, pointwise)), arrived)
     store_shifted(tile_peer, peer)
-    peer[ACTS:] = jax.nn.silu(pre_peer[...].astype(WIDE)).astype(LOW)
-    for copy in copies:
-        copy.wait()
-    peer[SLOPES:ACTS] = slope_of(pre_peer[...], grad_peer[...], pointwise[...])
+    store_factors_of(pre_peer, grad_peer, pointwise, peer)
     rights[0, :PIX] = own[SLOPES:ACTS]
     rights[0, PIX:] = peer[SLOPES:ACTS]
+    rights[1, :PIX] = grad[...]
     rights[1, PIX:] = grad_peer[...]
     for slot in range(SLOTS):
         pieces = []
@@ -353,7 +353,7 @@
         half = (block >= 8 * SLOTS).astype(jnp.int32)
         slot, place = (block - half * (8 * SLOTS)) // 8, lax.rem(block, 8)
         high, middle, low = place // 4, lax.rem(place // 2, 2), lax.rem(place, 2)
-        other = jnp.where(half == 0, low * 4 + high * 2 + middle, middle * 4 + low * 2 + high)
+        other = jnp.where(half == 0, low * 4 + high * 2 + middle, middle * 4 + high * 2 + low)
         sender = jnp.where(slot < PARTS[1][0], other, place)
         side = half ^ core
         plan[local * 8] = side
@@ -388,23 +388,32 @@
     out[...] = jnp.transpose(rows[...])[:BLK]
 
 
-def order_kernel(at, block_order, mine, mine_far, peer, peer_far, out):
+def order_kernel(at, block_order, mine, mine_low, mine_high, peer, peer_low, peer_high, out):
     count = NB // 8
     quarters = count // 4
-    for flip_core, (pieces, far) in enumerate(((mine, mine_far), (peer, peer_far))):
+    for flip_core, (pieces, low, high) in enumerate(
+        ((mine, mine_low, mine_high), (peer, peer_low, peer_high))
+    ):
         core = at[4] ^ flip_core
-        for index, piece in enumerate((pieces.at[0], pieces.at[1], pieces.at[2], far)):
-            quarter = (at[1] ^ (index % 2)) * 2 + (at[0] ^ (index // 2))
+        for index in range(4):
+            flip_x = jnp.where(core == 0, index // 2, index % 2)
+            quarter = (at[1] ^ (index // 2) ^ (index % 2) ^ flip_x) * 2 + (at[0] ^ flip_x)
             for local in range(quarters):
                 for line in range(4):
                     block = block_order[(line * 2 + core) * count + quarter * quarters + local]
                     to = pl.ds(pl.multiple_of(block * BLK, BLK), BLK)
-                    out[to, :] = piece[line, local * BLK : local * BLK + BLK]
+                    rows = slice(local * BLK, local * BLK + BLK)
+                    if index < 3:
+                        out[to, :] = pieces[index, line, rows]
+                    else:
+                        out[to, :] = (low, high)[line // 2][line % 2, rows]
 
 
 def widen_kernel(step, at, after, *refs):
     size = 256 >> (step + 1)
     ins, outs = refs[:4], refs[4:]
+    if step == 1:
+        outs[2][...], outs[3][...] = after[:2], after[2:]
     for part, (first, count) in enumerate(GATHERED):
         mine = place_of(at, part, step)
         for index, which in enumerate((mine, 1 - mine)):
@@ -464,6 +473,7 @@
     store_factors(total, rate[0], col_moment, new_col, factor)
 
     lane = lax.broadcasted_iota(jnp.int32, (1, 128), 1)
+    copies = []
     for line in range(7):
         values = jnp.zeros((1, 128), WIDE)
         for part in range(4):
@@ -481,7 +491,12 @@
             turned = pltpu.roll(row_table[pl.ds(from_row, 1), :], turn, 1)
             values = jnp.where(here, turned, values)
         new_row[line : line + 1] = values
-    copies = fetch(((update_rows, update_far), (new_master, master_far)), stored)
+        there = pl.ds(line * 4 * BLK, 4 * BLK)
+        pairs = ((update_rows, update_far), (new_master, master_far))
+        copies += fetch(
+            [(source.at[there, :], target.at[there, :]) for source, target in pairs],
+            stored.at[line],
+        )
 
     change = own_part[...] + add_taps(views, peer, 1 - core)
     hidden = old[...] - (learn_rate * factor[0:1]) * change
@@ -516,33 +531,23 @@
     pre_peer = swap(pre_act, MASK_CORE)
     grad_peer = swap(grad_output, MASK_CORE)
     rows_far = [far_away(array) for array in (pre_act, grad_output, pointwise_live)]
-    brought = call(
+    brought, grad_near, pointwise_near = call(
         own_kernel,
-        [((BROUGHT, CI), LOW)],
+        [((BROUGHT, CI), LOW), ((PIX, CO), LOW), ((CO, CO), LOW)],
         [SMEM, VMEM] + [HBM] * 3,
-        scratch=[
-            pltpu.VMEM((PIX, CO), LOW),
-            pltpu.VMEM((PIX, CO), LOW),
-            pltpu.VMEM((CO, CO), LOW),
-            pltpu.SemaphoreType.DMA((3,)),
-        ],
+        scratch=[pltpu.VMEM((PIX, CO), LOW), pltpu.SemaphoreType.DMA((3,))],
         moved=4 << 20,
-    )(at, saved_tiles[0], *rows_far)[0]
+    )(at, saved_tiles[0], *rows_far)
 
     keep, *sends = call(
         term_kernel,
         [((SLOTS, 128, CO), LOW)] + [((count, 128, CO), LOW) for _, count in PARTS],
-        [SMEM] + [VMEM] * 4 + [HBM] * 2,
-        scratch=[
-            pltpu.VMEM((BROUGHT, CI), LOW),
-            pltpu.VMEM((2, 2 * PIX, CO), LOW),
-            pltpu.VMEM((CO, CO), LOW),
-            pltpu.SemaphoreType.DMA((2,)),
-        ],
+        [SMEM] + [VMEM] * 6,
+        scratch=[pltpu.VMEM((BROUGHT, CI), LOW), pltpu.VMEM((2, 2 * PIX, CO), LOW)],
         flops=2 * 14 * 1024 * 256 * 256,
         moved=6 << 20,
         room=12,
-    )(at, brought, tile_peer[0], pre_peer, grad_peer, *rows_far[1:])
+    )(at, brought, tile_peer[0], pre_peer, grad_peer, grad_near, pointwise_near)
 
     packed = call(
         pack_kernel,
@@ -579,7 +584,7 @@
             pair = sends.pop()
             pair_near = swap(pair, MASK_NEAR)
     line, moments = sends
-    line_one, line_two = swap(line, MASK_Y), swap(line, MASK_X)
+    line_one, line_two = swap_mixed(line, (MASK_Y, MASK_X)), swap_mixed(line, (MASK_X, MASK_Y))
     own_moment, plan = call(
         moments_kernel,
         [((BLK, 128), WIDE), ((NB,), jnp.int32)],
@@ -598,12 +603,8 @@
         [SMEM] * 2 + [VMEM] * 6,
         moved=2 << 20,
     )(at, decay_rate, keep, swap(keep, MASK_FAR), own_moment, line, line_one, line_two)
-    line_far = swap(line_one, MASK_X)
-    natural = call(
-        order_kernel, [((NB * BLK, CO), LOW)], [SMEM] * 2 + [VMEM] * 4, moved=8 << 20
-    )(at, block_order, lines, line_far, swap(lines, MASK_CORE), swap(line_far, MASK_CORE))[0]
-
-    joined = scaled
+    line_far = swap_mixed(line_one, (MASK_X, MASK_Y))
+    joined, natural = scaled, None
     for step in range(2, -1, -1):
         pieces = []
         for part, value in enumerate(joined):
@@ -612,9 +613,19 @@
         outs = [((count, size, CO), LOW) for _, count in GATHERED]
         if step == 0:
             outs = [((SLOTS + 1, size, CO), LOW)]
+        if step == 1:
+            outs = outs + [((2, SLOTS * 16, CO), LOW)] * 2
         joined = call(
-            functools.partial(widen_kernel, step), outs, [SMEM, HBM] + [VMEM] * len(pieces)
+            functools.partial(widen_kernel, step),
+            outs,
+            [SMEM, VMEM if step == 1 else HBM] + [VMEM] * len(pieces),
         )(at, (natural, line_far, views)[step], *pieces)
+        if step == 1:
+            parts = [lines, *joined[2:]]
+            joined = joined[:2]
+            natural = call(
+                order_kernel, [((NB * BLK, CO), LOW)], [SMEM] * 2 + [VMEM] * 6, moved=8 << 20
+            )(at, block_order, *parts, *[swap(part, MASK_CORE) for part in parts])[0]
     mine = joined[0]
     peer = swap(mine, MASK_CORE)
     old = call(
@@ -649,7 +660,7 @@
             pltpu.VMEM((64, 128), WIDE),
             pltpu.VMEM((NB // 8 * BLK, CO), WIDE),
             pltpu.VMEM((NB // 8 * BLK, CO), WIDE),
-            pltpu.SemaphoreType.DMA((2,)),
+            pltpu.SemaphoreType.DMA((7, 2)),
         ],
         pin=False,
         flops=2 * 16 * 512 * 256 * 256,

time: 91.9 us -> 89.4 us (0.973)
  waiting for transfers between devices: 38 us -> 35.9 us
    ppermute x12 -> x15, starting transfers between devices: 14.9 us -> 17.9 us  [swap_mixed(): lax.ppermute(value, AXES, [(at, at ^ masks[at & 1]) for at in range(32)])]
    ppermute x13 -> x11, starting transfers between devices: 12 us -> 9.16 us  [swap(): return lax.ppermute(value, AXES, [(at, at ^ mask) for at in range(32)])]
    ppermute x12 -> x15, waiting for transfers between devices: 25.2 us -> 23 us  [swap_mixed(): lax.ppermute(value, AXES, [(at, at ^ masks[at & 1]) for at in range(32)])]
    ppermute x13 -> x11, waiting for transfers between devices: 12.9 us -> 12.9 us  [swap(): return lax.ppermute(value, AXES, [(at, at ^ mask) for at in range(32)])]
  transfers between devices with their start and end apart: 25 -> 26, of which waited for: 13 -> 16; matrix products, arithmetic and copies ran while one was open for 2% -> 2% of each run, Pallas kernels for 14% -> 14%
where the time goes in v7:
time: 89.4 us; the launch traced here: 89.2 us
  waiting for transfers between devices  35.9 us (40%)
  starting transfers between devices  27.1 us (30%)
  Pallas kernels  23 us (26%)
  between operations  1.61 us (2%)
  local copies, waits for them, and re-layouts  1.58 us (2%)
    ppermute x15, waiting for transfers between devices, swap_mixed(): lax.ppermute(value, AXES, [(at, at ^ masks[at & 1]) for at in range(32)])  23 us
    ppermute x15, starting transfers between devices, swap_mixed(): lax.ppermute(value, AXES, [(at, at ^ masks[at & 1]) for at in range(32)])  17.9 us
    ppermute x11, waiting for transfers between devices, swap(): return lax.ppermute(value, AXES, [(at, at ^ mask) for at in range(32)])  12.9 us
    ppermute x11, starting transfers between devices, swap(): return lax.ppermute(value, AXES, [(at, at ^ mask) for at in range(32)])  9.16 us
    pallas_call x1, Pallas kernels, shards(): call(finish_kernel, outs, [SMEM] * 3 + [VMEM] * 8, out_specs=[HBM] * 2 +...  3.71 us
    pallas_call x1, Pallas kernels, shards(): call(term_kernel, [((SLOTS, 128, CO), LOW)] + [((count, 128, CO), LOW) fo...  3.53 us
    pallas_call x1, Pallas kernels, shards(): call(moments_kernel, [((BLK, 128), WIDE), ((NB,), jnp.int32)], [SMEM] * 2...  2.67 us
    pallas_call x1, Pallas kernels, shards(): call(old_hidden_kernel, [((PIX, CO), WIDE)], [VMEM] * 2, flops=2 * 27 * 5...  1.99 us
  transfers between devices with their start and end apart: 26, of which 16 were waited for; matrix products, arithmetic and copies ran while one was open for 2% of the time, Pallas kernels for 14%

profile of v7, /device:TPU:0, one launch (start us, length us, event | category | flops | bytes accessed | tf_op | source)
XLA Modules:
  0.0 89.2 jit_solution(14657733411881905626)
XLA Ops:
  1.7 1.2 %copy.26 = bf16[1,4,18,18,256]{4,3,2,1,0:T(8,128)(2,1)S(1)} copy(bf16[1,4,18,18,256]{4,1,3,2,0:T(4,128)(2,1)} %param.12) | data formatting | bytes 1327104 | tf_op args[2]
  3.0 1.9 %shard_map.137 = (bf16[4480,256]{1,0:T(8,128)(2,1)S(1)}, bf16[512,256]{1,0:T(8,128)(2,1)S(1)}, bf16[256,256]{1,0:T(8,128)(2,1)S(1)}) custom-call(s32[5]{0:T(128)S(1)} %stack.23.at, bf16[4,18,18,256]{3,2,1,0:T(8,128)(2,1)S(1)} %bitcast.16, bf16[512,256]{1,0:T(8,128)(2,1)} %pre_far.1, bf16[512,256]{1,0:T(8,128)(2,1)} %grad_far.1, bf16[256,256]{1,0:T(8,128)(2,1)} %pointwise_far.1), custom_call_target="tpu_custom_call" | custom-call | bytes 4194304 | tf_op jit(solution)/shard_map/pallas_call | solution.py:534
  5.1 3.5 %shard_map.138 = (bf16[14,128,256]{2,1,0:T(8,128)(2,1)S(1)}, bf16[10,128,256]{2,1,0:T(8,128)(2,1)S(1)}, bf16[4,128,256]{2,1,0:T(8,128)(2,1)S(1)}) custom-call(s32[5]{0:T(128)S(1)} %stack.23.at, bf16[4480,256]{1,0:T(8,128)(2,1)S(1)} %get-tuple-element.37.own, bf16[4,18,18,256]{3,2,1,0:T(8,128)(2,1)S(1)} %bitcast.18, ...), custom_call_target="tpu_custom_call" | custom-call | flops 1879048192 | bytes 6291456 | tf_op jit(solution)/shard_map/pallas_call | solution.py:542
  8.7 2.6 %collective-permute-start.4 = (bf16[10,128,256]{2,1,0:T(8,128)(2,1)S(1)}, bf16[10,128,256]{2,1,0:T(8,128)(2,1)S(1)}, u32[]{:S(2)}, u32[]{:S(2)}) collective-permute-start(bf16[10,128,256]{2,1,0:T(8,128)(2,1)S(1)} %get-tuple-element.41), channel_id=1, source_target_pairs={{0,8},{1,17},{2,10},{3,19},{4,12},{5,21},{6,14},{7,23},{8,0},{9,25... | collective-permute-start | bytes 1966088 | tf_op jit(solution)/shard_map/ppermute | solution.py:143
  11.3 1.6 %collective-permute-start.5 = (bf16[4,128,256]{2,1,0:T(8,128)(2,1)S(1)}, bf16[4,128,256]{2,1,0:T(8,128)(2,1)S(1)}, u32[]{:S(2)}, u32[]{:S(2)}) collective-permute-start(bf16[4,128,256]{2,1,0:T(8,128)(2,1)S(1)} %get-tuple-element.42), channel_id=1, source_target_pairs={{0,2},{1,3},{2,0},{3,1},{4,6},{5,7},{6,4},{7,5},{8,10},{9,11},{10,... | collective-permute-start | bytes 786440 | tf_op jit(solution)/shard_map/ppermute | solution.py:143
  12.9 1.5 %shard_map.139.refs_0_ = bf16[15,16,256]{2,1,0:T(8,128)(2,1)S(1)} custom-call(s32[5]{0:T(128)S(1)} %stack.23.at, bf16[14,128,256]{2,1,0:T(8,128)(2,1)S(1)} %get-tuple-element.40.after.refs_2_, f32[896,256]{1,0:T(8,128)} %master.1, f32[7,128]{1,0:T(8,128)} %bitcast.19), custom_call_target="tpu_custom_call" | custom-call | tf_op jit(solution)/shard_map/pallas_call | solution.py:552
  14.4 2.7 %collective-permute-start.3 = (bf16[15,16,256]{2,1,0:T(8,128)(2,1)S(1)}, bf16[15,16,256]{2,1,0:T(8,128)(2,1)S(1)}, u32[]{:S(2)}, u32[]{:S(2)}) collective-permute-start(bf16[15,16,256]{2,1,0:T(8,128)(2,1)S(1)} %shard_map.139.refs_0_), channel_id=1, source_target_pairs={{0,4},{1,5},{2,6},{3,7},{4,0},{5,1},{6,2},{7,3},{8,12},{9,13},{10,... | collective-permute-start | bytes 368648 | tf_op jit(solution)/shard_map/ppermute | solution.py:139
  17.1 4.3 %collective-permute-done.3.refs_1_ = bf16[15,16,256]{2,1,0:T(8,128)(2,1)S(1)} collective-permute-done((bf16[15,16,256]{2,1,0:T(8,128)(2,1)S(1)}, bf16[15,16,256]{2,1,0:T(8,128)(2,1)S(1)}, u32[]{:S(2)}, u32[]{:S(2)}) %collective-permute-start.3) | collective-permute-done | bytes 122912 | tf_op jit(solution)/shard_map/ppermute | solution.py:139
  23.8 1.3 %collective-permute-start.8 = (bf16[4,64,256]{2,1,0:T(8,128)(2,1)S(1)}, bf16[4,64,256]{2,1,0:T(8,128)(2,1)S(1)}, u32[]{:S(2)}, u32[]{:S(2)}) collective-permute-start(bf16[4,64,256]{2,1,0:T(8,128)(2,1)S(1)} %get-tuple-element.46), channel_id=1, source_target_pairs={{0,8},{1,17},{2,10},{3,19},{4,12},{5,21},{6,14},{7,23},{8,0},{9,25... | collective-permute-start | bytes 393224 | tf_op jit(solution)/shard_map/ppermute | solution.py:143
  25.1 2.6 %collective-permute-start.6 = (bf16[2,15,16,256]{3,2,1,0:T(8,128)(2,1)S(1)}, bf16[2,15,16,256]{3,2,1,0:T(8,128)(2,1)S(1)}, u32[]{:S(2)}, u32[]{:S(2)}) collective-permute-start(bf16[2,15,16,256]{3,2,1,0:T(8,128)(2,1)S(1)} %get-tuple-element.43.refs_0_), channel_id=1, source_target_pairs={{0,2},{1,3},{2,0},{3,1},{4,6},{5,7},{6,4},{7,5},{8,10},{9,11},{10,... | collective-permute-start | bytes 737288 | tf_op jit(solution)/shard_map/ppermute | solution.py:139
  27.6 1.1 %collective-permute-done.8.refs_2_ = bf16[4,64,256]{2,1,0:T(8,128)(2,1)S(1)} collective-permute-done((bf16[4,64,256]{2,1,0:T(8,128)(2,1)S(1)}, bf16[4,64,256]{2,1,0:T(8,128)(2,1)S(1)}, u32[]{:S(2)}, u32[]{:S(2)}) %collective-permute-start.8) | collective-permute-done | bytes 131104 | tf_op jit(solution)/shard_map/ppermute | solution.py:143
  28.7 2.8 %collective-permute-done.7.refs_1_ = bf16[10,64,256]{2,1,0:T(8,128)(2,1)S(1)} collective-permute-done((bf16[10,64,256]{2,1,0:T(8,128)(2,1)S(1)}, bf16[10,64,256]{2,1,0:T(8,128)(2,1)S(1)}, u32[]{:S(2)}, u32[]{:S(2)}) %collective-permute-start.7) | collective-permute-done | bytes 327712 | tf_op jit(solution)/shard_map/ppermute | solution.py:143
  32.1 1.3 %collective-permute-start.9 = (bf16[10,32,256]{2,1,0:T(8,128)(2,1)S(1)}, bf16[10,32,256]{2,1,0:T(8,128)(2,1)S(1)}, u32[]{:S(2)}, u32[]{:S(2)}) collective-permute-start(bf16[10,32,256]{2,1,0:T(8,128)(2,1)S(1)} %get-tuple-element.48), channel_id=1, source_target_pairs={{0,2},{1,9},{2,0},{3,11},{4,6},{5,13},{6,4},{7,15},{8,10},{9,1},{1... | collective-permute-start | bytes 491528 | tf_op jit(solution)/shard_map/ppermute | solution.py:143
  34.5 3.1 %collective-permute-done.10.refs_4_ = bf16[4,32,256]{2,1,0:T(8,128)(2,1)S(1)} collective-permute-done((bf16[4,32,256]{2,1,0:T(8,128)(2,1)S(1)}, bf16[4,32,256]{2,1,0:T(8,128)(2,1)S(1)}, u32[]{:S(2)}, u32[]{:S(2)}) %collective-permute-start.10) | collective-permute-done | bytes 65568 | tf_op jit(solution)/shard_map/ppermute | solution.py:143
  38.3 1.9 %collective-permute-start.14 = (bf16[4,224,256]{2,1,0:T(8,128)(2,1)S(1)}, bf16[4,224,256]{2,1,0:T(8,128)(2,1)S(1)}, u32[]{:S(2)}, u32[]{:S(2)}) collective-permute-start(bf16[4,224,256]{2,1,0:T(8,128)(2,1)S(1)} %get-tuple-element.54.line), channel_id=1, source_target_pairs={{0,8},{1,17},{2,10},{3,19},{4,12},{5,21},{6,14},{7,23},{8,0},{9,25... | collective-permute-start | bytes 1376264 | tf_op jit(solution)/shard_map/ppermute | solution.py:143
  40.4 2.2 %collective-permute-start.12 = (bf16[14,32,256]{2,1,0:T(8,128)(2,1)S(1)}, bf16[14,32,256]{2,1,0:T(8,128)(2,1)S(1)}, u32[]{:S(2)}, u32[]{:S(2)}) collective-permute-start(bf16[14,32,256]{2,1,0:T(8,128)(2,1)S(1)} %get-tuple-element.52.own), channel_id=1, source_target_pairs={{0,4},{1,5},{2,6},{3,7},{4,0},{5,1},{6,2},{7,3},{8,12},{9,13},{10,... | collective-permute-start | bytes 688136 | tf_op jit(solution)/shard_map/ppermute | solution.py:139
  43.9 2.7 %shard_map.143 = (f32[32,128]{1,0:T(8,128)S(1)}, s32[224]{0:T(256)S(1)}) custom-call(s32[5]{0:T(128)S(1)} %stack.23.at, s32[224]{0:T(256)S(1)} %copy-done.1, bf16[4,16,256]{2,1,0:T(8,128)(2,1)S(1)} %get-tuple-element.50.mine, bf16[4,16,256]{2,1,0:T(8,128)(2,1)S(1)} %collective-permute-done.11.peer), custom_call_target="tpu_custom_call" | custom-call | tf_op jit(solution)/shard_map/pallas_call | solution.py:588
  46.5 5.9 %collective-permute-done.12.got = bf16[14,32,256]{2,1,0:T(8,128)(2,1)S(1)} collective-permute-done((bf16[14,32,256]{2,1,0:T(8,128)(2,1)S(1)}, bf16[14,32,256]{2,1,0:T(8,128)(2,1)S(1)}, u32[]{:S(2)}, u32[]{:S(2)}) %collective-permute-start.12) | collective-permute-done | bytes 229408 | tf_op jit(solution)/shard_map/ppermute | solution.py:139
  52.4 1.0 %shard_map.145 = (bf16[10,32,256]{2,1,0:T(8,128)(2,1)S(1)}, bf16[5,32,256]{2,1,0:T(8,128)(2,1)S(1)}, bf16[3,4,224,256]{3,2,1,0:T(8,128)(2,1)S(1)}) custom-call(s32[5]{0:T(128)S(1)} %stack.23.at, f32[1]{0:T(128)S(6)} %sub.16.rate, bf16[14,32,256]{2,1,0:T(8,128)(2,1)S(1)} %get-tuple-element.52.own, bf16[14,32,256]{2,1,0:T(8,128)(2,1)S(1)} %collective-permute-done.12.got, ...), custom_call_target="tpu_custom_call" | custom-call | bytes 2097152 | tf_op jit(solution)/shard_map/pallas_call | solution.py:600
  53.6 1.0 %collective-permute-start.15 = (bf16[4,224,256]{2,1,0:T(8,128)(2,1)S(1)}, bf16[4,224,256]{2,1,0:T(8,128)(2,1)S(1)}, u32[]{:S(2)}, u32[]{:S(2)}) collective-permute-start(bf16[4,224,256]{2,1,0:T(8,128)(2,1)S(1)} %collective-permute-done.13.line_one), channel_id=1, source_target_pairs={{0,8},{1,17},{2,10},{3,19},{4,12},{5,21},{6,14},{7,23},{8,0},{9,25... | collective-permute-start | bytes 1376264 | tf_op jit(solution)/shard_map/ppermute | solution.py:143
  54.6 1.3 %collective-permute-start.17 = (bf16[5,32,256]{2,1,0:T(8,128)(2,1)S(1)}, bf16[5,32,256]{2,1,0:T(8,128)(2,1)S(1)}, u32[]{:S(2)}, u32[]{:S(2)}) collective-permute-start(bf16[5,32,256]{2,1,0:T(8,128)(2,1)S(1)} %get-tuple-element.57.refs_2_), channel_id=1, source_target_pairs={{0,16},{1,9},{2,18},{3,11},{4,20},{5,13},{6,22},{7,15},{8,24},{9,1... | collective-permute-start | bytes 245768 | tf_op jit(solution)/shard_map/ppermute | solution.py:143
  56.3 3.7 %collective-permute-done.17.refs_3_ = bf16[5,32,256]{2,1,0:T(8,128)(2,1)S(1)} collective-permute-done((bf16[5,32,256]{2,1,0:T(8,128)(2,1)S(1)}, bf16[5,32,256]{2,1,0:T(8,128)(2,1)S(1)}, u32[]{:S(2)}, u32[]{:S(2)}) %collective-permute-start.17) | collective-permute-done | bytes 81952 | tf_op jit(solution)/shard_map/ppermute | solution.py:143
  60.5 1.3 %collective-permute-start.18 = (bf16[10,64,256]{2,1,0:T(8,128)(2,1)S(1)}, bf16[10,64,256]{2,1,0:T(8,128)(2,1)S(1)}, u32[]{:S(2)}, u32[]{:S(2)}) collective-permute-start(bf16[10,64,256]{2,1,0:T(8,128)(2,1)S(1)} %get-tuple-element.58.refs_0_), channel_id=1, source_target_pairs={{0,16},{1,3},{2,18},{3,1},{4,20},{5,7},{6,22},{7,5},{8,24},{9,11},... | collective-permute-start | bytes 983048 | tf_op jit(solution)/shard_map/ppermute | solution.py:143
  61.8 1.5 %collective-permute-start.19 = (bf16[5,64,256]{2,1,0:T(8,128)(2,1)S(1)}, bf16[5,64,256]{2,1,0:T(8,128)(2,1)S(1)}, u32[]{:S(2)}, u32[]{:S(2)}) collective-permute-start(bf16[5,64,256]{2,1,0:T(8,128)(2,1)S(1)} %get-tuple-element.59.refs_2_), channel_id=1, source_target_pairs={{0,8},{1,17},{2,10},{3,19},{4,12},{5,21},{6,14},{7,23},{8,0},{9,25... | collective-permute-start | bytes 491528 | tf_op jit(solution)/shard_map/ppermute | solution.py:143
  63.3 3.8 %collective-permute-done.19.refs_3_ = bf16[5,64,256]{2,1,0:T(8,128)(2,1)S(1)} collective-permute-done((bf16[5,64,256]{2,1,0:T(8,128)(2,1)S(1)}, bf16[5,64,256]{2,1,0:T(8,128)(2,1)S(1)}, u32[]{:S(2)}, u32[]{:S(2)}) %collective-permute-start.19) | collective-permute-done | bytes 163872 | tf_op jit(solution)/shard_map/ppermute | solution.py:143
  67.1 2.3 %collective-permute-done.18.refs_1_ = bf16[10,64,256]{2,1,0:T(8,128)(2,1)S(1)} collective-permute-done((bf16[10,64,256]{2,1,0:T(8,128)(2,1)S(1)}, bf16[10,64,256]{2,1,0:T(8,128)(2,1)S(1)}, u32[]{:S(2)}, u32[]{:S(2)}) %collective-permute-start.18) | collective-permute-done | bytes 327712 | tf_op jit(solution)/shard_map/ppermute | solution.py:143
  71.0 1.7 %collective-permute-start.24 = (bf16[5,128,256]{2,1,0:T(8,128)(2,1)S(1)}, bf16[5,128,256]{2,1,0:T(8,128)(2,1)S(1)}, u32[]{:S(2)}, u32[]{:S(2)}) collective-permute-start(bf16[5,128,256]{2,1,0:T(8,128)(2,1)S(1)} %get-tuple-element.63.refs_2_), channel_id=1, source_target_pairs={{0,2},{1,3},{2,0},{3,1},{4,6},{5,7},{6,4},{7,5},{8,10},{9,11},{10,... | collective-permute-start | bytes 983048 | tf_op jit(solution)/shard_map/ppermute | solution.py:143
  73.2 1.0 %collective-permute-done.21.peer_low = bf16[2,224,256]{2,1,0:T(8,128)(2,1)S(1)} collective-permute-done((bf16[2,224,256]{2,1,0:T(8,128)(2,1)S(1)}, bf16[2,224,256]{2,1,0:T(8,128)(2,1)S(1)}, u32[]{:S(2)}, u32[]{:S(2)}) %collective-permute-start.21) | collective-permute-done | bytes 229408 | tf_op jit(solution)/shard_map/ppermute | solution.py:139
  75.5 4.6 %collective-permute-done.24.refs_3_ = bf16[5,128,256]{2,1,0:T(8,128)(2,1)S(1)} collective-permute-done((bf16[5,128,256]{2,1,0:T(8,128)(2,1)S(1)}, bf16[5,128,256]{2,1,0:T(8,128)(2,1)S(1)}, u32[]{:S(2)}, u32[]{:S(2)}) %collective-permute-start.24) | collective-permute-done | bytes 327712 | tf_op jit(solution)/shard_map/ppermute | solution.py:143
  81.5 1.7 %shard_map.151.own_part = f32[512,256]{1,0:T(8,128)S(1)} custom-call(s32[5]{0:T(128)S(1)} %stack.23.at, bf16[3456,256]{1,0:T(8,128)(2,1)S(1)} %shard_map.144.after.views, bf16[15,256,256]{2,1,0:T(8,128)(2,1)S(1)} %shard_map.149.scaled.mine), custom_call_target="tpu_custom_call" | custom-call | flops 939524096 | bytes 4194304 | tf_op jit(solution)/shard_map/pallas_call | solution.py:638
  83.2 2.0 %shard_map.150.old = f32[512,256]{1,0:T(8,128)S(1)} custom-call(bf16[3456,256]{1,0:T(8,128)(2,1)S(1)} %shard_map.144.after.views, bf16[7168,256]{1,0:T(8,128)(2,1)S(1)} %shard_map.148.after.natural), custom_call_target="tpu_custom_call" | custom-call | flops 1811939328 | bytes 6291456 | tf_op jit(solution)/shard_map/pallas_call | solution.py:631
  85.5 3.7 %shard_map.152 = (f32[896,256]{1,0:T(8,128)}, f32[896,256]{1,0:T(8,128)}, f32[7,128]{1,0:T(8,128)}, f32[2,256]{1,0:T(2,128)}, bf16[512,256]{1,0:T(8,128)(2,1)}) custom-call(s32[5]{0:T(128)S(1)} %stack.23.at, s32[224]{0:T(256)S(1)} %get-tuple-element.51.plan, f32[1]{0:T(128)S(6)} %sub.16.rate, f32[2,256]{1,0:T(2,128)S(1)} %copy-done.2, ...), custom_call_target="tpu_custom_call" | custom-call | flops 1073741824 | bytes 16777216 | tf_op jit(solution)/shard_map/pallas_call | solution.py:653
  (48 shorter events, 12.9 us)
Async XLA Ops:
  0.6 4.3 %collective-permute-start = (bf16[1,4,18,18,256]{4,1,3,2,0:T(4,128)(2,1)}, bf16[1,4,18,18,256]{4,1,3,2,0:T(4,128)(2,1)S(1)}, u32[]{:S(2)}, u32[]{:S(2)}) collective-permute-start(bf16[1,4,18,18,256]{4,1,3,2,0:T(4,128)(2,1)} %param.12), channel_id=1, source_target_pairs={{0,1},{1,0},{2,3},{3,2},{4,5},{5,4},{6,7},{7,6},{8,9},{9,8},{10,11... | collective-permute-start | bytes 1990664 | tf_op jit(solution)/shard_map/ppermute | solution.py:139
  1.1 4.0 %collective-permute-start.1 = (bf16[512,256]{1,0:T(8,128)(2,1)}, bf16[512,256]{1,0:T(8,128)(2,1)S(1)}, u32[]{:S(2)}, u32[]{:S(2)}) collective-permute-start(bf16[512,256]{1,0:T(8,128)(2,1)} %pre_far.1), channel_id=1, source_target_pairs={{0,1},{1,0},{2,3},{3,2},{4,5},{5,4},{6,7},{7,6},{8,9},{9,8},{10,11... | collective-permute-start | bytes 786440 | tf_op jit(solution)/shard_map/ppermute | solution.py:139
  1.2 3.9 %collective-permute-start.2 = (bf16[512,256]{1,0:T(8,128)(2,1)}, bf16[512,256]{1,0:T(8,128)(2,1)S(1)}, u32[]{:S(2)}, u32[]{:S(2)}) collective-permute-start(bf16[512,256]{1,0:T(8,128)(2,1)} %grad_far.1), channel_id=1, source_target_pairs={{0,1},{1,0},{2,3},{3,2},{4,5},{5,4},{6,7},{7,6},{8,9},{9,8},{10,11... | collective-permute-start | bytes 786440 | tf_op jit(solution)/shard_map/ppermute | solution.py:139
  8.7 13.6 %collective-permute-start.4 = (bf16[10,128,256]{2,1,0:T(8,128)(2,1)S(1)}, bf16[10,128,256]{2,1,0:T(8,128)(2,1)S(1)}, u32[]{:S(2)}, u32[]{:S(2)}) collective-permute-start(bf16[10,128,256]{2,1,0:T(8,128)(2,1)S(1)} %get-tuple-element.41), channel_id=1, source_target_pairs={{0,8},{1,17},{2,10},{3,19},{4,12},{5,21},{6,14},{7,23},{8,0},{9,25... | collective-permute-start | bytes 1966088 | tf_op jit(solution)/shard_map/ppermute | solution.py:143
  11.3 11.0 %collective-permute-start.5 = (bf16[4,128,256]{2,1,0:T(8,128)(2,1)S(1)}, bf16[4,128,256]{2,1,0:T(8,128)(2,1)S(1)}, u32[]{:S(2)}, u32[]{:S(2)}) collective-permute-start(bf16[4,128,256]{2,1,0:T(8,128)(2,1)S(1)} %get-tuple-element.42), channel_id=1, source_target_pairs={{0,2},{1,3},{2,0},{3,1},{4,6},{5,7},{6,4},{7,5},{8,10},{9,11},{10,... | collective-permute-start | bytes 786440 | tf_op jit(solution)/shard_map/ppermute | solution.py:143
  14.4 29.5 %copy-start.1 = (s32[224]{0:T(256)S(1)}, s32[224]{0:T(256)}, u32[]{:S(2)}) copy-start(s32[224]{0:T(256)} %block_order.3) | copy-start | bytes 2692
  14.4 7.0 %collective-permute-start.3 = (bf16[15,16,256]{2,1,0:T(8,128)(2,1)S(1)}, bf16[15,16,256]{2,1,0:T(8,128)(2,1)S(1)}, u32[]{:S(2)}, u32[]{:S(2)}) collective-permute-start(bf16[15,16,256]{2,1,0:T(8,128)(2,1)S(1)} %shard_map.139.refs_0_), channel_id=1, source_target_pairs={{0,4},{1,5},{2,6},{3,7},{4,0},{5,1},{6,2},{7,3},{8,12},{9,13},{10,... | collective-permute-start | bytes 368648 | tf_op jit(solution)/shard_map/ppermute | solution.py:139
  23.0 32.9 %copy-start.3 = (bf16[1,4,18,18,256]{4,1,3,2,0:T(4,128)(2,1)S(1)}, bf16[1,4,18,18,256]{4,1,3,2,0:T(4,128)(2,1)}, u32[]{:S(2)}) copy-start(bf16[1,4,18,18,256]{4,1,3,2,0:T(4,128)(2,1)} %param.19) | copy-start | bytes 1990660
  23.0 8.5 %collective-permute-start.7 = (bf16[10,64,256]{2,1,0:T(8,128)(2,1)S(1)}, bf16[10,64,256]{2,1,0:T(8,128)(2,1)S(1)}, u32[]{:S(2)}, u32[]{:S(2)}) collective-permute-start(bf16[10,64,256]{2,1,0:T(8,128)(2,1)S(1)} %get-tuple-element.45), channel_id=1, source_target_pairs={{0,16},{1,3},{2,18},{3,1},{4,20},{5,7},{6,22},{7,5},{8,24},{9,11},... | collective-permute-start | bytes 983048 | tf_op jit(solution)/shard_map/ppermute | solution.py:143
  23.8 5.0 %collective-permute-start.8 = (bf16[4,64,256]{2,1,0:T(8,128)(2,1)S(1)}, bf16[4,64,256]{2,1,0:T(8,128)(2,1)S(1)}, u32[]{:S(2)}, u32[]{:S(2)}) collective-permute-start(bf16[4,64,256]{2,1,0:T(8,128)(2,1)S(1)} %get-tuple-element.46), channel_id=1, source_target_pairs={{0,8},{1,17},{2,10},{3,19},{4,12},{5,21},{6,14},{7,23},{8,0},{9,25... | collective-permute-start | bytes 393224 | tf_op jit(solution)/shard_map/ppermute | solution.py:143
  25.1 9.5 %collective-permute-start.6 = (bf16[2,15,16,256]{3,2,1,0:T(8,128)(2,1)S(1)}, bf16[2,15,16,256]{3,2,1,0:T(8,128)(2,1)S(1)}, u32[]{:S(2)}, u32[]{:S(2)}) collective-permute-start(bf16[2,15,16,256]{3,2,1,0:T(8,128)(2,1)S(1)} %get-tuple-element.43.refs_0_), channel_id=1, source_target_pairs={{0,2},{1,3},{2,0},{3,1},{4,6},{5,7},{6,4},{7,5},{8,10},{9,11},{10,... | collective-permute-start | bytes 737288 | tf_op jit(solution)/shard_map/ppermute | solution.py:139
  32.1 5.5 %collective-permute-start.9 = (bf16[10,32,256]{2,1,0:T(8,128)(2,1)S(1)}, bf16[10,32,256]{2,1,0:T(8,128)(2,1)S(1)}, u32[]{:S(2)}, u32[]{:S(2)}) collective-permute-start(bf16[10,32,256]{2,1,0:T(8,128)(2,1)S(1)} %get-tuple-element.48), channel_id=1, source_target_pairs={{0,2},{1,9},{2,0},{3,11},{4,6},{5,13},{6,4},{7,15},{8,10},{9,1},{1... | collective-permute-start | bytes 491528 | tf_op jit(solution)/shard_map/ppermute | solution.py:143
  33.4 4.3 %collective-permute-start.10 = (bf16[4,32,256]{2,1,0:T(8,128)(2,1)S(1)}, bf16[4,32,256]{2,1,0:T(8,128)(2,1)S(1)}, u32[]{:S(2)}, u32[]{:S(2)}) collective-permute-start(bf16[4,32,256]{2,1,0:T(8,128)(2,1)S(1)} %get-tuple-element.49), channel_id=1, source_target_pairs={{0,16},{1,9},{2,18},{3,11},{4,20},{5,13},{6,22},{7,15},{8,24},{9,1... | collective-permute-start | bytes 196616 | tf_op jit(solution)/shard_map/ppermute | solution.py:143
  38.3 14.2 %collective-permute-start.14 = (bf16[4,224,256]{2,1,0:T(8,128)(2,1)S(1)}, bf16[4,224,256]{2,1,0:T(8,128)(2,1)S(1)}, u32[]{:S(2)}, u32[]{:S(2)}) collective-permute-start(bf16[4,224,256]{2,1,0:T(8,128)(2,1)S(1)} %get-tuple-element.54.line), channel_id=1, source_target_pairs={{0,8},{1,17},{2,10},{3,19},{4,12},{5,21},{6,14},{7,23},{8,0},{9,25... | collective-permute-start | bytes 1376264 | tf_op jit(solution)/shard_map/ppermute | solution.py:143
  40.2 12.3 %collective-permute-start.13 = (bf16[4,224,256]{2,1,0:T(8,128)(2,1)S(1)}, bf16[4,224,256]{2,1,0:T(8,128)(2,1)S(1)}, u32[]{:S(2)}, u32[]{:S(2)}) collective-permute-start(bf16[4,224,256]{2,1,0:T(8,128)(2,1)S(1)} %get-tuple-element.54.line), channel_id=1, source_target_pairs={{0,16},{1,9},{2,18},{3,11},{4,20},{5,13},{6,22},{7,15},{8,24},{9,1... | collective-permute-start | bytes 1376264 | tf_op jit(solution)/shard_map/ppermute | solution.py:143
  40.4 12.0 %collective-permute-start.12 = (bf16[14,32,256]{2,1,0:T(8,128)(2,1)S(1)}, bf16[14,32,256]{2,1,0:T(8,128)(2,1)S(1)}, u32[]{:S(2)}, u32[]{:S(2)}) collective-permute-start(bf16[14,32,256]{2,1,0:T(8,128)(2,1)S(1)} %get-tuple-element.52.own), channel_id=1, source_target_pairs={{0,4},{1,5},{2,6},{3,7},{4,0},{5,1},{6,2},{7,3},{8,12},{9,13},{10,... | collective-permute-start | bytes 688136 | tf_op jit(solution)/shard_map/ppermute | solution.py:139
  42.7 1.2 %collective-permute-start.11 = (bf16[4,16,256]{2,1,0:T(8,128)(2,1)S(1)}, bf16[4,16,256]{2,1,0:T(8,128)(2,1)S(1)}, u32[]{:S(2)}, u32[]{:S(2)}) collective-permute-start(bf16[4,16,256]{2,1,0:T(8,128)(2,1)S(1)} %get-tuple-element.50.mine), channel_id=1, source_target_pairs={{0,1},{1,0},{2,3},{3,2},{4,5},{5,4},{6,7},{7,6},{8,9},{9,8},{10,11... | collective-permute-start | bytes 98312 | tf_op jit(solution)/shard_map/ppermute | solution.py:139
  53.4 21.1 %collective-permute-start.20 = (bf16[3,4,224,256]{3,2,1,0:T(8,128)(2,1)S(1)}, bf16[3,4,224,256]{3,2,1,0:T(8,128)(2,1)S(1)}, u32[]{:S(2)}, u32[]{:S(2)}) collective-permute-start(bf16[3,4,224,256]{3,2,1,0:T(8,128)(2,1)S(1)} %get-tuple-element.55.mine), channel_id=1, source_target_pairs={{0,1},{1,0},{2,3},{3,2},{4,5},{5,4},{6,7},{7,6},{8,9},{9,8},{10,11... | collective-permute-start | bytes 4128776 | tf_op jit(solution)/shard_map/ppermute | solution.py:139
  53.5 6.4 %collective-permute-start.16 = (bf16[10,32,256]{2,1,0:T(8,128)(2,1)S(1)}, bf16[10,32,256]{2,1,0:T(8,128)(2,1)S(1)}, u32[]{:S(2)}, u32[]{:S(2)}) collective-permute-start(bf16[10,32,256]{2,1,0:T(8,128)(2,1)S(1)} %get-tuple-element.56.refs_0_), channel_id=1, source_target_pairs={{0,2},{1,9},{2,0},{3,11},{4,6},{5,13},{6,4},{7,15},{8,10},{9,1},{1... | collective-permute-start | bytes 491528 | tf_op jit(solution)/shard_map/ppermute | solution.py:143
  53.6 13.5 %collective-permute-start.15 = (bf16[4,224,256]{2,1,0:T(8,128)(2,1)S(1)}, bf16[4,224,256]{2,1,0:T(8,128)(2,1)S(1)}, u32[]{:S(2)}, u32[]{:S(2)}) collective-permute-start(bf16[4,224,256]{2,1,0:T(8,128)(2,1)S(1)} %collective-permute-done.13.line_one), channel_id=1, source_target_pairs={{0,8},{1,17},{2,10},{3,19},{4,12},{5,21},{6,14},{7,23},{8,0},{9,25... | collective-permute-start | bytes 1376264 | tf_op jit(solution)/shard_map/ppermute | solution.py:143
  54.6 5.4 %collective-permute-start.17 = (bf16[5,32,256]{2,1,0:T(8,128)(2,1)S(1)}, bf16[5,32,256]{2,1,0:T(8,128)(2,1)S(1)}, u32[]{:S(2)}, u32[]{:S(2)}) collective-permute-start(bf16[5,32,256]{2,1,0:T(8,128)(2,1)S(1)} %get-tuple-element.57.refs_2_), channel_id=1, source_target_pairs={{0,16},{1,9},{2,18},{3,11},{4,20},{5,13},{6,22},{7,15},{8,24},{9,1... | collective-permute-start | bytes 245768 | tf_op jit(solution)/shard_map/ppermute | solution.py:143
  60.5 8.9 %collective-permute-start.18 = (bf16[10,64,256]{2,1,0:T(8,128)(2,1)S(1)}, bf16[10,64,256]{2,1,0:T(8,128)(2,1)S(1)}, u32[]{:S(2)}, u32[]{:S(2)}) collective-permute-start(bf16[10,64,256]{2,1,0:T(8,128)(2,1)S(1)} %get-tuple-element.58.refs_0_), channel_id=1, source_target_pairs={{0,16},{1,3},{2,18},{3,1},{4,20},{5,7},{6,22},{7,5},{8,24},{9,11},... | collective-permute-start | bytes 983048 | tf_op jit(solution)/shard_map/ppermute | solution.py:143
  61.8 5.3 %collective-permute-start.19 = (bf16[5,64,256]{2,1,0:T(8,128)(2,1)S(1)}, bf16[5,64,256]{2,1,0:T(8,128)(2,1)S(1)}, u32[]{:S(2)}, u32[]{:S(2)}) collective-permute-start(bf16[5,64,256]{2,1,0:T(8,128)(2,1)S(1)} %get-tuple-element.59.refs_2_), channel_id=1, source_target_pairs={{0,8},{1,17},{2,10},{3,19},{4,12},{5,21},{6,14},{7,23},{8,0},{9,25... | collective-permute-start | bytes 491528 | tf_op jit(solution)/shard_map/ppermute | solution.py:143
  70.1 10.7 %collective-permute-start.23 = (bf16[10,128,256]{2,1,0:T(8,128)(2,1)S(1)}, bf16[10,128,256]{2,1,0:T(8,128)(2,1)S(1)}, u32[]{:S(2)}, u32[]{:S(2)}) collective-permute-start(bf16[10,128,256]{2,1,0:T(8,128)(2,1)S(1)} %get-tuple-element.62.refs_0_), channel_id=1, source_target_pairs={{0,8},{1,17},{2,10},{3,19},{4,12},{5,21},{6,14},{7,23},{8,0},{9,25... | collective-permute-start | bytes 1966088 | tf_op jit(solution)/shard_map/ppermute | solution.py:143
  71.0 9.0 %collective-permute-start.24 = (bf16[5,128,256]{2,1,0:T(8,128)(2,1)S(1)}, bf16[5,128,256]{2,1,0:T(8,128)(2,1)S(1)}, u32[]{:S(2)}, u32[]{:S(2)}) collective-permute-start(bf16[5,128,256]{2,1,0:T(8,128)(2,1)S(1)} %get-tuple-element.63.refs_2_), channel_id=1, source_target_pairs={{0,2},{1,3},{2,0},{3,1},{4,6},{5,7},{6,4},{7,5},{8,10},{9,11},{10,... | collective-permute-start | bytes 983048 | tf_op jit(solution)/shard_map/ppermute | solution.py:143
  72.7 1.5 %collective-permute-start.21 = (bf16[2,224,256]{2,1,0:T(8,128)(2,1)S(1)}, bf16[2,224,256]{2,1,0:T(8,128)(2,1)S(1)}, u32[]{:S(2)}, u32[]{:S(2)}) collective-permute-start(bf16[2,224,256]{2,1,0:T(8,128)(2,1)S(1)} %get-tuple-element.60.mine_low), channel_id=1, source_target_pairs={{0,1},{1,0},{2,3},{3,2},{4,5},{5,4},{6,7},{7,6},{8,9},{9,8},{10,11... | collective-permute-start | bytes 688136 | tf_op jit(solution)/shard_map/ppermute | solution.py:139
  72.7 1.8 %collective-permute-start.22 = (bf16[2,224,256]{2,1,0:T(8,128)(2,1)S(1)}, bf16[2,224,256]{2,1,0:T(8,128)(2,1)S(1)}, u32[]{:S(2)}, u32[]{:S(2)}) collective-permute-start(bf16[2,224,256]{2,1,0:T(8,128)(2,1)S(1)} %get-tuple-element.61.mine_high), channel_id=1, source_target_pairs={{0,1},{1,0},{2,3},{3,2},{4,5},{5,4},{6,7},{7,6},{8,9},{9,8},{10,11... | collective-permute-start | bytes 688136 | tf_op jit(solution)/shard_map/ppermute | solution.py:139
  81.4 4.0 %collective-permute-start.25 = (bf16[15,256,256]{2,1,0:T(8,128)(2,1)S(1)}, bf16[15,256,256]{2,1,0:T(8,128)(2,1)S(1)}, u32[]{:S(2)}, u32[]{:S(2)}) collective-permute-start(bf16[15,256,256]{2,1,0:T(8,128)(2,1)S(1)} %shard_map.149.scaled.mine), channel_id=1, source_target_pairs={{0,1},{1,0},{2,3},{3,2},{4,5},{5,4},{6,7},{7,6},{8,9},{9,8},{10,11... | collective-permute-start | bytes 5898248 | tf_op jit(solution)/shard_map/ppermute | solution.py:139
  83.2 2.3 %copy-start = (f32[896,256]{1,0:T(8,128)S(1)}, f32[896,256]{1,0:T(8,128)}, u32[]{:S(2)}) copy-start(f32[896,256]{1,0:T(8,128)} %master.1) | copy-start | bytes 2752516
  83.2 2.3 %copy-start.2 = (f32[2,256]{1,0:T(2,128)S(1)}, f32[2,256]{1,0:T(2,128)}, u32[]{:S(2)}) copy-start(f32[2,256]{1,0:T(2,128)} %col_moment.1) | copy-start | bytes 6148

commit v8 on v7

--- a/solution.py
+++ b/solution.py
@@ -129,7 +129,7 @@
 HBM = pl.BlockSpec(memory_space=pl.ANY)
 MASK_CORE, MASK_NEAR, MASK_FAR, MASK_X, MASK_Y = 1, 2, 4, 8, 16
 PARTS = ((0, 10), (10, 4))
-ORDERS = (((0, 1, 2), (1, 2, 0)), ((2, 0, 1), (2, 1, 0)))
+ORDERS = (((0, 1, 2), (1, 0, 2)), ((2, 0, 1), (2, 1, 0)))
 MESSAGE = SLOTS
 GATHERED = ((0, 10), (10, 5))
 MASKS = (MASK_X, MASK_Y, MASK_NEAR)
@@ -152,9 +152,14 @@
     return at[zero] if zero == one else jnp.where(at[4] == 0, at[zero], at[one])
 
 
+def position():
+    group, shard = lax.axis_index("group"), lax.axis_index("shard")
+    return group % 2, group // 2, shard // 2 % 2, shard // 4, shard % 2
+
+
 def call(kernel, outs, in_specs, out_specs=None, scratch=(), flops=0, moved=0, room=8, pin=True):
     return pl.pallas_call(
-        kernel,
+        lambda *refs: kernel(position(), *refs),
         out_shape=[(pltpu.VMEM if pin else jax.ShapeDtypeStruct)(*out) for out in outs],
         in_specs=in_specs,
         out_specs=out_specs or [VMEM] * len(outs),
@@ -175,7 +180,7 @@
         ].reshape(SHIFTED, CI)
 
 
-def shift_kernel(tile, out):
+def shift_kernel(at, tile, out):
     store_shifted(tile, out)
 
 
@@ -353,7 +358,7 @@
         half = (block >= 8 * SLOTS).astype(jnp.int32)
         slot, place = (block - half * (8 * SLOTS)) // 8, lax.rem(block, 8)
         high, middle, low = place // 4, lax.rem(place // 2, 2), lax.rem(place, 2)
-        other = jnp.where(half == 0, low * 4 + high * 2 + middle, middle * 4 + high * 2 + low)
+        other = low * 4 + high * 2 + middle
         sender = jnp.where(slot < PARTS[1][0], other, place)
         side = half ^ core
         plan[local * 8] = side
@@ -429,7 +434,7 @@
     return jnp.concatenate([views[pl.ds(start, HW * HW), :] for start in starts], axis=0)
 
 
-def old_hidden_kernel(views, natural, hidden):
+def old_hidden_kernel(at, views, natural, hidden):
     total = jnp.zeros((PIX, CO), WIDE)
     for tap in range(27):
         weights = natural[tap * CI : tap * CI + CI]
@@ -459,26 +464,21 @@
     factor, row_table, update_rows, new_master, stored,
 ):
     core = at[4]
-    total = jnp.zeros((8, CO), WIDE)
-    for side, piece in enumerate((mine, peer)):
-        for sender in range(8):
-            message = piece[MESSAGE, sender * BLK : sender * BLK + 16].astype(WIDE)
-            message = message[:8] + message[8:]
-            total = total + message
-            for line in range(4):
-                to = (side * 8 + sender) * 4 + line
-                row_table[to : to + 1] = message[
-                    6 + line // 2 : 7 + line // 2, line % 2 * 128 : line % 2 * 128 + 128
-                ]
+    sums = [
+        [
+            piece[MESSAGE, sender * BLK : sender * BLK + 8].astype(WIDE)
+            + piece[MESSAGE, sender * BLK + 8 : sender * BLK + 16].astype(WIDE)
+            for sender in range(8)
+        ]
+        for piece in (mine, peer)
+    ]
+    total = sum(sums[0][1:] + sums[1], sums[0][0])
     store_factors(total, rate[0], col_moment, new_col, factor)
 
-    lane = lax.broadcasted_iota(jnp.int32, (1, 128), 1)
     copies = []
     for line in range(7):
-        values = jnp.zeros((1, 128), WIDE)
-        for part in range(4):
-            local = line * 4 + part
-            side, slot, first, kernel, from_row, turn = (plan[local * 8 + item] for item in range(6))
+        for local in range(line * 4, line * 4 + 4):
+            side, slot, first, kernel = (plan[local * 8 + item] for item in range(4))
             rows = slice(local * BLK, local * BLK + BLK)
             there = pl.ds(pl.multiple_of(first, BLK), BLK)
             value = jnp.where(
@@ -487,10 +487,6 @@
             update = value * factor[pl.ds(kernel, 1), :]
             update_rows[rows, :] = update
             new_master[rows, :] = master[rows, :] - learn_rate * update
-            here = (lane >= part * BLK) & (lane < part * BLK + BLK)
-            turned = pltpu.roll(row_table[pl.ds(from_row, 1), :], turn, 1)
-            values = jnp.where(here, turned, values)
-        new_row[line : line + 1] = values
         there = pl.ds(line * 4 * BLK, 4 * BLK)
         pairs = ((update_rows, update_far), (new_master, master_far))
         copies += fetch(
@@ -505,6 +501,23 @@
     next_output[...] = jnp.dot(
         jax.nn.silu(hidden).astype(LOW), weights.astype(LOW), preferred_element_type=WIDE
     ).astype(LOW)
+
+    for side, messages in enumerate(sums):
+        for sender in range(8):
+            for line in range(4):
+                to = (side * 8 + sender) * 4 + line
+                row_table[to : to + 1] = messages[sender][
+                    6 + line // 2 : 7 + line // 2, line % 2 * 128 : line % 2 * 128 + 128
+                ]
+    lane = lax.broadcasted_iota(jnp.int32, (1, 128), 1)
+    for line in range(7):
+        values = jnp.zeros((1, 128), WIDE)
+        for part in range(4):
+            from_row, turn = (plan[(line * 4 + part) * 8 + item] for item in (4, 5))
+            here = (lane >= part * BLK) & (lane < part * BLK + BLK)
+            turned = pltpu.roll(row_table[pl.ds(from_row, 1), :], turn, 1)
+            values = jnp.where(here, turned, values)
+        new_row[line : line + 1] = values
     for copy in copies:
         copy.wait()
 
@@ -521,10 +534,6 @@
     col_moment,
     next_tiles,
 ):
-    group, shard = lax.axis_index("group"), lax.axis_index("shard")
-    axis_y, axis_x = group // 2, group % 2
-    far, near, core = shard // 4, shard // 2 % 2, shard % 2
-    at = jnp.stack([axis_x, axis_y, near, far, core]).astype(jnp.int32)
     decay_rate = 1.0 - step_count.astype(WIDE) ** (-decay_power)
 
     tile_peer = swap(saved_tiles, MASK_CORE)
@@ -534,31 +543,31 @@
     brought, grad_near, pointwise_near = call(
         own_kernel,
         [((BROUGHT, CI), LOW), ((PIX, CO), LOW), ((CO, CO), LOW)],
-        [SMEM, VMEM] + [HBM] * 3,
+        [VMEM] + [HBM] * 3,
         scratch=[pltpu.VMEM((PIX, CO), LOW), pltpu.SemaphoreType.DMA((3,))],
         moved=4 << 20,
-    )(at, saved_tiles[0], *rows_far)
+    )(saved_tiles[0], *rows_far)
 
     keep, *sends = call(
         term_kernel,
         [((SLOTS, 128, CO), LOW)] + [((count, 128, CO), LOW) for _, count in PARTS],
-        [SMEM] + [VMEM] * 6,
+        [VMEM] * 6,
         scratch=[pltpu.VMEM((BROUGHT, CI), LOW), pltpu.VMEM((2, 2 * PIX, CO), LOW)],
         flops=2 * 14 * 1024 * 256 * 256,
         moved=6 << 20,
         room=12,
-    )(at, brought, tile_peer[0], pre_peer, grad_peer, grad_near, pointwise_near)
+    )(brought, tile_peer[0], pre_peer, grad_peer, grad_near, pointwise_near)
 
     packed = call(
         pack_kernel,
         [((SLOTS + 1, 16, CO), LOW)],
-        [SMEM] + [HBM] * 3,
+        [HBM] * 3,
         scratch=[
             pltpu.VMEM((SLOTS * 16, CO), WIDE),
             pltpu.VMEM((16, 128), WIDE),
             pltpu.SemaphoreType.DMA((2,)),
         ],
-    )(at, keep, far_away(master_rows), far_away(row_moment.reshape(7, 128)))[0]
+    )(keep, far_away(master_rows), far_away(row_moment.reshape(7, 128)))[0]
     packed_far = swap(packed, MASK_FAR)
     views = call(shift_kernel, [((3 * SHIFTED, CI), LOW)], [VMEM], moved=3 << 20)(next_tiles[0])[0]
 
@@ -577,9 +586,9 @@
         keep, *sends = call(
             functools.partial(fold_kernel, step),
             outs,
-            [SMEM] + [VMEM] * (len(extra) + 3),
+            [VMEM] * (len(extra) + 3),
             moved=1 << 20,
-        )(at, *extra, keep, *gots)
+        )(*extra, keep, *gots)
         if step == 1:
             pair = sends.pop()
             pair_near = swap(pair, MASK_NEAR)
@@ -588,7 +597,7 @@
     own_moment, plan = call(
         moments_kernel,
         [((BLK, 128), WIDE), ((NB,), jnp.int32)],
-        [SMEM] * 2 + [VMEM] * 2,
+        [SMEM] + [VMEM] * 2,
         out_specs=[VMEM, SMEM],
         pin=False,
         scratch=[
@@ -596,13 +605,13 @@
             pltpu.VMEM((128, 128), WIDE),
             pltpu.SMEM((NB,), jnp.int32),
         ],
-    )(at, block_order, moments, swap(moments, MASK_CORE))
+    )(block_order, moments, swap(moments, MASK_CORE))
     *scaled, lines = call(
         moment_kernel,
         [((count, BLK, CO), LOW) for _, count in GATHERED] + [((3, 4, SLOTS * 16, CO), LOW)],
-        [SMEM] * 2 + [VMEM] * 6,
+        [SMEM] + [VMEM] * 6,
         moved=2 << 20,
-    )(at, decay_rate, keep, swap(keep, MASK_FAR), own_moment, line, line_one, line_two)
+    )(decay_rate, keep, swap(keep, MASK_FAR), own_moment, line, line_one, line_two)
     line_far = swap_mixed(line_one, (MASK_X, MASK_Y))
     joined, natural = scaled, None
     for step in range(2, -1, -1):
@@ -618,14 +627,14 @@
         joined = call(
             functools.partial(widen_kernel, step),
             outs,
-            [SMEM, VMEM if step == 1 else HBM] + [VMEM] * len(pieces),
-        )(at, (natural, line_far, views)[step], *pieces)
+            [VMEM if step == 1 else HBM] + [VMEM] * len(pieces),
+        )((natural, line_far, views)[step], *pieces)
         if step == 1:
             parts = [lines, *joined[2:]]
             joined = joined[:2]
             natural = call(
-                order_kernel, [((NB * BLK, CO), LOW)], [SMEM] * 2 + [VMEM] * 6, moved=8 << 20
-            )(at, block_order, *parts, *[swap(part, MASK_CORE) for part in parts])[0]
+                order_kernel, [((NB * BLK, CO), LOW)], [SMEM] + [VMEM] * 6, moved=8 << 20
+            )(block_order, *parts, *[swap(part, MASK_CORE) for part in parts])[0]
     mine = joined[0]
     peer = swap(mine, MASK_CORE)
     old = call(
@@ -638,10 +647,10 @@
     half = call(
         half_hidden_kernel,
         [((PIX, CO), WIDE)],
-        [SMEM] + [VMEM] * 2,
+        [VMEM] * 2,
         flops=2 * 14 * 512 * 256 * 256,
         moved=4 << 20,
-    )(at, views, mine)[0]
+    )(views, mine)[0]
 
     outs = [
         ((NB // 8 * BLK, CO), WIDE),
@@ -653,7 +662,7 @@
     update_rows, new_master, new_row, new_col, next_output = call(
         finish_kernel,
         outs,
-        [SMEM] * 3 + [VMEM] * 8,
+        [SMEM] * 2 + [VMEM] * 8,
         out_specs=[HBM] * 2 + [VMEM] * 3,
         scratch=[
             pltpu.VMEM((2, CO), WIDE),
@@ -666,7 +675,7 @@
         flops=2 * 16 * 512 * 256 * 256,
         moved=16 << 20,
         room=16,
-    )(at, plan, decay_rate, col_moment, views, natural, master_rows, mine, peer, old, half)
+    )(plan, decay_rate, col_moment, views, natural, master_rows, mine, peer, old, half)
     return (update_rows, new_master, new_row.reshape(-1), new_col, next_output)
 
 

time: 89.4 us -> 84.2 us (0.942)
  Pallas kernels: 23 us -> 17 us
  waiting for transfers between devices: 35.9 us -> 37 us
    pallas_call x11, Pallas kernels: 14.3 us -> 10 us  [the longest x1 3.69 us: shards(): call(finish_kernel, outs, [SMEM] * 2 + [VMEM] * 8, out_specs=[HBM] * 2 +...]
    ppermute x11, waiting for transfers between devices: 12.9 us -> 14.5 us  [swap(): return lax.ppermute(value, AXES, [(at, at ^ mask) for at in range(32)])]
  transfers between devices with their start and end apart: 26 -> 26, of which waited for: 16 -> 14; matrix products, arithmetic and copies ran while one was open for 2% -> 2% of each run, Pallas kernels for 14% -> 11%
where the time goes in v8:
time: 84.2 us; the launch traced here: 84 us
  waiting for transfers between devices  37 us (44%)
  starting transfers between devices  26.8 us (32%)
  Pallas kernels  17 us (20%)
  between operations  1.55 us (2%)
  local copies, waits for them, and re-layouts  1.5 us (2%)
    ppermute x15, waiting for transfers between devices, swap_mixed(): lax.ppermute(value, AXES, [(at, at ^ masks[at & 1]) for at in range(32)])  22.6 us
    ppermute x15, starting transfers between devices, swap_mixed(): lax.ppermute(value, AXES, [(at, at ^ masks[at & 1]) for at in range(32)])  18.3 us
    ppermute x11, waiting for transfers between devices, swap(): return lax.ppermute(value, AXES, [(at, at ^ mask) for at in range(32)])  14.5 us
    ppermute x11, starting transfers between devices, swap(): return lax.ppermute(value, AXES, [(at, at ^ mask) for at in range(32)])  8.52 us
    pallas_call x1, Pallas kernels, shards(): call(finish_kernel, outs, [SMEM] * 2 + [VMEM] * 8, out_specs=[HBM] * 2 +...  3.69 us
    pallas_call x1, Pallas kernels, shards(): call(term_kernel, [((SLOTS, 128, CO), LOW)] + [((count, 128, CO), LOW) fo...  2.9 us
    pallas_call x1, Pallas kernels, shards(): call(moments_kernel, [((BLK, 128), WIDE), ((NB,), jnp.int32)], [SMEM] + [...  2.67 us
    pallas_call x1, Pallas kernels, shards(): call(old_hidden_kernel, [((PIX, CO), WIDE)], [VMEM] * 2, flops=2 * 27 * 5...  2 us
  transfers between devices with their start and end apart: 26, of which 14 were waited for; matrix products, arithmetic and copies ran while one was open for 2% of the time, Pallas kernels for 11%

profile of v8, /device:TPU:0, one launch (start us, length us, event | category | flops | bytes accessed | tf_op | source)
XLA Modules:
  0.0 84.0 jit_solution(4772005946193502796)
XLA Ops:
  1.7 1.2 %copy.26 = bf16[1,4,18,18,256]{4,3,2,1,0:T(8,128)(2,1)S(1)} copy(bf16[1,4,18,18,256]{4,1,3,2,0:T(4,128)(2,1)} %param.12) | data formatting | bytes 1327104 | tf_op args[2]
  2.9 1.4 %shard_map.137 = (bf16[4480,256]{1,0:T(8,128)(2,1)S(1)}, bf16[512,256]{1,0:T(8,128)(2,1)S(1)}, bf16[256,256]{1,0:T(8,128)(2,1)S(1)}) custom-call(bf16[4,18,18,256]{3,2,1,0:T(8,128)(2,1)S(1)} %bitcast.11, bf16[512,256]{1,0:T(8,128)(2,1)} %refs_1_.2, bf16[512,256]{1,0:T(8,128)(2,1)} %refs_2_.2, bf16[256,256]{1,0:T(8,128)(2,1)} %refs_3_.1), custom_call_target="tpu_custom_call" | custom-call | bytes 4194304 | tf_op jit(solution)/shard_map/pallas_call | solution.py:543
  4.5 2.9 %shard_map.138 = (bf16[14,128,256]{2,1,0:T(8,128)(2,1)S(1)}, bf16[10,128,256]{2,1,0:T(8,128)(2,1)S(1)}, bf16[4,128,256]{2,1,0:T(8,128)(2,1)S(1)}) custom-call(bf16[4480,256]{1,0:T(8,128)(2,1)S(1)} %get-tuple-element.37.refs_0_, bf16[4,18,18,256]{3,2,1,0:T(8,128)(2,1)S(1)} %bitcast.13, bf16[512,256]{1,0:T(8,128)(2,1)S(1)} %collective-permute-done.1.refs_2_, ...), custom_call_target="tpu_custom_call" | custom-call | flops 1879048192 | bytes 6291456 | tf_op jit(solution)/shard_map/pallas_call | solution.py:551
  7.4 2.6 %collective-permute-start.4 = (bf16[10,128,256]{2,1,0:T(8,128)(2,1)S(1)}, bf16[10,128,256]{2,1,0:T(8,128)(2,1)S(1)}, u32[]{:S(2)}, u32[]{:S(2)}) collective-permute-start(bf16[10,128,256]{2,1,0:T(8,128)(2,1)S(1)} %get-tuple-element.41), channel_id=1, source_target_pairs={{0,8},{1,17},{2,10},{3,19},{4,12},{5,21},{6,14},{7,23},{8,0},{9,25... | collective-permute-start | bytes 1966088 | tf_op jit(solution)/shard_map/ppermute | solution.py:143
  10.0 1.6 %collective-permute-start.5 = (bf16[4,128,256]{2,1,0:T(8,128)(2,1)S(1)}, bf16[4,128,256]{2,1,0:T(8,128)(2,1)S(1)}, u32[]{:S(2)}, u32[]{:S(2)}) collective-permute-start(bf16[4,128,256]{2,1,0:T(8,128)(2,1)S(1)} %get-tuple-element.42), channel_id=1, source_target_pairs={{0,2},{1,3},{2,0},{3,1},{4,6},{5,7},{6,4},{7,5},{8,10},{9,11},{10,... | collective-permute-start | bytes 786440 | tf_op jit(solution)/shard_map/ppermute | solution.py:143
  11.6 1.0 %shard_map.139.refs_0_ = bf16[15,16,256]{2,1,0:T(8,128)(2,1)S(1)} custom-call(bf16[14,128,256]{2,1,0:T(8,128)(2,1)S(1)} %get-tuple-element.40.refs_0_.refs_2_, f32[896,256]{1,0:T(8,128)} %refs_5_.1, f32[7,128]{1,0:T(8,128)} %bitcast.14), custom_call_target="tpu_custom_call" | custom-call | tf_op jit(solution)/shard_map/pallas_call | solution.py:561
  12.6 2.7 %collective-permute-start.3 = (bf16[15,16,256]{2,1,0:T(8,128)(2,1)S(1)}, bf16[15,16,256]{2,1,0:T(8,128)(2,1)S(1)}, u32[]{:S(2)}, u32[]{:S(2)}) collective-permute-start(bf16[15,16,256]{2,1,0:T(8,128)(2,1)S(1)} %shard_map.139.refs_0_), channel_id=1, source_target_pairs={{0,4},{1,5},{2,6},{3,7},{4,0},{5,1},{6,2},{7,3},{8,12},{9,13},{10,... | collective-permute-start | bytes 368648 | tf_op jit(solution)/shard_map/ppermute | solution.py:139
  15.2 4.9 %collective-permute-done.3.refs_1_ = bf16[15,16,256]{2,1,0:T(8,128)(2,1)S(1)} collective-permute-done((bf16[15,16,256]{2,1,0:T(8,128)(2,1)S(1)}, bf16[15,16,256]{2,1,0:T(8,128)(2,1)S(1)}, u32[]{:S(2)}, u32[]{:S(2)}) %collective-permute-start.3) | collective-permute-done | bytes 122912 | tf_op jit(solution)/shard_map/ppermute | solution.py:139
  20.1 0.9 %collective-permute-done.5.refs_4_ = bf16[4,128,256]{2,1,0:T(8,128)(2,1)S(1)} collective-permute-done((bf16[4,128,256]{2,1,0:T(8,128)(2,1)S(1)}, bf16[4,128,256]{2,1,0:T(8,128)(2,1)S(1)}, u32[]{:S(2)}, u32[]{:S(2)}) %collective-permute-start.5) | collective-permute-done | bytes 262176 | tf_op jit(solution)/shard_map/ppermute | solution.py:143
  21.6 1.6 %collective-permute-start.8 = (bf16[4,64,256]{2,1,0:T(8,128)(2,1)S(1)}, bf16[4,64,256]{2,1,0:T(8,128)(2,1)S(1)}, u32[]{:S(2)}, u32[]{:S(2)}) collective-permute-start(bf16[4,64,256]{2,1,0:T(8,128)(2,1)S(1)} %get-tuple-element.46), channel_id=1, source_target_pairs={{0,8},{1,17},{2,10},{3,19},{4,12},{5,21},{6,14},{7,23},{8,0},{9,25... | collective-permute-start | bytes 393224 | tf_op jit(solution)/shard_map/ppermute | solution.py:143
  23.2 2.6 %collective-permute-start.6 = (bf16[2,15,16,256]{3,2,1,0:T(8,128)(2,1)S(1)}, bf16[2,15,16,256]{3,2,1,0:T(8,128)(2,1)S(1)}, u32[]{:S(2)}, u32[]{:S(2)}) collective-permute-start(bf16[2,15,16,256]{3,2,1,0:T(8,128)(2,1)S(1)} %get-tuple-element.43.refs_0_), channel_id=1, source_target_pairs={{0,2},{1,3},{2,0},{3,1},{4,6},{5,7},{6,4},{7,5},{8,10},{9,11},{10,... | collective-permute-start | bytes 737288 | tf_op jit(solution)/shard_map/ppermute | solution.py:139
  25.8 2.2 %collective-permute-done.8.refs_2_ = bf16[4,64,256]{2,1,0:T(8,128)(2,1)S(1)} collective-permute-done((bf16[4,64,256]{2,1,0:T(8,128)(2,1)S(1)}, bf16[4,64,256]{2,1,0:T(8,128)(2,1)S(1)}, u32[]{:S(2)}, u32[]{:S(2)}) %collective-permute-start.8) | collective-permute-done | bytes 131104 | tf_op jit(solution)/shard_map/ppermute | solution.py:143
  28.0 1.1 %collective-permute-done.7.refs_1_ = bf16[10,64,256]{2,1,0:T(8,128)(2,1)S(1)} collective-permute-done((bf16[10,64,256]{2,1,0:T(8,128)(2,1)S(1)}, bf16[10,64,256]{2,1,0:T(8,128)(2,1)S(1)}, u32[]{:S(2)}, u32[]{:S(2)}) %collective-permute-start.7) | collective-permute-done | bytes 327712 | tf_op jit(solution)/shard_map/ppermute | solution.py:143
  29.2 3.2 %collective-permute-start.9 = (bf16[10,32,256]{2,1,0:T(8,128)(2,1)S(1)}, bf16[10,32,256]{2,1,0:T(8,128)(2,1)S(1)}, u32[]{:S(2)}, u32[]{:S(2)}) collective-permute-start(bf16[10,32,256]{2,1,0:T(8,128)(2,1)S(1)} %get-tuple-element.48), channel_id=1, source_target_pairs={{0,2},{1,3},{2,0},{3,1},{4,6},{5,7},{6,4},{7,5},{8,10},{9,11},{10,... | collective-permute-start | bytes 491528 | tf_op jit(solution)/shard_map/ppermute | solution.py:143
  32.7 4.0 %collective-permute-done.10.refs_4_ = bf16[4,32,256]{2,1,0:T(8,128)(2,1)S(1)} collective-permute-done((bf16[4,32,256]{2,1,0:T(8,128)(2,1)S(1)}, bf16[4,32,256]{2,1,0:T(8,128)(2,1)S(1)}, u32[]{:S(2)}, u32[]{:S(2)}) %collective-permute-start.10) | collective-permute-done | bytes 65568 | tf_op jit(solution)/shard_map/ppermute | solution.py:143
  37.5 1.6 %collective-permute-start.12 = (bf16[14,32,256]{2,1,0:T(8,128)(2,1)S(1)}, bf16[14,32,256]{2,1,0:T(8,128)(2,1)S(1)}, u32[]{:S(2)}, u32[]{:S(2)}) collective-permute-start(bf16[14,32,256]{2,1,0:T(8,128)(2,1)S(1)} %get-tuple-element.52.refs_1_), channel_id=1, source_target_pairs={{0,4},{1,5},{2,6},{3,7},{4,0},{5,1},{6,2},{7,3},{8,12},{9,13},{10,... | collective-permute-start | bytes 688136 | tf_op jit(solution)/shard_map/ppermute | solution.py:139
  40.3 2.7 %shard_map.143 = (f32[32,128]{1,0:T(8,128)S(1)}, s32[224]{0:T(256)S(1)}) custom-call(s32[224]{0:T(256)S(1)} %copy-done.1, bf16[4,16,256]{2,1,0:T(8,128)(2,1)S(1)} %get-tuple-element.50.refs_1_, bf16[4,16,256]{2,1,0:T(8,128)(2,1)S(1)} %collective-permute-done.11.refs_2_), custom_call_target="tpu_custom_call" | custom-call | tf_op jit(solution)/shard_map/pallas_call | solution.py:597
  43.0 7.0 %collective-permute-done.12.refs_2_ = bf16[14,32,256]{2,1,0:T(8,128)(2,1)S(1)} collective-permute-done((bf16[14,32,256]{2,1,0:T(8,128)(2,1)S(1)}, bf16[14,32,256]{2,1,0:T(8,128)(2,1)S(1)}, u32[]{:S(2)}, u32[]{:S(2)}) %collective-permute-start.12) | collective-permute-done | bytes 229408 | tf_op jit(solution)/shard_map/ppermute | solution.py:139
  51.4 1.2 %collective-permute-start.17 = (bf16[5,32,256]{2,1,0:T(8,128)(2,1)S(1)}, bf16[5,32,256]{2,1,0:T(8,128)(2,1)S(1)}, u32[]{:S(2)}, u32[]{:S(2)}) collective-permute-start(bf16[5,32,256]{2,1,0:T(8,128)(2,1)S(1)} %get-tuple-element.57.refs_3_), channel_id=1, source_target_pairs={{0,16},{1,9},{2,18},{3,11},{4,20},{5,13},{6,22},{7,15},{8,24},{9,1... | collective-permute-start | bytes 245768 | tf_op jit(solution)/shard_map/ppermute | solution.py:143
  53.0 3.7 %collective-permute-done.17.refs_4_ = bf16[5,32,256]{2,1,0:T(8,128)(2,1)S(1)} collective-permute-done((bf16[5,32,256]{2,1,0:T(8,128)(2,1)S(1)}, bf16[5,32,256]{2,1,0:T(8,128)(2,1)S(1)}, u32[]{:S(2)}, u32[]{:S(2)}) %collective-permute-start.17) | collective-permute-done | bytes 81952 | tf_op jit(solution)/shard_map/ppermute | solution.py:143
  57.2 1.7 %collective-permute-start.18 = (bf16[10,64,256]{2,1,0:T(8,128)(2,1)S(1)}, bf16[10,64,256]{2,1,0:T(8,128)(2,1)S(1)}, u32[]{:S(2)}, u32[]{:S(2)}) collective-permute-start(bf16[10,64,256]{2,1,0:T(8,128)(2,1)S(1)} %get-tuple-element.58.refs_1_), channel_id=1, source_target_pairs={{0,16},{1,9},{2,18},{3,11},{4,20},{5,13},{6,22},{7,15},{8,24},{9,1... | collective-permute-start | bytes 983048 | tf_op jit(solution)/shard_map/ppermute | solution.py:143
  58.9 0.9 %collective-permute-start.19 = (bf16[5,64,256]{2,1,0:T(8,128)(2,1)S(1)}, bf16[5,64,256]{2,1,0:T(8,128)(2,1)S(1)}, u32[]{:S(2)}, u32[]{:S(2)}) collective-permute-start(bf16[5,64,256]{2,1,0:T(8,128)(2,1)S(1)} %get-tuple-element.59.refs_3_), channel_id=1, source_target_pairs={{0,8},{1,17},{2,10},{3,19},{4,12},{5,21},{6,14},{7,23},{8,0},{9,25... | collective-permute-start | bytes 491528 | tf_op jit(solution)/shard_map/ppermute | solution.py:143
  59.8 5.4 %collective-permute-done.19.refs_4_ = bf16[5,64,256]{2,1,0:T(8,128)(2,1)S(1)} collective-permute-done((bf16[5,64,256]{2,1,0:T(8,128)(2,1)S(1)}, bf16[5,64,256]{2,1,0:T(8,128)(2,1)S(1)}, u32[]{:S(2)}, u32[]{:S(2)}) %collective-permute-start.19) | collective-permute-done | bytes 163872 | tf_op jit(solution)/shard_map/ppermute | solution.py:143
  65.4 1.3 %collective-permute-start.23 = (bf16[10,128,256]{2,1,0:T(8,128)(2,1)S(1)}, bf16[10,128,256]{2,1,0:T(8,128)(2,1)S(1)}, u32[]{:S(2)}, u32[]{:S(2)}) collective-permute-start(bf16[10,128,256]{2,1,0:T(8,128)(2,1)S(1)} %get-tuple-element.62.refs_1_), channel_id=1, source_target_pairs={{0,8},{1,17},{2,10},{3,19},{4,12},{5,21},{6,14},{7,23},{8,0},{9,25... | collective-permute-start | bytes 1966088 | tf_op jit(solution)/shard_map/ppermute | solution.py:143
  66.7 1.7 %collective-permute-start.24 = (bf16[5,128,256]{2,1,0:T(8,128)(2,1)S(1)}, bf16[5,128,256]{2,1,0:T(8,128)(2,1)S(1)}, u32[]{:S(2)}, u32[]{:S(2)}) collective-permute-start(bf16[5,128,256]{2,1,0:T(8,128)(2,1)S(1)} %get-tuple-element.63.refs_3_), channel_id=1, source_target_pairs={{0,2},{1,3},{2,0},{3,1},{4,6},{5,7},{6,4},{7,5},{8,10},{9,11},{10,... | collective-permute-start | bytes 983048 | tf_op jit(solution)/shard_map/ppermute | solution.py:143
  69.0 1.0 %collective-permute-done.21.refs_5_ = bf16[2,224,256]{2,1,0:T(8,128)(2,1)S(1)} collective-permute-done((bf16[2,224,256]{2,1,0:T(8,128)(2,1)S(1)}, bf16[2,224,256]{2,1,0:T(8,128)(2,1)S(1)}, u32[]{:S(2)}, u32[]{:S(2)}) %collective-permute-start.21) | collective-permute-done | bytes 229408 | tf_op jit(solution)/shard_map/ppermute | solution.py:139
  70.3 1.0 %shard_map.148.refs_0_.refs_1_.refs_4_ = bf16[7168,256]{1,0:T(8,128)(2,1)S(1)} custom-call(s32[224]{0:T(256)S(1)} %copy-done.1, bf16[3,4,224,256]{3,2,1,0:T(8,128)(2,1)S(1)} %get-tuple-element.55.refs_1_, bf16[2,224,256]{2,1,0:T(8,128)(2,1)S(1)} %get-tuple-element.60.refs_2_, bf16[2,224,256]{2,1,0:T(8,128)(2,1)S(1)} %get-tuple-element.61.refs_3_, ...), custom_call_target="tpu_custom_call" | custom-call | bytes 8388608 | tf_op jit(solution)/shard_map/pallas_call | solution.py:635
  71.3 4.8 %collective-permute-done.24.refs_4_ = bf16[5,128,256]{2,1,0:T(8,128)(2,1)S(1)} collective-permute-done((bf16[5,128,256]{2,1,0:T(8,128)(2,1)S(1)}, bf16[5,128,256]{2,1,0:T(8,128)(2,1)S(1)}, u32[]{:S(2)}, u32[]{:S(2)}) %collective-permute-start.24) | collective-permute-done | bytes 327712 | tf_op jit(solution)/shard_map/ppermute | solution.py:143
  76.3 1.1 %shard_map.151.refs_9_ = f32[512,256]{1,0:T(8,128)S(1)} custom-call(bf16[3456,256]{1,0:T(8,128)(2,1)S(1)} %shard_map.144.refs_0_.refs_3_, bf16[15,256,256]{2,1,0:T(8,128)(2,1)S(1)} %shard_map.149.refs_1_.refs_6_), custom_call_target="tpu_custom_call" | custom-call | flops 939524096 | bytes 4194304 | tf_op jit(solution)/shard_map/pallas_call | solution.py:647
  77.5 2.0 %shard_map.150.refs_8_ = f32[512,256]{1,0:T(8,128)S(1)} custom-call(bf16[3456,256]{1,0:T(8,128)(2,1)S(1)} %shard_map.144.refs_0_.refs_3_, bf16[7168,256]{1,0:T(8,128)(2,1)S(1)} %shard_map.148.refs_0_.refs_1_.refs_4_), custom_call_target="tpu_custom_call" | custom-call | flops 1811939328 | bytes 6291456 | tf_op jit(solution)/shard_map/pallas_call | solution.py:640
  79.5 0.8 collective-permute-done.25.refs_7_
  80.3 3.7 %shard_map.152 = (f32[896,256]{1,0:T(8,128)}, f32[896,256]{1,0:T(8,128)}, f32[7,128]{1,0:T(8,128)}, f32[2,256]{1,0:T(2,128)}, bf16[512,256]{1,0:T(8,128)(2,1)}) custom-call(s32[224]{0:T(256)S(1)} %get-tuple-element.51.refs_0_, f32[1]{0:T(128)S(6)} %sub.3.refs_0_.refs_1_, f32[2,256]{1,0:T(2,128)S(1)} %copy-done.2, ...), custom_call_target="tpu_custom_call" | custom-call | flops 1073741824 | bytes 16777216 | tf_op jit(solution)/shard_map/pallas_call | solution.py:662
  (47 shorter events, 6.8 us)
Async XLA Ops:
  0.6 3.7 %collective-permute-start = (bf16[1,4,18,18,256]{4,1,3,2,0:T(4,128)(2,1)}, bf16[1,4,18,18,256]{4,1,3,2,0:T(4,128)(2,1)S(1)}, u32[]{:S(2)}, u32[]{:S(2)}) collective-permute-start(bf16[1,4,18,18,256]{4,1,3,2,0:T(4,128)(2,1)} %param.12), channel_id=1, source_target_pairs={{0,1},{1,0},{2,3},{3,2},{4,5},{5,4},{6,7},{7,6},{8,9},{9,8},{10,11... | collective-permute-start | bytes 1990664 | tf_op jit(solution)/shard_map/ppermute | solution.py:139
  1.1 3.3 %collective-permute-start.1 = (bf16[512,256]{1,0:T(8,128)(2,1)}, bf16[512,256]{1,0:T(8,128)(2,1)S(1)}, u32[]{:S(2)}, u32[]{:S(2)}) collective-permute-start(bf16[512,256]{1,0:T(8,128)(2,1)} %refs_1_.2), channel_id=1, source_target_pairs={{0,1},{1,0},{2,3},{3,2},{4,5},{5,4},{6,7},{7,6},{8,9},{9,8},{10,11... | collective-permute-start | bytes 786440 | tf_op jit(solution)/shard_map/ppermute | solution.py:139
  1.2 3.2 %collective-permute-start.2 = (bf16[512,256]{1,0:T(8,128)(2,1)}, bf16[512,256]{1,0:T(8,128)(2,1)S(1)}, u32[]{:S(2)}, u32[]{:S(2)}) collective-permute-start(bf16[512,256]{1,0:T(8,128)(2,1)} %refs_2_.2), channel_id=1, source_target_pairs={{0,1},{1,0},{2,3},{3,2},{4,5},{5,4},{6,7},{7,6},{8,9},{9,8},{10,11... | collective-permute-start | bytes 786440 | tf_op jit(solution)/shard_map/ppermute | solution.py:139
  7.4 13.7 %collective-permute-start.4 = (bf16[10,128,256]{2,1,0:T(8,128)(2,1)S(1)}, bf16[10,128,256]{2,1,0:T(8,128)(2,1)S(1)}, u32[]{:S(2)}, u32[]{:S(2)}) collective-permute-start(bf16[10,128,256]{2,1,0:T(8,128)(2,1)S(1)} %get-tuple-element.41), channel_id=1, source_target_pairs={{0,8},{1,17},{2,10},{3,19},{4,12},{5,21},{6,14},{7,23},{8,0},{9,25... | collective-permute-start | bytes 1966088 | tf_op jit(solution)/shard_map/ppermute | solution.py:143
  10.0 11.0 %collective-permute-start.5 = (bf16[4,128,256]{2,1,0:T(8,128)(2,1)S(1)}, bf16[4,128,256]{2,1,0:T(8,128)(2,1)S(1)}, u32[]{:S(2)}, u32[]{:S(2)}) collective-permute-start(bf16[4,128,256]{2,1,0:T(8,128)(2,1)S(1)} %get-tuple-element.42), channel_id=1, source_target_pairs={{0,2},{1,3},{2,0},{3,1},{4,6},{5,7},{6,4},{7,5},{8,10},{9,11},{10,... | collective-permute-start | bytes 786440 | tf_op jit(solution)/shard_map/ppermute | solution.py:143
  12.5 27.7 %copy-start.1 = (s32[224]{0:T(256)S(1)}, s32[224]{0:T(256)}, u32[]{:S(2)}) copy-start(s32[224]{0:T(256)} %refs_0_.3) | copy-start | bytes 2692
  12.6 7.5 %collective-permute-start.3 = (bf16[15,16,256]{2,1,0:T(8,128)(2,1)S(1)}, bf16[15,16,256]{2,1,0:T(8,128)(2,1)S(1)}, u32[]{:S(2)}, u32[]{:S(2)}) collective-permute-start(bf16[15,16,256]{2,1,0:T(8,128)(2,1)S(1)} %shard_map.139.refs_0_), channel_id=1, source_target_pairs={{0,4},{1,5},{2,6},{3,7},{4,0},{5,1},{6,2},{7,3},{8,12},{9,13},{10,... | collective-permute-start | bytes 368648 | tf_op jit(solution)/shard_map/ppermute | solution.py:139
  21.2 31.4 %copy-start.3 = (bf16[1,4,18,18,256]{4,1,3,2,0:T(4,128)(2,1)S(1)}, bf16[1,4,18,18,256]{4,1,3,2,0:T(4,128)(2,1)}, u32[]{:S(2)}) copy-start(bf16[1,4,18,18,256]{4,1,3,2,0:T(4,128)(2,1)} %param.19) | copy-start | bytes 1990660
  21.2 8.0 %collective-permute-start.7 = (bf16[10,64,256]{2,1,0:T(8,128)(2,1)S(1)}, bf16[10,64,256]{2,1,0:T(8,128)(2,1)S(1)}, u32[]{:S(2)}, u32[]{:S(2)}) collective-permute-start(bf16[10,64,256]{2,1,0:T(8,128)(2,1)S(1)} %get-tuple-element.45), channel_id=1, source_target_pairs={{0,16},{1,9},{2,18},{3,11},{4,20},{5,13},{6,22},{7,15},{8,24},{9,1... | collective-permute-start | bytes 983048 | tf_op jit(solution)/shard_map/ppermute | solution.py:143
  21.6 6.4 %collective-permute-start.8 = (bf16[4,64,256]{2,1,0:T(8,128)(2,1)S(1)}, bf16[4,64,256]{2,1,0:T(8,128)(2,1)S(1)}, u32[]{:S(2)}, u32[]{:S(2)}) collective-permute-start(bf16[4,64,256]{2,1,0:T(8,128)(2,1)S(1)} %get-tuple-element.46), channel_id=1, source_target_pairs={{0,8},{1,17},{2,10},{3,19},{4,12},{5,21},{6,14},{7,23},{8,0},{9,25... | collective-permute-start | bytes 393224 | tf_op jit(solution)/shard_map/ppermute | solution.py:143
  23.2 9.5 %collective-permute-start.6 = (bf16[2,15,16,256]{3,2,1,0:T(8,128)(2,1)S(1)}, bf16[2,15,16,256]{3,2,1,0:T(8,128)(2,1)S(1)}, u32[]{:S(2)}, u32[]{:S(2)}) collective-permute-start(bf16[2,15,16,256]{3,2,1,0:T(8,128)(2,1)S(1)} %get-tuple-element.43.refs_0_), channel_id=1, source_target_pairs={{0,2},{1,3},{2,0},{3,1},{4,6},{5,7},{6,4},{7,5},{8,10},{9,11},{10,... | collective-permute-start | bytes 737288 | tf_op jit(solution)/shard_map/ppermute | solution.py:139
  29.2 7.5 %collective-permute-start.9 = (bf16[10,32,256]{2,1,0:T(8,128)(2,1)S(1)}, bf16[10,32,256]{2,1,0:T(8,128)(2,1)S(1)}, u32[]{:S(2)}, u32[]{:S(2)}) collective-permute-start(bf16[10,32,256]{2,1,0:T(8,128)(2,1)S(1)} %get-tuple-element.48), channel_id=1, source_target_pairs={{0,2},{1,3},{2,0},{3,1},{4,6},{5,7},{6,4},{7,5},{8,10},{9,11},{10,... | collective-permute-start | bytes 491528 | tf_op jit(solution)/shard_map/ppermute | solution.py:143
  32.4 4.3 %collective-permute-start.10 = (bf16[4,32,256]{2,1,0:T(8,128)(2,1)S(1)}, bf16[4,32,256]{2,1,0:T(8,128)(2,1)S(1)}, u32[]{:S(2)}, u32[]{:S(2)}) collective-permute-start(bf16[4,32,256]{2,1,0:T(8,128)(2,1)S(1)} %get-tuple-element.49), channel_id=1, source_target_pairs={{0,16},{1,9},{2,18},{3,11},{4,20},{5,13},{6,22},{7,15},{8,24},{9,1... | collective-permute-start | bytes 196616 | tf_op jit(solution)/shard_map/ppermute | solution.py:143
  36.7 13.2 %collective-permute-start.14 = (bf16[4,224,256]{2,1,0:T(8,128)(2,1)S(1)}, bf16[4,224,256]{2,1,0:T(8,128)(2,1)S(1)}, u32[]{:S(2)}, u32[]{:S(2)}) collective-permute-start(bf16[4,224,256]{2,1,0:T(8,128)(2,1)S(1)} %get-tuple-element.54.refs_4_), channel_id=1, source_target_pairs={{0,8},{1,17},{2,10},{3,19},{4,12},{5,21},{6,14},{7,23},{8,0},{9,25... | collective-permute-start | bytes 1376264 | tf_op jit(solution)/shard_map/ppermute | solution.py:143
  37.3 12.6 %collective-permute-start.13 = (bf16[4,224,256]{2,1,0:T(8,128)(2,1)S(1)}, bf16[4,224,256]{2,1,0:T(8,128)(2,1)S(1)}, u32[]{:S(2)}, u32[]{:S(2)}) collective-permute-start(bf16[4,224,256]{2,1,0:T(8,128)(2,1)S(1)} %get-tuple-element.54.refs_4_), channel_id=1, source_target_pairs={{0,16},{1,9},{2,18},{3,11},{4,20},{5,13},{6,22},{7,15},{8,24},{9,1... | collective-permute-start | bytes 1376264 | tf_op jit(solution)/shard_map/ppermute | solution.py:143
  37.5 12.5 %collective-permute-start.12 = (bf16[14,32,256]{2,1,0:T(8,128)(2,1)S(1)}, bf16[14,32,256]{2,1,0:T(8,128)(2,1)S(1)}, u32[]{:S(2)}, u32[]{:S(2)}) collective-permute-start(bf16[14,32,256]{2,1,0:T(8,128)(2,1)S(1)} %get-tuple-element.52.refs_1_), channel_id=1, source_target_pairs={{0,4},{1,5},{2,6},{3,7},{4,0},{5,1},{6,2},{7,3},{8,12},{9,13},{10,... | collective-permute-start | bytes 688136 | tf_op jit(solution)/shard_map/ppermute | solution.py:139
  39.1 1.2 %collective-permute-start.11 = (bf16[4,16,256]{2,1,0:T(8,128)(2,1)S(1)}, bf16[4,16,256]{2,1,0:T(8,128)(2,1)S(1)}, u32[]{:S(2)}, u32[]{:S(2)}) collective-permute-start(bf16[4,16,256]{2,1,0:T(8,128)(2,1)S(1)} %get-tuple-element.50.refs_1_), channel_id=1, source_target_pairs={{0,1},{1,0},{2,3},{3,2},{4,5},{5,4},{6,7},{7,6},{8,9},{9,8},{10,11... | collective-permute-start | bytes 98312 | tf_op jit(solution)/shard_map/ppermute | solution.py:139
  50.4 19.9 %collective-permute-start.20 = (bf16[3,4,224,256]{3,2,1,0:T(8,128)(2,1)S(1)}, bf16[3,4,224,256]{3,2,1,0:T(8,128)(2,1)S(1)}, u32[]{:S(2)}, u32[]{:S(2)}) collective-permute-start(bf16[3,4,224,256]{3,2,1,0:T(8,128)(2,1)S(1)} %get-tuple-element.55.refs_1_), channel_id=1, source_target_pairs={{0,1},{1,0},{2,3},{3,2},{4,5},{5,4},{6,7},{7,6},{8,9},{9,8},{10,11... | collective-permute-start | bytes 4128776 | tf_op jit(solution)/shard_map/ppermute | solution.py:139
  50.5 6.6 %collective-permute-start.16 = (bf16[10,32,256]{2,1,0:T(8,128)(2,1)S(1)}, bf16[10,32,256]{2,1,0:T(8,128)(2,1)S(1)}, u32[]{:S(2)}, u32[]{:S(2)}) collective-permute-start(bf16[10,32,256]{2,1,0:T(8,128)(2,1)S(1)} %get-tuple-element.56.refs_1_), channel_id=1, source_target_pairs={{0,2},{1,3},{2,0},{3,1},{4,6},{5,7},{6,4},{7,5},{8,10},{9,11},{10,... | collective-permute-start | bytes 491528 | tf_op jit(solution)/shard_map/ppermute | solution.py:143
  50.6 14.7 %collective-permute-start.15 = (bf16[4,224,256]{2,1,0:T(8,128)(2,1)S(1)}, bf16[4,224,256]{2,1,0:T(8,128)(2,1)S(1)}, u32[]{:S(2)}, u32[]{:S(2)}) collective-permute-start(bf16[4,224,256]{2,1,0:T(8,128)(2,1)S(1)} %collective-permute-done.13.refs_5_), channel_id=1, source_target_pairs={{0,8},{1,17},{2,10},{3,19},{4,12},{5,21},{6,14},{7,23},{8,0},{9,25... | collective-permute-start | bytes 1376264 | tf_op jit(solution)/shard_map/ppermute | solution.py:143
  51.4 5.4 %collective-permute-start.17 = (bf16[5,32,256]{2,1,0:T(8,128)(2,1)S(1)}, bf16[5,32,256]{2,1,0:T(8,128)(2,1)S(1)}, u32[]{:S(2)}, u32[]{:S(2)}) collective-permute-start(bf16[5,32,256]{2,1,0:T(8,128)(2,1)S(1)} %get-tuple-element.57.refs_3_), channel_id=1, source_target_pairs={{0,16},{1,9},{2,18},{3,11},{4,20},{5,13},{6,22},{7,15},{8,24},{9,1... | collective-permute-start | bytes 245768 | tf_op jit(solution)/shard_map/ppermute | solution.py:143
  57.2 8.1 %collective-permute-start.18 = (bf16[10,64,256]{2,1,0:T(8,128)(2,1)S(1)}, bf16[10,64,256]{2,1,0:T(8,128)(2,1)S(1)}, u32[]{:S(2)}, u32[]{:S(2)}) collective-permute-start(bf16[10,64,256]{2,1,0:T(8,128)(2,1)S(1)} %get-tuple-element.58.refs_1_), channel_id=1, source_target_pairs={{0,16},{1,9},{2,18},{3,11},{4,20},{5,13},{6,22},{7,15},{8,24},{9,1... | collective-permute-start | bytes 983048 | tf_op jit(solution)/shard_map/ppermute | solution.py:143
  58.9 6.4 %collective-permute-start.19 = (bf16[5,64,256]{2,1,0:T(8,128)(2,1)S(1)}, bf16[5,64,256]{2,1,0:T(8,128)(2,1)S(1)}, u32[]{:S(2)}, u32[]{:S(2)}) collective-permute-start(bf16[5,64,256]{2,1,0:T(8,128)(2,1)S(1)} %get-tuple-element.59.refs_3_), channel_id=1, source_target_pairs={{0,8},{1,17},{2,10},{3,19},{4,12},{5,21},{6,14},{7,23},{8,0},{9,25... | collective-permute-start | bytes 491528 | tf_op jit(solution)/shard_map/ppermute | solution.py:143
  65.4 10.7 %collective-permute-start.23 = (bf16[10,128,256]{2,1,0:T(8,128)(2,1)S(1)}, bf16[10,128,256]{2,1,0:T(8,128)(2,1)S(1)}, u32[]{:S(2)}, u32[]{:S(2)}) collective-permute-start(bf16[10,128,256]{2,1,0:T(8,128)(2,1)S(1)} %get-tuple-element.62.refs_1_), channel_id=1, source_target_pairs={{0,8},{1,17},{2,10},{3,19},{4,12},{5,21},{6,14},{7,23},{8,0},{9,25... | collective-permute-start | bytes 1966088 | tf_op jit(solution)/shard_map/ppermute | solution.py:143
  66.7 9.3 %collective-permute-start.24 = (bf16[5,128,256]{2,1,0:T(8,128)(2,1)S(1)}, bf16[5,128,256]{2,1,0:T(8,128)(2,1)S(1)}, u32[]{:S(2)}, u32[]{:S(2)}) collective-permute-start(bf16[5,128,256]{2,1,0:T(8,128)(2,1)S(1)} %get-tuple-element.63.refs_3_), channel_id=1, source_target_pairs={{0,2},{1,3},{2,0},{3,1},{4,6},{5,7},{6,4},{7,5},{8,10},{9,11},{10,... | collective-permute-start | bytes 983048 | tf_op jit(solution)/shard_map/ppermute | solution.py:143
  68.5 1.5 %collective-permute-start.21 = (bf16[2,224,256]{2,1,0:T(8,128)(2,1)S(1)}, bf16[2,224,256]{2,1,0:T(8,128)(2,1)S(1)}, u32[]{:S(2)}, u32[]{:S(2)}) collective-permute-start(bf16[2,224,256]{2,1,0:T(8,128)(2,1)S(1)} %get-tuple-element.60.refs_2_), channel_id=1, source_target_pairs={{0,1},{1,0},{2,3},{3,2},{4,5},{5,4},{6,7},{7,6},{8,9},{9,8},{10,11... | collective-permute-start | bytes 688136 | tf_op jit(solution)/shard_map/ppermute | solution.py:139
  68.5 1.8 %collective-permute-start.22 = (bf16[2,224,256]{2,1,0:T(8,128)(2,1)S(1)}, bf16[2,224,256]{2,1,0:T(8,128)(2,1)S(1)}, u32[]{:S(2)}, u32[]{:S(2)}) collective-permute-start(bf16[2,224,256]{2,1,0:T(8,128)(2,1)S(1)} %get-tuple-element.61.refs_3_), channel_id=1, source_target_pairs={{0,1},{1,0},{2,3},{3,2},{4,5},{5,4},{6,7},{7,6},{8,9},{9,8},{10,11... | collective-permute-start | bytes 688136 | tf_op jit(solution)/shard_map/ppermute | solution.py:139
  76.2 4.0 %collective-permute-start.25 = (bf16[15,256,256]{2,1,0:T(8,128)(2,1)S(1)}, bf16[15,256,256]{2,1,0:T(8,128)(2,1)S(1)}, u32[]{:S(2)}, u32[]{:S(2)}) collective-permute-start(bf16[15,256,256]{2,1,0:T(8,128)(2,1)S(1)} %shard_map.149.refs_1_.refs_6_), channel_id=1, source_target_pairs={{0,1},{1,0},{2,3},{3,2},{4,5},{5,4},{6,7},{7,6},{8,9},{9,8},{10,11... | collective-permute-start | bytes 5898248 | tf_op jit(solution)/shard_map/ppermute | solution.py:139
  77.5 2.8 %copy-start = (f32[896,256]{1,0:T(8,128)S(1)}, f32[896,256]{1,0:T(8,128)}, u32[]{:S(2)}) copy-start(f32[896,256]{1,0:T(8,128)} %refs_5_.1) | copy-start | bytes 2752516
  77.5 2.8 %copy-start.2 = (f32[2,256]{1,0:T(2,128)S(1)}, f32[2,256]{1,0:T(2,128)}, u32[]{:S(2)}) copy-start(f32[2,256]{1,0:T(2,128)} %refs_2_.3) | copy-start | bytes 6148

commit v9 on v8

--- a/solution.py
+++ b/solution.py
@@ -460,8 +460,8 @@
 
 def finish_kernel(
     at, plan, rate, col_moment, views, natural, master, mine, peer, old, own_part,
-    update_far, master_far, new_row, new_col, next_output,
-    factor, row_table, update_rows, new_master, stored,
+    update_far, master_far, row_far, col_far, output_far,
+    factor, row_table, update_rows, new_master, new_row, new_col, next_output, stored, rest_stored,
 ):
     core = at[4]
     sums = [
@@ -475,7 +475,13 @@
     total = sum(sums[0][1:] + sums[1], sums[0][0])
     store_factors(total, rate[0], col_moment, new_col, factor)
 
-    copies = []
+    def store(source, target, index):
+        copy = pltpu.make_async_copy(source, target, rest_stored.at[index])
+        copy.start()
+        return [copy]
+
+    copies = store(new_col, col_far, 0)
+
     for line in range(7):
         for local in range(line * 4, line * 4 + 4):
             side, slot, first, kernel = (plan[local * 8 + item] for item in range(4))
@@ -501,6 +507,7 @@
     next_output[...] = jnp.dot(
         jax.nn.silu(hidden).astype(LOW), weights.astype(LOW), preferred_element_type=WIDE
     ).astype(LOW)
+    copies += store(next_output, output_far, 1)
 
     for side, messages in enumerate(sums):
         for sender in range(8):
@@ -518,6 +525,7 @@
             turned = pltpu.roll(row_table[pl.ds(from_row, 1), :], turn, 1)
             values = jnp.where(here, turned, values)
         new_row[line : line + 1] = values
+    copies += store(new_row, row_far, 2)
     for copy in copies:
         copy.wait()
 
@@ -663,13 +671,17 @@
         finish_kernel,
         outs,
         [SMEM] * 2 + [VMEM] * 8,
-        out_specs=[HBM] * 2 + [VMEM] * 3,
+        out_specs=[HBM] * 5,
         scratch=[
             pltpu.VMEM((2, CO), WIDE),
             pltpu.VMEM((64, 128), WIDE),
             pltpu.VMEM((NB // 8 * BLK, CO), WIDE),
             pltpu.VMEM((NB // 8 * BLK, CO), WIDE),
+            pltpu.VMEM((7, 128), WIDE),
+            pltpu.VMEM((2, CO), WIDE),
+            pltpu.VMEM((PIX, CO), LOW),
             pltpu.SemaphoreType.DMA((7, 2)),
+            pltpu.SemaphoreType.DMA((3,)),
         ],
         pin=False,
         flops=2 * 16 * 512 * 256 * 256,

time: 84.2 us -> 83.6 us (level)
  transfers between devices with their start and end apart: 26 -> 26, of which waited for: 14 -> 14; matrix products, arithmetic and copies ran while one was open for 2% -> 2% of each run, Pallas kernels for 11% -> 12%
where the time goes in v9:
time: 83.6 us; the launch traced here: 83.4 us
  waiting for transfers between devices  37 us (44%)
  starting transfers between devices  26.8 us (32%)
  Pallas kernels  16.5 us (20%)
  between operations  1.55 us (2%)
  local copies, waits for them, and re-layouts  1.5 us (2%)
    ppermute x15, waiting for transfers between devices, swap_mixed(): lax.ppermute(value, AXES, [(at, at ^ masks[at & 1]) for at in range(32)])  22.6 us
    ppermute x15, starting transfers between devices, swap_mixed(): lax.ppermute(value, AXES, [(at, at ^ masks[at & 1]) for at in range(32)])  18.3 us
    ppermute x11, waiting for transfers between devices, swap(): return lax.ppermute(value, AXES, [(at, at ^ mask) for at in range(32)])  14.5 us
    ppermute x11, starting transfers between devices, swap(): return lax.ppermute(value, AXES, [(at, at ^ mask) for at in range(32)])  8.52 us
    pallas_call x1, Pallas kernels, shards(): call(finish_kernel, outs, [SMEM] * 2 + [VMEM] * 8, out_specs=[HBM] * 5, s...  3.1 us
    pallas_call x1, Pallas kernels, shards(): call(term_kernel, [((SLOTS, 128, CO), LOW)] + [((count, 128, CO), LOW) fo...  2.9 us
    pallas_call x1, Pallas kernels, shards(): call(moments_kernel, [((BLK, 128), WIDE), ((NB,), jnp.int32)], [SMEM] + [...  2.67 us
    pallas_call x1, Pallas kernels, shards(): call(old_hidden_kernel, [((PIX, CO), WIDE)], [VMEM] * 2, flops=2 * 27 * 5...  2 us
  transfers between devices with their start and end apart: 26, of which 14 were waited for; matrix products, arithmetic and copies ran while one was open for 2% of the time, Pallas kernels for 12%

profile of v9, /device:TPU:0, one launch (start us, length us, event | category | flops | bytes accessed | tf_op | source)
XLA Modules:
  0.0 83.4 jit_solution(7489534874416960443)
XLA Ops:
  1.7 1.2 %copy.26 = bf16[1,4,18,18,256]{4,3,2,1,0:T(8,128)(2,1)S(1)} copy(bf16[1,4,18,18,256]{4,1,3,2,0:T(4,128)(2,1)} %param.12) | data formatting | bytes 1327104 | tf_op args[2]
  2.9 1.4 %shard_map.137 = (bf16[4480,256]{1,0:T(8,128)(2,1)S(1)}, bf16[512,256]{1,0:T(8,128)(2,1)S(1)}, bf16[256,256]{1,0:T(8,128)(2,1)S(1)}) custom-call(bf16[4,18,18,256]{3,2,1,0:T(8,128)(2,1)S(1)} %bitcast.11, bf16[512,256]{1,0:T(8,128)(2,1)} %refs_1_.2, bf16[512,256]{1,0:T(8,128)(2,1)} %refs_2_.2, bf16[256,256]{1,0:T(8,128)(2,1)} %refs_3_.1), custom_call_target="tpu_custom_call" | custom-call | bytes 4194304 | tf_op jit(solution)/shard_map/pallas_call | solution.py:551
  4.5 2.9 %shard_map.138 = (bf16[14,128,256]{2,1,0:T(8,128)(2,1)S(1)}, bf16[10,128,256]{2,1,0:T(8,128)(2,1)S(1)}, bf16[4,128,256]{2,1,0:T(8,128)(2,1)S(1)}) custom-call(bf16[4480,256]{1,0:T(8,128)(2,1)S(1)} %get-tuple-element.37.refs_0_, bf16[4,18,18,256]{3,2,1,0:T(8,128)(2,1)S(1)} %bitcast.13, bf16[512,256]{1,0:T(8,128)(2,1)S(1)} %collective-permute-done.1.refs_2_, ...), custom_call_target="tpu_custom_call" | custom-call | flops 1879048192 | bytes 6291456 | tf_op jit(solution)/shard_map/pallas_call | solution.py:559
  7.4 2.6 %collective-permute-start.4 = (bf16[10,128,256]{2,1,0:T(8,128)(2,1)S(1)}, bf16[10,128,256]{2,1,0:T(8,128)(2,1)S(1)}, u32[]{:S(2)}, u32[]{:S(2)}) collective-permute-start(bf16[10,128,256]{2,1,0:T(8,128)(2,1)S(1)} %get-tuple-element.41), channel_id=1, source_target_pairs={{0,8},{1,17},{2,10},{3,19},{4,12},{5,21},{6,14},{7,23},{8,0},{9,25... | collective-permute-start | bytes 1966088 | tf_op jit(solution)/shard_map/ppermute | solution.py:143
  10.0 1.6 %collective-permute-start.5 = (bf16[4,128,256]{2,1,0:T(8,128)(2,1)S(1)}, bf16[4,128,256]{2,1,0:T(8,128)(2,1)S(1)}, u32[]{:S(2)}, u32[]{:S(2)}) collective-permute-start(bf16[4,128,256]{2,1,0:T(8,128)(2,1)S(1)} %get-tuple-element.42), channel_id=1, source_target_pairs={{0,2},{1,3},{2,0},{3,1},{4,6},{5,7},{6,4},{7,5},{8,10},{9,11},{10,... | collective-permute-start | bytes 786440 | tf_op jit(solution)/shard_map/ppermute | solution.py:143
  11.6 1.0 %shard_map.139.refs_0_ = bf16[15,16,256]{2,1,0:T(8,128)(2,1)S(1)} custom-call(bf16[14,128,256]{2,1,0:T(8,128)(2,1)S(1)} %get-tuple-element.40.refs_0_.refs_2_, f32[896,256]{1,0:T(8,128)} %refs_5_.1, f32[7,128]{1,0:T(8,128)} %bitcast.14), custom_call_target="tpu_custom_call" | custom-call | tf_op jit(solution)/shard_map/pallas_call | solution.py:569
  12.6 2.7 %collective-permute-start.3 = (bf16[15,16,256]{2,1,0:T(8,128)(2,1)S(1)}, bf16[15,16,256]{2,1,0:T(8,128)(2,1)S(1)}, u32[]{:S(2)}, u32[]{:S(2)}) collective-permute-start(bf16[15,16,256]{2,1,0:T(8,128)(2,1)S(1)} %shard_map.139.refs_0_), channel_id=1, source_target_pairs={{0,4},{1,5},{2,6},{3,7},{4,0},{5,1},{6,2},{7,3},{8,12},{9,13},{10,... | collective-permute-start | bytes 368648 | tf_op jit(solution)/shard_map/ppermute | solution.py:139
  15.2 4.9 %collective-permute-done.3.refs_1_ = bf16[15,16,256]{2,1,0:T(8,128)(2,1)S(1)} collective-permute-done((bf16[15,16,256]{2,1,0:T(8,128)(2,1)S(1)}, bf16[15,16,256]{2,1,0:T(8,128)(2,1)S(1)}, u32[]{:S(2)}, u32[]{:S(2)}) %collective-permute-start.3) | collective-permute-done | bytes 122912 | tf_op jit(solution)/shard_map/ppermute | solution.py:139
  20.1 0.9 %collective-permute-done.5.refs_4_ = bf16[4,128,256]{2,1,0:T(8,128)(2,1)S(1)} collective-permute-done((bf16[4,128,256]{2,1,0:T(8,128)(2,1)S(1)}, bf16[4,128,256]{2,1,0:T(8,128)(2,1)S(1)}, u32[]{:S(2)}, u32[]{:S(2)}) %collective-permute-start.5) | collective-permute-done | bytes 262176 | tf_op jit(solution)/shard_map/ppermute | solution.py:143
  21.6 1.6 %collective-permute-start.8 = (bf16[4,64,256]{2,1,0:T(8,128)(2,1)S(1)}, bf16[4,64,256]{2,1,0:T(8,128)(2,1)S(1)}, u32[]{:S(2)}, u32[]{:S(2)}) collective-permute-start(bf16[4,64,256]{2,1,0:T(8,128)(2,1)S(1)} %get-tuple-element.46), channel_id=1, source_target_pairs={{0,8},{1,17},{2,10},{3,19},{4,12},{5,21},{6,14},{7,23},{8,0},{9,25... | collective-permute-start | bytes 393224 | tf_op jit(solution)/shard_map/ppermute | solution.py:143
  23.2 2.6 %collective-permute-start.6 = (bf16[2,15,16,256]{3,2,1,0:T(8,128)(2,1)S(1)}, bf16[2,15,16,256]{3,2,1,0:T(8,128)(2,1)S(1)}, u32[]{:S(2)}, u32[]{:S(2)}) collective-permute-start(bf16[2,15,16,256]{3,2,1,0:T(8,128)(2,1)S(1)} %get-tuple-element.43.refs_0_), channel_id=1, source_target_pairs={{0,2},{1,3},{2,0},{3,1},{4,6},{5,7},{6,4},{7,5},{8,10},{9,11},{10,... | collective-permute-start | bytes 737288 | tf_op jit(solution)/shard_map/ppermute | solution.py:139
  25.8 2.2 %collective-permute-done.8.refs_2_ = bf16[4,64,256]{2,1,0:T(8,128)(2,1)S(1)} collective-permute-done((bf16[4,64,256]{2,1,0:T(8,128)(2,1)S(1)}, bf16[4,64,256]{2,1,0:T(8,128)(2,1)S(1)}, u32[]{:S(2)}, u32[]{:S(2)}) %collective-permute-start.8) | collective-permute-done | bytes 131104 | tf_op jit(solution)/shard_map/ppermute | solution.py:143
  28.0 1.1 %collective-permute-done.7.refs_1_ = bf16[10,64,256]{2,1,0:T(8,128)(2,1)S(1)} collective-permute-done((bf16[10,64,256]{2,1,0:T(8,128)(2,1)S(1)}, bf16[10,64,256]{2,1,0:T(8,128)(2,1)S(1)}, u32[]{:S(2)}, u32[]{:S(2)}) %collective-permute-start.7) | collective-permute-done | bytes 327712 | tf_op jit(solution)/shard_map/ppermute | solution.py:143
  29.2 3.2 %collective-permute-start.9 = (bf16[10,32,256]{2,1,0:T(8,128)(2,1)S(1)}, bf16[10,32,256]{2,1,0:T(8,128)(2,1)S(1)}, u32[]{:S(2)}, u32[]{:S(2)}) collective-permute-start(bf16[10,32,256]{2,1,0:T(8,128)(2,1)S(1)} %get-tuple-element.48), channel_id=1, source_target_pairs={{0,2},{1,3},{2,0},{3,1},{4,6},{5,7},{6,4},{7,5},{8,10},{9,11},{10,... | collective-permute-start | bytes 491528 | tf_op jit(solution)/shard_map/ppermute | solution.py:143
  32.7 4.0 %collective-permute-done.10.refs_4_ = bf16[4,32,256]{2,1,0:T(8,128)(2,1)S(1)} collective-permute-done((bf16[4,32,256]{2,1,0:T(8,128)(2,1)S(1)}, bf16[4,32,256]{2,1,0:T(8,128)(2,1)S(1)}, u32[]{:S(2)}, u32[]{:S(2)}) %collective-permute-start.10) | collective-permute-done | bytes 65568 | tf_op jit(solution)/shard_map/ppermute | solution.py:143
  37.5 1.6 %collective-permute-start.12 = (bf16[14,32,256]{2,1,0:T(8,128)(2,1)S(1)}, bf16[14,32,256]{2,1,0:T(8,128)(2,1)S(1)}, u32[]{:S(2)}, u32[]{:S(2)}) collective-permute-start(bf16[14,32,256]{2,1,0:T(8,128)(2,1)S(1)} %get-tuple-element.52.refs_1_), channel_id=1, source_target_pairs={{0,4},{1,5},{2,6},{3,7},{4,0},{5,1},{6,2},{7,3},{8,12},{9,13},{10,... | collective-permute-start | bytes 688136 | tf_op jit(solution)/shard_map/ppermute | solution.py:139
  40.3 2.7 %shard_map.143 = (f32[32,128]{1,0:T(8,128)S(1)}, s32[224]{0:T(256)S(1)}) custom-call(s32[224]{0:T(256)S(1)} %copy-done.1, bf16[4,16,256]{2,1,0:T(8,128)(2,1)S(1)} %get-tuple-element.50.refs_1_, bf16[4,16,256]{2,1,0:T(8,128)(2,1)S(1)} %collective-permute-done.11.refs_2_), custom_call_target="tpu_custom_call" | custom-call | tf_op jit(solution)/shard_map/pallas_call | solution.py:605
  43.0 7.0 %collective-permute-done.12.refs_2_ = bf16[14,32,256]{2,1,0:T(8,128)(2,1)S(1)} collective-permute-done((bf16[14,32,256]{2,1,0:T(8,128)(2,1)S(1)}, bf16[14,32,256]{2,1,0:T(8,128)(2,1)S(1)}, u32[]{:S(2)}, u32[]{:S(2)}) %collective-permute-start.12) | collective-permute-done | bytes 229408 | tf_op jit(solution)/shard_map/ppermute | solution.py:139
  51.4 1.2 %collective-permute-start.17 = (bf16[5,32,256]{2,1,0:T(8,128)(2,1)S(1)}, bf16[5,32,256]{2,1,0:T(8,128)(2,1)S(1)}, u32[]{:S(2)}, u32[]{:S(2)}) collective-permute-start(bf16[5,32,256]{2,1,0:T(8,128)(2,1)S(1)} %get-tuple-element.57.refs_3_), channel_id=1, source_target_pairs={{0,16},{1,9},{2,18},{3,11},{4,20},{5,13},{6,22},{7,15},{8,24},{9,1... | collective-permute-start | bytes 245768 | tf_op jit(solution)/shard_map/ppermute | solution.py:143
  53.0 3.7 %collective-permute-done.17.refs_4_ = bf16[5,32,256]{2,1,0:T(8,128)(2,1)S(1)} collective-permute-done((bf16[5,32,256]{2,1,0:T(8,128)(2,1)S(1)}, bf16[5,32,256]{2,1,0:T(8,128)(2,1)S(1)}, u32[]{:S(2)}, u32[]{:S(2)}) %collective-permute-start.17) | collective-permute-done | bytes 81952 | tf_op jit(solution)/shard_map/ppermute | solution.py:143
  57.2 1.7 %collective-permute-start.18 = (bf16[10,64,256]{2,1,0:T(8,128)(2,1)S(1)}, bf16[10,64,256]{2,1,0:T(8,128)(2,1)S(1)}, u32[]{:S(2)}, u32[]{:S(2)}) collective-permute-start(bf16[10,64,256]{2,1,0:T(8,128)(2,1)S(1)} %get-tuple-element.58.refs_1_), channel_id=1, source_target_pairs={{0,16},{1,9},{2,18},{3,11},{4,20},{5,13},{6,22},{7,15},{8,24},{9,1... | collective-permute-start | bytes 983048 | tf_op jit(solution)/shard_map/ppermute | solution.py:143
  58.9 0.9 %collective-permute-start.19 = (bf16[5,64,256]{2,1,0:T(8,128)(2,1)S(1)}, bf16[5,64,256]{2,1,0:T(8,128)(2,1)S(1)}, u32[]{:S(2)}, u32[]{:S(2)}) collective-permute-start(bf16[5,64,256]{2,1,0:T(8,128)(2,1)S(1)} %get-tuple-element.59.refs_3_), channel_id=1, source_target_pairs={{0,8},{1,17},{2,10},{3,19},{4,12},{5,21},{6,14},{7,23},{8,0},{9,25... | collective-permute-start | bytes 491528 | tf_op jit(solution)/shard_map/ppermute | solution.py:143
  59.8 5.4 %collective-permute-done.19.refs_4_ = bf16[5,64,256]{2,1,0:T(8,128)(2,1)S(1)} collective-permute-done((bf16[5,64,256]{2,1,0:T(8,128)(2,1)S(1)}, bf16[5,64,256]{2,1,0:T(8,128)(2,1)S(1)}, u32[]{:S(2)}, u32[]{:S(2)}) %collective-permute-start.19) | collective-permute-done | bytes 163872 | tf_op jit(solution)/shard_map/ppermute | solution.py:143
  65.4 1.3 %collective-permute-start.23 = (bf16[10,128,256]{2,1,0:T(8,128)(2,1)S(1)}, bf16[10,128,256]{2,1,0:T(8,128)(2,1)S(1)}, u32[]{:S(2)}, u32[]{:S(2)}) collective-permute-start(bf16[10,128,256]{2,1,0:T(8,128)(2,1)S(1)} %get-tuple-element.62.refs_1_), channel_id=1, source_target_pairs={{0,8},{1,17},{2,10},{3,19},{4,12},{5,21},{6,14},{7,23},{8,0},{9,25... | collective-permute-start | bytes 1966088 | tf_op jit(solution)/shard_map/ppermute | solution.py:143
  66.7 1.7 %collective-permute-start.24 = (bf16[5,128,256]{2,1,0:T(8,128)(2,1)S(1)}, bf16[5,128,256]{2,1,0:T(8,128)(2,1)S(1)}, u32[]{:S(2)}, u32[]{:S(2)}) collective-permute-start(bf16[5,128,256]{2,1,0:T(8,128)(2,1)S(1)} %get-tuple-element.63.refs_3_), channel_id=1, source_target_pairs={{0,2},{1,3},{2,0},{3,1},{4,6},{5,7},{6,4},{7,5},{8,10},{9,11},{10,... | collective-permute-start | bytes 983048 | tf_op jit(solution)/shard_map/ppermute | solution.py:143
  69.0 1.0 %collective-permute-done.21.refs_5_ = bf16[2,224,256]{2,1,0:T(8,128)(2,1)S(1)} collective-permute-done((bf16[2,224,256]{2,1,0:T(8,128)(2,1)S(1)}, bf16[2,224,256]{2,1,0:T(8,128)(2,1)S(1)}, u32[]{:S(2)}, u32[]{:S(2)}) %collective-permute-start.21) | collective-permute-done | bytes 229408 | tf_op jit(solution)/shard_map/ppermute | solution.py:139
  70.3 1.0 %shard_map.148.refs_0_.refs_1_.refs_4_ = bf16[7168,256]{1,0:T(8,128)(2,1)S(1)} custom-call(s32[224]{0:T(256)S(1)} %copy-done.1, bf16[3,4,224,256]{3,2,1,0:T(8,128)(2,1)S(1)} %get-tuple-element.55.refs_1_, bf16[2,224,256]{2,1,0:T(8,128)(2,1)S(1)} %get-tuple-element.60.refs_2_, bf16[2,224,256]{2,1,0:T(8,128)(2,1)S(1)} %get-tuple-element.61.refs_3_, ...), custom_call_target="tpu_custom_call" | custom-call | bytes 8388608 | tf_op jit(solution)/shard_map/pallas_call | solution.py:643
  71.3 4.8 %collective-permute-done.24.refs_4_ = bf16[5,128,256]{2,1,0:T(8,128)(2,1)S(1)} collective-permute-done((bf16[5,128,256]{2,1,0:T(8,128)(2,1)S(1)}, bf16[5,128,256]{2,1,0:T(8,128)(2,1)S(1)}, u32[]{:S(2)}, u32[]{:S(2)}) %collective-permute-start.24) | collective-permute-done | bytes 327712 | tf_op jit(solution)/shard_map/ppermute | solution.py:143
  76.3 1.1 %shard_map.151.refs_9_ = f32[512,256]{1,0:T(8,128)S(1)} custom-call(bf16[3456,256]{1,0:T(8,128)(2,1)S(1)} %shard_map.144.refs_0_.refs_3_, bf16[15,256,256]{2,1,0:T(8,128)(2,1)S(1)} %shard_map.149.refs_1_.refs_6_), custom_call_target="tpu_custom_call" | custom-call | flops 939524096 | bytes 4194304 | tf_op jit(solution)/shard_map/pallas_call | solution.py:655
  77.5 2.0 %shard_map.150.refs_8_ = f32[512,256]{1,0:T(8,128)S(1)} custom-call(bf16[3456,256]{1,0:T(8,128)(2,1)S(1)} %shard_map.144.refs_0_.refs_3_, bf16[7168,256]{1,0:T(8,128)(2,1)S(1)} %shard_map.148.refs_0_.refs_1_.refs_4_), custom_call_target="tpu_custom_call" | custom-call | flops 1811939328 | bytes 6291456 | tf_op jit(solution)/shard_map/pallas_call | solution.py:648
  79.5 0.8 collective-permute-done.25.refs_7_
  80.3 3.1 %shard_map.152 = (f32[896,256]{1,0:T(8,128)}, f32[896,256]{1,0:T(8,128)}, f32[7,128]{1,0:T(8,128)}, f32[2,256]{1,0:T(2,128)}, bf16[512,256]{1,0:T(8,128)(2,1)}) custom-call(s32[224]{0:T(256)S(1)} %get-tuple-element.51.refs_0_, f32[1]{0:T(128)S(6)} %sub.3.refs_0_.refs_1_, f32[2,256]{1,0:T(2,128)S(1)} %copy-done.2, ...), custom_call_target="tpu_custom_call" | custom-call | flops 1073741824 | bytes 16777216 | tf_op jit(solution)/shard_map/pallas_call | solution.py:670
  (47 shorter events, 6.8 us)
Async XLA Ops:
  0.6 3.7 %collective-permute-start = (bf16[1,4,18,18,256]{4,1,3,2,0:T(4,128)(2,1)}, bf16[1,4,18,18,256]{4,1,3,2,0:T(4,128)(2,1)S(1)}, u32[]{:S(2)}, u32[]{:S(2)}) collective-permute-start(bf16[1,4,18,18,256]{4,1,3,2,0:T(4,128)(2,1)} %param.12), channel_id=1, source_target_pairs={{0,1},{1,0},{2,3},{3,2},{4,5},{5,4},{6,7},{7,6},{8,9},{9,8},{10,11... | collective-permute-start | bytes 1990664 | tf_op jit(solution)/shard_map/ppermute | solution.py:139
  1.1 3.3 %collective-permute-start.1 = (bf16[512,256]{1,0:T(8,128)(2,1)}, bf16[512,256]{1,0:T(8,128)(2,1)S(1)}, u32[]{:S(2)}, u32[]{:S(2)}) collective-permute-start(bf16[512,256]{1,0:T(8,128)(2,1)} %refs_1_.2), channel_id=1, source_target_pairs={{0,1},{1,0},{2,3},{3,2},{4,5},{5,4},{6,7},{7,6},{8,9},{9,8},{10,11... | collective-permute-start | bytes 786440 | tf_op jit(solution)/shard_map/ppermute | solution.py:139
  1.2 3.2 %collective-permute-start.2 = (bf16[512,256]{1,0:T(8,128)(2,1)}, bf16[512,256]{1,0:T(8,128)(2,1)S(1)}, u32[]{:S(2)}, u32[]{:S(2)}) collective-permute-start(bf16[512,256]{1,0:T(8,128)(2,1)} %refs_2_.2), channel_id=1, source_target_pairs={{0,1},{1,0},{2,3},{3,2},{4,5},{5,4},{6,7},{7,6},{8,9},{9,8},{10,11... | collective-permute-start | bytes 786440 | tf_op jit(solution)/shard_map/ppermute | solution.py:139
  7.4 13.7 %collective-permute-start.4 = (bf16[10,128,256]{2,1,0:T(8,128)(2,1)S(1)}, bf16[10,128,256]{2,1,0:T(8,128)(2,1)S(1)}, u32[]{:S(2)}, u32[]{:S(2)}) collective-permute-start(bf16[10,128,256]{2,1,0:T(8,128)(2,1)S(1)} %get-tuple-element.41), channel_id=1, source_target_pairs={{0,8},{1,17},{2,10},{3,19},{4,12},{5,21},{6,14},{7,23},{8,0},{9,25... | collective-permute-start | bytes 1966088 | tf_op jit(solution)/shard_map/ppermute | solution.py:143
  10.0 11.0 %collective-permute-start.5 = (bf16[4,128,256]{2,1,0:T(8,128)(2,1)S(1)}, bf16[4,128,256]{2,1,0:T(8,128)(2,1)S(1)}, u32[]{:S(2)}, u32[]{:S(2)}) collective-permute-start(bf16[4,128,256]{2,1,0:T(8,128)(2,1)S(1)} %get-tuple-element.42), channel_id=1, source_target_pairs={{0,2},{1,3},{2,0},{3,1},{4,6},{5,7},{6,4},{7,5},{8,10},{9,11},{10,... | collective-permute-start | bytes 786440 | tf_op jit(solution)/shard_map/ppermute | solution.py:143
  12.5 27.7 %copy-start.1 = (s32[224]{0:T(256)S(1)}, s32[224]{0:T(256)}, u32[]{:S(2)}) copy-start(s32[224]{0:T(256)} %refs_0_.3) | copy-start | bytes 2692
  12.6 7.5 %collective-permute-start.3 = (bf16[15,16,256]{2,1,0:T(8,128)(2,1)S(1)}, bf16[15,16,256]{2,1,0:T(8,128)(2,1)S(1)}, u32[]{:S(2)}, u32[]{:S(2)}) collective-permute-start(bf16[15,16,256]{2,1,0:T(8,128)(2,1)S(1)} %shard_map.139.refs_0_), channel_id=1, source_target_pairs={{0,4},{1,5},{2,6},{3,7},{4,0},{5,1},{6,2},{7,3},{8,12},{9,13},{10,... | collective-permute-start | bytes 368648 | tf_op jit(solution)/shard_map/ppermute | solution.py:139
  21.2 31.4 %copy-start.3 = (bf16[1,4,18,18,256]{4,1,3,2,0:T(4,128)(2,1)S(1)}, bf16[1,4,18,18,256]{4,1,3,2,0:T(4,128)(2,1)}, u32[]{:S(2)}) copy-start(bf16[1,4,18,18,256]{4,1,3,2,0:T(4,128)(2,1)} %param.19) | copy-start | bytes 1990660
  21.2 8.0 %collective-permute-start.7 = (bf16[10,64,256]{2,1,0:T(8,128)(2,1)S(1)}, bf16[10,64,256]{2,1,0:T(8,128)(2,1)S(1)}, u32[]{:S(2)}, u32[]{:S(2)}) collective-permute-start(bf16[10,64,256]{2,1,0:T(8,128)(2,1)S(1)} %get-tuple-element.45), channel_id=1, source_target_pairs={{0,16},{1,9},{2,18},{3,11},{4,20},{5,13},{6,22},{7,15},{8,24},{9,1... | collective-permute-start | bytes 983048 | tf_op jit(solution)/shard_map/ppermute | solution.py:143
  21.6 6.4 %collective-permute-start.8 = (bf16[4,64,256]{2,1,0:T(8,128)(2,1)S(1)}, bf16[4,64,256]{2,1,0:T(8,128)(2,1)S(1)}, u32[]{:S(2)}, u32[]{:S(2)}) collective-permute-start(bf16[4,64,256]{2,1,0:T(8,128)(2,1)S(1)} %get-tuple-element.46), channel_id=1, source_target_pairs={{0,8},{1,17},{2,10},{3,19},{4,12},{5,21},{6,14},{7,23},{8,0},{9,25... | collective-permute-start | bytes 393224 | tf_op jit(solution)/shard_map/ppermute | solution.py:143
  23.2 9.5 %collective-permute-start.6 = (bf16[2,15,16,256]{3,2,1,0:T(8,128)(2,1)S(1)}, bf16[2,15,16,256]{3,2,1,0:T(8,128)(2,1)S(1)}, u32[]{:S(2)}, u32[]{:S(2)}) collective-permute-start(bf16[2,15,16,256]{3,2,1,0:T(8,128)(2,1)S(1)} %get-tuple-element.43.refs_0_), channel_id=1, source_target_pairs={{0,2},{1,3},{2,0},{3,1},{4,6},{5,7},{6,4},{7,5},{8,10},{9,11},{10,... | collective-permute-start | bytes 737288 | tf_op jit(solution)/shard_map/ppermute | solution.py:139
  29.2 7.5 %collective-permute-start.9 = (bf16[10,32,256]{2,1,0:T(8,128)(2,1)S(1)}, bf16[10,32,256]{2,1,0:T(8,128)(2,1)S(1)}, u32[]{:S(2)}, u32[]{:S(2)}) collective-permute-start(bf16[10,32,256]{2,1,0:T(8,128)(2,1)S(1)} %get-tuple-element.48), channel_id=1, source_target_pairs={{0,2},{1,3},{2,0},{3,1},{4,6},{5,7},{6,4},{7,5},{8,10},{9,11},{10,... | collective-permute-start | bytes 491528 | tf_op jit(solution)/shard_map/ppermute | solution.py:143
  32.4 4.3 %collective-permute-start.10 = (bf16[4,32,256]{2,1,0:T(8,128)(2,1)S(1)}, bf16[4,32,256]{2,1,0:T(8,128)(2,1)S(1)}, u32[]{:S(2)}, u32[]{:S(2)}) collective-permute-start(bf16[4,32,256]{2,1,0:T(8,128)(2,1)S(1)} %get-tuple-element.49), channel_id=1, source_target_pairs={{0,16},{1,9},{2,18},{3,11},{4,20},{5,13},{6,22},{7,15},{8,24},{9,1... | collective-permute-start | bytes 196616 | tf_op jit(solution)/shard_map/ppermute | solution.py:143
  36.7 13.2 %collective-permute-start.14 = (bf16[4,224,256]{2,1,0:T(8,128)(2,1)S(1)}, bf16[4,224,256]{2,1,0:T(8,128)(2,1)S(1)}, u32[]{:S(2)}, u32[]{:S(2)}) collective-permute-start(bf16[4,224,256]{2,1,0:T(8,128)(2,1)S(1)} %get-tuple-element.54.refs_4_), channel_id=1, source_target_pairs={{0,8},{1,17},{2,10},{3,19},{4,12},{5,21},{6,14},{7,23},{8,0},{9,25... | collective-permute-start | bytes 1376264 | tf_op jit(solution)/shard_map/ppermute | solution.py:143
  37.3 12.6 %collective-permute-start.13 = (bf16[4,224,256]{2,1,0:T(8,128)(2,1)S(1)}, bf16[4,224,256]{2,1,0:T(8,128)(2,1)S(1)}, u32[]{:S(2)}, u32[]{:S(2)}) collective-permute-start(bf16[4,224,256]{2,1,0:T(8,128)(2,1)S(1)} %get-tuple-element.54.refs_4_), channel_id=1, source_target_pairs={{0,16},{1,9},{2,18},{3,11},{4,20},{5,13},{6,22},{7,15},{8,24},{9,1... | collective-permute-start | bytes 1376264 | tf_op jit(solution)/shard_map/ppermute | solution.py:143
  37.5 12.5 %collective-permute-start.12 = (bf16[14,32,256]{2,1,0:T(8,128)(2,1)S(1)}, bf16[14,32,256]{2,1,0:T(8,128)(2,1)S(1)}, u32[]{:S(2)}, u32[]{:S(2)}) collective-permute-start(bf16[14,32,256]{2,1,0:T(8,128)(2,1)S(1)} %get-tuple-element.52.refs_1_), channel_id=1, source_target_pairs={{0,4},{1,5},{2,6},{3,7},{4,0},{5,1},{6,2},{7,3},{8,12},{9,13},{10,... | collective-permute-start | bytes 688136 | tf_op jit(solution)/shard_map/ppermute | solution.py:139
  39.1 1.2 %collective-permute-start.11 = (bf16[4,16,256]{2,1,0:T(8,128)(2,1)S(1)}, bf16[4,16,256]{2,1,0:T(8,128)(2,1)S(1)}, u32[]{:S(2)}, u32[]{:S(2)}) collective-permute-start(bf16[4,16,256]{2,1,0:T(8,128)(2,1)S(1)} %get-tuple-element.50.refs_1_), channel_id=1, source_target_pairs={{0,1},{1,0},{2,3},{3,2},{4,5},{5,4},{6,7},{7,6},{8,9},{9,8},{10,11... | collective-permute-start | bytes 98312 | tf_op jit(solution)/shard_map/ppermute | solution.py:139
  50.4 19.9 %collective-permute-start.20 = (bf16[3,4,224,256]{3,2,1,0:T(8,128)(2,1)S(1)}, bf16[3,4,224,256]{3,2,1,0:T(8,128)(2,1)S(1)}, u32[]{:S(2)}, u32[]{:S(2)}) collective-permute-start(bf16[3,4,224,256]{3,2,1,0:T(8,128)(2,1)S(1)} %get-tuple-element.55.refs_1_), channel_id=1, source_target_pairs={{0,1},{1,0},{2,3},{3,2},{4,5},{5,4},{6,7},{7,6},{8,9},{9,8},{10,11... | collective-permute-start | bytes 4128776 | tf_op jit(solution)/shard_map/ppermute | solution.py:139
  50.5 6.6 %collective-permute-start.16 = (bf16[10,32,256]{2,1,0:T(8,128)(2,1)S(1)}, bf16[10,32,256]{2,1,0:T(8,128)(2,1)S(1)}, u32[]{:S(2)}, u32[]{:S(2)}) collective-permute-start(bf16[10,32,256]{2,1,0:T(8,128)(2,1)S(1)} %get-tuple-element.56.refs_1_), channel_id=1, source_target_pairs={{0,2},{1,3},{2,0},{3,1},{4,6},{5,7},{6,4},{7,5},{8,10},{9,11},{10,... | collective-permute-start | bytes 491528 | tf_op jit(solution)/shard_map/ppermute | solution.py:143
  50.6 14.7 %collective-permute-start.15 = (bf16[4,224,256]{2,1,0:T(8,128)(2,1)S(1)}, bf16[4,224,256]{2,1,0:T(8,128)(2,1)S(1)}, u32[]{:S(2)}, u32[]{:S(2)}) collective-permute-start(bf16[4,224,256]{2,1,0:T(8,128)(2,1)S(1)} %collective-permute-done.13.refs_5_), channel_id=1, source_target_pairs={{0,8},{1,17},{2,10},{3,19},{4,12},{5,21},{6,14},{7,23},{8,0},{9,25... | collective-permute-start | bytes 1376264 | tf_op jit(solution)/shard_map/ppermute | solution.py:143
  51.4 5.4 %collective-permute-start.17 = (bf16[5,32,256]{2,1,0:T(8,128)(2,1)S(1)}, bf16[5,32,256]{2,1,0:T(8,128)(2,1)S(1)}, u32[]{:S(2)}, u32[]{:S(2)}) collective-permute-start(bf16[5,32,256]{2,1,0:T(8,128)(2,1)S(1)} %get-tuple-element.57.refs_3_), channel_id=1, source_target_pairs={{0,16},{1,9},{2,18},{3,11},{4,20},{5,13},{6,22},{7,15},{8,24},{9,1... | collective-permute-start | bytes 245768 | tf_op jit(solution)/shard_map/ppermute | solution.py:143
  57.2 8.1 %collective-permute-start.18 = (bf16[10,64,256]{2,1,0:T(8,128)(2,1)S(1)}, bf16[10,64,256]{2,1,0:T(8,128)(2,1)S(1)}, u32[]{:S(2)}, u32[]{:S(2)}) collective-permute-start(bf16[10,64,256]{2,1,0:T(8,128)(2,1)S(1)} %get-tuple-element.58.refs_1_), channel_id=1, source_target_pairs={{0,16},{1,9},{2,18},{3,11},{4,20},{5,13},{6,22},{7,15},{8,24},{9,1... | collective-permute-start | bytes 983048 | tf_op jit(solution)/shard_map/ppermute | solution.py:143
  58.9 6.4 %collective-permute-start.19 = (bf16[5,64,256]{2,1,0:T(8,128)(2,1)S(1)}, bf16[5,64,256]{2,1,0:T(8,128)(2,1)S(1)}, u32[]{:S(2)}, u32[]{:S(2)}) collective-permute-start(bf16[5,64,256]{2,1,0:T(8,128)(2,1)S(1)} %get-tuple-element.59.refs_3_), channel_id=1, source_target_pairs={{0,8},{1,17},{2,10},{3,19},{4,12},{5,21},{6,14},{7,23},{8,0},{9,25... | collective-permute-start | bytes 491528 | tf_op jit(solution)/shard_map/ppermute | solution.py:143
  65.4 10.7 %collective-permute-start.23 = (bf16[10,128,256]{2,1,0:T(8,128)(2,1)S(1)}, bf16[10,128,256]{2,1,0:T(8,128)(2,1)S(1)}, u32[]{:S(2)}, u32[]{:S(2)}) collective-permute-start(bf16[10,128,256]{2,1,0:T(8,128)(2,1)S(1)} %get-tuple-element.62.refs_1_), channel_id=1, source_target_pairs={{0,8},{1,17},{2,10},{3,19},{4,12},{5,21},{6,14},{7,23},{8,0},{9,25... | collective-permute-start | bytes 1966088 | tf_op jit(solution)/shard_map/ppermute | solution.py:143
  66.7 9.3 %collective-permute-start.24 = (bf16[5,128,256]{2,1,0:T(8,128)(2,1)S(1)}, bf16[5,128,256]{2,1,0:T(8,128)(2,1)S(1)}, u32[]{:S(2)}, u32[]{:S(2)}) collective-permute-start(bf16[5,128,256]{2,1,0:T(8,128)(2,1)S(1)} %get-tuple-element.63.refs_3_), channel_id=1, source_target_pairs={{0,2},{1,3},{2,0},{3,1},{4,6},{5,7},{6,4},{7,5},{8,10},{9,11},{10,... | collective-permute-start | bytes 983048 | tf_op jit(solution)/shard_map/ppermute | solution.py:143
  68.5 1.5 %collective-permute-start.21 = (bf16[2,224,256]{2,1,0:T(8,128)(2,1)S(1)}, bf16[2,224,256]{2,1,0:T(8,128)(2,1)S(1)}, u32[]{:S(2)}, u32[]{:S(2)}) collective-permute-start(bf16[2,224,256]{2,1,0:T(8,128)(2,1)S(1)} %get-tuple-element.60.refs_2_), channel_id=1, source_target_pairs={{0,1},{1,0},{2,3},{3,2},{4,5},{5,4},{6,7},{7,6},{8,9},{9,8},{10,11... | collective-permute-start | bytes 688136 | tf_op jit(solution)/shard_map/ppermute | solution.py:139
  68.5 1.8 %collective-permute-start.22 = (bf16[2,224,256]{2,1,0:T(8,128)(2,1)S(1)}, bf16[2,224,256]{2,1,0:T(8,128)(2,1)S(1)}, u32[]{:S(2)}, u32[]{:S(2)}) collective-permute-start(bf16[2,224,256]{2,1,0:T(8,128)(2,1)S(1)} %get-tuple-element.61.refs_3_), channel_id=1, source_target_pairs={{0,1},{1,0},{2,3},{3,2},{4,5},{5,4},{6,7},{7,6},{8,9},{9,8},{10,11... | collective-permute-start | bytes 688136 | tf_op jit(solution)/shard_map/ppermute | solution.py:139
  76.2 4.0 %collective-permute-start.25 = (bf16[15,256,256]{2,1,0:T(8,128)(2,1)S(1)}, bf16[15,256,256]{2,1,0:T(8,128)(2,1)S(1)}, u32[]{:S(2)}, u32[]{:S(2)}) collective-permute-start(bf16[15,256,256]{2,1,0:T(8,128)(2,1)S(1)} %shard_map.149.refs_1_.refs_6_), channel_id=1, source_target_pairs={{0,1},{1,0},{2,3},{3,2},{4,5},{5,4},{6,7},{7,6},{8,9},{9,8},{10,11... | collective-permute-start | bytes 5898248 | tf_op jit(solution)/shard_map/ppermute | solution.py:139
  77.5 2.8 %copy-start = (f32[896,256]{1,0:T(8,128)S(1)}, f32[896,256]{1,0:T(8,128)}, u32[]{:S(2)}) copy-start(f32[896,256]{1,0:T(8,128)} %refs_5_.1) | copy-start | bytes 2752516
  77.5 2.8 %copy-start.2 = (f32[2,256]{1,0:T(2,128)S(1)}, f32[2,256]{1,0:T(2,128)}, u32[]{:S(2)}) copy-start(f32[2,256]{1,0:T(2,128)} %refs_2_.3) | copy-start | bytes 6148

commit v10 on v9

--- a/solution.py
+++ b/solution.py
@@ -464,14 +464,12 @@
     factor, row_table, update_rows, new_master, new_row, new_col, next_output, stored, rest_stored,
 ):
     core = at[4]
-    sums = [
-        [
-            piece[MESSAGE, sender * BLK : sender * BLK + 8].astype(WIDE)
-            + piece[MESSAGE, sender * BLK + 8 : sender * BLK + 16].astype(WIDE)
-            for sender in range(8)
+    sums = []
+    for piece in (mine, peer):
+        messages = [
+            piece[MESSAGE, sender * BLK : sender * BLK + 16].astype(WIDE) for sender in range(8)
         ]
-        for piece in (mine, peer)
-    ]
+        sums.append([message[:8] + message[8:] for message in messages])
     total = sum(sums[0][1:] + sums[1], sums[0][0])
     store_factors(total, rate[0], col_moment, new_col, factor)
 

time: 83.6 us -> 83.6 us (level)
  no operation moved by 1% of the time
where the time goes in v10:
time: 83.6 us; the launch traced here: 83.4 us
  waiting for transfers between devices  37 us (44%)
  starting transfers between devices  26.8 us (32%)
  Pallas kernels  16.5 us (20%)
  between operations  1.55 us (2%)
  local copies, waits for them, and re-layouts  1.5 us (2%)
    ppermute x15, waiting for transfers between devices, swap_mixed(): lax.ppermute(value, AXES, [(at, at ^ masks[at & 1]) for at in range(32)])  22.6 us
    ppermute x15, starting transfers between devices, swap_mixed(): lax.ppermute(value, AXES, [(at, at ^ masks[at & 1]) for at in range(32)])  18.3 us
    ppermute x11, waiting for transfers between devices, swap(): return lax.ppermute(value, AXES, [(at, at ^ mask) for at in range(32)])  14.5 us
    ppermute x11, starting transfers between devices, swap(): return lax.ppermute(value, AXES, [(at, at ^ mask) for at in range(32)])  8.52 us
    pallas_call x1, Pallas kernels, shards(): call(finish_kernel, outs, [SMEM] * 2 + [VMEM] * 8, out_specs=[HBM] * 5, s...  3.1 us
    pallas_call x1, Pallas kernels, shards(): call(term_kernel, [((SLOTS, 128, CO), LOW)] + [((count, 128, CO), LOW) fo...  2.9 us
    pallas_call x1, Pallas kernels, shards(): call(moments_kernel, [((BLK, 128), WIDE), ((NB,), jnp.int32)], [SMEM] + [...  2.67 us
    pallas_call x1, Pallas kernels, shards(): call(old_hidden_kernel, [((PIX, CO), WIDE)], [VMEM] * 2, flops=2 * 27 * 5...  2 us
  transfers between devices with their start and end apart: 26, of which 14 were waited for; matrix products, arithmetic and copies ran while one was open for 2% of the time, Pallas kernels for 12%

profile of v10, /device:TPU:0, one launch (start us, length us, event | category | flops | bytes accessed | tf_op | source)
XLA Modules:
  0.0 83.4 jit_solution(9963148666610840327)
XLA Ops:
  1.7 1.2 %copy.26 = bf16[1,4,18,18,256]{4,3,2,1,0:T(8,128)(2,1)S(1)} copy(bf16[1,4,18,18,256]{4,1,3,2,0:T(4,128)(2,1)} %param.12) | data formatting | bytes 1327104 | tf_op args[2]
  2.9 1.4 %shard_map.137 = (bf16[4480,256]{1,0:T(8,128)(2,1)S(1)}, bf16[512,256]{1,0:T(8,128)(2,1)S(1)}, bf16[256,256]{1,0:T(8,128)(2,1)S(1)}) custom-call(bf16[4,18,18,256]{3,2,1,0:T(8,128)(2,1)S(1)} %bitcast.11, bf16[512,256]{1,0:T(8,128)(2,1)} %refs_1_.2, bf16[512,256]{1,0:T(8,128)(2,1)} %refs_2_.2, bf16[256,256]{1,0:T(8,128)(2,1)} %refs_3_.1), custom_call_target="tpu_custom_call" | custom-call | bytes 4194304 | tf_op jit(solution)/shard_map/pallas_call | solution.py:549
  4.5 2.9 %shard_map.138 = (bf16[14,128,256]{2,1,0:T(8,128)(2,1)S(1)}, bf16[10,128,256]{2,1,0:T(8,128)(2,1)S(1)}, bf16[4,128,256]{2,1,0:T(8,128)(2,1)S(1)}) custom-call(bf16[4480,256]{1,0:T(8,128)(2,1)S(1)} %get-tuple-element.37.refs_0_, bf16[4,18,18,256]{3,2,1,0:T(8,128)(2,1)S(1)} %bitcast.13, bf16[512,256]{1,0:T(8,128)(2,1)S(1)} %collective-permute-done.1.refs_2_, ...), custom_call_target="tpu_custom_call" | custom-call | flops 1879048192 | bytes 6291456 | tf_op jit(solution)/shard_map/pallas_call | solution.py:557
  7.4 2.6 %collective-permute-start.4 = (bf16[10,128,256]{2,1,0:T(8,128)(2,1)S(1)}, bf16[10,128,256]{2,1,0:T(8,128)(2,1)S(1)}, u32[]{:S(2)}, u32[]{:S(2)}) collective-permute-start(bf16[10,128,256]{2,1,0:T(8,128)(2,1)S(1)} %get-tuple-element.41), channel_id=1, source_target_pairs={{0,8},{1,17},{2,10},{3,19},{4,12},{5,21},{6,14},{7,23},{8,0},{9,25... | collective-permute-start | bytes 1966088 | tf_op jit(solution)/shard_map/ppermute | solution.py:143
  10.0 1.6 %collective-permute-start.5 = (bf16[4,128,256]{2,1,0:T(8,128)(2,1)S(1)}, bf16[4,128,256]{2,1,0:T(8,128)(2,1)S(1)}, u32[]{:S(2)}, u32[]{:S(2)}) collective-permute-start(bf16[4,128,256]{2,1,0:T(8,128)(2,1)S(1)} %get-tuple-element.42), channel_id=1, source_target_pairs={{0,2},{1,3},{2,0},{3,1},{4,6},{5,7},{6,4},{7,5},{8,10},{9,11},{10,... | collective-permute-start | bytes 786440 | tf_op jit(solution)/shard_map/ppermute | solution.py:143
  11.6 1.0 %shard_map.139.refs_0_ = bf16[15,16,256]{2,1,0:T(8,128)(2,1)S(1)} custom-call(bf16[14,128,256]{2,1,0:T(8,128)(2,1)S(1)} %get-tuple-element.40.refs_0_.refs_2_, f32[896,256]{1,0:T(8,128)} %refs_5_.1, f32[7,128]{1,0:T(8,128)} %bitcast.14), custom_call_target="tpu_custom_call" | custom-call | tf_op jit(solution)/shard_map/pallas_call | solution.py:567
  12.6 2.7 %collective-permute-start.3 = (bf16[15,16,256]{2,1,0:T(8,128)(2,1)S(1)}, bf16[15,16,256]{2,1,0:T(8,128)(2,1)S(1)}, u32[]{:S(2)}, u32[]{:S(2)}) collective-permute-start(bf16[15,16,256]{2,1,0:T(8,128)(2,1)S(1)} %shard_map.139.refs_0_), channel_id=1, source_target_pairs={{0,4},{1,5},{2,6},{3,7},{4,0},{5,1},{6,2},{7,3},{8,12},{9,13},{10,... | collective-permute-start | bytes 368648 | tf_op jit(solution)/shard_map/ppermute | solution.py:139
  15.2 4.9 %collective-permute-done.3.refs_1_ = bf16[15,16,256]{2,1,0:T(8,128)(2,1)S(1)} collective-permute-done((bf16[15,16,256]{2,1,0:T(8,128)(2,1)S(1)}, bf16[15,16,256]{2,1,0:T(8,128)(2,1)S(1)}, u32[]{:S(2)}, u32[]{:S(2)}) %collective-permute-start.3) | collective-permute-done | bytes 122912 | tf_op jit(solution)/shard_map/ppermute | solution.py:139
  20.1 0.9 %collective-permute-done.5.refs_4_ = bf16[4,128,256]{2,1,0:T(8,128)(2,1)S(1)} collective-permute-done((bf16[4,128,256]{2,1,0:T(8,128)(2,1)S(1)}, bf16[4,128,256]{2,1,0:T(8,128)(2,1)S(1)}, u32[]{:S(2)}, u32[]{:S(2)}) %collective-permute-start.5) | collective-permute-done | bytes 262176 | tf_op jit(solution)/shard_map/ppermute | solution.py:143
  21.6 1.6 %collective-permute-start.8 = (bf16[4,64,256]{2,1,0:T(8,128)(2,1)S(1)}, bf16[4,64,256]{2,1,0:T(8,128)(2,1)S(1)}, u32[]{:S(2)}, u32[]{:S(2)}) collective-permute-start(bf16[4,64,256]{2,1,0:T(8,128)(2,1)S(1)} %get-tuple-element.46), channel_id=1, source_target_pairs={{0,8},{1,17},{2,10},{3,19},{4,12},{5,21},{6,14},{7,23},{8,0},{9,25... | collective-permute-start | bytes 393224 | tf_op jit(solution)/shard_map/ppermute | solution.py:143
  23.2 2.6 %collective-permute-start.6 = (bf16[2,15,16,256]{3,2,1,0:T(8,128)(2,1)S(1)}, bf16[2,15,16,256]{3,2,1,0:T(8,128)(2,1)S(1)}, u32[]{:S(2)}, u32[]{:S(2)}) collective-permute-start(bf16[2,15,16,256]{3,2,1,0:T(8,128)(2,1)S(1)} %get-tuple-element.43.refs_0_), channel_id=1, source_target_pairs={{0,2},{1,3},{2,0},{3,1},{4,6},{5,7},{6,4},{7,5},{8,10},{9,11},{10,... | collective-permute-start | bytes 737288 | tf_op jit(solution)/shard_map/ppermute | solution.py:139
  25.8 2.2 %collective-permute-done.8.refs_2_ = bf16[4,64,256]{2,1,0:T(8,128)(2,1)S(1)} collective-permute-done((bf16[4,64,256]{2,1,0:T(8,128)(2,1)S(1)}, bf16[4,64,256]{2,1,0:T(8,128)(2,1)S(1)}, u32[]{:S(2)}, u32[]{:S(2)}) %collective-permute-start.8) | collective-permute-done | bytes 131104 | tf_op jit(solution)/shard_map/ppermute | solution.py:143
  28.0 1.1 %collective-permute-done.7.refs_1_ = bf16[10,64,256]{2,1,0:T(8,128)(2,1)S(1)} collective-permute-done((bf16[10,64,256]{2,1,0:T(8,128)(2,1)S(1)}, bf16[10,64,256]{2,1,0:T(8,128)(2,1)S(1)}, u32[]{:S(2)}, u32[]{:S(2)}) %collective-permute-start.7) | collective-permute-done | bytes 327712 | tf_op jit(solution)/shard_map/ppermute | solution.py:143
  29.2 3.2 %collective-permute-start.9 = (bf16[10,32,256]{2,1,0:T(8,128)(2,1)S(1)}, bf16[10,32,256]{2,1,0:T(8,128)(2,1)S(1)}, u32[]{:S(2)}, u32[]{:S(2)}) collective-permute-start(bf16[10,32,256]{2,1,0:T(8,128)(2,1)S(1)} %get-tuple-element.48), channel_id=1, source_target_pairs={{0,2},{1,3},{2,0},{3,1},{4,6},{5,7},{6,4},{7,5},{8,10},{9,11},{10,... | collective-permute-start | bytes 491528 | tf_op jit(solution)/shard_map/ppermute | solution.py:143
  32.7 4.0 %collective-permute-done.10.refs_4_ = bf16[4,32,256]{2,1,0:T(8,128)(2,1)S(1)} collective-permute-done((bf16[4,32,256]{2,1,0:T(8,128)(2,1)S(1)}, bf16[4,32,256]{2,1,0:T(8,128)(2,1)S(1)}, u32[]{:S(2)}, u32[]{:S(2)}) %collective-permute-start.10) | collective-permute-done | bytes 65568 | tf_op jit(solution)/shard_map/ppermute | solution.py:143
  37.5 1.6 %collective-permute-start.12 = (bf16[14,32,256]{2,1,0:T(8,128)(2,1)S(1)}, bf16[14,32,256]{2,1,0:T(8,128)(2,1)S(1)}, u32[]{:S(2)}, u32[]{:S(2)}) collective-permute-start(bf16[14,32,256]{2,1,0:T(8,128)(2,1)S(1)} %get-tuple-element.52.refs_1_), channel_id=1, source_target_pairs={{0,4},{1,5},{2,6},{3,7},{4,0},{5,1},{6,2},{7,3},{8,12},{9,13},{10,... | collective-permute-start | bytes 688136 | tf_op jit(solution)/shard_map/ppermute | solution.py:139
  40.3 2.7 %shard_map.143 = (f32[32,128]{1,0:T(8,128)S(1)}, s32[224]{0:T(256)S(1)}) custom-call(s32[224]{0:T(256)S(1)} %copy-done.1, bf16[4,16,256]{2,1,0:T(8,128)(2,1)S(1)} %get-tuple-element.50.refs_1_, bf16[4,16,256]{2,1,0:T(8,128)(2,1)S(1)} %collective-permute-done.11.refs_2_), custom_call_target="tpu_custom_call" | custom-call | tf_op jit(solution)/shard_map/pallas_call | solution.py:603
  43.0 7.0 %collective-permute-done.12.refs_2_ = bf16[14,32,256]{2,1,0:T(8,128)(2,1)S(1)} collective-permute-done((bf16[14,32,256]{2,1,0:T(8,128)(2,1)S(1)}, bf16[14,32,256]{2,1,0:T(8,128)(2,1)S(1)}, u32[]{:S(2)}, u32[]{:S(2)}) %collective-permute-start.12) | collective-permute-done | bytes 229408 | tf_op jit(solution)/shard_map/ppermute | solution.py:139
  51.4 1.2 %collective-permute-start.17 = (bf16[5,32,256]{2,1,0:T(8,128)(2,1)S(1)}, bf16[5,32,256]{2,1,0:T(8,128)(2,1)S(1)}, u32[]{:S(2)}, u32[]{:S(2)}) collective-permute-start(bf16[5,32,256]{2,1,0:T(8,128)(2,1)S(1)} %get-tuple-element.57.refs_3_), channel_id=1, source_target_pairs={{0,16},{1,9},{2,18},{3,11},{4,20},{5,13},{6,22},{7,15},{8,24},{9,1... | collective-permute-start | bytes 245768 | tf_op jit(solution)/shard_map/ppermute | solution.py:143
  53.0 3.7 %collective-permute-done.17.refs_4_ = bf16[5,32,256]{2,1,0:T(8,128)(2,1)S(1)} collective-permute-done((bf16[5,32,256]{2,1,0:T(8,128)(2,1)S(1)}, bf16[5,32,256]{2,1,0:T(8,128)(2,1)S(1)}, u32[]{:S(2)}, u32[]{:S(2)}) %collective-permute-start.17) | collective-permute-done | bytes 81952 | tf_op jit(solution)/shard_map/ppermute | solution.py:143
  57.2 1.7 %collective-permute-start.18 = (bf16[10,64,256]{2,1,0:T(8,128)(2,1)S(1)}, bf16[10,64,256]{2,1,0:T(8,128)(2,1)S(1)}, u32[]{:S(2)}, u32[]{:S(2)}) collective-permute-start(bf16[10,64,256]{2,1,0:T(8,128)(2,1)S(1)} %get-tuple-element.58.refs_1_), channel_id=1, source_target_pairs={{0,16},{1,9},{2,18},{3,11},{4,20},{5,13},{6,22},{7,15},{8,24},{9,1... | collective-permute-start | bytes 983048 | tf_op jit(solution)/shard_map/ppermute | solution.py:143
  58.9 0.9 %collective-permute-start.19 = (bf16[5,64,256]{2,1,0:T(8,128)(2,1)S(1)}, bf16[5,64,256]{2,1,0:T(8,128)(2,1)S(1)}, u32[]{:S(2)}, u32[]{:S(2)}) collective-permute-start(bf16[5,64,256]{2,1,0:T(8,128)(2,1)S(1)} %get-tuple-element.59.refs_3_), channel_id=1, source_target_pairs={{0,8},{1,17},{2,10},{3,19},{4,12},{5,21},{6,14},{7,23},{8,0},{9,25... | collective-permute-start | bytes 491528 | tf_op jit(solution)/shard_map/ppermute | solution.py:143
  59.8 5.4 %collective-permute-done.19.refs_4_ = bf16[5,64,256]{2,1,0:T(8,128)(2,1)S(1)} collective-permute-done((bf16[5,64,256]{2,1,0:T(8,128)(2,1)S(1)}, bf16[5,64,256]{2,1,0:T(8,128)(2,1)S(1)}, u32[]{:S(2)}, u32[]{:S(2)}) %collective-permute-start.19) | collective-permute-done | bytes 163872 | tf_op jit(solution)/shard_map/ppermute | solution.py:143
  65.4 1.3 %collective-permute-start.23 = (bf16[10,128,256]{2,1,0:T(8,128)(2,1)S(1)}, bf16[10,128,256]{2,1,0:T(8,128)(2,1)S(1)}, u32[]{:S(2)}, u32[]{:S(2)}) collective-permute-start(bf16[10,128,256]{2,1,0:T(8,128)(2,1)S(1)} %get-tuple-element.62.refs_1_), channel_id=1, source_target_pairs={{0,8},{1,17},{2,10},{3,19},{4,12},{5,21},{6,14},{7,23},{8,0},{9,25... | collective-permute-start | bytes 1966088 | tf_op jit(solution)/shard_map/ppermute | solution.py:143
  66.7 1.7 %collective-permute-start.24 = (bf16[5,128,256]{2,1,0:T(8,128)(2,1)S(1)}, bf16[5,128,256]{2,1,0:T(8,128)(2,1)S(1)}, u32[]{:S(2)}, u32[]{:S(2)}) collective-permute-start(bf16[5,128,256]{2,1,0:T(8,128)(2,1)S(1)} %get-tuple-element.63.refs_3_), channel_id=1, source_target_pairs={{0,2},{1,3},{2,0},{3,1},{4,6},{5,7},{6,4},{7,5},{8,10},{9,11},{10,... | collective-permute-start | bytes 983048 | tf_op jit(solution)/shard_map/ppermute | solution.py:143
  69.0 1.0 %collective-permute-done.21.refs_5_ = bf16[2,224,256]{2,1,0:T(8,128)(2,1)S(1)} collective-permute-done((bf16[2,224,256]{2,1,0:T(8,128)(2,1)S(1)}, bf16[2,224,256]{2,1,0:T(8,128)(2,1)S(1)}, u32[]{:S(2)}, u32[]{:S(2)}) %collective-permute-start.21) | collective-permute-done | bytes 229408 | tf_op jit(solution)/shard_map/ppermute | solution.py:139
  70.3 1.0 %shard_map.148.refs_0_.refs_1_.refs_4_ = bf16[7168,256]{1,0:T(8,128)(2,1)S(1)} custom-call(s32[224]{0:T(256)S(1)} %copy-done.1, bf16[3,4,224,256]{3,2,1,0:T(8,128)(2,1)S(1)} %get-tuple-element.55.refs_1_, bf16[2,224,256]{2,1,0:T(8,128)(2,1)S(1)} %get-tuple-element.60.refs_2_, bf16[2,224,256]{2,1,0:T(8,128)(2,1)S(1)} %get-tuple-element.61.refs_3_, ...), custom_call_target="tpu_custom_call" | custom-call | bytes 8388608 | tf_op jit(solution)/shard_map/pallas_call | solution.py:641
  71.3 4.8 %collective-permute-done.24.refs_4_ = bf16[5,128,256]{2,1,0:T(8,128)(2,1)S(1)} collective-permute-done((bf16[5,128,256]{2,1,0:T(8,128)(2,1)S(1)}, bf16[5,128,256]{2,1,0:T(8,128)(2,1)S(1)}, u32[]{:S(2)}, u32[]{:S(2)}) %collective-permute-start.24) | collective-permute-done | bytes 327712 | tf_op jit(solution)/shard_map/ppermute | solution.py:143
  76.3 1.1 %shard_map.151.refs_9_ = f32[512,256]{1,0:T(8,128)S(1)} custom-call(bf16[3456,256]{1,0:T(8,128)(2,1)S(1)} %shard_map.144.refs_0_.refs_3_, bf16[15,256,256]{2,1,0:T(8,128)(2,1)S(1)} %shard_map.149.refs_1_.refs_6_), custom_call_target="tpu_custom_call" | custom-call | flops 939524096 | bytes 4194304 | tf_op jit(solution)/shard_map/pallas_call | solution.py:653
  77.5 2.0 %shard_map.150.refs_8_ = f32[512,256]{1,0:T(8,128)S(1)} custom-call(bf16[3456,256]{1,0:T(8,128)(2,1)S(1)} %shard_map.144.refs_0_.refs_3_, bf16[7168,256]{1,0:T(8,128)(2,1)S(1)} %shard_map.148.refs_0_.refs_1_.refs_4_), custom_call_target="tpu_custom_call" | custom-call | flops 1811939328 | bytes 6291456 | tf_op jit(solution)/shard_map/pallas_call | solution.py:646
  79.5 0.8 collective-permute-done.25.refs_7_
  80.3 3.1 %shard_map.152 = (f32[896,256]{1,0:T(8,128)}, f32[896,256]{1,0:T(8,128)}, f32[7,128]{1,0:T(8,128)}, f32[2,256]{1,0:T(2,128)}, bf16[512,256]{1,0:T(8,128)(2,1)}) custom-call(s32[224]{0:T(256)S(1)} %get-tuple-element.51.refs_0_, f32[1]{0:T(128)S(6)} %sub.3.refs_0_.refs_1_, f32[2,256]{1,0:T(2,128)S(1)} %copy-done.2, ...), custom_call_target="tpu_custom_call" | custom-call | flops 1073741824 | bytes 16777216 | tf_op jit(solution)/shard_map/pallas_call | solution.py:668
  (47 shorter events, 6.8 us)
Async XLA Ops:
  0.6 3.7 %collective-permute-start = (bf16[1,4,18,18,256]{4,1,3,2,0:T(4,128)(2,1)}, bf16[1,4,18,18,256]{4,1,3,2,0:T(4,128)(2,1)S(1)}, u32[]{:S(2)}, u32[]{:S(2)}) collective-permute-start(bf16[1,4,18,18,256]{4,1,3,2,0:T(4,128)(2,1)} %param.12), channel_id=1, source_target_pairs={{0,1},{1,0},{2,3},{3,2},{4,5},{5,4},{6,7},{7,6},{8,9},{9,8},{10,11... | collective-permute-start | bytes 1990664 | tf_op jit(solution)/shard_map/ppermute | solution.py:139
  1.1 3.3 %collective-permute-start.1 = (bf16[512,256]{1,0:T(8,128)(2,1)}, bf16[512,256]{1,0:T(8,128)(2,1)S(1)}, u32[]{:S(2)}, u32[]{:S(2)}) collective-permute-start(bf16[512,256]{1,0:T(8,128)(2,1)} %refs_1_.2), channel_id=1, source_target_pairs={{0,1},{1,0},{2,3},{3,2},{4,5},{5,4},{6,7},{7,6},{8,9},{9,8},{10,11... | collective-permute-start | bytes 786440 | tf_op jit(solution)/shard_map/ppermute | solution.py:139
  1.2 3.2 %collective-permute-start.2 = (bf16[512,256]{1,0:T(8,128)(2,1)}, bf16[512,256]{1,0:T(8,128)(2,1)S(1)}, u32[]{:S(2)}, u32[]{:S(2)}) collective-permute-start(bf16[512,256]{1,0:T(8,128)(2,1)} %refs_2_.2), channel_id=1, source_target_pairs={{0,1},{1,0},{2,3},{3,2},{4,5},{5,4},{6,7},{7,6},{8,9},{9,8},{10,11... | collective-permute-start | bytes 786440 | tf_op jit(solution)/shard_map/ppermute | solution.py:139
  7.4 13.7 %collective-permute-start.4 = (bf16[10,128,256]{2,1,0:T(8,128)(2,1)S(1)}, bf16[10,128,256]{2,1,0:T(8,128)(2,1)S(1)}, u32[]{:S(2)}, u32[]{:S(2)}) collective-permute-start(bf16[10,128,256]{2,1,0:T(8,128)(2,1)S(1)} %get-tuple-element.41), channel_id=1, source_target_pairs={{0,8},{1,17},{2,10},{3,19},{4,12},{5,21},{6,14},{7,23},{8,0},{9,25... | collective-permute-start | bytes 1966088 | tf_op jit(solution)/shard_map/ppermute | solution.py:143
  10.0 11.0 %collective-permute-start.5 = (bf16[4,128,256]{2,1,0:T(8,128)(2,1)S(1)}, bf16[4,128,256]{2,1,0:T(8,128)(2,1)S(1)}, u32[]{:S(2)}, u32[]{:S(2)}) collective-permute-start(bf16[4,128,256]{2,1,0:T(8,128)(2,1)S(1)} %get-tuple-element.42), channel_id=1, source_target_pairs={{0,2},{1,3},{2,0},{3,1},{4,6},{5,7},{6,4},{7,5},{8,10},{9,11},{10,... | collective-permute-start | bytes 786440 | tf_op jit(solution)/shard_map/ppermute | solution.py:143
  12.5 27.7 %copy-start.1 = (s32[224]{0:T(256)S(1)}, s32[224]{0:T(256)}, u32[]{:S(2)}) copy-start(s32[224]{0:T(256)} %refs_0_.3) | copy-start | bytes 2692
  12.6 7.5 %collective-permute-start.3 = (bf16[15,16,256]{2,1,0:T(8,128)(2,1)S(1)}, bf16[15,16,256]{2,1,0:T(8,128)(2,1)S(1)}, u32[]{:S(2)}, u32[]{:S(2)}) collective-permute-start(bf16[15,16,256]{2,1,0:T(8,128)(2,1)S(1)} %shard_map.139.refs_0_), channel_id=1, source_target_pairs={{0,4},{1,5},{2,6},{3,7},{4,0},{5,1},{6,2},{7,3},{8,12},{9,13},{10,... | collective-permute-start | bytes 368648 | tf_op jit(solution)/shard_map/ppermute | solution.py:139
  21.2 31.4 %copy-start.3 = (bf16[1,4,18,18,256]{4,1,3,2,0:T(4,128)(2,1)S(1)}, bf16[1,4,18,18,256]{4,1,3,2,0:T(4,128)(2,1)}, u32[]{:S(2)}) copy-start(bf16[1,4,18,18,256]{4,1,3,2,0:T(4,128)(2,1)} %param.19) | copy-start | bytes 1990660
  21.2 8.0 %collective-permute-start.7 = (bf16[10,64,256]{2,1,0:T(8,128)(2,1)S(1)}, bf16[10,64,256]{2,1,0:T(8,128)(2,1)S(1)}, u32[]{:S(2)}, u32[]{:S(2)}) collective-permute-start(bf16[10,64,256]{2,1,0:T(8,128)(2,1)S(1)} %get-tuple-element.45), channel_id=1, source_target_pairs={{0,16},{1,9},{2,18},{3,11},{4,20},{5,13},{6,22},{7,15},{8,24},{9,1... | collective-permute-start | bytes 983048 | tf_op jit(solution)/shard_map/ppermute | solution.py:143
  21.6 6.4 %collective-permute-start.8 = (bf16[4,64,256]{2,1,0:T(8,128)(2,1)S(1)}, bf16[4,64,256]{2,1,0:T(8,128)(2,1)S(1)}, u32[]{:S(2)}, u32[]{:S(2)}) collective-permute-start(bf16[4,64,256]{2,1,0:T(8,128)(2,1)S(1)} %get-tuple-element.46), channel_id=1, source_target_pairs={{0,8},{1,17},{2,10},{3,19},{4,12},{5,21},{6,14},{7,23},{8,0},{9,25... | collective-permute-start | bytes 393224 | tf_op jit(solution)/shard_map/ppermute | solution.py:143
  23.2 9.5 %collective-permute-start.6 = (bf16[2,15,16,256]{3,2,1,0:T(8,128)(2,1)S(1)}, bf16[2,15,16,256]{3,2,1,0:T(8,128)(2,1)S(1)}, u32[]{:S(2)}, u32[]{:S(2)}) collective-permute-start(bf16[2,15,16,256]{3,2,1,0:T(8,128)(2,1)S(1)} %get-tuple-element.43.refs_0_), channel_id=1, source_target_pairs={{0,2},{1,3},{2,0},{3,1},{4,6},{5,7},{6,4},{7,5},{8,10},{9,11},{10,... | collective-permute-start | bytes 737288 | tf_op jit(solution)/shard_map/ppermute | solution.py:139
  29.2 7.5 %collective-permute-start.9 = (bf16[10,32,256]{2,1,0:T(8,128)(2,1)S(1)}, bf16[10,32,256]{2,1,0:T(8,128)(2,1)S(1)}, u32[]{:S(2)}, u32[]{:S(2)}) collective-permute-start(bf16[10,32,256]{2,1,0:T(8,128)(2,1)S(1)} %get-tuple-element.48), channel_id=1, source_target_pairs={{0,2},{1,3},{2,0},{3,1},{4,6},{5,7},{6,4},{7,5},{8,10},{9,11},{10,... | collective-permute-start | bytes 491528 | tf_op jit(solution)/shard_map/ppermute | solution.py:143
  32.4 4.3 %collective-permute-start.10 = (bf16[4,32,256]{2,1,0:T(8,128)(2,1)S(1)}, bf16[4,32,256]{2,1,0:T(8,128)(2,1)S(1)}, u32[]{:S(2)}, u32[]{:S(2)}) collective-permute-start(bf16[4,32,256]{2,1,0:T(8,128)(2,1)S(1)} %get-tuple-element.49), channel_id=1, source_target_pairs={{0,16},{1,9},{2,18},{3,11},{4,20},{5,13},{6,22},{7,15},{8,24},{9,1... | collective-permute-start | bytes 196616 | tf_op jit(solution)/shard_map/ppermute | solution.py:143
  36.7 13.2 %collective-permute-start.14 = (bf16[4,224,256]{2,1,0:T(8,128)(2,1)S(1)}, bf16[4,224,256]{2,1,0:T(8,128)(2,1)S(1)}, u32[]{:S(2)}, u32[]{:S(2)}) collective-permute-start(bf16[4,224,256]{2,1,0:T(8,128)(2,1)S(1)} %get-tuple-element.54.refs_4_), channel_id=1, source_target_pairs={{0,8},{1,17},{2,10},{3,19},{4,12},{5,21},{6,14},{7,23},{8,0},{9,25... | collective-permute-start | bytes 1376264 | tf_op jit(solution)/shard_map/ppermute | solution.py:143
  37.3 12.6 %collective-permute-start.13 = (bf16[4,224,256]{2,1,0:T(8,128)(2,1)S(1)}, bf16[4,224,256]{2,1,0:T(8,128)(2,1)S(1)}, u32[]{:S(2)}, u32[]{:S(2)}) collective-permute-start(bf16[4,224,256]{2,1,0:T(8,128)(2,1)S(1)} %get-tuple-element.54.refs_4_), channel_id=1, source_target_pairs={{0,16},{1,9},{2,18},{3,11},{4,20},{5,13},{6,22},{7,15},{8,24},{9,1... | collective-permute-start | bytes 1376264 | tf_op jit(solution)/shard_map/ppermute | solution.py:143
  37.5 12.5 %collective-permute-start.12 = (bf16[14,32,256]{2,1,0:T(8,128)(2,1)S(1)}, bf16[14,32,256]{2,1,0:T(8,128)(2,1)S(1)}, u32[]{:S(2)}, u32[]{:S(2)}) collective-permute-start(bf16[14,32,256]{2,1,0:T(8,128)(2,1)S(1)} %get-tuple-element.52.refs_1_), channel_id=1, source_target_pairs={{0,4},{1,5},{2,6},{3,7},{4,0},{5,1},{6,2},{7,3},{8,12},{9,13},{10,... | collective-permute-start | bytes 688136 | tf_op jit(solution)/shard_map/ppermute | solution.py:139
  39.1 1.2 %collective-permute-start.11 = (bf16[4,16,256]{2,1,0:T(8,128)(2,1)S(1)}, bf16[4,16,256]{2,1,0:T(8,128)(2,1)S(1)}, u32[]{:S(2)}, u32[]{:S(2)}) collective-permute-start(bf16[4,16,256]{2,1,0:T(8,128)(2,1)S(1)} %get-tuple-element.50.refs_1_), channel_id=1, source_target_pairs={{0,1},{1,0},{2,3},{3,2},{4,5},{5,4},{6,7},{7,6},{8,9},{9,8},{10,11... | collective-permute-start | bytes 98312 | tf_op jit(solution)/shard_map/ppermute | solution.py:139
  50.4 19.9 %collective-permute-start.20 = (bf16[3,4,224,256]{3,2,1,0:T(8,128)(2,1)S(1)}, bf16[3,4,224,256]{3,2,1,0:T(8,128)(2,1)S(1)}, u32[]{:S(2)}, u32[]{:S(2)}) collective-permute-start(bf16[3,4,224,256]{3,2,1,0:T(8,128)(2,1)S(1)} %get-tuple-element.55.refs_1_), channel_id=1, source_target_pairs={{0,1},{1,0},{2,3},{3,2},{4,5},{5,4},{6,7},{7,6},{8,9},{9,8},{10,11... | collective-permute-start | bytes 4128776 | tf_op jit(solution)/shard_map/ppermute | solution.py:139
  50.5 6.6 %collective-permute-start.16 = (bf16[10,32,256]{2,1,0:T(8,128)(2,1)S(1)}, bf16[10,32,256]{2,1,0:T(8,128)(2,1)S(1)}, u32[]{:S(2)}, u32[]{:S(2)}) collective-permute-start(bf16[10,32,256]{2,1,0:T(8,128)(2,1)S(1)} %get-tuple-element.56.refs_1_), channel_id=1, source_target_pairs={{0,2},{1,3},{2,0},{3,1},{4,6},{5,7},{6,4},{7,5},{8,10},{9,11},{10,... | collective-permute-start | bytes 491528 | tf_op jit(solution)/shard_map/ppermute | solution.py:143
  50.6 14.7 %collective-permute-start.15 = (bf16[4,224,256]{2,1,0:T(8,128)(2,1)S(1)}, bf16[4,224,256]{2,1,0:T(8,128)(2,1)S(1)}, u32[]{:S(2)}, u32[]{:S(2)}) collective-permute-start(bf16[4,224,256]{2,1,0:T(8,128)(2,1)S(1)} %collective-permute-done.13.refs_5_), channel_id=1, source_target_pairs={{0,8},{1,17},{2,10},{3,19},{4,12},{5,21},{6,14},{7,23},{8,0},{9,25... | collective-permute-start | bytes 1376264 | tf_op jit(solution)/shard_map/ppermute | solution.py:143
  51.4 5.4 %collective-permute-start.17 = (bf16[5,32,256]{2,1,0:T(8,128)(2,1)S(1)}, bf16[5,32,256]{2,1,0:T(8,128)(2,1)S(1)}, u32[]{:S(2)}, u32[]{:S(2)}) collective-permute-start(bf16[5,32,256]{2,1,0:T(8,128)(2,1)S(1)} %get-tuple-element.57.refs_3_), channel_id=1, source_target_pairs={{0,16},{1,9},{2,18},{3,11},{4,20},{5,13},{6,22},{7,15},{8,24},{9,1... | collective-permute-start | bytes 245768 | tf_op jit(solution)/shard_map/ppermute | solution.py:143
  57.2 8.1 %collective-permute-start.18 = (bf16[10,64,256]{2,1,0:T(8,128)(2,1)S(1)}, bf16[10,64,256]{2,1,0:T(8,128)(2,1)S(1)}, u32[]{:S(2)}, u32[]{:S(2)}) collective-permute-start(bf16[10,64,256]{2,1,0:T(8,128)(2,1)S(1)} %get-tuple-element.58.refs_1_), channel_id=1, source_target_pairs={{0,16},{1,9},{2,18},{3,11},{4,20},{5,13},{6,22},{7,15},{8,24},{9,1... | collective-permute-start | bytes 983048 | tf_op jit(solution)/shard_map/ppermute | solution.py:143
  58.9 6.4 %collective-permute-start.19 = (bf16[5,64,256]{2,1,0:T(8,128)(2,1)S(1)}, bf16[5,64,256]{2,1,0:T(8,128)(2,1)S(1)}, u32[]{:S(2)}, u32[]{:S(2)}) collective-permute-start(bf16[5,64,256]{2,1,0:T(8,128)(2,1)S(1)} %get-tuple-element.59.refs_3_), channel_id=1, source_target_pairs={{0,8},{1,17},{2,10},{3,19},{4,12},{5,21},{6,14},{7,23},{8,0},{9,25... | collective-permute-start | bytes 491528 | tf_op jit(solution)/shard_map/ppermute | solution.py:143
  65.4 10.7 %collective-permute-start.23 = (bf16[10,128,256]{2,1,0:T(8,128)(2,1)S(1)}, bf16[10,128,256]{2,1,0:T(8,128)(2,1)S(1)}, u32[]{:S(2)}, u32[]{:S(2)}) collective-permute-start(bf16[10,128,256]{2,1,0:T(8,128)(2,1)S(1)} %get-tuple-element.62.refs_1_), channel_id=1, source_target_pairs={{0,8},{1,17},{2,10},{3,19},{4,12},{5,21},{6,14},{7,23},{8,0},{9,25... | collective-permute-start | bytes 1966088 | tf_op jit(solution)/shard_map/ppermute | solution.py:143
  66.7 9.3 %collective-permute-start.24 = (bf16[5,128,256]{2,1,0:T(8,128)(2,1)S(1)}, bf16[5,128,256]{2,1,0:T(8,128)(2,1)S(1)}, u32[]{:S(2)}, u32[]{:S(2)}) collective-permute-start(bf16[5,128,256]{2,1,0:T(8,128)(2,1)S(1)} %get-tuple-element.63.refs_3_), channel_id=1, source_target_pairs={{0,2},{1,3},{2,0},{3,1},{4,6},{5,7},{6,4},{7,5},{8,10},{9,11},{10,... | collective-permute-start | bytes 983048 | tf_op jit(solution)/shard_map/ppermute | solution.py:143
  68.5 1.5 %collective-permute-start.21 = (bf16[2,224,256]{2,1,0:T(8,128)(2,1)S(1)}, bf16[2,224,256]{2,1,0:T(8,128)(2,1)S(1)}, u32[]{:S(2)}, u32[]{:S(2)}) collective-permute-start(bf16[2,224,256]{2,1,0:T(8,128)(2,1)S(1)} %get-tuple-element.60.refs_2_), channel_id=1, source_target_pairs={{0,1},{1,0},{2,3},{3,2},{4,5},{5,4},{6,7},{7,6},{8,9},{9,8},{10,11... | collective-permute-start | bytes 688136 | tf_op jit(solution)/shard_map/ppermute | solution.py:139
  68.5 1.8 %collective-permute-start.22 = (bf16[2,224,256]{2,1,0:T(8,128)(2,1)S(1)}, bf16[2,224,256]{2,1,0:T(8,128)(2,1)S(1)}, u32[]{:S(2)}, u32[]{:S(2)}) collective-permute-start(bf16[2,224,256]{2,1,0:T(8,128)(2,1)S(1)} %get-tuple-element.61.refs_3_), channel_id=1, source_target_pairs={{0,1},{1,0},{2,3},{3,2},{4,5},{5,4},{6,7},{7,6},{8,9},{9,8},{10,11... | collective-permute-start | bytes 688136 | tf_op jit(solution)/shard_map/ppermute | solution.py:139
  76.2 4.0 %collective-permute-start.25 = (bf16[15,256,256]{2,1,0:T(8,128)(2,1)S(1)}, bf16[15,256,256]{2,1,0:T(8,128)(2,1)S(1)}, u32[]{:S(2)}, u32[]{:S(2)}) collective-permute-start(bf16[15,256,256]{2,1,0:T(8,128)(2,1)S(1)} %shard_map.149.refs_1_.refs_6_), channel_id=1, source_target_pairs={{0,1},{1,0},{2,3},{3,2},{4,5},{5,4},{6,7},{7,6},{8,9},{9,8},{10,11... | collective-permute-start | bytes 5898248 | tf_op jit(solution)/shard_map/ppermute | solution.py:139
  77.5 2.8 %copy-start = (f32[896,256]{1,0:T(8,128)S(1)}, f32[896,256]{1,0:T(8,128)}, u32[]{:S(2)}) copy-start(f32[896,256]{1,0:T(8,128)} %refs_5_.1) | copy-start | bytes 2752516
  77.5 2.8 %copy-start.2 = (f32[2,256]{1,0:T(2,128)S(1)}, f32[2,256]{1,0:T(2,128)}, u32[]{:S(2)}) copy-start(f32[2,256]{1,0:T(2,128)} %refs_2_.3) | copy-start | bytes 6148

commit v11 on v10

--- a/solution.py
+++ b/solution.py
@@ -128,10 +128,10 @@
 SMEM = pl.BlockSpec(memory_space=pltpu.SMEM)
 HBM = pl.BlockSpec(memory_space=pl.ANY)
 MASK_CORE, MASK_NEAR, MASK_FAR, MASK_X, MASK_Y = 1, 2, 4, 8, 16
-PARTS = ((0, 10), (10, 4))
+PARTS = ((0, 11), (11, 3))
 ORDERS = (((0, 1, 2), (1, 0, 2)), ((2, 0, 1), (2, 1, 0)))
 MESSAGE = SLOTS
-GATHERED = ((0, 10), (10, 5))
+GATHERED = ((0, 11), (11, 4))
 MASKS = (MASK_X, MASK_Y, MASK_NEAR)
 
 

time: 83.6 us -> 83.4 us (level)
  waiting for transfers between devices: 37 us -> 35.6 us
  starting transfers between devices: 26.8 us -> 28.1 us
    ppermute x11, waiting for transfers between devices: 14.5 us -> 12.1 us  [swap(): return lax.ppermute(value, AXES, [(at, at ^ mask) for at in range(32)])]
    ppermute x15, starting transfers between devices: 18.3 us -> 19.6 us  [swap_mixed(): lax.ppermute(value, AXES, [(at, at ^ masks[at & 1]) for at in range(32)])]
    ppermute x15, waiting for transfers between devices: 22.6 us -> 23.5 us  [swap_mixed(): lax.ppermute(value, AXES, [(at, at ^ masks[at & 1]) for at in range(32)])]
  transfers between devices with their start and end apart: 26 -> 26, of which waited for: 14 -> 15; matrix products, arithmetic and copies ran while one was open for 2% -> 2% of each run, Pallas kernels for 12% -> 12%
where the time goes in v11:
time: 83.4 us; the launch traced here: 83.2 us
  waiting for transfers between devices  35.6 us (43%)
  starting transfers between devices  28.1 us (34%)
  Pallas kernels  16.5 us (20%)
  between operations  1.54 us (2%)
  local copies, waits for them, and re-layouts  1.5 us (2%)
    ppermute x15, waiting for transfers between devices, swap_mixed(): lax.ppermute(value, AXES, [(at, at ^ masks[at & 1]) for at in range(32)])  23.5 us
    ppermute x15, starting transfers between devices, swap_mixed(): lax.ppermute(value, AXES, [(at, at ^ masks[at & 1]) for at in range(32)])  19.6 us
    ppermute x11, waiting for transfers between devices, swap(): return lax.ppermute(value, AXES, [(at, at ^ mask) for at in range(32)])  12.1 us
    ppermute x11, starting transfers between devices, swap(): return lax.ppermute(value, AXES, [(at, at ^ mask) for at in range(32)])  8.52 us
    pallas_call x1, Pallas kernels, shards(): call(finish_kernel, outs, [SMEM] * 2 + [VMEM] * 8, out_specs=[HBM] * 5, s...  3.1 us
    pallas_call x1, Pallas kernels, shards(): call(term_kernel, [((SLOTS, 128, CO), LOW)] + [((count, 128, CO), LOW) fo...  2.89 us
    pallas_call x1, Pallas kernels, shards(): call(moments_kernel, [((BLK, 128), WIDE), ((NB,), jnp.int32)], [SMEM] + [...  2.67 us
    pallas_call x1, Pallas kernels, shards(): call(old_hidden_kernel, [((PIX, CO), WIDE)], [VMEM] * 2, flops=2 * 27 * 5...  2 us
  transfers between devices with their start and end apart: 26, of which 15 were waited for; matrix products, arithmetic and copies ran while one was open for 2% of the time, Pallas kernels for 12%

profile of v11, /device:TPU:0, one launch (start us, length us, event | category | flops | bytes accessed | tf_op | source)
XLA Modules:
  0.0 83.2 jit_solution(7679632247843519115)
XLA Ops:
  1.7 1.2 %copy.26 = bf16[1,4,18,18,256]{4,3,2,1,0:T(8,128)(2,1)S(1)} copy(bf16[1,4,18,18,256]{4,1,3,2,0:T(4,128)(2,1)} %param.12) | data formatting | bytes 1327104 | tf_op args[2]
  2.9 1.4 %shard_map.137 = (bf16[4480,256]{1,0:T(8,128)(2,1)S(1)}, bf16[512,256]{1,0:T(8,128)(2,1)S(1)}, bf16[256,256]{1,0:T(8,128)(2,1)S(1)}) custom-call(bf16[4,18,18,256]{3,2,1,0:T(8,128)(2,1)S(1)} %bitcast.11, bf16[512,256]{1,0:T(8,128)(2,1)} %refs_1_.2, bf16[512,256]{1,0:T(8,128)(2,1)} %refs_2_.2, bf16[256,256]{1,0:T(8,128)(2,1)} %refs_3_.1), custom_call_target="tpu_custom_call" | custom-call | bytes 4194304 | tf_op jit(solution)/shard_map/pallas_call | solution.py:549
  4.5 2.9 %shard_map.138 = (bf16[14,128,256]{2,1,0:T(8,128)(2,1)S(1)}, bf16[11,128,256]{2,1,0:T(8,128)(2,1)S(1)}, bf16[3,128,256]{2,1,0:T(8,128)(2,1)S(1)}) custom-call(bf16[4480,256]{1,0:T(8,128)(2,1)S(1)} %get-tuple-element.37.refs_0_, bf16[4,18,18,256]{3,2,1,0:T(8,128)(2,1)S(1)} %bitcast.13, bf16[512,256]{1,0:T(8,128)(2,1)S(1)} %collective-permute-done.1.refs_2_, ...), custom_call_target="tpu_custom_call" | custom-call | flops 1879048192 | bytes 6291456 | tf_op jit(solution)/shard_map/pallas_call | solution.py:557
  7.4 2.6 %collective-permute-start.4 = (bf16[11,128,256]{2,1,0:T(8,128)(2,1)S(1)}, bf16[11,128,256]{2,1,0:T(8,128)(2,1)S(1)}, u32[]{:S(2)}, u32[]{:S(2)}) collective-permute-start(bf16[11,128,256]{2,1,0:T(8,128)(2,1)S(1)} %get-tuple-element.41), channel_id=1, source_target_pairs={{0,8},{1,17},{2,10},{3,19},{4,12},{5,21},{6,14},{7,23},{8,0},{9,25... | collective-permute-start | bytes 2162696 | tf_op jit(solution)/shard_map/ppermute | solution.py:143
  10.0 1.6 %collective-permute-start.5 = (bf16[3,128,256]{2,1,0:T(8,128)(2,1)S(1)}, bf16[3,128,256]{2,1,0:T(8,128)(2,1)S(1)}, u32[]{:S(2)}, u32[]{:S(2)}) collective-permute-start(bf16[3,128,256]{2,1,0:T(8,128)(2,1)S(1)} %get-tuple-element.42), channel_id=1, source_target_pairs={{0,2},{1,3},{2,0},{3,1},{4,6},{5,7},{6,4},{7,5},{8,10},{9,11},{10,... | collective-permute-start | bytes 589832 | tf_op jit(solution)/shard_map/ppermute | solution.py:143
  12.5 2.7 %collective-permute-start.3 = (bf16[15,16,256]{2,1,0:T(8,128)(2,1)S(1)}, bf16[15,16,256]{2,1,0:T(8,128)(2,1)S(1)}, u32[]{:S(2)}, u32[]{:S(2)}) collective-permute-start(bf16[15,16,256]{2,1,0:T(8,128)(2,1)S(1)} %shard_map.139.refs_0_), channel_id=1, source_target_pairs={{0,4},{1,5},{2,6},{3,7},{4,0},{5,1},{6,2},{7,3},{8,12},{9,13},{10,... | collective-permute-start | bytes 368648 | tf_op jit(solution)/shard_map/ppermute | solution.py:139
  15.2 3.9 %collective-permute-done.3.refs_1_ = bf16[15,16,256]{2,1,0:T(8,128)(2,1)S(1)} collective-permute-done((bf16[15,16,256]{2,1,0:T(8,128)(2,1)S(1)}, bf16[15,16,256]{2,1,0:T(8,128)(2,1)S(1)}, u32[]{:S(2)}, u32[]{:S(2)}) %collective-permute-start.3) | collective-permute-done | bytes 122912 | tf_op jit(solution)/shard_map/ppermute | solution.py:139
  19.8 1.7 %collective-permute-start.7 = (bf16[11,64,256]{2,1,0:T(8,128)(2,1)S(1)}, bf16[11,64,256]{2,1,0:T(8,128)(2,1)S(1)}, u32[]{:S(2)}, u32[]{:S(2)}) collective-permute-start(bf16[11,64,256]{2,1,0:T(8,128)(2,1)S(1)} %get-tuple-element.45), channel_id=1, source_target_pairs={{0,16},{1,9},{2,18},{3,11},{4,20},{5,13},{6,22},{7,15},{8,24},{9,1... | collective-permute-start | bytes 1081352 | tf_op jit(solution)/shard_map/ppermute | solution.py:143
  21.5 1.5 %collective-permute-start.8 = (bf16[3,64,256]{2,1,0:T(8,128)(2,1)S(1)}, bf16[3,64,256]{2,1,0:T(8,128)(2,1)S(1)}, u32[]{:S(2)}, u32[]{:S(2)}) collective-permute-start(bf16[3,64,256]{2,1,0:T(8,128)(2,1)S(1)} %get-tuple-element.46), channel_id=1, source_target_pairs={{0,8},{1,17},{2,10},{3,19},{4,12},{5,21},{6,14},{7,23},{8,0},{9,25... | collective-permute-start | bytes 294920 | tf_op jit(solution)/shard_map/ppermute | solution.py:143
  23.0 1.6 %collective-permute-start.6 = (bf16[2,15,16,256]{3,2,1,0:T(8,128)(2,1)S(1)}, bf16[2,15,16,256]{3,2,1,0:T(8,128)(2,1)S(1)}, u32[]{:S(2)}, u32[]{:S(2)}) collective-permute-start(bf16[2,15,16,256]{3,2,1,0:T(8,128)(2,1)S(1)} %get-tuple-element.43.refs_0_), channel_id=1, source_target_pairs={{0,2},{1,3},{2,0},{3,1},{4,6},{5,7},{6,4},{7,5},{8,10},{9,11},{10,... | collective-permute-start | bytes 737288 | tf_op jit(solution)/shard_map/ppermute | solution.py:139
  24.6 2.3 %collective-permute-done.8.refs_2_ = bf16[3,64,256]{2,1,0:T(8,128)(2,1)S(1)} collective-permute-done((bf16[3,64,256]{2,1,0:T(8,128)(2,1)S(1)}, bf16[3,64,256]{2,1,0:T(8,128)(2,1)S(1)}, u32[]{:S(2)}, u32[]{:S(2)}) %collective-permute-start.8) | collective-permute-done | bytes 98336 | tf_op jit(solution)/shard_map/ppermute | solution.py:143
  26.9 1.4 %collective-permute-done.7.refs_1_ = bf16[11,64,256]{2,1,0:T(8,128)(2,1)S(1)} collective-permute-done((bf16[11,64,256]{2,1,0:T(8,128)(2,1)S(1)}, bf16[11,64,256]{2,1,0:T(8,128)(2,1)S(1)}, u32[]{:S(2)}, u32[]{:S(2)}) %collective-permute-start.7) | collective-permute-done | bytes 360480 | tf_op jit(solution)/shard_map/ppermute | solution.py:143
  28.3 2.7 %collective-permute-start.9 = (bf16[11,32,256]{2,1,0:T(8,128)(2,1)S(1)}, bf16[11,32,256]{2,1,0:T(8,128)(2,1)S(1)}, u32[]{:S(2)}, u32[]{:S(2)}) collective-permute-start(bf16[11,32,256]{2,1,0:T(8,128)(2,1)S(1)} %get-tuple-element.48), channel_id=1, source_target_pairs={{0,2},{1,3},{2,0},{3,1},{4,6},{5,7},{6,4},{7,5},{8,10},{9,11},{10,... | collective-permute-start | bytes 540680 | tf_op jit(solution)/shard_map/ppermute | solution.py:143
  31.5 3.7 %collective-permute-done.10.refs_4_ = bf16[3,32,256]{2,1,0:T(8,128)(2,1)S(1)} collective-permute-done((bf16[3,32,256]{2,1,0:T(8,128)(2,1)S(1)}, bf16[3,32,256]{2,1,0:T(8,128)(2,1)S(1)}, u32[]{:S(2)}, u32[]{:S(2)}) %collective-permute-start.10) | collective-permute-done | bytes 49184 | tf_op jit(solution)/shard_map/ppermute | solution.py:143
  35.2 1.0 %collective-permute-start.14 = (bf16[4,224,256]{2,1,0:T(8,128)(2,1)S(1)}, bf16[4,224,256]{2,1,0:T(8,128)(2,1)S(1)}, u32[]{:S(2)}, u32[]{:S(2)}) collective-permute-start(bf16[4,224,256]{2,1,0:T(8,128)(2,1)S(1)} %get-tuple-element.54.refs_4_), channel_id=1, source_target_pairs={{0,8},{1,17},{2,10},{3,19},{4,12},{5,21},{6,14},{7,23},{8,0},{9,25... | collective-permute-start | bytes 1376264 | tf_op jit(solution)/shard_map/ppermute | solution.py:143
  36.9 2.6 %collective-permute-start.12 = (bf16[14,32,256]{2,1,0:T(8,128)(2,1)S(1)}, bf16[14,32,256]{2,1,0:T(8,128)(2,1)S(1)}, u32[]{:S(2)}, u32[]{:S(2)}) collective-permute-start(bf16[14,32,256]{2,1,0:T(8,128)(2,1)S(1)} %get-tuple-element.52.refs_1_), channel_id=1, source_target_pairs={{0,4},{1,5},{2,6},{3,7},{4,0},{5,1},{6,2},{7,3},{8,12},{9,13},{10,... | collective-permute-start | bytes 688136 | tf_op jit(solution)/shard_map/ppermute | solution.py:139
  40.7 2.7 %shard_map.143 = (f32[32,128]{1,0:T(8,128)S(1)}, s32[224]{0:T(256)S(1)}) custom-call(s32[224]{0:T(256)S(1)} %copy-done.1, bf16[4,16,256]{2,1,0:T(8,128)(2,1)S(1)} %get-tuple-element.50.refs_1_, bf16[4,16,256]{2,1,0:T(8,128)(2,1)S(1)} %collective-permute-done.11.refs_2_), custom_call_target="tpu_custom_call" | custom-call | tf_op jit(solution)/shard_map/pallas_call | solution.py:603
  43.4 5.5 %collective-permute-done.12.refs_2_ = bf16[14,32,256]{2,1,0:T(8,128)(2,1)S(1)} collective-permute-done((bf16[14,32,256]{2,1,0:T(8,128)(2,1)S(1)}, bf16[14,32,256]{2,1,0:T(8,128)(2,1)S(1)}, u32[]{:S(2)}, u32[]{:S(2)}) %collective-permute-start.12) | collective-permute-done | bytes 229408 | tf_op jit(solution)/shard_map/ppermute | solution.py:139
  50.3 1.7 %collective-permute-start.17 = (bf16[4,32,256]{2,1,0:T(8,128)(2,1)S(1)}, bf16[4,32,256]{2,1,0:T(8,128)(2,1)S(1)}, u32[]{:S(2)}, u32[]{:S(2)}) collective-permute-start(bf16[4,32,256]{2,1,0:T(8,128)(2,1)S(1)} %get-tuple-element.57.refs_3_), channel_id=1, source_target_pairs={{0,16},{1,9},{2,18},{3,11},{4,20},{5,13},{6,22},{7,15},{8,24},{9,1... | collective-permute-start | bytes 196616 | tf_op jit(solution)/shard_map/ppermute | solution.py:143
  52.4 2.9 %collective-permute-done.17.refs_4_ = bf16[4,32,256]{2,1,0:T(8,128)(2,1)S(1)} collective-permute-done((bf16[4,32,256]{2,1,0:T(8,128)(2,1)S(1)}, bf16[4,32,256]{2,1,0:T(8,128)(2,1)S(1)}, u32[]{:S(2)}, u32[]{:S(2)}) %collective-permute-start.17) | collective-permute-done | bytes 65568 | tf_op jit(solution)/shard_map/ppermute | solution.py:143
  55.3 1.1 %collective-permute-done.16.refs_2_ = bf16[11,32,256]{2,1,0:T(8,128)(2,1)S(1)} collective-permute-done((bf16[11,32,256]{2,1,0:T(8,128)(2,1)S(1)}, bf16[11,32,256]{2,1,0:T(8,128)(2,1)S(1)}, u32[]{:S(2)}, u32[]{:S(2)}) %collective-permute-start.16) | collective-permute-done | bytes 180256 | tf_op jit(solution)/shard_map/ppermute | solution.py:143
  56.5 1.7 %collective-permute-start.18 = (bf16[11,64,256]{2,1,0:T(8,128)(2,1)S(1)}, bf16[11,64,256]{2,1,0:T(8,128)(2,1)S(1)}, u32[]{:S(2)}, u32[]{:S(2)}) collective-permute-start(bf16[11,64,256]{2,1,0:T(8,128)(2,1)S(1)} %get-tuple-element.58.refs_1_), channel_id=1, source_target_pairs={{0,16},{1,9},{2,18},{3,11},{4,20},{5,13},{6,22},{7,15},{8,24},{9,1... | collective-permute-start | bytes 1081352 | tf_op jit(solution)/shard_map/ppermute | solution.py:143
  58.8 5.6 %collective-permute-done.19.refs_4_ = bf16[4,64,256]{2,1,0:T(8,128)(2,1)S(1)} collective-permute-done((bf16[4,64,256]{2,1,0:T(8,128)(2,1)S(1)}, bf16[4,64,256]{2,1,0:T(8,128)(2,1)S(1)}, u32[]{:S(2)}, u32[]{:S(2)}) %collective-permute-start.19) | collective-permute-done | bytes 131104 | tf_op jit(solution)/shard_map/ppermute | solution.py:143
  64.5 1.4 %collective-permute-start.23 = (bf16[11,128,256]{2,1,0:T(8,128)(2,1)S(1)}, bf16[11,128,256]{2,1,0:T(8,128)(2,1)S(1)}, u32[]{:S(2)}, u32[]{:S(2)}) collective-permute-start(bf16[11,128,256]{2,1,0:T(8,128)(2,1)S(1)} %get-tuple-element.62.refs_1_), channel_id=1, source_target_pairs={{0,8},{1,17},{2,10},{3,19},{4,12},{5,21},{6,14},{7,23},{8,0},{9,25... | collective-permute-start | bytes 2162696 | tf_op jit(solution)/shard_map/ppermute | solution.py:143
  66.0 1.1 %collective-permute-start.24 = (bf16[4,128,256]{2,1,0:T(8,128)(2,1)S(1)}, bf16[4,128,256]{2,1,0:T(8,128)(2,1)S(1)}, u32[]{:S(2)}, u32[]{:S(2)}) collective-permute-start(bf16[4,128,256]{2,1,0:T(8,128)(2,1)S(1)} %get-tuple-element.63.refs_3_), channel_id=1, source_target_pairs={{0,2},{1,3},{2,0},{3,1},{4,6},{5,7},{6,4},{7,5},{8,10},{9,11},{10,... | collective-permute-start | bytes 786440 | tf_op jit(solution)/shard_map/ppermute | solution.py:143
  67.6 1.0 %collective-permute-done.21.refs_5_ = bf16[2,224,256]{2,1,0:T(8,128)(2,1)S(1)} collective-permute-done((bf16[2,224,256]{2,1,0:T(8,128)(2,1)S(1)}, bf16[2,224,256]{2,1,0:T(8,128)(2,1)S(1)}, u32[]{:S(2)}, u32[]{:S(2)}) %collective-permute-start.21) | collective-permute-done | bytes 229408 | tf_op jit(solution)/shard_map/ppermute | solution.py:139
  68.9 1.0 %shard_map.148.refs_0_.refs_1_.refs_4_ = bf16[7168,256]{1,0:T(8,128)(2,1)S(1)} custom-call(s32[224]{0:T(256)S(1)} %copy-done.1, bf16[3,4,224,256]{3,2,1,0:T(8,128)(2,1)S(1)} %get-tuple-element.55.refs_1_, bf16[2,224,256]{2,1,0:T(8,128)(2,1)S(1)} %get-tuple-element.60.refs_2_, bf16[2,224,256]{2,1,0:T(8,128)(2,1)S(1)} %get-tuple-element.61.refs_3_, ...), custom_call_target="tpu_custom_call" | custom-call | bytes 8388608 | tf_op jit(solution)/shard_map/pallas_call | solution.py:641
  69.9 4.1 %collective-permute-done.24.refs_4_ = bf16[4,128,256]{2,1,0:T(8,128)(2,1)S(1)} collective-permute-done((bf16[4,128,256]{2,1,0:T(8,128)(2,1)S(1)}, bf16[4,128,256]{2,1,0:T(8,128)(2,1)S(1)}, u32[]{:S(2)}, u32[]{:S(2)}) %collective-permute-start.24) | collective-permute-done | bytes 262176 | tf_op jit(solution)/shard_map/ppermute | solution.py:143
  74.0 1.9 %collective-permute-done.23.refs_2_ = bf16[11,128,256]{2,1,0:T(8,128)(2,1)S(1)} collective-permute-done((bf16[11,128,256]{2,1,0:T(8,128)(2,1)S(1)}, bf16[11,128,256]{2,1,0:T(8,128)(2,1)S(1)}, u32[]{:S(2)}, u32[]{:S(2)}) %collective-permute-start.23) | collective-permute-done | bytes 720928 | tf_op jit(solution)/shard_map/ppermute | solution.py:143
  76.1 1.1 %shard_map.151.refs_9_ = f32[512,256]{1,0:T(8,128)S(1)} custom-call(bf16[3456,256]{1,0:T(8,128)(2,1)S(1)} %shard_map.144.refs_0_.refs_3_, bf16[15,256,256]{2,1,0:T(8,128)(2,1)S(1)} %shard_map.149.refs_1_.refs_6_), custom_call_target="tpu_custom_call" | custom-call | flops 939524096 | bytes 4194304 | tf_op jit(solution)/shard_map/pallas_call | solution.py:653
  77.3 2.0 %shard_map.150.refs_8_ = f32[512,256]{1,0:T(8,128)S(1)} custom-call(bf16[3456,256]{1,0:T(8,128)(2,1)S(1)} %shard_map.144.refs_0_.refs_3_, bf16[7168,256]{1,0:T(8,128)(2,1)S(1)} %shard_map.148.refs_0_.refs_1_.refs_4_), custom_call_target="tpu_custom_call" | custom-call | flops 1811939328 | bytes 6291456 | tf_op jit(solution)/shard_map/pallas_call | solution.py:646
  80.1 3.1 %shard_map.152 = (f32[896,256]{1,0:T(8,128)}, f32[896,256]{1,0:T(8,128)}, f32[7,128]{1,0:T(8,128)}, f32[2,256]{1,0:T(2,128)}, bf16[512,256]{1,0:T(8,128)(2,1)}) custom-call(s32[224]{0:T(256)S(1)} %get-tuple-element.51.refs_0_, f32[1]{0:T(128)S(6)} %sub.3.refs_0_.refs_1_, f32[2,256]{1,0:T(2,128)S(1)} %copy-done.2, ...), custom_call_target="tpu_custom_call" | custom-call | flops 1073741824 | bytes 16777216 | tf_op jit(solution)/shard_map/pallas_call | solution.py:668
  (47 shorter events, 9.0 us)
Async XLA Ops:
  0.6 3.7 %collective-permute-start = (bf16[1,4,18,18,256]{4,1,3,2,0:T(4,128)(2,1)}, bf16[1,4,18,18,256]{4,1,3,2,0:T(4,128)(2,1)S(1)}, u32[]{:S(2)}, u32[]{:S(2)}) collective-permute-start(bf16[1,4,18,18,256]{4,1,3,2,0:T(4,128)(2,1)} %param.12), channel_id=1, source_target_pairs={{0,1},{1,0},{2,3},{3,2},{4,5},{5,4},{6,7},{7,6},{8,9},{9,8},{10,11... | collective-permute-start | bytes 1990664 | tf_op jit(solution)/shard_map/ppermute | solution.py:139
  1.1 3.3 %collective-permute-start.1 = (bf16[512,256]{1,0:T(8,128)(2,1)}, bf16[512,256]{1,0:T(8,128)(2,1)S(1)}, u32[]{:S(2)}, u32[]{:S(2)}) collective-permute-start(bf16[512,256]{1,0:T(8,128)(2,1)} %refs_1_.2), channel_id=1, source_target_pairs={{0,1},{1,0},{2,3},{3,2},{4,5},{5,4},{6,7},{7,6},{8,9},{9,8},{10,11... | collective-permute-start | bytes 786440 | tf_op jit(solution)/shard_map/ppermute | solution.py:139
  1.2 3.2 %collective-permute-start.2 = (bf16[512,256]{1,0:T(8,128)(2,1)}, bf16[512,256]{1,0:T(8,128)(2,1)S(1)}, u32[]{:S(2)}, u32[]{:S(2)}) collective-permute-start(bf16[512,256]{1,0:T(8,128)(2,1)} %refs_2_.2), channel_id=1, source_target_pairs={{0,1},{1,0},{2,3},{3,2},{4,5},{5,4},{6,7},{7,6},{8,9},{9,8},{10,11... | collective-permute-start | bytes 786440 | tf_op jit(solution)/shard_map/ppermute | solution.py:139
  7.4 12.3 %collective-permute-start.4 = (bf16[11,128,256]{2,1,0:T(8,128)(2,1)S(1)}, bf16[11,128,256]{2,1,0:T(8,128)(2,1)S(1)}, u32[]{:S(2)}, u32[]{:S(2)}) collective-permute-start(bf16[11,128,256]{2,1,0:T(8,128)(2,1)S(1)} %get-tuple-element.41), channel_id=1, source_target_pairs={{0,8},{1,17},{2,10},{3,19},{4,12},{5,21},{6,14},{7,23},{8,0},{9,25... | collective-permute-start | bytes 2162696 | tf_op jit(solution)/shard_map/ppermute | solution.py:143
  10.0 9.6 %collective-permute-start.5 = (bf16[3,128,256]{2,1,0:T(8,128)(2,1)S(1)}, bf16[3,128,256]{2,1,0:T(8,128)(2,1)S(1)}, u32[]{:S(2)}, u32[]{:S(2)}) collective-permute-start(bf16[3,128,256]{2,1,0:T(8,128)(2,1)S(1)} %get-tuple-element.42), channel_id=1, source_target_pairs={{0,2},{1,3},{2,0},{3,1},{4,6},{5,7},{6,4},{7,5},{8,10},{9,11},{10,... | collective-permute-start | bytes 589832 | tf_op jit(solution)/shard_map/ppermute | solution.py:143
  12.5 28.2 %copy-start.1 = (s32[224]{0:T(256)S(1)}, s32[224]{0:T(256)}, u32[]{:S(2)}) copy-start(s32[224]{0:T(256)} %refs_0_.3) | copy-start | bytes 2692
  12.5 6.6 %collective-permute-start.3 = (bf16[15,16,256]{2,1,0:T(8,128)(2,1)S(1)}, bf16[15,16,256]{2,1,0:T(8,128)(2,1)S(1)}, u32[]{:S(2)}, u32[]{:S(2)}) collective-permute-start(bf16[15,16,256]{2,1,0:T(8,128)(2,1)S(1)} %shard_map.139.refs_0_), channel_id=1, source_target_pairs={{0,4},{1,5},{2,6},{3,7},{4,0},{5,1},{6,2},{7,3},{8,12},{9,13},{10,... | collective-permute-start | bytes 368648 | tf_op jit(solution)/shard_map/ppermute | solution.py:139
  19.7 32.2 %copy-start.3 = (bf16[1,4,18,18,256]{4,1,3,2,0:T(4,128)(2,1)S(1)}, bf16[1,4,18,18,256]{4,1,3,2,0:T(4,128)(2,1)}, u32[]{:S(2)}) copy-start(bf16[1,4,18,18,256]{4,1,3,2,0:T(4,128)(2,1)} %param.19) | copy-start | bytes 1990660
  19.8 8.5 %collective-permute-start.7 = (bf16[11,64,256]{2,1,0:T(8,128)(2,1)S(1)}, bf16[11,64,256]{2,1,0:T(8,128)(2,1)S(1)}, u32[]{:S(2)}, u32[]{:S(2)}) collective-permute-start(bf16[11,64,256]{2,1,0:T(8,128)(2,1)S(1)} %get-tuple-element.45), channel_id=1, source_target_pairs={{0,16},{1,9},{2,18},{3,11},{4,20},{5,13},{6,22},{7,15},{8,24},{9,1... | collective-permute-start | bytes 1081352 | tf_op jit(solution)/shard_map/ppermute | solution.py:143
  21.5 5.4 %collective-permute-start.8 = (bf16[3,64,256]{2,1,0:T(8,128)(2,1)S(1)}, bf16[3,64,256]{2,1,0:T(8,128)(2,1)S(1)}, u32[]{:S(2)}, u32[]{:S(2)}) collective-permute-start(bf16[3,64,256]{2,1,0:T(8,128)(2,1)S(1)} %get-tuple-element.46), channel_id=1, source_target_pairs={{0,8},{1,17},{2,10},{3,19},{4,12},{5,21},{6,14},{7,23},{8,0},{9,25... | collective-permute-start | bytes 294920 | tf_op jit(solution)/shard_map/ppermute | solution.py:143
  23.0 8.5 %collective-permute-start.6 = (bf16[2,15,16,256]{3,2,1,0:T(8,128)(2,1)S(1)}, bf16[2,15,16,256]{3,2,1,0:T(8,128)(2,1)S(1)}, u32[]{:S(2)}, u32[]{:S(2)}) collective-permute-start(bf16[2,15,16,256]{3,2,1,0:T(8,128)(2,1)S(1)} %get-tuple-element.43.refs_0_), channel_id=1, source_target_pairs={{0,2},{1,3},{2,0},{3,1},{4,6},{5,7},{6,4},{7,5},{8,10},{9,11},{10,... | collective-permute-start | bytes 737288 | tf_op jit(solution)/shard_map/ppermute | solution.py:139
  28.3 6.8 %collective-permute-start.9 = (bf16[11,32,256]{2,1,0:T(8,128)(2,1)S(1)}, bf16[11,32,256]{2,1,0:T(8,128)(2,1)S(1)}, u32[]{:S(2)}, u32[]{:S(2)}) collective-permute-start(bf16[11,32,256]{2,1,0:T(8,128)(2,1)S(1)} %get-tuple-element.48), channel_id=1, source_target_pairs={{0,2},{1,3},{2,0},{3,1},{4,6},{5,7},{6,4},{7,5},{8,10},{9,11},{10,... | collective-permute-start | bytes 540680 | tf_op jit(solution)/shard_map/ppermute | solution.py:143
  31.0 4.2 %collective-permute-start.10 = (bf16[3,32,256]{2,1,0:T(8,128)(2,1)S(1)}, bf16[3,32,256]{2,1,0:T(8,128)(2,1)S(1)}, u32[]{:S(2)}, u32[]{:S(2)}) collective-permute-start(bf16[3,32,256]{2,1,0:T(8,128)(2,1)S(1)} %get-tuple-element.49), channel_id=1, source_target_pairs={{0,16},{1,9},{2,18},{3,11},{4,20},{5,13},{6,22},{7,15},{8,24},{9,1... | collective-permute-start | bytes 147464 | tf_op jit(solution)/shard_map/ppermute | solution.py:143
  35.2 13.7 %collective-permute-start.14 = (bf16[4,224,256]{2,1,0:T(8,128)(2,1)S(1)}, bf16[4,224,256]{2,1,0:T(8,128)(2,1)S(1)}, u32[]{:S(2)}, u32[]{:S(2)}) collective-permute-start(bf16[4,224,256]{2,1,0:T(8,128)(2,1)S(1)} %get-tuple-element.54.refs_4_), channel_id=1, source_target_pairs={{0,8},{1,17},{2,10},{3,19},{4,12},{5,21},{6,14},{7,23},{8,0},{9,25... | collective-permute-start | bytes 1376264 | tf_op jit(solution)/shard_map/ppermute | solution.py:143
  36.3 12.6 %collective-permute-start.13 = (bf16[4,224,256]{2,1,0:T(8,128)(2,1)S(1)}, bf16[4,224,256]{2,1,0:T(8,128)(2,1)S(1)}, u32[]{:S(2)}, u32[]{:S(2)}) collective-permute-start(bf16[4,224,256]{2,1,0:T(8,128)(2,1)S(1)} %get-tuple-element.54.refs_4_), channel_id=1, source_target_pairs={{0,16},{1,9},{2,18},{3,11},{4,20},{5,13},{6,22},{7,15},{8,24},{9,1... | collective-permute-start | bytes 1376264 | tf_op jit(solution)/shard_map/ppermute | solution.py:143
  36.9 12.0 %collective-permute-start.12 = (bf16[14,32,256]{2,1,0:T(8,128)(2,1)S(1)}, bf16[14,32,256]{2,1,0:T(8,128)(2,1)S(1)}, u32[]{:S(2)}, u32[]{:S(2)}) collective-permute-start(bf16[14,32,256]{2,1,0:T(8,128)(2,1)S(1)} %get-tuple-element.52.refs_1_), channel_id=1, source_target_pairs={{0,4},{1,5},{2,6},{3,7},{4,0},{5,1},{6,2},{7,3},{8,12},{9,13},{10,... | collective-permute-start | bytes 688136 | tf_op jit(solution)/shard_map/ppermute | solution.py:139
  39.5 1.2 %collective-permute-start.11 = (bf16[4,16,256]{2,1,0:T(8,128)(2,1)S(1)}, bf16[4,16,256]{2,1,0:T(8,128)(2,1)S(1)}, u32[]{:S(2)}, u32[]{:S(2)}) collective-permute-start(bf16[4,16,256]{2,1,0:T(8,128)(2,1)S(1)} %get-tuple-element.50.refs_1_), channel_id=1, source_target_pairs={{0,1},{1,0},{2,3},{3,2},{4,5},{5,4},{6,7},{7,6},{8,9},{9,8},{10,11... | collective-permute-start | bytes 98312 | tf_op jit(solution)/shard_map/ppermute | solution.py:139
  49.4 19.5 %collective-permute-start.20 = (bf16[3,4,224,256]{3,2,1,0:T(8,128)(2,1)S(1)}, bf16[3,4,224,256]{3,2,1,0:T(8,128)(2,1)S(1)}, u32[]{:S(2)}, u32[]{:S(2)}) collective-permute-start(bf16[3,4,224,256]{3,2,1,0:T(8,128)(2,1)S(1)} %get-tuple-element.55.refs_1_), channel_id=1, source_target_pairs={{0,1},{1,0},{2,3},{3,2},{4,5},{5,4},{6,7},{7,6},{8,9},{9,8},{10,11... | collective-permute-start | bytes 4128776 | tf_op jit(solution)/shard_map/ppermute | solution.py:139
  49.4 7.0 %collective-permute-start.16 = (bf16[11,32,256]{2,1,0:T(8,128)(2,1)S(1)}, bf16[11,32,256]{2,1,0:T(8,128)(2,1)S(1)}, u32[]{:S(2)}, u32[]{:S(2)}) collective-permute-start(bf16[11,32,256]{2,1,0:T(8,128)(2,1)S(1)} %get-tuple-element.56.refs_1_), channel_id=1, source_target_pairs={{0,2},{1,3},{2,0},{3,1},{4,6},{5,7},{6,4},{7,5},{8,10},{9,11},{10,... | collective-permute-start | bytes 540680 | tf_op jit(solution)/shard_map/ppermute | solution.py:143
  50.0 14.5 %collective-permute-start.15 = (bf16[4,224,256]{2,1,0:T(8,128)(2,1)S(1)}, bf16[4,224,256]{2,1,0:T(8,128)(2,1)S(1)}, u32[]{:S(2)}, u32[]{:S(2)}) collective-permute-start(bf16[4,224,256]{2,1,0:T(8,128)(2,1)S(1)} %collective-permute-done.13.refs_5_), channel_id=1, source_target_pairs={{0,8},{1,17},{2,10},{3,19},{4,12},{5,21},{6,14},{7,23},{8,0},{9,25... | collective-permute-start | bytes 1376264 | tf_op jit(solution)/shard_map/ppermute | solution.py:143
  50.3 5.0 %collective-permute-start.17 = (bf16[4,32,256]{2,1,0:T(8,128)(2,1)S(1)}, bf16[4,32,256]{2,1,0:T(8,128)(2,1)S(1)}, u32[]{:S(2)}, u32[]{:S(2)}) collective-permute-start(bf16[4,32,256]{2,1,0:T(8,128)(2,1)S(1)} %get-tuple-element.57.refs_3_), channel_id=1, source_target_pairs={{0,16},{1,9},{2,18},{3,11},{4,20},{5,13},{6,22},{7,15},{8,24},{9,1... | collective-permute-start | bytes 196616 | tf_op jit(solution)/shard_map/ppermute | solution.py:143
  56.5 8.0 %collective-permute-start.18 = (bf16[11,64,256]{2,1,0:T(8,128)(2,1)S(1)}, bf16[11,64,256]{2,1,0:T(8,128)(2,1)S(1)}, u32[]{:S(2)}, u32[]{:S(2)}) collective-permute-start(bf16[11,64,256]{2,1,0:T(8,128)(2,1)S(1)} %get-tuple-element.58.refs_1_), channel_id=1, source_target_pairs={{0,16},{1,9},{2,18},{3,11},{4,20},{5,13},{6,22},{7,15},{8,24},{9,1... | collective-permute-start | bytes 1081352 | tf_op jit(solution)/shard_map/ppermute | solution.py:143
  58.2 6.2 %collective-permute-start.19 = (bf16[4,64,256]{2,1,0:T(8,128)(2,1)S(1)}, bf16[4,64,256]{2,1,0:T(8,128)(2,1)S(1)}, u32[]{:S(2)}, u32[]{:S(2)}) collective-permute-start(bf16[4,64,256]{2,1,0:T(8,128)(2,1)S(1)} %get-tuple-element.59.refs_3_), channel_id=1, source_target_pairs={{0,8},{1,17},{2,10},{3,19},{4,12},{5,21},{6,14},{7,23},{8,0},{9,25... | collective-permute-start | bytes 393224 | tf_op jit(solution)/shard_map/ppermute | solution.py:143
  64.5 11.4 %collective-permute-start.23 = (bf16[11,128,256]{2,1,0:T(8,128)(2,1)S(1)}, bf16[11,128,256]{2,1,0:T(8,128)(2,1)S(1)}, u32[]{:S(2)}, u32[]{:S(2)}) collective-permute-start(bf16[11,128,256]{2,1,0:T(8,128)(2,1)S(1)} %get-tuple-element.62.refs_1_), channel_id=1, source_target_pairs={{0,8},{1,17},{2,10},{3,19},{4,12},{5,21},{6,14},{7,23},{8,0},{9,25... | collective-permute-start | bytes 2162696 | tf_op jit(solution)/shard_map/ppermute | solution.py:143
  66.0 8.0 %collective-permute-start.24 = (bf16[4,128,256]{2,1,0:T(8,128)(2,1)S(1)}, bf16[4,128,256]{2,1,0:T(8,128)(2,1)S(1)}, u32[]{:S(2)}, u32[]{:S(2)}) collective-permute-start(bf16[4,128,256]{2,1,0:T(8,128)(2,1)S(1)} %get-tuple-element.63.refs_3_), channel_id=1, source_target_pairs={{0,2},{1,3},{2,0},{3,1},{4,6},{5,7},{6,4},{7,5},{8,10},{9,11},{10,... | collective-permute-start | bytes 786440 | tf_op jit(solution)/shard_map/ppermute | solution.py:143
  67.1 1.5 %collective-permute-start.21 = (bf16[2,224,256]{2,1,0:T(8,128)(2,1)S(1)}, bf16[2,224,256]{2,1,0:T(8,128)(2,1)S(1)}, u32[]{:S(2)}, u32[]{:S(2)}) collective-permute-start(bf16[2,224,256]{2,1,0:T(8,128)(2,1)S(1)} %get-tuple-element.60.refs_2_), channel_id=1, source_target_pairs={{0,1},{1,0},{2,3},{3,2},{4,5},{5,4},{6,7},{7,6},{8,9},{9,8},{10,11... | collective-permute-start | bytes 688136 | tf_op jit(solution)/shard_map/ppermute | solution.py:139
  67.1 1.8 %collective-permute-start.22 = (bf16[2,224,256]{2,1,0:T(8,128)(2,1)S(1)}, bf16[2,224,256]{2,1,0:T(8,128)(2,1)S(1)}, u32[]{:S(2)}, u32[]{:S(2)}) collective-permute-start(bf16[2,224,256]{2,1,0:T(8,128)(2,1)S(1)} %get-tuple-element.61.refs_3_), channel_id=1, source_target_pairs={{0,1},{1,0},{2,3},{3,2},{4,5},{5,4},{6,7},{7,6},{8,9},{9,8},{10,11... | collective-permute-start | bytes 688136 | tf_op jit(solution)/shard_map/ppermute | solution.py:139
  76.1 4.0 %collective-permute-start.25 = (bf16[15,256,256]{2,1,0:T(8,128)(2,1)S(1)}, bf16[15,256,256]{2,1,0:T(8,128)(2,1)S(1)}, u32[]{:S(2)}, u32[]{:S(2)}) collective-permute-start(bf16[15,256,256]{2,1,0:T(8,128)(2,1)S(1)} %shard_map.149.refs_1_.refs_6_), channel_id=1, source_target_pairs={{0,1},{1,0},{2,3},{3,2},{4,5},{5,4},{6,7},{7,6},{8,9},{9,8},{10,11... | collective-permute-start | bytes 5898248 | tf_op jit(solution)/shard_map/ppermute | solution.py:139
  77.3 2.8 %copy-start = (f32[896,256]{1,0:T(8,128)S(1)}, f32[896,256]{1,0:T(8,128)}, u32[]{:S(2)}) copy-start(f32[896,256]{1,0:T(8,128)} %refs_5_.1) | copy-start | bytes 2752516
  77.3 2.8 %copy-start.2 = (f32[2,256]{1,0:T(2,128)S(1)}, f32[2,256]{1,0:T(2,128)}, u32[]{:S(2)}) copy-start(f32[2,256]{1,0:T(2,128)} %refs_2_.3) | copy-start | bytes 6148

commit v12 on v10

--- a/solution.py
+++ b/solution.py
@@ -498,15 +498,6 @@
             stored.at[line],
         )
 
-    change = own_part[...] + add_taps(views, peer, 1 - core)
-    hidden = old[...] - (learn_rate * factor[0:1]) * change
-    small = jnp.where(core == 1, mine[SLOTS - 1].astype(WIDE), peer[SLOTS - 1].astype(WIDE))
-    weights = natural[27 * CI :].astype(WIDE) - small * (learn_rate * factor[1:2])
-    next_output[...] = jnp.dot(
-        jax.nn.silu(hidden).astype(LOW), weights.astype(LOW), preferred_element_type=WIDE
-    ).astype(LOW)
-    copies += store(next_output, output_far, 1)
-
     for side, messages in enumerate(sums):
         for sender in range(8):
             for line in range(4):
@@ -524,6 +515,15 @@
             values = jnp.where(here, turned, values)
         new_row[line : line + 1] = values
     copies += store(new_row, row_far, 2)
+
+    change = own_part[...] + add_taps(views, peer, 1 - core)
+    hidden = old[...] - (learn_rate * factor[0:1]) * change
+    small = jnp.where(core == 1, mine[SLOTS - 1].astype(WIDE), peer[SLOTS - 1].astype(WIDE))
+    weights = natural[27 * CI :].astype(WIDE) - small * (learn_rate * factor[1:2])
+    next_output[...] = jnp.dot(
+        jax.nn.silu(hidden).astype(LOW), weights.astype(LOW), preferred_element_type=WIDE
+    ).astype(LOW)
+    copies += store(next_output, output_far, 1)
     for copy in copies:
         copy.wait()
 

time: 83.6 us -> 83.6 us (level)
  no operation moved by 1% of the time
where the time goes in v12:
time: 83.6 us; the launch traced here: 83.4 us
  waiting for transfers between devices  37 us (44%)
  starting transfers between devices  26.8 us (32%)
  Pallas kernels  16.5 us (20%)
  between operations  1.55 us (2%)
  local copies, waits for them, and re-layouts  1.5 us (2%)
    ppermute x15, waiting for transfers between devices, swap_mixed(): lax.ppermute(value, AXES, [(at, at ^ masks[at & 1]) for at in range(32)])  22.6 us
    ppermute x15, starting transfers between devices, swap_mixed(): lax.ppermute(value, AXES, [(at, at ^ masks[at & 1]) for at in range(32)])  18.3 us
    ppermute x11, waiting for transfers between devices, swap(): return lax.ppermute(value, AXES, [(at, at ^ mask) for at in range(32)])  14.5 us
    ppermute x11, starting transfers between devices, swap(): return lax.ppermute(value, AXES, [(at, at ^ mask) for at in range(32)])  8.52 us
    pallas_call x1, Pallas kernels, shards(): call(finish_kernel, outs, [SMEM] * 2 + [VMEM] * 8, out_specs=[HBM] * 5, s...  3.1 us
    pallas_call x1, Pallas kernels, shards(): call(term_kernel, [((SLOTS, 128, CO), LOW)] + [((count, 128, CO), LOW) fo...  2.9 us
    pallas_call x1, Pallas kernels, shards(): call(moments_kernel, [((BLK, 128), WIDE), ((NB,), jnp.int32)], [SMEM] + [...  2.67 us
    pallas_call x1, Pallas kernels, shards(): call(old_hidden_kernel, [((PIX, CO), WIDE)], [VMEM] * 2, flops=2 * 27 * 5...  2 us
  transfers between devices with their start and end apart: 26, of which 14 were waited for; matrix products, arithmetic and copies ran while one was open for 2% of the time, Pallas kernels for 12%

profile of v12, /device:TPU:0, one launch (start us, length us, event | category | flops | bytes accessed | tf_op | source)
XLA Modules:
  0.0 83.4 jit_solution(786962680306850964)
XLA Ops:
  1.7 1.2 %copy.26 = bf16[1,4,18,18,256]{4,3,2,1,0:T(8,128)(2,1)S(1)} copy(bf16[1,4,18,18,256]{4,1,3,2,0:T(4,128)(2,1)} %param.12) | data formatting | bytes 1327104 | tf_op args[2]
  2.9 1.4 %shard_map.137 = (bf16[4480,256]{1,0:T(8,128)(2,1)S(1)}, bf16[512,256]{1,0:T(8,128)(2,1)S(1)}, bf16[256,256]{1,0:T(8,128)(2,1)S(1)}) custom-call(bf16[4,18,18,256]{3,2,1,0:T(8,128)(2,1)S(1)} %bitcast.11, bf16[512,256]{1,0:T(8,128)(2,1)} %refs_1_.2, bf16[512,256]{1,0:T(8,128)(2,1)} %refs_2_.2, bf16[256,256]{1,0:T(8,128)(2,1)} %refs_3_.1), custom_call_target="tpu_custom_call" | custom-call | bytes 4194304 | tf_op jit(solution)/shard_map/pallas_call | solution.py:549
  4.5 2.9 %shard_map.138 = (bf16[14,128,256]{2,1,0:T(8,128)(2,1)S(1)}, bf16[10,128,256]{2,1,0:T(8,128)(2,1)S(1)}, bf16[4,128,256]{2,1,0:T(8,128)(2,1)S(1)}) custom-call(bf16[4480,256]{1,0:T(8,128)(2,1)S(1)} %get-tuple-element.37.refs_0_, bf16[4,18,18,256]{3,2,1,0:T(8,128)(2,1)S(1)} %bitcast.13, bf16[512,256]{1,0:T(8,128)(2,1)S(1)} %collective-permute-done.1.refs_2_, ...), custom_call_target="tpu_custom_call" | custom-call | flops 1879048192 | bytes 6291456 | tf_op jit(solution)/shard_map/pallas_call | solution.py:557
  7.4 2.6 %collective-permute-start.4 = (bf16[10,128,256]{2,1,0:T(8,128)(2,1)S(1)}, bf16[10,128,256]{2,1,0:T(8,128)(2,1)S(1)}, u32[]{:S(2)}, u32[]{:S(2)}) collective-permute-start(bf16[10,128,256]{2,1,0:T(8,128)(2,1)S(1)} %get-tuple-element.41), channel_id=1, source_target_pairs={{0,8},{1,17},{2,10},{3,19},{4,12},{5,21},{6,14},{7,23},{8,0},{9,25... | collective-permute-start | bytes 1966088 | tf_op jit(solution)/shard_map/ppermute | solution.py:143
  10.0 1.6 %collective-permute-start.5 = (bf16[4,128,256]{2,1,0:T(8,128)(2,1)S(1)}, bf16[4,128,256]{2,1,0:T(8,128)(2,1)S(1)}, u32[]{:S(2)}, u32[]{:S(2)}) collective-permute-start(bf16[4,128,256]{2,1,0:T(8,128)(2,1)S(1)} %get-tuple-element.42), channel_id=1, source_target_pairs={{0,2},{1,3},{2,0},{3,1},{4,6},{5,7},{6,4},{7,5},{8,10},{9,11},{10,... | collective-permute-start | bytes 786440 | tf_op jit(solution)/shard_map/ppermute | solution.py:143
  11.6 1.0 %shard_map.139.refs_0_ = bf16[15,16,256]{2,1,0:T(8,128)(2,1)S(1)} custom-call(bf16[14,128,256]{2,1,0:T(8,128)(2,1)S(1)} %get-tuple-element.40.refs_0_.refs_2_, f32[896,256]{1,0:T(8,128)} %refs_5_.1, f32[7,128]{1,0:T(8,128)} %bitcast.14), custom_call_target="tpu_custom_call" | custom-call | tf_op jit(solution)/shard_map/pallas_call | solution.py:567
  12.6 2.7 %collective-permute-start.3 = (bf16[15,16,256]{2,1,0:T(8,128)(2,1)S(1)}, bf16[15,16,256]{2,1,0:T(8,128)(2,1)S(1)}, u32[]{:S(2)}, u32[]{:S(2)}) collective-permute-start(bf16[15,16,256]{2,1,0:T(8,128)(2,1)S(1)} %shard_map.139.refs_0_), channel_id=1, source_target_pairs={{0,4},{1,5},{2,6},{3,7},{4,0},{5,1},{6,2},{7,3},{8,12},{9,13},{10,... | collective-permute-start | bytes 368648 | tf_op jit(solution)/shard_map/ppermute | solution.py:139
  15.2 4.9 %collective-permute-done.3.refs_1_ = bf16[15,16,256]{2,1,0:T(8,128)(2,1)S(1)} collective-permute-done((bf16[15,16,256]{2,1,0:T(8,128)(2,1)S(1)}, bf16[15,16,256]{2,1,0:T(8,128)(2,1)S(1)}, u32[]{:S(2)}, u32[]{:S(2)}) %collective-permute-start.3) | collective-permute-done | bytes 122912 | tf_op jit(solution)/shard_map/ppermute | solution.py:139
  20.1 0.9 %collective-permute-done.5.refs_4_ = bf16[4,128,256]{2,1,0:T(8,128)(2,1)S(1)} collective-permute-done((bf16[4,128,256]{2,1,0:T(8,128)(2,1)S(1)}, bf16[4,128,256]{2,1,0:T(8,128)(2,1)S(1)}, u32[]{:S(2)}, u32[]{:S(2)}) %collective-permute-start.5) | collective-permute-done | bytes 262176 | tf_op jit(solution)/shard_map/ppermute | solution.py:143
  21.6 1.6 %collective-permute-start.8 = (bf16[4,64,256]{2,1,0:T(8,128)(2,1)S(1)}, bf16[4,64,256]{2,1,0:T(8,128)(2,1)S(1)}, u32[]{:S(2)}, u32[]{:S(2)}) collective-permute-start(bf16[4,64,256]{2,1,0:T(8,128)(2,1)S(1)} %get-tuple-element.46), channel_id=1, source_target_pairs={{0,8},{1,17},{2,10},{3,19},{4,12},{5,21},{6,14},{7,23},{8,0},{9,25... | collective-permute-start | bytes 393224 | tf_op jit(solution)/shard_map/ppermute | solution.py:143
  23.2 2.6 %collective-permute-start.6 = (bf16[2,15,16,256]{3,2,1,0:T(8,128)(2,1)S(1)}, bf16[2,15,16,256]{3,2,1,0:T(8,128)(2,1)S(1)}, u32[]{:S(2)}, u32[]{:S(2)}) collective-permute-start(bf16[2,15,16,256]{3,2,1,0:T(8,128)(2,1)S(1)} %get-tuple-element.43.refs_0_), channel_id=1, source_target_pairs={{0,2},{1,3},{2,0},{3,1},{4,6},{5,7},{6,4},{7,5},{8,10},{9,11},{10,... | collective-permute-start | bytes 737288 | tf_op jit(solution)/shard_map/ppermute | solution.py:139
  25.8 2.2 %collective-permute-done.8.refs_2_ = bf16[4,64,256]{2,1,0:T(8,128)(2,1)S(1)} collective-permute-done((bf16[4,64,256]{2,1,0:T(8,128)(2,1)S(1)}, bf16[4,64,256]{2,1,0:T(8,128)(2,1)S(1)}, u32[]{:S(2)}, u32[]{:S(2)}) %collective-permute-start.8) | collective-permute-done | bytes 131104 | tf_op jit(solution)/shard_map/ppermute | solution.py:143
  28.0 1.1 %collective-permute-done.7.refs_1_ = bf16[10,64,256]{2,1,0:T(8,128)(2,1)S(1)} collective-permute-done((bf16[10,64,256]{2,1,0:T(8,128)(2,1)S(1)}, bf16[10,64,256]{2,1,0:T(8,128)(2,1)S(1)}, u32[]{:S(2)}, u32[]{:S(2)}) %collective-permute-start.7) | collective-permute-done | bytes 327712 | tf_op jit(solution)/shard_map/ppermute | solution.py:143
  29.2 3.2 %collective-permute-start.9 = (bf16[10,32,256]{2,1,0:T(8,128)(2,1)S(1)}, bf16[10,32,256]{2,1,0:T(8,128)(2,1)S(1)}, u32[]{:S(2)}, u32[]{:S(2)}) collective-permute-start(bf16[10,32,256]{2,1,0:T(8,128)(2,1)S(1)} %get-tuple-element.48), channel_id=1, source_target_pairs={{0,2},{1,3},{2,0},{3,1},{4,6},{5,7},{6,4},{7,5},{8,10},{9,11},{10,... | collective-permute-start | bytes 491528 | tf_op jit(solution)/shard_map/ppermute | solution.py:143
  32.7 4.0 %collective-permute-done.10.refs_4_ = bf16[4,32,256]{2,1,0:T(8,128)(2,1)S(1)} collective-permute-done((bf16[4,32,256]{2,1,0:T(8,128)(2,1)S(1)}, bf16[4,32,256]{2,1,0:T(8,128)(2,1)S(1)}, u32[]{:S(2)}, u32[]{:S(2)}) %collective-permute-start.10) | collective-permute-done | bytes 65568 | tf_op jit(solution)/shard_map/ppermute | solution.py:143
  37.5 1.6 %collective-permute-start.12 = (bf16[14,32,256]{2,1,0:T(8,128)(2,1)S(1)}, bf16[14,32,256]{2,1,0:T(8,128)(2,1)S(1)}, u32[]{:S(2)}, u32[]{:S(2)}) collective-permute-start(bf16[14,32,256]{2,1,0:T(8,128)(2,1)S(1)} %get-tuple-element.52.refs_1_), channel_id=1, source_target_pairs={{0,4},{1,5},{2,6},{3,7},{4,0},{5,1},{6,2},{7,3},{8,12},{9,13},{10,... | collective-permute-start | bytes 688136 | tf_op jit(solution)/shard_map/ppermute | solution.py:139
  40.3 2.7 %shard_map.143 = (f32[32,128]{1,0:T(8,128)S(1)}, s32[224]{0:T(256)S(1)}) custom-call(s32[224]{0:T(256)S(1)} %copy-done.1, bf16[4,16,256]{2,1,0:T(8,128)(2,1)S(1)} %get-tuple-element.50.refs_1_, bf16[4,16,256]{2,1,0:T(8,128)(2,1)S(1)} %collective-permute-done.11.refs_2_), custom_call_target="tpu_custom_call" | custom-call | tf_op jit(solution)/shard_map/pallas_call | solution.py:603
  43.0 7.0 %collective-permute-done.12.refs_2_ = bf16[14,32,256]{2,1,0:T(8,128)(2,1)S(1)} collective-permute-done((bf16[14,32,256]{2,1,0:T(8,128)(2,1)S(1)}, bf16[14,32,256]{2,1,0:T(8,128)(2,1)S(1)}, u32[]{:S(2)}, u32[]{:S(2)}) %collective-permute-start.12) | collective-permute-done | bytes 229408 | tf_op jit(solution)/shard_map/ppermute | solution.py:139
  51.4 1.2 %collective-permute-start.17 = (bf16[5,32,256]{2,1,0:T(8,128)(2,1)S(1)}, bf16[5,32,256]{2,1,0:T(8,128)(2,1)S(1)}, u32[]{:S(2)}, u32[]{:S(2)}) collective-permute-start(bf16[5,32,256]{2,1,0:T(8,128)(2,1)S(1)} %get-tuple-element.57.refs_3_), channel_id=1, source_target_pairs={{0,16},{1,9},{2,18},{3,11},{4,20},{5,13},{6,22},{7,15},{8,24},{9,1... | collective-permute-start | bytes 245768 | tf_op jit(solution)/shard_map/ppermute | solution.py:143
  53.0 3.7 %collective-permute-done.17.refs_4_ = bf16[5,32,256]{2,1,0:T(8,128)(2,1)S(1)} collective-permute-done((bf16[5,32,256]{2,1,0:T(8,128)(2,1)S(1)}, bf16[5,32,256]{2,1,0:T(8,128)(2,1)S(1)}, u32[]{:S(2)}, u32[]{:S(2)}) %collective-permute-start.17) | collective-permute-done | bytes 81952 | tf_op jit(solution)/shard_map/ppermute | solution.py:143
  57.2 1.7 %collective-permute-start.18 = (bf16[10,64,256]{2,1,0:T(8,128)(2,1)S(1)}, bf16[10,64,256]{2,1,0:T(8,128)(2,1)S(1)}, u32[]{:S(2)}, u32[]{:S(2)}) collective-permute-start(bf16[10,64,256]{2,1,0:T(8,128)(2,1)S(1)} %get-tuple-element.58.refs_1_), channel_id=1, source_target_pairs={{0,16},{1,9},{2,18},{3,11},{4,20},{5,13},{6,22},{7,15},{8,24},{9,1... | collective-permute-start | bytes 983048 | tf_op jit(solution)/shard_map/ppermute | solution.py:143
  58.9 0.9 %collective-permute-start.19 = (bf16[5,64,256]{2,1,0:T(8,128)(2,1)S(1)}, bf16[5,64,256]{2,1,0:T(8,128)(2,1)S(1)}, u32[]{:S(2)}, u32[]{:S(2)}) collective-permute-start(bf16[5,64,256]{2,1,0:T(8,128)(2,1)S(1)} %get-tuple-element.59.refs_3_), channel_id=1, source_target_pairs={{0,8},{1,17},{2,10},{3,19},{4,12},{5,21},{6,14},{7,23},{8,0},{9,25... | collective-permute-start | bytes 491528 | tf_op jit(solution)/shard_map/ppermute | solution.py:143
  59.8 5.4 %collective-permute-done.19.refs_4_ = bf16[5,64,256]{2,1,0:T(8,128)(2,1)S(1)} collective-permute-done((bf16[5,64,256]{2,1,0:T(8,128)(2,1)S(1)}, bf16[5,64,256]{2,1,0:T(8,128)(2,1)S(1)}, u32[]{:S(2)}, u32[]{:S(2)}) %collective-permute-start.19) | collective-permute-done | bytes 163872 | tf_op jit(solution)/shard_map/ppermute | solution.py:143
  65.4 1.3 %collective-permute-start.23 = (bf16[10,128,256]{2,1,0:T(8,128)(2,1)S(1)}, bf16[10,128,256]{2,1,0:T(8,128)(2,1)S(1)}, u32[]{:S(2)}, u32[]{:S(2)}) collective-permute-start(bf16[10,128,256]{2,1,0:T(8,128)(2,1)S(1)} %get-tuple-element.62.refs_1_), channel_id=1, source_target_pairs={{0,8},{1,17},{2,10},{3,19},{4,12},{5,21},{6,14},{7,23},{8,0},{9,25... | collective-permute-start | bytes 1966088 | tf_op jit(solution)/shard_map/ppermute | solution.py:143
  66.7 1.7 %collective-permute-start.24 = (bf16[5,128,256]{2,1,0:T(8,128)(2,1)S(1)}, bf16[5,128,256]{2,1,0:T(8,128)(2,1)S(1)}, u32[]{:S(2)}, u32[]{:S(2)}) collective-permute-start(bf16[5,128,256]{2,1,0:T(8,128)(2,1)S(1)} %get-tuple-element.63.refs_3_), channel_id=1, source_target_pairs={{0,2},{1,3},{2,0},{3,1},{4,6},{5,7},{6,4},{7,5},{8,10},{9,11},{10,... | collective-permute-start | bytes 983048 | tf_op jit(solution)/shard_map/ppermute | solution.py:143
  69.0 1.0 %collective-permute-done.21.refs_5_ = bf16[2,224,256]{2,1,0:T(8,128)(2,1)S(1)} collective-permute-done((bf16[2,224,256]{2,1,0:T(8,128)(2,1)S(1)}, bf16[2,224,256]{2,1,0:T(8,128)(2,1)S(1)}, u32[]{:S(2)}, u32[]{:S(2)}) %collective-permute-start.21) | collective-permute-done | bytes 229408 | tf_op jit(solution)/shard_map/ppermute | solution.py:139
  70.3 1.0 %shard_map.148.refs_0_.refs_1_.refs_4_ = bf16[7168,256]{1,0:T(8,128)(2,1)S(1)} custom-call(s32[224]{0:T(256)S(1)} %copy-done.1, bf16[3,4,224,256]{3,2,1,0:T(8,128)(2,1)S(1)} %get-tuple-element.55.refs_1_, bf16[2,224,256]{2,1,0:T(8,128)(2,1)S(1)} %get-tuple-element.60.refs_2_, bf16[2,224,256]{2,1,0:T(8,128)(2,1)S(1)} %get-tuple-element.61.refs_3_, ...), custom_call_target="tpu_custom_call" | custom-call | bytes 8388608 | tf_op jit(solution)/shard_map/pallas_call | solution.py:641
  71.3 4.8 %collective-permute-done.24.refs_4_ = bf16[5,128,256]{2,1,0:T(8,128)(2,1)S(1)} collective-permute-done((bf16[5,128,256]{2,1,0:T(8,128)(2,1)S(1)}, bf16[5,128,256]{2,1,0:T(8,128)(2,1)S(1)}, u32[]{:S(2)}, u32[]{:S(2)}) %collective-permute-start.24) | collective-permute-done | bytes 327712 | tf_op jit(solution)/shard_map/ppermute | solution.py:143
  76.3 1.1 %shard_map.151.refs_9_ = f32[512,256]{1,0:T(8,128)S(1)} custom-call(bf16[3456,256]{1,0:T(8,128)(2,1)S(1)} %shard_map.144.refs_0_.refs_3_, bf16[15,256,256]{2,1,0:T(8,128)(2,1)S(1)} %shard_map.149.refs_1_.refs_6_), custom_call_target="tpu_custom_call" | custom-call | flops 939524096 | bytes 4194304 | tf_op jit(solution)/shard_map/pallas_call | solution.py:653
  77.5 2.0 %shard_map.150.refs_8_ = f32[512,256]{1,0:T(8,128)S(1)} custom-call(bf16[3456,256]{1,0:T(8,128)(2,1)S(1)} %shard_map.144.refs_0_.refs_3_, bf16[7168,256]{1,0:T(8,128)(2,1)S(1)} %shard_map.148.refs_0_.refs_1_.refs_4_), custom_call_target="tpu_custom_call" | custom-call | flops 1811939328 | bytes 6291456 | tf_op jit(solution)/shard_map/pallas_call | solution.py:646
  79.5 0.8 collective-permute-done.25.refs_7_
  80.3 3.1 %shard_map.152 = (f32[896,256]{1,0:T(8,128)}, f32[896,256]{1,0:T(8,128)}, f32[7,128]{1,0:T(8,128)}, f32[2,256]{1,0:T(2,128)}, bf16[512,256]{1,0:T(8,128)(2,1)}) custom-call(s32[224]{0:T(256)S(1)} %get-tuple-element.51.refs_0_, f32[1]{0:T(128)S(6)} %sub.3.refs_0_.refs_1_, f32[2,256]{1,0:T(2,128)S(1)} %copy-done.2, ...), custom_call_target="tpu_custom_call" | custom-call | flops 1073741824 | bytes 16777216 | tf_op jit(solution)/shard_map/pallas_call | solution.py:668
  (47 shorter events, 6.8 us)
Async XLA Ops:
  0.6 3.7 %collective-permute-start = (bf16[1,4,18,18,256]{4,1,3,2,0:T(4,128)(2,1)}, bf16[1,4,18,18,256]{4,1,3,2,0:T(4,128)(2,1)S(1)}, u32[]{:S(2)}, u32[]{:S(2)}) collective-permute-start(bf16[1,4,18,18,256]{4,1,3,2,0:T(4,128)(2,1)} %param.12), channel_id=1, source_target_pairs={{0,1},{1,0},{2,3},{3,2},{4,5},{5,4},{6,7},{7,6},{8,9},{9,8},{10,11... | collective-permute-start | bytes 1990664 | tf_op jit(solution)/shard_map/ppermute | solution.py:139
  1.1 3.3 %collective-permute-start.1 = (bf16[512,256]{1,0:T(8,128)(2,1)}, bf16[512,256]{1,0:T(8,128)(2,1)S(1)}, u32[]{:S(2)}, u32[]{:S(2)}) collective-permute-start(bf16[512,256]{1,0:T(8,128)(2,1)} %refs_1_.2), channel_id=1, source_target_pairs={{0,1},{1,0},{2,3},{3,2},{4,5},{5,4},{6,7},{7,6},{8,9},{9,8},{10,11... | collective-permute-start | bytes 786440 | tf_op jit(solution)/shard_map/ppermute | solution.py:139
  1.2 3.2 %collective-permute-start.2 = (bf16[512,256]{1,0:T(8,128)(2,1)}, bf16[512,256]{1,0:T(8,128)(2,1)S(1)}, u32[]{:S(2)}, u32[]{:S(2)}) collective-permute-start(bf16[512,256]{1,0:T(8,128)(2,1)} %refs_2_.2), channel_id=1, source_target_pairs={{0,1},{1,0},{2,3},{3,2},{4,5},{5,4},{6,7},{7,6},{8,9},{9,8},{10,11... | collective-permute-start | bytes 786440 | tf_op jit(solution)/shard_map/ppermute | solution.py:139
  7.4 13.7 %collective-permute-start.4 = (bf16[10,128,256]{2,1,0:T(8,128)(2,1)S(1)}, bf16[10,128,256]{2,1,0:T(8,128)(2,1)S(1)}, u32[]{:S(2)}, u32[]{:S(2)}) collective-permute-start(bf16[10,128,256]{2,1,0:T(8,128)(2,1)S(1)} %get-tuple-element.41), channel_id=1, source_target_pairs={{0,8},{1,17},{2,10},{3,19},{4,12},{5,21},{6,14},{7,23},{8,0},{9,25... | collective-permute-start | bytes 1966088 | tf_op jit(solution)/shard_map/ppermute | solution.py:143
  10.0 11.0 %collective-permute-start.5 = (bf16[4,128,256]{2,1,0:T(8,128)(2,1)S(1)}, bf16[4,128,256]{2,1,0:T(8,128)(2,1)S(1)}, u32[]{:S(2)}, u32[]{:S(2)}) collective-permute-start(bf16[4,128,256]{2,1,0:T(8,128)(2,1)S(1)} %get-tuple-element.42), channel_id=1, source_target_pairs={{0,2},{1,3},{2,0},{3,1},{4,6},{5,7},{6,4},{7,5},{8,10},{9,11},{10,... | collective-permute-start | bytes 786440 | tf_op jit(solution)/shard_map/ppermute | solution.py:143
  12.5 27.7 %copy-start.1 = (s32[224]{0:T(256)S(1)}, s32[224]{0:T(256)}, u32[]{:S(2)}) copy-start(s32[224]{0:T(256)} %refs_0_.3) | copy-start | bytes 2692
  12.6 7.5 %collective-permute-start.3 = (bf16[15,16,256]{2,1,0:T(8,128)(2,1)S(1)}, bf16[15,16,256]{2,1,0:T(8,128)(2,1)S(1)}, u32[]{:S(2)}, u32[]{:S(2)}) collective-permute-start(bf16[15,16,256]{2,1,0:T(8,128)(2,1)S(1)} %shard_map.139.refs_0_), channel_id=1, source_target_pairs={{0,4},{1,5},{2,6},{3,7},{4,0},{5,1},{6,2},{7,3},{8,12},{9,13},{10,... | collective-permute-start | bytes 368648 | tf_op jit(solution)/shard_map/ppermute | solution.py:139
  21.2 31.4 %copy-start.3 = (bf16[1,4,18,18,256]{4,1,3,2,0:T(4,128)(2,1)S(1)}, bf16[1,4,18,18,256]{4,1,3,2,0:T(4,128)(2,1)}, u32[]{:S(2)}) copy-start(bf16[1,4,18,18,256]{4,1,3,2,0:T(4,128)(2,1)} %param.19) | copy-start | bytes 1990660
  21.2 8.0 %collective-permute-start.7 = (bf16[10,64,256]{2,1,0:T(8,128)(2,1)S(1)}, bf16[10,64,256]{2,1,0:T(8,128)(2,1)S(1)}, u32[]{:S(2)}, u32[]{:S(2)}) collective-permute-start(bf16[10,64,256]{2,1,0:T(8,128)(2,1)S(1)} %get-tuple-element.45), channel_id=1, source_target_pairs={{0,16},{1,9},{2,18},{3,11},{4,20},{5,13},{6,22},{7,15},{8,24},{9,1... | collective-permute-start | bytes 983048 | tf_op jit(solution)/shard_map/ppermute | solution.py:143
  21.6 6.4 %collective-permute-start.8 = (bf16[4,64,256]{2,1,0:T(8,128)(2,1)S(1)}, bf16[4,64,256]{2,1,0:T(8,128)(2,1)S(1)}, u32[]{:S(2)}, u32[]{:S(2)}) collective-permute-start(bf16[4,64,256]{2,1,0:T(8,128)(2,1)S(1)} %get-tuple-element.46), channel_id=1, source_target_pairs={{0,8},{1,17},{2,10},{3,19},{4,12},{5,21},{6,14},{7,23},{8,0},{9,25... | collective-permute-start | bytes 393224 | tf_op jit(solution)/shard_map/ppermute | solution.py:143
  23.2 9.5 %collective-permute-start.6 = (bf16[2,15,16,256]{3,2,1,0:T(8,128)(2,1)S(1)}, bf16[2,15,16,256]{3,2,1,0:T(8,128)(2,1)S(1)}, u32[]{:S(2)}, u32[]{:S(2)}) collective-permute-start(bf16[2,15,16,256]{3,2,1,0:T(8,128)(2,1)S(1)} %get-tuple-element.43.refs_0_), channel_id=1, source_target_pairs={{0,2},{1,3},{2,0},{3,1},{4,6},{5,7},{6,4},{7,5},{8,10},{9,11},{10,... | collective-permute-start | bytes 737288 | tf_op jit(solution)/shard_map/ppermute | solution.py:139
  29.2 7.5 %collective-permute-start.9 = (bf16[10,32,256]{2,1,0:T(8,128)(2,1)S(1)}, bf16[10,32,256]{2,1,0:T(8,128)(2,1)S(1)}, u32[]{:S(2)}, u32[]{:S(2)}) collective-permute-start(bf16[10,32,256]{2,1,0:T(8,128)(2,1)S(1)} %get-tuple-element.48), channel_id=1, source_target_pairs={{0,2},{1,3},{2,0},{3,1},{4,6},{5,7},{6,4},{7,5},{8,10},{9,11},{10,... | collective-permute-start | bytes 491528 | tf_op jit(solution)/shard_map/ppermute | solution.py:143
  32.4 4.3 %collective-permute-start.10 = (bf16[4,32,256]{2,1,0:T(8,128)(2,1)S(1)}, bf16[4,32,256]{2,1,0:T(8,128)(2,1)S(1)}, u32[]{:S(2)}, u32[]{:S(2)}) collective-permute-start(bf16[4,32,256]{2,1,0:T(8,128)(2,1)S(1)} %get-tuple-element.49), channel_id=1, source_target_pairs={{0,16},{1,9},{2,18},{3,11},{4,20},{5,13},{6,22},{7,15},{8,24},{9,1... | collective-permute-start | bytes 196616 | tf_op jit(solution)/shard_map/ppermute | solution.py:143
  36.7 13.2 %collective-permute-start.14 = (bf16[4,224,256]{2,1,0:T(8,128)(2,1)S(1)}, bf16[4,224,256]{2,1,0:T(8,128)(2,1)S(1)}, u32[]{:S(2)}, u32[]{:S(2)}) collective-permute-start(bf16[4,224,256]{2,1,0:T(8,128)(2,1)S(1)} %get-tuple-element.54.refs_4_), channel_id=1, source_target_pairs={{0,8},{1,17},{2,10},{3,19},{4,12},{5,21},{6,14},{7,23},{8,0},{9,25... | collective-permute-start | bytes 1376264 | tf_op jit(solution)/shard_map/ppermute | solution.py:143
  37.3 12.6 %collective-permute-start.13 = (bf16[4,224,256]{2,1,0:T(8,128)(2,1)S(1)}, bf16[4,224,256]{2,1,0:T(8,128)(2,1)S(1)}, u32[]{:S(2)}, u32[]{:S(2)}) collective-permute-start(bf16[4,224,256]{2,1,0:T(8,128)(2,1)S(1)} %get-tuple-element.54.refs_4_), channel_id=1, source_target_pairs={{0,16},{1,9},{2,18},{3,11},{4,20},{5,13},{6,22},{7,15},{8,24},{9,1... | collective-permute-start | bytes 1376264 | tf_op jit(solution)/shard_map/ppermute | solution.py:143
  37.5 12.5 %collective-permute-start.12 = (bf16[14,32,256]{2,1,0:T(8,128)(2,1)S(1)}, bf16[14,32,256]{2,1,0:T(8,128)(2,1)S(1)}, u32[]{:S(2)}, u32[]{:S(2)}) collective-permute-start(bf16[14,32,256]{2,1,0:T(8,128)(2,1)S(1)} %get-tuple-element.52.refs_1_), channel_id=1, source_target_pairs={{0,4},{1,5},{2,6},{3,7},{4,0},{5,1},{6,2},{7,3},{8,12},{9,13},{10,... | collective-permute-start | bytes 688136 | tf_op jit(solution)/shard_map/ppermute | solution.py:139
  39.1 1.2 %collective-permute-start.11 = (bf16[4,16,256]{2,1,0:T(8,128)(2,1)S(1)}, bf16[4,16,256]{2,1,0:T(8,128)(2,1)S(1)}, u32[]{:S(2)}, u32[]{:S(2)}) collective-permute-start(bf16[4,16,256]{2,1,0:T(8,128)(2,1)S(1)} %get-tuple-element.50.refs_1_), channel_id=1, source_target_pairs={{0,1},{1,0},{2,3},{3,2},{4,5},{5,4},{6,7},{7,6},{8,9},{9,8},{10,11... | collective-permute-start | bytes 98312 | tf_op jit(solution)/shard_map/ppermute | solution.py:139
  50.4 19.9 %collective-permute-start.20 = (bf16[3,4,224,256]{3,2,1,0:T(8,128)(2,1)S(1)}, bf16[3,4,224,256]{3,2,1,0:T(8,128)(2,1)S(1)}, u32[]{:S(2)}, u32[]{:S(2)}) collective-permute-start(bf16[3,4,224,256]{3,2,1,0:T(8,128)(2,1)S(1)} %get-tuple-element.55.refs_1_), channel_id=1, source_target_pairs={{0,1},{1,0},{2,3},{3,2},{4,5},{5,4},{6,7},{7,6},{8,9},{9,8},{10,11... | collective-permute-start | bytes 4128776 | tf_op jit(solution)/shard_map/ppermute | solution.py:139
  50.5 6.6 %collective-permute-start.16 = (bf16[10,32,256]{2,1,0:T(8,128)(2,1)S(1)}, bf16[10,32,256]{2,1,0:T(8,128)(2,1)S(1)}, u32[]{:S(2)}, u32[]{:S(2)}) collective-permute-start(bf16[10,32,256]{2,1,0:T(8,128)(2,1)S(1)} %get-tuple-element.56.refs_1_), channel_id=1, source_target_pairs={{0,2},{1,3},{2,0},{3,1},{4,6},{5,7},{6,4},{7,5},{8,10},{9,11},{10,... | collective-permute-start | bytes 491528 | tf_op jit(solution)/shard_map/ppermute | solution.py:143
  50.6 14.7 %collective-permute-start.15 = (bf16[4,224,256]{2,1,0:T(8,128)(2,1)S(1)}, bf16[4,224,256]{2,1,0:T(8,128)(2,1)S(1)}, u32[]{:S(2)}, u32[]{:S(2)}) collective-permute-start(bf16[4,224,256]{2,1,0:T(8,128)(2,1)S(1)} %collective-permute-done.13.refs_5_), channel_id=1, source_target_pairs={{0,8},{1,17},{2,10},{3,19},{4,12},{5,21},{6,14},{7,23},{8,0},{9,25... | collective-permute-start | bytes 1376264 | tf_op jit(solution)/shard_map/ppermute | solution.py:143
  51.4 5.4 %collective-permute-start.17 = (bf16[5,32,256]{2,1,0:T(8,128)(2,1)S(1)}, bf16[5,32,256]{2,1,0:T(8,128)(2,1)S(1)}, u32[]{:S(2)}, u32[]{:S(2)}) collective-permute-start(bf16[5,32,256]{2,1,0:T(8,128)(2,1)S(1)} %get-tuple-element.57.refs_3_), channel_id=1, source_target_pairs={{0,16},{1,9},{2,18},{3,11},{4,20},{5,13},{6,22},{7,15},{8,24},{9,1... | collective-permute-start | bytes 245768 | tf_op jit(solution)/shard_map/ppermute | solution.py:143
  57.2 8.1 %collective-permute-start.18 = (bf16[10,64,256]{2,1,0:T(8,128)(2,1)S(1)}, bf16[10,64,256]{2,1,0:T(8,128)(2,1)S(1)}, u32[]{:S(2)}, u32[]{:S(2)}) collective-permute-start(bf16[10,64,256]{2,1,0:T(8,128)(2,1)S(1)} %get-tuple-element.58.refs_1_), channel_id=1, source_target_pairs={{0,16},{1,9},{2,18},{3,11},{4,20},{5,13},{6,22},{7,15},{8,24},{9,1... | collective-permute-start | bytes 983048 | tf_op jit(solution)/shard_map/ppermute | solution.py:143
  58.9 6.4 %collective-permute-start.19 = (bf16[5,64,256]{2,1,0:T(8,128)(2,1)S(1)}, bf16[5,64,256]{2,1,0:T(8,128)(2,1)S(1)}, u32[]{:S(2)}, u32[]{:S(2)}) collective-permute-start(bf16[5,64,256]{2,1,0:T(8,128)(2,1)S(1)} %get-tuple-element.59.refs_3_), channel_id=1, source_target_pairs={{0,8},{1,17},{2,10},{3,19},{4,12},{5,21},{6,14},{7,23},{8,0},{9,25... | collective-permute-start | bytes 491528 | tf_op jit(solution)/shard_map/ppermute | solution.py:143
  65.4 10.7 %collective-permute-start.23 = (bf16[10,128,256]{2,1,0:T(8,128)(2,1)S(1)}, bf16[10,128,256]{2,1,0:T(8,128)(2,1)S(1)}, u32[]{:S(2)}, u32[]{:S(2)}) collective-permute-start(bf16[10,128,256]{2,1,0:T(8,128)(2,1)S(1)} %get-tuple-element.62.refs_1_), channel_id=1, source_target_pairs={{0,8},{1,17},{2,10},{3,19},{4,12},{5,21},{6,14},{7,23},{8,0},{9,25... | collective-permute-start | bytes 1966088 | tf_op jit(solution)/shard_map/ppermute | solution.py:143
  66.7 9.3 %collective-permute-start.24 = (bf16[5,128,256]{2,1,0:T(8,128)(2,1)S(1)}, bf16[5,128,256]{2,1,0:T(8,128)(2,1)S(1)}, u32[]{:S(2)}, u32[]{:S(2)}) collective-permute-start(bf16[5,128,256]{2,1,0:T(8,128)(2,1)S(1)} %get-tuple-element.63.refs_3_), channel_id=1, source_target_pairs={{0,2},{1,3},{2,0},{3,1},{4,6},{5,7},{6,4},{7,5},{8,10},{9,11},{10,... | collective-permute-start | bytes 983048 | tf_op jit(solution)/shard_map/ppermute | solution.py:143
  68.5 1.5 %collective-permute-start.21 = (bf16[2,224,256]{2,1,0:T(8,128)(2,1)S(1)}, bf16[2,224,256]{2,1,0:T(8,128)(2,1)S(1)}, u32[]{:S(2)}, u32[]{:S(2)}) collective-permute-start(bf16[2,224,256]{2,1,0:T(8,128)(2,1)S(1)} %get-tuple-element.60.refs_2_), channel_id=1, source_target_pairs={{0,1},{1,0},{2,3},{3,2},{4,5},{5,4},{6,7},{7,6},{8,9},{9,8},{10,11... | collective-permute-start | bytes 688136 | tf_op jit(solution)/shard_map/ppermute | solution.py:139
  68.5 1.8 %collective-permute-start.22 = (bf16[2,224,256]{2,1,0:T(8,128)(2,1)S(1)}, bf16[2,224,256]{2,1,0:T(8,128)(2,1)S(1)}, u32[]{:S(2)}, u32[]{:S(2)}) collective-permute-start(bf16[2,224,256]{2,1,0:T(8,128)(2,1)S(1)} %get-tuple-element.61.refs_3_), channel_id=1, source_target_pairs={{0,1},{1,0},{2,3},{3,2},{4,5},{5,4},{6,7},{7,6},{8,9},{9,8},{10,11... | collective-permute-start | bytes 688136 | tf_op jit(solution)/shard_map/ppermute | solution.py:139
  76.2 4.0 %collective-permute-start.25 = (bf16[15,256,256]{2,1,0:T(8,128)(2,1)S(1)}, bf16[15,256,256]{2,1,0:T(8,128)(2,1)S(1)}, u32[]{:S(2)}, u32[]{:S(2)}) collective-permute-start(bf16[15,256,256]{2,1,0:T(8,128)(2,1)S(1)} %shard_map.149.refs_1_.refs_6_), channel_id=1, source_target_pairs={{0,1},{1,0},{2,3},{3,2},{4,5},{5,4},{6,7},{7,6},{8,9},{9,8},{10,11... | collective-permute-start | bytes 5898248 | tf_op jit(solution)/shard_map/ppermute | solution.py:139
  77.5 2.8 %copy-start = (f32[896,256]{1,0:T(8,128)S(1)}, f32[896,256]{1,0:T(8,128)}, u32[]{:S(2)}) copy-start(f32[896,256]{1,0:T(8,128)} %refs_5_.1) | copy-start | bytes 2752516
  77.5 2.8 %copy-start.2 = (f32[2,256]{1,0:T(2,128)S(1)}, f32[2,256]{1,0:T(2,128)}, u32[]{:S(2)}) copy-start(f32[2,256]{1,0:T(2,128)} %refs_2_.3) | copy-start | bytes 6148
